TPU v7x, 32 devices: a whole 2x2x4 slice. The times are simulated.
32 devices in a mesh: groups: 2 (over y), tile: 4 (over z), sub: 4 (over x, core).
Axes of the slice: x: 2, y: 2, z: 4, core: 2. Of those that a mesh axis runs over, the one named last changes fastest.
Arguments:
- embeddings: bfloat16 [16384, 1024], P(('groups', 'tile')), parts along dimension 0, may hold values from -12 to 12
- cluster_ids: int32 [16384], P(('groups', 'tile')), parts along dimension 0, may hold values from -1 to 1, as said below
Outputs:
- scores: float32 [16384], P(('groups', 'tile', 'sub')), parts along dimension 0
There are 2 independent parts, one for each index of `groups`. A program takes and returns all parts, laid end to end along the dimension named above; each array names one. Nothing has to cross between parts.
Inputs may be any that keep to these rules, and one draw needn't show every extreme that they name: `cluster_ids`: each cluster occupies consecutive whole blocks of 128 rows in increasing order of cluster number, every cluster from 0 to 1 present; inside a cluster's last block the unused rows at its end are -1, and only there. The rows of one cluster lie on at most 4 consecutive indices of tile.
All inputs are finite; a program needn't handle non-finite values.
Results may differ from a plain program's by a relative error of at most 0.00087.
Values may be sent and summed in bfloat16 or wider, within the bound.
No kernel may reach another device: no remote copies, remote signals or barrier semaphores. Data moves between devices by JAX's collectives and lax.ppermute only.
A program may use at most 128 MiB of HBM per device.

v0:
```python
import jax
import jax.numpy as jnp
from jax import lax
from jax.sharding import PartitionSpec as P

SPAN = 4


inverse_temp = 10.0
norm_eps = 1e-06


def unit_rows(embeddings):
    values = embeddings.astype(jnp.float32)
    scale = lax.rsqrt(jnp.sum(values * values, axis=1, keepdims=True) + norm_eps)
    return (values * scale).astype(jnp.bfloat16)


def pair_terms(unit, tags, piece, piece_tags, order):
    same = (tags[:, None] == piece_tags[None, :]) & (tags[:, None] > 0) & order
    cosine = lax.dot_general(
        unit, piece, (((1,), (1,)), ((), ())), preferred_element_type=jnp.float32
    )
    weight = jnp.where(same, jnp.exp(inverse_temp * (cosine - 1.0)), 0.0)
    return (jnp.sum(weight, axis=1), jnp.sum(weight, axis=0))


def shards(embeddings, cluster_ids):
    unit = unit_rows(embeddings)
    tags = cluster_ids + 1
    groups = lax.axis_size("sub")
    member = lax.axis_index("sub")
    owners = lax.axis_size("tile")
    place = lax.axis_index("tile")
    rows_here = unit.shape[0]
    width = rows_here // groups
    own_piece = lax.dynamic_slice_in_dim(unit, member * width, width, 0)
    own_tags = lax.dynamic_slice_in_dim(tags, member * width, width, 0)
    offsets = list(range(1 - SPAN, SPAN))
    lowest = offsets[0]
    highest = offsets[-1]
    distance = place - jnp.arange(owners, dtype=jnp.int32)
    keep = (distance >= lowest) & (distance <= highest) & (distance != 0)
    outgoing = jnp.where(keep[:, None, None], own_piece[None, :, :], jnp.zeros((), jnp.bfloat16))
    outgoing_tags = jnp.where(keep[:, None], own_tags[None, :], 0)
    arrived, arrived_tags = (
        lax.all_to_all(outgoing, "tile", split_axis=0, concat_axis=0, tiled=True),
        lax.all_to_all(outgoing_tags, "tile", split_axis=0, concat_axis=0, tiled=True),
    )
    local_rows = jnp.arange(rows_here, dtype=jnp.int32)[:, None]
    slice_rows = member * width + jnp.arange(width, dtype=jnp.int32)[None, :]
    everywhere = jnp.ones((rows_here, width), dtype=bool)
    row_total = jnp.zeros((rows_here,), jnp.float32)
    column_sums = []
    for offset in offsets:
        if offset == 0:
            piece, piece_tags = (own_piece, own_tags)
            order = local_rows != slice_rows
        else:
            source = place + offset
            valid = (source >= 0) & (source < owners)
            index = jnp.clip(source, 0, owners - 1)
            fetch_piece = lax.dynamic_index_in_dim(arrived, index, 0, keepdims=False)
            fetch_piece_tags = lax.dynamic_index_in_dim(arrived_tags, index, 0, keepdims=False)
            piece = fetch_piece
            piece_tags = jnp.where(valid, fetch_piece_tags, 0)
            order = everywhere
        row_part, column_part = pair_terms(unit, tags, piece, piece_tags, order)
        row_total = row_total + row_part
        column_sums.append(column_part)
    density = lax.psum_scatter(row_total, "sub", scatter_dimension=0, tiled=True)
    return jnp.log(1.0 + density)


def solution(mesh):
    in_specs = (P(("groups", "tile"), None), P(("groups", "tile")))
    out_specs = P(("groups", "tile", "sub"))
    return jax.shard_map(shards, mesh=mesh, in_specs=in_specs, out_specs=out_specs, check_vma=False)
```

profile of v0, /device:TPU:0, one launch (start us, length us, event | category | flops | bytes accessed | tf_op | source)
XLA Modules:
  0.0 149.4 jit_solution(16951307898386843363)
XLA Ops:
  0.0 0.7 broadcast_add_fusion
  0.7 0.1 dynamic_slice.44
  0.8 0.7 broadcast_select_fusion.1
  1.5 6.3 %all-to-all-start = ((s32[4,1,512]{2,1,0:T(1,128)}), s32[4,1,512]{2,1,0:T(1,128)S(1)}, u32[]{:S(2)}, u32[]{:S(2)}) async-start(s32[4,1,512]{2,1,0:T(1,128)} %broadcast_select_fusion.1), calls=%async_computation | async-start | bytes 16384 | tf_op jit(solution)/shard_map/all_to_all | solution.py:48
  7.8 0.0 copy-start
  7.8 3.2 %fusion = f32[2048]{0:T(1024)S(1)} fusion(bf16[2048,1024]{1,0:T(8,128)(2,1)} %param.2), kind=kLoop, calls=%fused_computation.2 | loop fusion | flops 6289408 | bytes 4202496 | tf_op jit(solution)/shard_map/reduce_sum | solution.py:15
  11.0 0.2 copy-done
  11.2 0.7 fusion.1
  12.0 0.0 copy-start.1
  12.0 1.9 %copy-done.1 = bf16[2048,1024]{1,0:T(8,128)(2,1)} copy-done((bf16[2048,1024]{1,0:T(8,128)(2,1)}, bf16[2048,1024]{1,0:T(8,128)(2,1)S(1)}, u32[]{:S(2)}) %copy-start.1) | copy-done | bytes 4194328
  13.9 0.1 constant_dynamic-slice_fusion.5
  14.0 2.3 %broadcast_select_fusion = bf16[4,512,1024]{2,1,0:T(8,128)(2,1)} fusion(pred[4]{0:T(512)(128)(4,1)S(1)} %compare_and_fusion, bf16[512,1024]{1,0:T(8,128)(2,1)S(1)} %constant_dynamic-slice_fusion.5), kind=kLoop, calls=%fused_computation.12 | loop fusion | flops 2097152 | bytes 5242884 | tf_op jit(solution)/shard_map/jit(_where)/select_n | solution.py:44
  16.3 0.0 copy-start.4
  16.3 0.0 copy-start.3
  16.3 0.0 all-to-all-done
  16.3 5.2 %all-to-all-start.1 = ((bf16[4,512,1024]{2,1,0:T(8,128)(2,1)}), bf16[4,512,1024]{2,1,0:T(8,128)(2,1)}, u32[]{:S(2)}, u32[]{:S(2)}) async-start(bf16[4,512,1024]{2,1,0:T(8,128)(2,1)} %broadcast_select_fusion), calls=%async_computation.1 | async-start | bytes 8388608 | tf_op jit(solution)/shard_map/all_to_all | solution.py:47
  21.5 0.0 copy-done.4
  21.5 0.6 dynamic-slice.6
  22.8 0.0 copy-done.3
  22.8 6.2 %select_reduce_fusion.3 = f32[2048]{0:T(1024)S(1)} fusion(bf16[2048,1024]{1,0:T(8,128)(2,1)} %copy-done.1, bf16[512,1024]{1,0:T(8,128)(2,1)S(1)} %constant_dynamic-slice_fusion.5, s32[512]{0:T(512)S(1)} %iota_add_fusion, s32[2048]{0:T(1024)S(1)} %broadcast_add_fusion, s32[512]{0:T(512)S(1)} %dynamic_slice.44, pred[2048]{0:T(1024)(128)(4,1)S(1)} %broadcast_compare_fusion), kind=kOutput, calls=%fused_computation.7 | convolution fusion | flops 2155870208 | bytes 5265408 | tf_op jit(solution)/shard_map/dot_general | solution.py:21
  29.0 85.5 %all-to-all-done.1 = bf16[4,512,1024]{2,1,0:T(8,128)(2,1)} async-done(((bf16[4,512,1024]{2,1,0:T(8,128)(2,1)}), bf16[4,512,1024]{2,1,0:T(8,128)(2,1)}, u32[]{:S(2)}, u32[]{:S(2)}) %all-to-all-start.1) | async-done | bytes 4194336 | tf_op jit(solution)/shard_map/all_to_all | solution.py:47
  114.5 0.0 copy-start.2
  114.5 5.8 %select_reduce_fusion = f32[2048]{0:T(1024)S(1)} fusion(bf16[2048,1024]{1,0:T(8,128)(2,1)} %copy-done.1, s32[2048]{0:T(1024)S(1)} %broadcast_add_fusion, s32[512]{0:T(512)S(1)} %bitcast.38, pred[2048]{0:T(1024)(128)(4,1)S(1)} %broadcast_compare_fusion, bf16[4,512,1024]{2,1,0:T(8,128)(2,1)} %all-to-all-done.1, s32[]{:T(128)S(6)} %min.24), kind=kOutput, calls=%fused_computation.4 | convolution fusion | flops 2153773056 | bytes 5263364 | tf_op jit(solution)/shard_map/dot_general | solution.py:21
  120.4 0.0 copy-done.2
  120.4 4.4 %select_reduce_fusion.1 = f32[2048]{0:T(1024)S(1)} fusion(bf16[2048,1024]{1,0:T(8,128)(2,1)S(1)} %copy-done.2, s32[2048]{0:T(1024)S(1)} %broadcast_add_fusion, s32[512]{0:T(512)S(1)} %bitcast.37, pred[2048]{0:T(1024)(128)(4,1)S(1)} %broadcast_compare_fusion, bf16[4,512,1024]{2,1,0:T(8,128)(2,1)} %all-to-all-done.1, s32[]{:T(128)S(6)} %min.23), kind=kOutput, calls=%fused_computation.5 | convolution fusion | flops 2153773056 | bytes 5263364 | tf_op jit(solution)/shard_map/dot_general | solution.py:21
  124.8 4.4 %select_reduce_fusion.2 = f32[2048]{0:T(1024)S(1)} fusion(bf16[2048,1024]{1,0:T(8,128)(2,1)S(1)} %copy-done.2, s32[2048]{0:T(1024)S(1)} %broadcast_add_fusion, s32[512]{0:T(512)S(1)} %bitcast.36, pred[2048]{0:T(1024)(128)(4,1)S(1)} %broadcast_compare_fusion, bf16[4,512,1024]{2,1,0:T(8,128)(2,1)} %all-to-all-done.1, s32[]{:T(128)S(6)} %min.22), kind=kOutput, calls=%fused_computation.6 | convolution fusion | flops 2153773056 | bytes 5263364 | tf_op jit(solution)/shard_map/dot_general | solution.py:21
  129.2 4.4 %select_reduce_fusion.4 = f32[2048]{0:T(1024)S(1)} fusion(bf16[2048,1024]{1,0:T(8,128)(2,1)S(1)} %copy-done.2, s32[2048]{0:T(1024)S(1)} %broadcast_add_fusion, s32[512]{0:T(512)S(1)} %bitcast.35, pred[2048]{0:T(1024)(128)(4,1)S(1)} %broadcast_compare_fusion, bf16[4,512,1024]{2,1,0:T(8,128)(2,1)} %all-to-all-done.1, s32[]{:T(128)S(6)} %min.21), kind=kOutput, calls=%fused_computation.9 | convolution fusion | flops 2153773056 | bytes 5263364 | tf_op jit(solution)/shard_map/dot_general | solution.py:21
  133.7 4.7 %select_reduce_fusion.5 = f32[2048]{0:T(1024)S(1)} fusion(bf16[2048,1024]{1,0:T(8,128)(2,1)S(1)} %copy-done.2, s32[2048]{0:T(1024)S(1)} %broadcast_add_fusion, s32[512]{0:T(512)S(1)} %bitcast.34, pred[2048]{0:T(1024)(128)(4,1)S(1)} %broadcast_compare_fusion, bf16[4,512,1024]{2,1,0:T(8,128)(2,1)} %all-to-all-done.1, s32[]{:T(128)S(6)} %min.20), kind=kOutput, calls=%fused_computation.10 | convolution fusion | flops 2153773056 | bytes 5263364 | tf_op jit(solution)/shard_map/dot_general | solution.py:21
  138.3 4.4 %select_reduce_fusion.6 = f32[2048]{0:T(1024)S(1)} fusion(bf16[2048,1024]{1,0:T(8,128)(2,1)S(1)} %copy-done.2, s32[2048]{0:T(1024)S(1)} %broadcast_add_fusion, s32[512]{0:T(512)S(1)} %bitcast.33, pred[2048]{0:T(1024)(128)(4,1)S(1)} %broadcast_compare_fusion, bf16[4,512,1024]{2,1,0:T(8,128)(2,1)} %all-to-all-done.1, s32[]{:T(128)S(6)} %min.19), kind=kOutput, calls=%fused_computation.11 | convolution fusion | flops 2153773056 | bytes 5263364 | tf_op jit(solution)/shard_map/dot_general | solution.py:21
  142.8 6.0 %all-reduce = f32[2048]{0:T(1024)S(1)} all-reduce(f32[2048]{0:T(1024)S(1)} %add_add_fusion), channel_id=2, replica_groups=mesh['groups'=2,'tile'=4,'sub'=4] {'sub'}, use_global_device_ids=true, to_apply=%region_8.9.clone | all-reduce | flops 2048 | bytes 16384
  148.8 0.7 fusion.21
  (6 shorter events, 0.1 us)
Async XLA Ops:
  1.5 14.8 %all-to-all-start = ((s32[4,1,512]{2,1,0:T(1,128)}), s32[4,1,512]{2,1,0:T(1,128)S(1)}, u32[]{:S(2)}, u32[]{:S(2)}) async-start(s32[4,1,512]{2,1,0:T(1,128)} %broadcast_select_fusion.1), calls=%async_computation | async-start | bytes 16384 | tf_op jit(solution)/shard_map/all_to_all | solution.py:48
  7.8 3.4 %copy-start = (bf16[2048,1024]{1,0:T(8,128)(2,1)S(1)}, bf16[2048,1024]{1,0:T(8,128)(2,1)}, u32[]{:S(2)}) copy-start(bf16[2048,1024]{1,0:T(8,128)(2,1)} %param.2) | copy-start | bytes 12582916
  12.0 1.9 %copy-start.1 = (bf16[2048,1024]{1,0:T(8,128)(2,1)}, bf16[2048,1024]{1,0:T(8,128)(2,1)S(1)}, u32[]{:S(2)}) copy-start(bf16[2048,1024]{1,0:T(8,128)(2,1)S(1)} %fusion.1) | copy-start | bytes 12582916
  16.3 5.2 %copy-start.4 = (u32[32]{0:T(128)S(1)}, u32[32]{0:T(128)}, u32[]{:S(2)}) copy-start(u32[32]{0:T(128)} %constant.93) | copy-start | bytes 388
  16.3 6.5 %copy-start.3 = (s32[2048]{0:T(1024)S(1)}, s32[2048]{0:T(1024)}, u32[]{:S(2)}) copy-start(s32[2048]{0:T(1024)} %param.3) | copy-start | bytes 24580
  16.3 98.2 %all-to-all-start.1 = ((bf16[4,512,1024]{2,1,0:T(8,128)(2,1)}), bf16[4,512,1024]{2,1,0:T(8,128)(2,1)}, u32[]{:S(2)}, u32[]{:S(2)}) async-start(bf16[4,512,1024]{2,1,0:T(8,128)(2,1)} %broadcast_select_fusion), calls=%async_computation.1 | async-start | bytes 8388608 | tf_op jit(solution)/shard_map/all_to_all | solution.py:47
  114.5 5.8 %copy-start.2 = (bf16[2048,1024]{1,0:T(8,128)(2,1)S(1)}, bf16[2048,1024]{1,0:T(8,128)(2,1)}, u32[]{:S(2)}) copy-start(bf16[2048,1024]{1,0:T(8,128)(2,1)} %copy-done.1) | copy-start | bytes 12582916
where the time goes:
time: 150 us; the launch traced here: 149 us
  waiting for transfers between devices  85.5 us (57%)
  matrix products  34.4 us (23%)
  starting transfers between devices  11.5 us (8%)
  other arithmetic  8.38 us (6%)
  blocking collectives  5.95 us (4%)
  local copies, waits for them, and re-layouts  2.86 us (2%)
    all_to_all x1, waiting for transfers between devices, shards(): lax.all_to_all(outgoing, 'tile', split_axis=0, concat_axis=0, tiled=True)  85.5 us
    dot_general x7, matrix products, pair_terms(): lax.dot_general(unit, piece, (((1,), (1,)), ((), ())), preferred_element_...  34.4 us
    all_to_all x1, starting transfers between devices, shards(): lax.all_to_all(outgoing_tags, 'tile', split_axis=0, concat_axis=0, tiled=...  6.32 us
    unnamed x1, blocking collectives  5.95 us
    all_to_all x1, starting transfers between devices, shards(): lax.all_to_all(outgoing, 'tile', split_axis=0, concat_axis=0, tiled=True)  5.22 us
    reduce_sum x1, other arithmetic, unit_rows(): jnp.sum(values * values, axis=1, keepdims=True) + norm_eps  3.22 us
  transfers between devices with their start and end apart: 2, of which 1 were waited for; matrix products, arithmetic and copies ran while one was open for 9% of the time, Pallas kernels for 0%

commit v1 on v0

v1 whole, which is shorter than its diff:
```python
import functools
import math

import jax
import jax.numpy as jnp
import numpy as np
from jax import lax
from jax.experimental import pallas as pl
from jax.experimental.pallas import tpu as pltpu
from jax.sharding import PartitionSpec as P

BLOCK = 128
QUAD = 4
SPAN = 4

inverse_temp = 10.0
norm_eps = 1e-06
GAIN = inverse_temp * math.log2(math.e)
OFF = -1000.0

STEP = 512
SUBSTEP = 256


def normalised(values):
    values = values.astype(jnp.float32)
    scale = lax.rsqrt(jnp.sum(values * values, axis=1, keepdims=True) + norm_eps)
    return (values * scale).astype(jnp.bfloat16)


def products(rows, columns):
    return lax.dot_general(
        rows, columns, (((1,), (1,)), ((), ())), preferred_element_type=jnp.float32
    )


def column_bias(tag, col_tags, col_valid):
    lane = lax.broadcasted_iota(jnp.int32, (1, BLOCK), 1)
    parts = []
    for ctag, cvalid in zip(col_tags, col_valid):
        count = jnp.where((ctag == tag) & (tag >= 0), cvalid, 0)
        parts.append(jnp.where(lane < count, -GAIN, OFF))
    return jnp.concatenate(parts, axis=1) if len(parts) > 1 else parts[0]


def lane_sums(weight):
    total = weight[:, :BLOCK]
    for start in range(BLOCK, weight.shape[1], BLOCK):
        total = total + weight[:, start : start + BLOCK]
    return jnp.sum(total.T, axis=0, keepdims=True)


def self_kernel(blocks, width, meta, rows_ref, piece_ref, unit_ref, sums_ref, piece_unit):
    step = pl.program_id(0)

    @pl.when(step == 0)
    def _():
        for start in range(0, width * BLOCK, BLOCK):
            piece_unit[pl.ds(start, BLOCK), :] = normalised(piece_ref[pl.ds(start, BLOCK), :])

    first_col = meta[2 * blocks] * width
    per_step = STEP // BLOCK
    for part in range(STEP // SUBSTEP):
        unit = normalised(rows_ref[pl.ds(part * SUBSTEP, SUBSTEP), :])
        unit_ref[pl.ds(part * SUBSTEP, SUBSTEP), :] = unit
        cosine = products(unit, piece_unit[...])
        for half in range(SUBSTEP // BLOCK):
            local = part * (SUBSTEP // BLOCK) + half
            block = step * per_step + local
            bias = column_bias(
                meta[block],
                [meta[first_col + k] for k in range(width)],
                [meta[blocks + first_col + k] for k in range(width)],
            )
            weight = jnp.exp2(cosine[half * BLOCK : (half + 1) * BLOCK] * GAIN + bias)
            row = lax.broadcasted_iota(jnp.int32, weight.shape, 0)
            col = lax.broadcasted_iota(jnp.int32, weight.shape, 1)
            shift = (block - first_col) * BLOCK
            weight = jnp.where((row < meta[blocks + block]) & (col - row != shift), weight, 0.0)
            sums_ref[pl.ds(block, 1), :] = lane_sums(weight)


def cross_terms(count, blocks, share, step, meta, base, unit_ref, piece_unit, row_sums, col_sums):
    per_step = STEP // BLOCK
    stride = blocks + 2 * share
    for part in range(STEP // SUBSTEP):
        cosine = products(unit_ref[pl.ds(part * SUBSTEP, SUBSTEP), :], piece_unit[...])
        for half in range(SUBSTEP // BLOCK):
            block = step * per_step + part * (SUBSTEP // BLOCK) + half
            biases = []
            for chunk in range(count):
                at = base + chunk * stride
                biases.append(
                    column_bias(
                        meta[at + block],
                        [meta[at + blocks + k] for k in range(share)],
                        [meta[at + blocks + share + k] for k in range(share)],
                    )
                )
            bias = jnp.concatenate(biases, axis=1) if count > 1 else biases[0]
            weight = jnp.exp2(cosine[half * BLOCK : (half + 1) * BLOCK] * GAIN + bias)
            row = lax.broadcasted_iota(jnp.int32, weight.shape, 0)
            weight = jnp.where(row < meta[block], weight, 0.0)
            row_sums[pl.ds(block, 1), :] = lane_sums(weight)
            partial = weight[0:8]
            for start in range(8, BLOCK, 8):
                partial = partial + weight[start : start + 8]
            col_sums[...] += partial


def first_kernel(blocks, share, meta, unit_ref, piece_ref, before_ref, sums_ref, cols_ref, piece_unit, rows, cols):
    step = pl.program_id(0)

    @pl.when(step == 0)
    def _():
        for start in range(0, share * BLOCK, BLOCK):
            piece_unit[pl.ds(start, BLOCK), :] = normalised(piece_ref[pl.ds(start, BLOCK), :])
        cols[...] = jnp.zeros_like(cols)

    cross_terms(1, blocks, share, step, meta, blocks, unit_ref, piece_unit, rows, cols)

    @pl.when(step == pl.num_programs(0) - 1)
    def _():
        sums_ref[...] = rows[...] + before_ref[...]
        total = jnp.sum(cols[...], axis=0, keepdims=True)
        for k in range(share):
            cols_ref[k : k + 1, :] = total[:, k * BLOCK : (k + 1) * BLOCK]


def last_kernel(
    blocks, share, meta, unit_ref, second_ref, third_ref, before_ref, first_cols_ref, extra_ref, out_ref,
    piece_unit, rows, cols,
):
    step = pl.program_id(0)
    size = share * BLOCK

    @pl.when(step == 0)
    def _():
        for start in range(0, size, BLOCK):
            piece_unit[pl.ds(start, BLOCK), :] = normalised(second_ref[pl.ds(start, BLOCK), :])
            piece_unit[pl.ds(size + start, BLOCK), :] = normalised(third_ref[pl.ds(start, BLOCK), :])
        cols[...] = jnp.zeros_like(cols)

    stride = blocks + 2 * share
    cross_terms(2, blocks, share, step, meta, blocks + stride, unit_ref, piece_unit, rows, cols)

    @pl.when(step == pl.num_programs(0) - 1)
    def _():
        tail = blocks + 3 * stride
        place, bad = meta[tail], meta[tail + 1]
        out_ref[...] = jnp.zeros_like(out_ref)
        out_ref[pl.ds(pl.multiple_of(place * blocks, 8), blocks), :] = rows[...] + before_ref[...]
        total = jnp.sum(cols[...], axis=0, keepdims=True)
        for chunk in range(3):
            for k in range(share):
                if chunk == 0:
                    value = first_cols_ref[k : k + 1, :]
                else:
                    at = ((chunk - 1) * share + k) * BLOCK
                    value = total[:, at : at + BLOCK]
                target = meta[tail + 2 + chunk] + k
                out_ref[pl.ds(target, 1), :] += value

        @pl.when(bad > 0)
        def _():
            out_ref[...] = extra_ref[...]


def whole(shape):
    return pl.BlockSpec(shape, lambda *_: (0,) * len(shape))


def call(kernel, meta, operands, in_specs, out_shapes, out_specs, scratch, grid, flops):
    return pl.pallas_call(
        kernel,
        grid_spec=pltpu.PrefetchScalarGridSpec(
            num_scalar_prefetch=1,
            grid=grid,
            in_specs=in_specs,
            out_specs=out_specs,
            scratch_shapes=scratch,
        ),
        out_shape=out_shapes,
        compiler_params=pltpu.CompilerParams(
            vmem_limit_bytes=32 * 1024 * 1024, dimension_semantics=("arbitrary",)
        ),
        cost_estimate=pl.CostEstimate(flops=flops, bytes_accessed=6 * 1024 * 1024, transcendentals=flops // 2048),
    )(meta, *operands)


def every_pair(embeddings, cluster_ids):
    unit = normalised(embeddings)
    tags = cluster_ids + 1
    groups = lax.axis_size("sub")
    member = lax.axis_index("sub")
    owners = lax.axis_size("tile")
    place = lax.axis_index("tile")
    rows_here = unit.shape[0]
    width = rows_here // groups
    own_piece = lax.dynamic_slice_in_dim(unit, member * width, width, 0)
    own_tags = lax.dynamic_slice_in_dim(tags, member * width, width, 0)
    distance = place - jnp.arange(owners, dtype=jnp.int32)
    keep = (jnp.abs(distance) < SPAN) & (distance != 0)
    outgoing = jnp.where(keep[:, None, None], own_piece[None, :, :], jnp.zeros((), jnp.bfloat16))
    outgoing_tags = jnp.where(keep[:, None], own_tags[None, :], 0)
    arrived = lax.all_to_all(outgoing, "tile", split_axis=0, concat_axis=0, tiled=True)
    arrived_tags = lax.all_to_all(outgoing_tags, "tile", split_axis=0, concat_axis=0, tiled=True)
    local_rows = jnp.arange(rows_here, dtype=jnp.int32)[:, None]
    slice_rows = member * width + jnp.arange(width, dtype=jnp.int32)[None, :]
    total = jnp.zeros((rows_here,), jnp.float32)
    for offset in range(1 - SPAN, SPAN):
        if offset == 0:
            piece, piece_tags, order = own_piece, own_tags, local_rows != slice_rows
        else:
            source = place + offset
            valid = (source >= 0) & (source < owners)
            index = jnp.clip(source, 0, owners - 1)
            piece = lax.dynamic_index_in_dim(arrived, index, 0, keepdims=False)
            piece_tags = lax.dynamic_index_in_dim(arrived_tags, index, 0, keepdims=False)
            piece_tags = jnp.where(valid, piece_tags, 0)
            order = True
        same = (tags[:, None] == piece_tags[None, :]) & (tags[:, None] > 0) & order
        weight = jnp.where(same, jnp.exp(inverse_temp * (products(unit, piece) - 1.0)), 0.0)
        total = total + jnp.sum(weight, axis=1)
    return total


def uncovered(tags, blocks):
    size = tags.shape[1]
    index = jnp.arange(size, dtype=jnp.int32)
    tile, inside = index // blocks, index % blocks
    part = tile % QUAD
    half = blocks // 2
    left, right = part[:, None], part[None, :]
    far_left = (inside < half)[:, None]
    far_right = (inside >= half)[None, :]
    missed = (
        (tile[:, None] // QUAD != tile[None, :] // QUAD)
        | ((left == 0) & (right == 3))
        | ((left == 0) & (right == 2) & far_right)
        | ((left == 1) & (right == 3) & far_left)
        | ((left == 1) & (right == 2) & far_left & far_right)
    )
    missed = missed & (tile[:, None] < tile[None, :])
    same = (tags[:, :, None] == tags[:, None, :]) & (tags[:, :, None] >= 0)
    return jnp.any(same & missed[None])


def shards(embeddings, cluster_ids):
    tiles, subs = lax.axis_size("tile"), lax.axis_size("sub")
    place, member = lax.axis_index("tile"), lax.axis_index("sub")
    rows, depth = embeddings.shape
    blocks = rows // BLOCK
    width = blocks // subs
    share = width // 2
    part = place % QUAD
    quads = range(0, tiles, QUAD)

    first_at = jnp.where(
        part == 1, blocks // 2 + member * share, jnp.where(part == 2, member * share, member * width)
    )
    second_at = member * width + share
    size = share * BLOCK
    first_out = lax.dynamic_slice_in_dim(embeddings, first_at * BLOCK, size, 0)
    second_out = lax.dynamic_slice_in_dim(embeddings, second_at * BLOCK, size, 0)
    first = lax.ppermute(
        first_out, "tile", [p for q in quads for p in ((q, q + 1), (q + 3, q + 2), (q + 1, q + 3), (q + 2, q))]
    )
    second = lax.ppermute(second_out, "tile", [p for q in quads for p in ((q, q + 1), (q + 3, q + 2))])
    third = lax.ppermute(first_out, "tile", [p for q in quads for p in ((q + 1, q + 2), (q + 2, q + 1))])

    by_block = cluster_ids.reshape(blocks, BLOCK)
    tag = jnp.max(by_block, axis=1)
    used = jnp.sum((by_block >= 0).astype(jnp.int32), axis=1)
    info = lax.all_gather(jnp.stack([tag, used]), ("groups", "tile"))
    info = info.reshape(-1, tiles, 2, blocks)
    tags_all = info[:, :, 0].reshape(-1, tiles * blocks)
    bad = uncovered(tags_all, blocks)
    mine = lax.dynamic_index_in_dim(info, lax.axis_index("groups"), 0, keepdims=False)
    group_tags = mine[:, 0].reshape(-1)
    group_used = mine[:, 1].reshape(-1)

    outer_from = jnp.where(part == 1, place - 1, place + 1)
    near_at = jnp.where(part == 1, member * share, blocks // 2 + member * share)
    inner = (part == 1) | (part == 2)
    first_from = jnp.where(
        inner,
        outer_from * blocks + member * width,
        jnp.where(part == 3, (place - 2) * blocks + blocks // 2, (place + 2) * blocks) + member * share,
    )
    second_from = jnp.where(inner, outer_from * blocks + second_at, 0)
    third_from = jnp.where(inner, jnp.where(part == 1, place + 1, place - 1) * blocks + near_at, 0)
    own_block = jnp.arange(blocks, dtype=jnp.int32)
    far = (part == 1) & (own_block >= blocks // 2)

    def chunk_meta(start, valid, own_tags):
        ctag = lax.dynamic_slice_in_dim(group_tags, start, share, 0)
        cused = lax.dynamic_slice_in_dim(group_used, start, share, 0)
        return [jnp.where(valid, own_tags, -1), ctag, cused]

    meta = jnp.concatenate(
        [used]
        + chunk_meta(first_from, True, tag)
        + chunk_meta(second_from, inner, tag)
        + chunk_meta(third_from, inner, jnp.where(far, -1, tag))
        + [jnp.stack([place, bad.astype(jnp.int32), first_from, second_from, third_from]).astype(jnp.int32)]
    )
    own_meta = jnp.concatenate([tag, used, member[None]]).astype(jnp.int32)

    extra = lax.cond(
        bad,
        lambda: lax.dynamic_update_slice(
            jnp.zeros((tiles * rows,), jnp.float32), every_pair(embeddings, cluster_ids), (place * rows,)
        ),
        lambda: jnp.zeros((tiles * rows,), jnp.float32),
    ).reshape(tiles * blocks, BLOCK)

    grid = (rows // STEP,)
    step_rows = pl.BlockSpec((STEP, depth), lambda i, _: (i, 0))
    row_sums = jax.ShapeDtypeStruct((blocks, BLOCK), jnp.float32)
    unit, own_sums = call(
        functools.partial(self_kernel, blocks, width),
        own_meta,
        (embeddings, embeddings),
        [step_rows, pl.BlockSpec((width * BLOCK, depth), lambda i, m: (m[2 * blocks], 0))],
        [jax.ShapeDtypeStruct((rows, depth), jnp.bfloat16), row_sums],
        [step_rows, whole((blocks, BLOCK))],
        [pltpu.VMEM((width * BLOCK, depth), jnp.bfloat16)],
        grid,
        2 * rows * width * BLOCK * depth,
    )
    sums, first_cols = call(
        functools.partial(first_kernel, blocks, share),
        meta,
        (unit, first, own_sums),
        [step_rows, whole((size, depth)), whole((blocks, BLOCK))],
        [row_sums, jax.ShapeDtypeStruct((share, BLOCK), jnp.float32)],
        [whole((blocks, BLOCK)), whole((share, BLOCK))],
        [
            pltpu.VMEM((size, depth), jnp.bfloat16),
            pltpu.VMEM((blocks, BLOCK), jnp.float32),
            pltpu.VMEM((8, size), jnp.float32),
        ],
        grid,
        2 * rows * size * depth,
    )
    partial = call(
        functools.partial(last_kernel, blocks, share),
        meta,
        (unit, second, third, sums, first_cols, extra),
        [
            step_rows,
            whole((size, depth)),
            whole((size, depth)),
            whole((blocks, BLOCK)),
            whole((share, BLOCK)),
            whole((tiles * blocks, BLOCK)),
        ],
        jax.ShapeDtypeStruct((tiles * blocks, BLOCK), jnp.float32),
        whole((tiles * blocks, BLOCK)),
        [
            pltpu.VMEM((2 * size, depth), jnp.bfloat16),
            pltpu.VMEM((blocks, BLOCK), jnp.float32),
            pltpu.VMEM((8, 2 * size), jnp.float32),
        ],
        grid,
        4 * rows * size * depth,
    )
    density = lax.psum_scatter(partial.reshape(-1), ("tile", "sub"), scatter_dimension=0, tiled=True)
    return jnp.log(1.0 + density)


def solution(mesh):
    in_specs = (P(("groups", "tile"), None), P(("groups", "tile")))
    out_specs = P(("groups", "tile", "sub"))
    return jax.shard_map(shards, mesh=mesh, in_specs=in_specs, out_specs=out_specs, check_vma=False)
```

time: 150 us -> 121 us (0.81)
  waiting for transfers between devices: 85.5 us -> 0.01 us
  blocking collectives: 5.95 us -> 87.2 us
  matrix products: 34.4 us -> 0 us
  Pallas kernels: 0 us -> 15.8 us
  other arithmetic: 8.38 us -> 2.53 us
  starting transfers between devices: 11.5 us -> 9.46 us
  local copies, waits for them, and re-layouts: 2.86 us -> 4.46 us
    all_to_all x2 -> x0, waiting for transfers between devices: 85.5 us -> none  [the longest x1 85.5 us: shards(): lax.all_to_all(outgoing, 'tile', split_axis=0, concat_axis=0, tiled=True)]
    unnamed x1, blocking collectives: 5.95 us -> 57.6 us
    dot_general x7 -> x0, matrix products: 34.4 us -> none  [pair_terms(): lax.dot_general(unit, piece, (((1,), (1,)), ((), ())), preferred_element_...]
    all_gather x0 -> x1, blocking collectives: none -> 29.6 us  [shards(): info = lax.all_gather(jnp.stack([tag, used]), ('groups', 'tile'))]
    pallas_call x0 -> x3, Pallas kernels: none -> 15.8 us  [call(): pl.pallas_call(kernel, grid_spec=pltpu.PrefetchScalarGridSpec(num_scalar_...]
    all_to_all x2 -> x0, starting transfers between devices: 11.5 us -> none  [the longest x1 6.32 us: shards(): lax.all_to_all(outgoing_tags, 'tile', split_axis=0, concat_axis=0, tiled=...]
    ppermute x0 -> x3, starting transfers between devices: none -> 9.46 us  [the longest x1 5.75 us: shards(): lax.ppermute(second_out, 'tile', [p for q in quads for p in ((q, q + 1),...]
    reduce_sum x1 -> x0, other arithmetic: 3.22 us -> none  [unit_rows(): jnp.sum(values * values, axis=1, keepdims=True) + norm_eps]
  transfers between devices with their start and end apart: 2 -> 3, of which waited for: 1 -> 0; matrix products, arithmetic and copies ran while one was open for 9% -> 4% of each run, Pallas kernels for 0% -> 9%
where the time goes in v1:
time: 121 us
  blocking collectives  87.2 us (72%)
  Pallas kernels  15.8 us (13%)
  starting transfers between devices  9.46 us (8%)
  local copies, waits for them, and re-layouts  4.46 us (4%)
  other arithmetic  2.53 us (2%)
  between operations  1.6 us (1%)
    unnamed x1, blocking collectives  57.6 us
    all_gather x1, blocking collectives, shards(): info = lax.all_gather(jnp.stack([tag, used]), ('groups', 'tile'))  29.6 us
    pallas_call x3, Pallas kernels, call(): pl.pallas_call(kernel, grid_spec=pltpu.PrefetchScalarGridSpec(num_scalar_...  15.8 us
    ppermute x1, starting transfers between devices, shards(): lax.ppermute(second_out, 'tile', [p for q in quads for p in ((q, q + 1),...  5.75 us
    ppermute x1, starting transfers between devices, shards(): lax.ppermute(first_out, 'tile', [p for q in quads for p in ((q, q + 1), (...  3.02 us
  transfers between devices with their start and end apart: 3, of which 0 were waited for; matrix products, arithmetic and copies ran while one was open for 4% of the time, Pallas kernels for 9%

profile of v1, /device:TPU:0, one launch (start us, length us, event | category | flops | bytes accessed | tf_op | source)
XLA Modules:
  0.0 121.1 jit_solution(5854046433046378344)
XLA Ops:
  0.0 2.1 %constant_dynamic-slice_fusion.7 = (bf16[256,1024]{1,0:T(8,128)(2,1)S(1)}, bf16[256,1024]{1,0:T(8,128)(2,1)}) fusion(bf16[2048,1024]{1,0:T(8,128)(2,1)} %piece_ref.1, s32[]{:T(128)S(6)} %select_n.319, s32[]{:T(128)S(6)} %select_n.316), kind=kLoop, calls=%fused_computation.76 | loop fusion | bytes 2097160 | tf_op jit(solution)/shard_map/dynamic_slice | solution.py:264
  2.1 3.0 %collective-permute-start.2 = (bf16[256,1024]{1,0:T(8,128)(2,1)S(1)}, bf16[256,1024]{1,0:T(8,128)(2,1)S(1)}, u32[]{:S(2)}, u32[]{:S(2)}) collective-permute-start(bf16[256,1024]{1,0:T(8,128)(2,1)S(1)} %get-tuple-element.36), channel_id=1, source_target_pairs={{0,4},{12,8},{4,12},{8,0},{1,5},{13,9},{5,13},{9,1},{2,6},{14,10},... | collective-permute-start | bytes 1572872 | tf_op jit(solution)/shard_map/ppermute | solution.py:266
  5.1 0.7 collective-permute-start.1
  5.8 5.8 %collective-permute-start = (bf16[256,1024]{1,0:T(8,128)(2,1)}, bf16[256,1024]{1,0:T(8,128)(2,1)S(1)}, u32[]{:S(2)}, u32[]{:S(2)}) collective-permute-start(bf16[256,1024]{1,0:T(8,128)(2,1)} %get-tuple-element.37), channel_id=1, source_target_pairs={{0,4},{12,8},{1,5},{13,9},{2,6},{14,10},{3,7},{15,11},{16,20},{28,... | collective-permute-start | bytes 1572872 | tf_op jit(solution)/shard_map/ppermute | solution.py:269
  11.6 0.8 bitcast_reduce_fusion
  12.5 29.6 %all-gather.1 = s32[8,2,16]{2,1,0:T(2,128)S(1)} all-gather(s32[1,2,16]{2,1,0:T(2,128)S(1)} %add_bitcast_fusion), channel_id=2, replica_groups=mesh['groups'=2,'tile'=4,'sub'=4] {'groups','tile'}, dimensions={0}, use_global_device_ids=true | all-gather | bytes 1152 | tf_op jit(solution)/shard_map/all_gather | solution.py:275
  42.1 0.1 eq.153
  42.2 0.1 reshape_squeeze.7
  42.3 0.1 reshape_squeeze.6
  42.4 0.1 compare_and_fusion.1
  42.5 0.8 and_reduce_fusion
  44.1 1.3 %dynamic-slice.6 = u32[1]{0:T(128)} dynamic-slice(u32[32]{0:T(128)} %constant.229, u32[]{:T(128)S(6)} %add.243), dynamic_slice_sizes={1} | dynamic-slice | bytes 12
  46.1 0.6 conditional.1
  46.1 0.6 reshape.515
  46.7 0.1 fusion.22
  46.8 0.1 concatenate.6.meta
  46.9 0.1 pad_add_fusion.meta
  46.9 7.2 %shard_map.28 = (bf16[2048,1024]{1,0:T(8,128)(2,1)S(1)}, f32[16,128]{1,0:T(8,128)S(1)}) custom-call(s32[33]{0:T(128)S(1)} %pad_add_fusion.meta, bf16[2048,1024]{1,0:T(8,128)(2,1)} %piece_ref.1, bf16[2048,1024]{1,0:T(8,128)(2,1)} %piece_ref.1), custom_call_target="tpu_custom_call" | custom-call | flops 2147483648 | bytes 6291456 | tf_op jit(solution)/shard_map/pallas_call | solution.py:174
  54.1 0.0 collective-permute-done.2.piece_ref
  54.2 3.2 %shard_map.29 = (f32[16,128]{1,0:T(8,128)S(1)}, f32[2,128]{1,0:T(2,128)S(1)}) custom-call(s32[81]{0:T(128)S(1)} %concatenate.6.meta, bf16[2048,1024]{1,0:T(8,128)(2,1)S(1)} %get-tuple-element.22.unit_ref, bf16[256,1024]{1,0:T(8,128)(2,1)S(1)} %collective-permute-done.2.piece_ref, f32[16,128]{1,0:T(8,128)S(1)} %get-tuple-element.23.before_ref), custom_call_target="tpu_custom_call" | custom-call | flops 1073741824 | bytes 6291456 | tf_op jit(solution)/shard_map/pallas_call | solution.py:174
  57.4 0.0 collective-permute-done.second_ref
  57.4 0.0 collective-permute-done.1.third_ref
  57.4 5.4 %shard_map.30 = f32[64,128]{1,0:T(8,128)S(1)} custom-call(s32[81]{0:T(128)S(1)} %concatenate.6.meta, bf16[2048,1024]{1,0:T(8,128)(2,1)S(1)} %get-tuple-element.22.unit_ref, bf16[256,1024]{1,0:T(8,128)(2,1)S(1)} %collective-permute-done.second_ref, bf16[256,1024]{1,0:T(8,128)(2,1)S(1)} %collective-permute-done.1.third_ref, ...), custom_call_target="tpu_custom_call" | custom-call | flops 2147483648 | bytes 6291456 | tf_op jit(solution)/shard_map/pallas_call | solution.py:174
  62.8 57.6 %all-reduce = f32[8192]{0:T(1024)S(1)} all-reduce(f32[8192]{0:T(1024)S(1)} %bitcast.56), channel_id=3, replica_groups=mesh['groups'=2,'tile'=4,'sub'=4] {'tile','sub'}, use_global_device_ids=true, to_apply=%region_13.14.clone | all-reduce | flops 8192 | bytes 65536
  120.4 0.7 fusion.21
  (10 shorter events, 0.1 us)
Async XLA Ops:
  2.1 52.1 %collective-permute-start.2 = (bf16[256,1024]{1,0:T(8,128)(2,1)S(1)}, bf16[256,1024]{1,0:T(8,128)(2,1)S(1)}, u32[]{:S(2)}, u32[]{:S(2)}) collective-permute-start(bf16[256,1024]{1,0:T(8,128)(2,1)S(1)} %get-tuple-element.36), channel_id=1, source_target_pairs={{0,4},{12,8},{4,12},{8,0},{1,5},{13,9},{5,13},{9,1},{2,6},{14,10},... | collective-permute-start | bytes 1572872 | tf_op jit(solution)/shard_map/ppermute | solution.py:266
  5.1 52.3 %collective-permute-start.1 = (bf16[256,1024]{1,0:T(8,128)(2,1)S(1)}, bf16[256,1024]{1,0:T(8,128)(2,1)S(1)}, u32[]{:S(2)}, u32[]{:S(2)}) collective-permute-start(bf16[256,1024]{1,0:T(8,128)(2,1)S(1)} %get-tuple-element.36), channel_id=1, source_target_pairs={{4,8},{8,4},{5,9},{9,5},{6,10},{10,6},{7,11},{11,7},{20,24},{24,20... | collective-permute-start | bytes 1572872 | tf_op jit(solution)/shard_map/ppermute | solution.py:270
  5.8 51.6 %collective-permute-start = (bf16[256,1024]{1,0:T(8,128)(2,1)}, bf16[256,1024]{1,0:T(8,128)(2,1)S(1)}, u32[]{:S(2)}, u32[]{:S(2)}) collective-permute-start(bf16[256,1024]{1,0:T(8,128)(2,1)} %get-tuple-element.37), channel_id=1, source_target_pairs={{0,4},{12,8},{1,5},{13,9},{2,6},{14,10},{3,7},{15,11},{16,20},{28,... | collective-permute-start | bytes 1572872 | tf_op jit(solution)/shard_map/ppermute | solution.py:269

commit v2 on v1

--- a/solution.py
+++ b/solution.py
@@ -19,7 +19,6 @@
 OFF = -1000.0
 
 STEP = 512
-SUBSTEP = 256
 
 
 def normalised(values):
@@ -50,43 +49,33 @@
     return jnp.sum(total.T, axis=0, keepdims=True)
 
 
-def self_kernel(blocks, width, meta, rows_ref, piece_ref, unit_ref, sums_ref, piece_unit):
-    step = pl.program_id(0)
-
-    @pl.when(step == 0)
-    def _():
-        for start in range(0, width * BLOCK, BLOCK):
-            piece_unit[pl.ds(start, BLOCK), :] = normalised(piece_ref[pl.ds(start, BLOCK), :])
-
+def self_kernel(blocks, width, meta, rows_ref, unit_ref, sums_ref):
+    for start in range(0, blocks * BLOCK, STEP):
+        unit_ref[start : start + STEP, :] = normalised(rows_ref[start : start + STEP, :])
     first_col = meta[2 * blocks] * width
-    per_step = STEP // BLOCK
-    for part in range(STEP // SUBSTEP):
-        unit = normalised(rows_ref[pl.ds(part * SUBSTEP, SUBSTEP), :])
-        unit_ref[pl.ds(part * SUBSTEP, SUBSTEP), :] = unit
-        cosine = products(unit, piece_unit[...])
-        for half in range(SUBSTEP // BLOCK):
-            local = part * (SUBSTEP // BLOCK) + half
-            block = step * per_step + local
-            bias = column_bias(
-                meta[block],
-                [meta[first_col + k] for k in range(width)],
-                [meta[blocks + first_col + k] for k in range(width)],
-            )
-            weight = jnp.exp2(cosine[half * BLOCK : (half + 1) * BLOCK] * GAIN + bias)
+    share = unit_ref[pl.ds(pl.multiple_of(first_col * BLOCK, width * BLOCK), width * BLOCK), :]
+    col_tags = [meta[first_col + k] for k in range(width)]
+    col_used = [meta[blocks + first_col + k] for k in range(width)]
+    for start in range(0, blocks * BLOCK, STEP):
+        cosine = products(unit_ref[start : start + STEP, :], share)
+        for inner in range(0, STEP, BLOCK):
+            block = (start + inner) // BLOCK
+            bias = column_bias(meta[block], col_tags, col_used)
+            weight = jnp.exp2(cosine[inner : inner + BLOCK] * GAIN + bias)
             row = lax.broadcasted_iota(jnp.int32, weight.shape, 0)
             col = lax.broadcasted_iota(jnp.int32, weight.shape, 1)
             shift = (block - first_col) * BLOCK
             weight = jnp.where((row < meta[blocks + block]) & (col - row != shift), weight, 0.0)
-            sums_ref[pl.ds(block, 1), :] = lane_sums(weight)
-
-
-def cross_terms(count, blocks, share, step, meta, base, unit_ref, piece_unit, row_sums, col_sums):
-    per_step = STEP // BLOCK
+            sums_ref[block : block + 1, :] = lane_sums(weight)
+
+
+def cross_terms(count, blocks, share, meta, base, unit_ref, piece_unit, row_sums):
     stride = blocks + 2 * share
-    for part in range(STEP // SUBSTEP):
-        cosine = products(unit_ref[pl.ds(part * SUBSTEP, SUBSTEP), :], piece_unit[...])
-        for half in range(SUBSTEP // BLOCK):
-            block = step * per_step + part * (SUBSTEP // BLOCK) + half
+    columns = None
+    for start in range(0, blocks * BLOCK, STEP):
+        cosine = products(unit_ref[start : start + STEP, :], piece_unit[...])
+        for inner in range(0, STEP, BLOCK):
+            block = (start + inner) // BLOCK
             biases = []
             for chunk in range(count):
                 at = base + chunk * stride
@@ -98,93 +87,67 @@
                     )
                 )
             bias = jnp.concatenate(biases, axis=1) if count > 1 else biases[0]
-            weight = jnp.exp2(cosine[half * BLOCK : (half + 1) * BLOCK] * GAIN + bias)
+            weight = jnp.exp2(cosine[inner : inner + BLOCK] * GAIN + bias)
             row = lax.broadcasted_iota(jnp.int32, weight.shape, 0)
             weight = jnp.where(row < meta[block], weight, 0.0)
-            row_sums[pl.ds(block, 1), :] = lane_sums(weight)
+            row_sums(block, lane_sums(weight))
             partial = weight[0:8]
-            for start in range(8, BLOCK, 8):
-                partial = partial + weight[start : start + 8]
-            col_sums[...] += partial
-
-
-def first_kernel(blocks, share, meta, unit_ref, piece_ref, before_ref, sums_ref, cols_ref, piece_unit, rows, cols):
-    step = pl.program_id(0)
-
-    @pl.when(step == 0)
+            for at in range(8, BLOCK, 8):
+                partial = partial + weight[at : at + 8]
+            columns = partial if columns is None else columns + partial
+    return jnp.sum(columns, axis=0, keepdims=True)
+
+
+def first_kernel(blocks, share, meta, unit_ref, piece_ref, before_ref, sums_ref, cols_ref, piece_unit):
+    piece_unit[...] = normalised(piece_ref[...])
+
+    def row_sums(block, value):
+        sums_ref[block : block + 1, :] = before_ref[block : block + 1, :] + value
+
+    total = cross_terms(1, blocks, share, meta, blocks, unit_ref, piece_unit, row_sums)
+    for k in range(share):
+        cols_ref[k : k + 1, :] = total[:, k * BLOCK : (k + 1) * BLOCK]
+
+
+def last_kernel(
+    blocks, share, meta, unit_ref, second_ref, third_ref, before_ref, first_cols_ref, extra_ref, out_ref, piece_unit
+):
+    size = share * BLOCK
+    piece_unit[:size, :] = normalised(second_ref[...])
+    piece_unit[size:, :] = normalised(third_ref[...])
+    stride = blocks + 2 * share
+    tail = blocks + 3 * stride
+    place, bad = meta[tail], meta[tail + 1]
+    out_ref[...] = jnp.zeros_like(out_ref)
+
+    def row_sums(block, value):
+        out_ref[pl.ds(place * blocks + block, 1), :] = before_ref[block : block + 1, :] + value
+
+    total = cross_terms(2, blocks, share, meta, blocks + stride, unit_ref, piece_unit, row_sums)
+    for chunk in range(3):
+        for k in range(share):
+            if chunk == 0:
+                value = first_cols_ref[k : k + 1, :]
+            else:
+                at = ((chunk - 1) * share + k) * BLOCK
+                value = total[:, at : at + BLOCK]
+            out_ref[pl.ds(meta[tail + 2 + chunk] + k, 1), :] += value
+
+    @pl.when(bad > 0)
     def _():
-        for start in range(0, share * BLOCK, BLOCK):
-            piece_unit[pl.ds(start, BLOCK), :] = normalised(piece_ref[pl.ds(start, BLOCK), :])
-        cols[...] = jnp.zeros_like(cols)
-
-    cross_terms(1, blocks, share, step, meta, blocks, unit_ref, piece_unit, rows, cols)
-
-    @pl.when(step == pl.num_programs(0) - 1)
-    def _():
-        sums_ref[...] = rows[...] + before_ref[...]
-        total = jnp.sum(cols[...], axis=0, keepdims=True)
-        for k in range(share):
-            cols_ref[k : k + 1, :] = total[:, k * BLOCK : (k + 1) * BLOCK]
-
-
-def last_kernel(
-    blocks, share, meta, unit_ref, second_ref, third_ref, before_ref, first_cols_ref, extra_ref, out_ref,
-    piece_unit, rows, cols,
-):
-    step = pl.program_id(0)
-    size = share * BLOCK
-
-    @pl.when(step == 0)
-    def _():
-        for start in range(0, size, BLOCK):
-            piece_unit[pl.ds(start, BLOCK), :] = normalised(second_ref[pl.ds(start, BLOCK), :])
-            piece_unit[pl.ds(size + start, BLOCK), :] = normalised(third_ref[pl.ds(start, BLOCK), :])
-        cols[...] = jnp.zeros_like(cols)
-
-    stride = blocks + 2 * share
-    cross_terms(2, blocks, share, step, meta, blocks + stride, unit_ref, piece_unit, rows, cols)
-
-    @pl.when(step == pl.num_programs(0) - 1)
-    def _():
-        tail = blocks + 3 * stride
-        place, bad = meta[tail], meta[tail + 1]
-        out_ref[...] = jnp.zeros_like(out_ref)
-        out_ref[pl.ds(pl.multiple_of(place * blocks, 8), blocks), :] = rows[...] + before_ref[...]
-        total = jnp.sum(cols[...], axis=0, keepdims=True)
-        for chunk in range(3):
-            for k in range(share):
-                if chunk == 0:
-                    value = first_cols_ref[k : k + 1, :]
-                else:
-                    at = ((chunk - 1) * share + k) * BLOCK
-                    value = total[:, at : at + BLOCK]
-                target = meta[tail + 2 + chunk] + k
-                out_ref[pl.ds(target, 1), :] += value
-
-        @pl.when(bad > 0)
-        def _():
-            out_ref[...] = extra_ref[...]
-
-
-def whole(shape):
-    return pl.BlockSpec(shape, lambda *_: (0,) * len(shape))
-
-
-def call(kernel, meta, operands, in_specs, out_shapes, out_specs, scratch, grid, flops):
+        out_ref[...] = extra_ref[...]
+
+
+def call(kernel, meta, operands, out_shapes, scratch, flops):
+    vmem = pl.BlockSpec(memory_space=pltpu.VMEM)
     return pl.pallas_call(
         kernel,
-        grid_spec=pltpu.PrefetchScalarGridSpec(
-            num_scalar_prefetch=1,
-            grid=grid,
-            in_specs=in_specs,
-            out_specs=out_specs,
-            scratch_shapes=scratch,
-        ),
+        in_specs=[pl.BlockSpec(memory_space=pltpu.SMEM)] + [vmem] * len(operands),
+        out_specs=jax.tree.map(lambda _: vmem, out_shapes),
         out_shape=out_shapes,
-        compiler_params=pltpu.CompilerParams(
-            vmem_limit_bytes=32 * 1024 * 1024, dimension_semantics=("arbitrary",)
-        ),
-        cost_estimate=pl.CostEstimate(flops=flops, bytes_accessed=6 * 1024 * 1024, transcendentals=flops // 2048),
+        scratch_shapes=scratch,
+        compiler_params=pltpu.CompilerParams(vmem_limit_bytes=40 * 1024 * 1024),
+        cost_estimate=pl.CostEstimate(flops=flops, bytes_accessed=1024 * 1024, transcendentals=flops // 2048),
     )(meta, *operands)
 
 
@@ -269,11 +232,15 @@
     second = lax.ppermute(second_out, "tile", [p for q in quads for p in ((q, q + 1), (q + 3, q + 2))])
     third = lax.ppermute(first_out, "tile", [p for q in quads for p in ((q + 1, q + 2), (q + 2, q + 1))])
 
+    count = lax.axis_size("groups") * tiles
+    everyone = lax.all_to_all(
+        jnp.broadcast_to(cluster_ids[None], (count, rows)), ("groups", "tile"), split_axis=0, concat_axis=0, tiled=True
+    ).reshape(count, blocks, BLOCK)
+    info = jnp.stack([jnp.max(everyone, axis=2), jnp.sum((everyone >= 0).astype(jnp.int32), axis=2)], axis=1)
+    info = info.reshape(-1, tiles, 2, blocks)
     by_block = cluster_ids.reshape(blocks, BLOCK)
     tag = jnp.max(by_block, axis=1)
     used = jnp.sum((by_block >= 0).astype(jnp.int32), axis=1)
-    info = lax.all_gather(jnp.stack([tag, used]), ("groups", "tile"))
-    info = info.reshape(-1, tiles, 2, blocks)
     tags_all = info[:, :, 0].reshape(-1, tiles * blocks)
     bad = uncovered(tags_all, blocks)
     mine = lax.dynamic_index_in_dim(info, lax.axis_index("groups"), 0, keepdims=False)
@@ -315,59 +282,35 @@
         lambda: jnp.zeros((tiles * rows,), jnp.float32),
     ).reshape(tiles * blocks, BLOCK)
 
-    grid = (rows // STEP,)
-    step_rows = pl.BlockSpec((STEP, depth), lambda i, _: (i, 0))
     row_sums = jax.ShapeDtypeStruct((blocks, BLOCK), jnp.float32)
     unit, own_sums = call(
         functools.partial(self_kernel, blocks, width),
         own_meta,
-        (embeddings, embeddings),
-        [step_rows, pl.BlockSpec((width * BLOCK, depth), lambda i, m: (m[2 * blocks], 0))],
+        (embeddings,),
         [jax.ShapeDtypeStruct((rows, depth), jnp.bfloat16), row_sums],
-        [step_rows, whole((blocks, BLOCK))],
-        [pltpu.VMEM((width * BLOCK, depth), jnp.bfloat16)],
-        grid,
+        [],
         2 * rows * width * BLOCK * depth,
     )
     sums, first_cols = call(
         functools.partial(first_kernel, blocks, share),
         meta,
         (unit, first, own_sums),
-        [step_rows, whole((size, depth)), whole((blocks, BLOCK))],
         [row_sums, jax.ShapeDtypeStruct((share, BLOCK), jnp.float32)],
-        [whole((blocks, BLOCK)), whole((share, BLOCK))],
-        [
-            pltpu.VMEM((size, depth), jnp.bfloat16),
-            pltpu.VMEM((blocks, BLOCK), jnp.float32),
-            pltpu.VMEM((8, size), jnp.float32),
-        ],
-        grid,
+        [pltpu.VMEM((size, depth), jnp.bfloat16)],
         2 * rows * size * depth,
     )
     partial = call(
         functools.partial(last_kernel, blocks, share),
         meta,
         (unit, second, third, sums, first_cols, extra),
-        [
-            step_rows,
-            whole((size, depth)),
-            whole((size, depth)),
-            whole((blocks, BLOCK)),
-            whole((share, BLOCK)),
-            whole((tiles * blocks, BLOCK)),
-        ],
         jax.ShapeDtypeStruct((tiles * blocks, BLOCK), jnp.float32),
-        whole((tiles * blocks, BLOCK)),
-        [
-            pltpu.VMEM((2 * size, depth), jnp.bfloat16),
-            pltpu.VMEM((blocks, BLOCK), jnp.float32),
-            pltpu.VMEM((8, 2 * size), jnp.float32),
-        ],
-        grid,
+        [pltpu.VMEM((2 * size, depth), jnp.bfloat16)],
         4 * rows * size * depth,
     )
-    density = lax.psum_scatter(partial.reshape(-1), ("tile", "sub"), scatter_dimension=0, tiled=True)
-    return jnp.log(1.0 + density)
+    parts = lax.all_to_all(
+        partial.reshape(tiles * subs, rows // subs), ("tile", "sub"), split_axis=0, concat_axis=0, tiled=True
+    )
+    return jnp.log(1.0 + jnp.sum(parts, axis=0))
 
 
 def solution(mesh):

time: 121 us -> 56.1 us (0.46)
  blocking collectives: 87.2 us -> 12.1 us
  starting transfers between devices: 9.46 us -> 15.3 us
  local copies, waits for them, and re-layouts: 4.46 us -> 8.58 us
  waiting for transfers between devices: 0.01 us -> 3.13 us
  Pallas kernels: 15.8 us -> 12.9 us
    unnamed x1 -> x0, blocking collectives: 57.6 us -> none
    all_gather x1 -> x0, blocking collectives: 29.6 us -> none  [shards(): info = lax.all_gather(jnp.stack([tag, used]), ('groups', 'tile'))]
    all_to_all x0 -> x1, blocking collectives: none -> 12.1 us  [shards(): lax.all_to_all(partial.reshape(tiles * subs, rows // subs), ('tile', 'sub...]
    all_to_all x0 -> x1, starting transfers between devices: none -> 7.63 us  [shards(): lax.all_to_all(jnp.broadcast_to(cluster_ids[None], (count, rows)), ('grou...]
    all_to_all x0 -> x1, waiting for transfers between devices: none -> 3.12 us  [shards(): lax.all_to_all(jnp.broadcast_to(cluster_ids[None], (count, rows)), ('grou...]
    pallas_call x3, Pallas kernels: 15.8 us -> 12.9 us  [call(): pl.pallas_call(kernel, in_specs=[pl.BlockSpec(memory_space=pltpu.SMEM)] +...]
    unnamed x1 -> x6, local copies, waits for them, and re-layouts: 1.32 us -> 4.11 us
    ppermute x1, starting transfers between devices: 5.75 us -> 3.95 us  [shards(): lax.ppermute(second_out, 'tile', [p for q in quads for p in ((q, q + 1),...]
  transfers between devices with their start and end apart: 3 -> 4, of which waited for: 0 -> 1; matrix products, arithmetic and copies ran while one was open for 4% -> 8% of each run, Pallas kernels for 9% -> 16%
where the time goes in v2:
time: 56.1 us; the launch traced here: 55.6 us
  starting transfers between devices  15.3 us (27%)
  Pallas kernels  12.9 us (23%)
  blocking collectives  12.1 us (22%)
  local copies, waits for them, and re-layouts  8.58 us (15%)
  waiting for transfers between devices  3.13 us (6%)
  other arithmetic  2.78 us (5%)
  between operations  0.81 us (1%)
    pallas_call x3, Pallas kernels, call(): pl.pallas_call(kernel, in_specs=[pl.BlockSpec(memory_space=pltpu.SMEM)] +...  12.9 us
    all_to_all x1, blocking collectives, shards(): lax.all_to_all(partial.reshape(tiles * subs, rows // subs), ('tile', 'sub...  12.1 us
    all_to_all x1, starting transfers between devices, shards(): lax.all_to_all(jnp.broadcast_to(cluster_ids[None], (count, rows)), ('grou...  7.63 us
    unnamed x6, local copies, waits for them, and re-layouts  4.11 us
    ppermute x1, starting transfers between devices, shards(): lax.ppermute(second_out, 'tile', [p for q in quads for p in ((q, q + 1),...  3.95 us
    all_to_all x1, waiting for transfers between devices, shards(): lax.all_to_all(jnp.broadcast_to(cluster_ids[None], (count, rows)), ('grou...  3.12 us
    ppermute x1, starting transfers between devices, shards(): lax.ppermute(first_out, 'tile', [p for q in quads for p in ((q, q + 1), (...  3.02 us
    dynamic_slice x1, local copies, waits for them, and re-layouts, shards(): first_out = lax.dynamic_slice_in_dim(embeddings, first_at * BLOCK, size, 0)  2.06 us
  transfers between devices with their start and end apart: 4, of which 1 were waited for; matrix products, arithmetic and copies ran while one was open for 8% of the time, Pallas kernels for 16%

profile of v2, /device:TPU:0, one launch (start us, length us, event | category | flops | bytes accessed | tf_op | source)
XLA Modules:
  0.0 55.6 jit_solution(16447212842485948376)
XLA Ops:
  0.0 2.1 %constant_dynamic-slice_fusion.7 = (bf16[256,1024]{1,0:T(8,128)(2,1)S(1)}, bf16[256,1024]{1,0:T(8,128)(2,1)}) fusion(bf16[2048,1024]{1,0:T(8,128)(2,1)} %rows_ref.1, s32[]{:T(128)S(6)} %select_n.319, s32[]{:T(128)S(6)} %select_n.316), kind=kLoop, calls=%fused_computation.76 | loop fusion | bytes 2097160 | tf_op jit(solution)/shard_map/dynamic_slice | solution.py:227
  2.1 3.0 %collective-permute-start.2 = (bf16[256,1024]{1,0:T(8,128)(2,1)S(1)}, bf16[256,1024]{1,0:T(8,128)(2,1)S(1)}, u32[]{:S(2)}, u32[]{:S(2)}) collective-permute-start(bf16[256,1024]{1,0:T(8,128)(2,1)S(1)} %get-tuple-element.38), channel_id=1, source_target_pairs={{0,4},{12,8},{4,12},{8,0},{1,5},{13,9},{5,13},{9,1},{2,6},{14,10},... | collective-permute-start | bytes 1572872 | tf_op jit(solution)/shard_map/ppermute | solution.py:229
  5.1 0.7 %collective-permute-start.1 = (bf16[256,1024]{1,0:T(8,128)(2,1)S(1)}, bf16[256,1024]{1,0:T(8,128)(2,1)S(1)}, u32[]{:S(2)}, u32[]{:S(2)}) collective-permute-start(bf16[256,1024]{1,0:T(8,128)(2,1)S(1)} %get-tuple-element.38), channel_id=1, source_target_pairs={{4,8},{8,4},{5,9},{9,5},{6,10},{10,6},{7,11},{11,7},{20,24},{24,20... | collective-permute-start | bytes 1572872 | tf_op jit(solution)/shard_map/ppermute | solution.py:233
  5.8 1.4 %broadcast_in_dim.72 = s32[8,1,2048]{2,1,0:T(1,128)} broadcast(s32[2048]{0:T(1024)} %param.5), dimensions={2} | broadcast | bytes 73728 | tf_op jit(solution)/shard_map/broadcast_in_dim | solution.py:237
  7.1 0.0 copy-start.5
  7.1 7.6 %all-to-all-start.2 = ((s32[8,1,2048]{2,1,0:T(1,128)}), s32[8,1,2048]{2,1,0:T(1,128)S(1)}, u32[]{:S(2)}, u32[]{:S(2)}) async-start(s32[8,1,2048]{2,1,0:T(1,128)} %broadcast_in_dim.72), calls=%async_computation.2 | async-start | bytes 131072 | tf_op jit(solution)/shard_map/all_to_all | solution.py:236
  14.8 3.9 %collective-permute-start = (bf16[256,1024]{1,0:T(8,128)(2,1)}, bf16[256,1024]{1,0:T(8,128)(2,1)S(1)}, u32[]{:S(2)}, u32[]{:S(2)}) collective-permute-start(bf16[256,1024]{1,0:T(8,128)(2,1)} %get-tuple-element.39), channel_id=1, source_target_pairs={{0,4},{12,8},{1,5},{13,9},{2,6},{14,10},{3,7},{15,11},{16,20},{28,... | collective-permute-start | bytes 1572872 | tf_op jit(solution)/shard_map/ppermute | solution.py:232
  18.8 0.8 %bitcast_reduce_fusion = (s32[16]{0:T(128)S(1)}, s32[16]{0:T(128)S(1)}) fusion(s32[2048]{0:T(1024)} %param.5), kind=kLoop, calls=%fused_computation.57 | loop fusion | flops 8160 | bytes 8320 | tf_op jit(solution)/shard_map/reduce_max | solution.py:242
  19.7 0.1 pad_add_fusion.meta
  19.8 0.1 compare_and_fusion.1
  19.9 6.7 %shard_map.28 = (bf16[2048,1024]{1,0:T(8,128)(2,1)S(1)}, f32[16,128]{1,0:T(8,128)S(1)}) custom-call(s32[33]{0:T(128)S(1)} %pad_add_fusion.meta, bf16[2048,1024]{1,0:T(8,128)(2,1)} %rows_ref.1), custom_call_target="tpu_custom_call" | custom-call | flops 2147483648 | bytes 1048576 | tf_op jit(solution)/shard_map/pallas_call | solution.py:143
  26.6 0.0 copy-start
  26.6 1.9 %copy-done = bf16[2048,1024]{1,0:T(8,128)(2,1)} copy-done((bf16[2048,1024]{1,0:T(8,128)(2,1)}, bf16[2048,1024]{1,0:T(8,128)(2,1)S(1)}, u32[]{:S(2)}) %copy-start) | copy-done | bytes 4194328
  28.5 3.1 %all-to-all-done.2 = s32[8,1,2048]{2,1,0:T(1,128)S(1)} async-done(((s32[8,1,2048]{2,1,0:T(1,128)}), s32[8,1,2048]{2,1,0:T(1,128)S(1)}, u32[]{:S(2)}, u32[]{:S(2)}) %all-to-all-start.2) | async-done | bytes 65568 | tf_op jit(solution)/shard_map/all_to_all | solution.py:236
  31.7 0.3 convert_reduce_fusion
  32.0 0.1 eq.153
  32.1 0.1 reshape_squeeze.7
  32.2 0.1 reshape_squeeze.6
  32.3 0.8 %and_reduce_fusion = pred[]{:T(512)} fusion(s32[2,64]{1,0:T(2,128)S(1)} %eq.153, pred[64,64]{1,0:T(8,128)(4,1)S(1)} %compare_and_fusion.1, pred[2,64]{1,0:T(4,128)(4,1)S(1)} %broadcast_compare_fusion.1), kind=kLoop, calls=%fused_computation.53 | loop fusion | flops 32767 | bytes 4737 | tf_op jit(solution)/shard_map/reduce_or | solution.py:209
  33.1 0.0 copy-done.5
  33.7 0.6 %conditional.1 = (f32[64,128]{1,0:T(8,128)}) conditional(s32[]{:T(128)} %convert_element_type.21, () %tuple.13, (s32[2048]{0:T(1024)S(1)}, bf16[2048,1024]{1,0:T(8,128)(2,1)}, s32[]{:T(128)}) %tuple.38), branch_computations={%region_5.6_spmd, %region_6.15_spmd} | conditional | flops 15093213184 | bytes 119907000 | solution.py:277
  33.7 0.6 %reshape.532 = f32[64,128]{1,0:T(8,128)} broadcast(f32[]{:T(128)} %constant.190.clone), dimensions={} | broadcast | bytes 32772 | tf_op jit(solution)/shard_map/reshape | solution.py:283
  34.3 0.1 fusion.22
  34.4 0.1 concatenate.7.meta
  34.5 0.0 collective-permute-done.2.piece_ref
  34.5 0.0 copy-start.1
  34.5 2.2 %copy-done.1 = bf16[2048,1024]{1,0:T(8,128)(2,1)S(1)} copy-done((bf16[2048,1024]{1,0:T(8,128)(2,1)S(1)}, bf16[2048,1024]{1,0:T(8,128)(2,1)}, u32[]{:S(2)}) %copy-start.1) | copy-done | bytes 4194328
  36.7 2.2 %shard_map.29 = (f32[16,128]{1,0:T(8,128)S(1)}, f32[2,128]{1,0:T(2,128)S(1)}) custom-call(s32[81]{0:T(128)S(1)} %concatenate.7.meta, bf16[2048,1024]{1,0:T(8,128)(2,1)S(1)} %copy-done.1, bf16[256,1024]{1,0:T(8,128)(2,1)S(1)} %collective-permute-done.2.piece_ref, f32[16,128]{1,0:T(8,128)S(1)} %get-tuple-element.23.before_ref), custom_call_target="tpu_custom_call" | custom-call | flops 1073741824 | bytes 1048576 | tf_op jit(solution)/shard_map/pallas_call | solution.py:143
  38.9 0.0 collective-permute-done.second_ref
  38.9 0.0 collective-permute-done.1.third_ref
  38.9 3.9 %shard_map.30 = f32[64,128]{1,0:T(8,128)S(1)} custom-call(s32[81]{0:T(128)S(1)} %concatenate.7.meta, bf16[2048,1024]{1,0:T(8,128)(2,1)S(1)} %copy-done.1, bf16[256,1024]{1,0:T(8,128)(2,1)S(1)} %collective-permute-done.second_ref, bf16[256,1024]{1,0:T(8,128)(2,1)S(1)} %collective-permute-done.1.third_ref, f32[16,128]{1,0:T(8,128)S(1)} %get-tuple-element.24.before_ref, ...), custom_call_target="tpu_custom_call" | custom-call | flops 2147483648 | bytes 1048576 | tf_op jit(solution)/shard_map/pallas_call | solution.py:143
  42.8 12.1 %all_to_all.24 = f32[16,1,512]{2,1,0:T(1,128)S(1)} all-to-all(f32[16,1,512]{2,1,0:T(1,128)S(1)} %bitcast.51), channel_id=1, replica_groups=mesh['groups'=2,'tile'=4,'sub'=4] {'tile','sub'}, dimensions={0} | all-to-all | bytes 65536 | tf_op jit(solution)/shard_map/all_to_all | solution.py:310
  55.0 0.6 %add_log_fusion = f32[512]{0:T(512)} fusion(f32[512]{0:T(512)S(1)} %reduce_sum.101), kind=kLoop, calls=%fused_computation.64 | loop fusion | flops 512 | bytes 4096 | tf_op jit(solution)/shard_map/log | solution.py:313
  (10 shorter events, 0.1 us)
Async XLA Ops:
  2.1 32.4 %collective-permute-start.2 = (bf16[256,1024]{1,0:T(8,128)(2,1)S(1)}, bf16[256,1024]{1,0:T(8,128)(2,1)S(1)}, u32[]{:S(2)}, u32[]{:S(2)}) collective-permute-start(bf16[256,1024]{1,0:T(8,128)(2,1)S(1)} %get-tuple-element.38), channel_id=1, source_target_pairs={{0,4},{12,8},{4,12},{8,0},{1,5},{13,9},{5,13},{9,1},{2,6},{14,10},... | collective-permute-start | bytes 1572872 | tf_op jit(solution)/shard_map/ppermute | solution.py:229
  5.1 33.8 %collective-permute-start.1 = (bf16[256,1024]{1,0:T(8,128)(2,1)S(1)}, bf16[256,1024]{1,0:T(8,128)(2,1)S(1)}, u32[]{:S(2)}, u32[]{:S(2)}) collective-permute-start(bf16[256,1024]{1,0:T(8,128)(2,1)S(1)} %get-tuple-element.38), channel_id=1, source_target_pairs={{4,8},{8,4},{5,9},{9,5},{6,10},{10,6},{7,11},{11,7},{20,24},{24,20... | collective-permute-start | bytes 1572872 | tf_op jit(solution)/shard_map/ppermute | solution.py:233
  7.1 25.9 %copy-start.5 = (s32[2048]{0:T(1024)S(1)}, s32[2048]{0:T(1024)}, u32[]{:S(2)}) copy-start(s32[2048]{0:T(1024)} %param.5) | copy-start | bytes 24580
  7.1 24.5 %all-to-all-start.2 = ((s32[8,1,2048]{2,1,0:T(1,128)}), s32[8,1,2048]{2,1,0:T(1,128)S(1)}, u32[]{:S(2)}, u32[]{:S(2)}) async-start(s32[8,1,2048]{2,1,0:T(1,128)} %broadcast_in_dim.72), calls=%async_computation.2 | async-start | bytes 131072 | tf_op jit(solution)/shard_map/all_to_all | solution.py:236
  14.8 24.1 %collective-permute-start = (bf16[256,1024]{1,0:T(8,128)(2,1)}, bf16[256,1024]{1,0:T(8,128)(2,1)S(1)}, u32[]{:S(2)}, u32[]{:S(2)}) collective-permute-start(bf16[256,1024]{1,0:T(8,128)(2,1)} %get-tuple-element.39), channel_id=1, source_target_pairs={{0,4},{12,8},{1,5},{13,9},{2,6},{14,10},{3,7},{15,11},{16,20},{28,... | collective-permute-start | bytes 1572872 | tf_op jit(solution)/shard_map/ppermute | solution.py:232
  26.6 1.9 %copy-start = (bf16[2048,1024]{1,0:T(8,128)(2,1)}, bf16[2048,1024]{1,0:T(8,128)(2,1)S(1)}, u32[]{:S(2)}) copy-start(bf16[2048,1024]{1,0:T(8,128)(2,1)S(1)} %get-tuple-element.22.unit_ref) | copy-start | bytes 12582916
  34.5 2.2 %copy-start.1 = (bf16[2048,1024]{1,0:T(8,128)(2,1)S(1)}, bf16[2048,1024]{1,0:T(8,128)(2,1)}, u32[]{:S(2)}) copy-start(bf16[2048,1024]{1,0:T(8,128)(2,1)} %copy-done) | copy-start | bytes 12582916

commit v3 on v0

v3 whole, which is shorter than its diff:
```python
import functools
import math

import jax
import jax.numpy as jnp
import numpy as np
from jax import lax
from jax.experimental import pallas as pl
from jax.experimental.pallas import tpu as pltpu
from jax.sharding import PartitionSpec as P

BLOCK = 128
QUAD = 4
SPAN = 4

inverse_temp = 10.0
norm_eps = 1e-06
GAIN = inverse_temp * math.log2(math.e)
OFF = -1000.0

STEP = 512


def normalised(values):
    values = values.astype(jnp.float32)
    scale = lax.rsqrt(jnp.sum(values * values, axis=1, keepdims=True) + norm_eps)
    return (values * scale).astype(jnp.bfloat16)


def products(rows, columns):
    return lax.dot_general(
        rows, columns, (((1,), (1,)), ((), ())), preferred_element_type=jnp.float32
    )


def column_bias(tag, column_tags):
    return jnp.where(column_tags == tag.astype(jnp.float32), -GAIN, OFF)


def lane_sums(weight):
    total = weight[:, :BLOCK]
    for start in range(BLOCK, weight.shape[1], BLOCK):
        total = total + weight[:, start : start + BLOCK]
    return jnp.sum(total.T, axis=0, keepdims=True)


def self_kernel(blocks, width, meta, rows_ref, tags_ref, unit_ref, sums_ref):
    for start in range(0, blocks * BLOCK, STEP):
        unit_ref[start : start + STEP, :] = normalised(rows_ref[start : start + STEP, :])
    first_col = meta[5 * blocks] * width
    share = unit_ref[pl.ds(pl.multiple_of(first_col * BLOCK, width * BLOCK), width * BLOCK), :]
    column_tags = tags_ref[...].astype(jnp.float32)
    for start in range(0, blocks * BLOCK, STEP):
        cosine = products(unit_ref[start : start + STEP, :], share)
        for inner in range(0, STEP, BLOCK):
            block = (start + inner) // BLOCK
            bias = column_bias(meta[block], column_tags)
            weight = jnp.exp2(cosine[inner : inner + BLOCK] * GAIN + bias)
            row = lax.broadcasted_iota(jnp.int32, weight.shape, 0)
            col = lax.broadcasted_iota(jnp.int32, weight.shape, 1)
            shift = (block - first_col) * BLOCK
            weight = jnp.where((row < meta[blocks + block]) & (col - row != shift), weight, 0.0)
            sums_ref[block : block + 1, :] = lane_sums(weight)


def cross_kernel(blocks, size, chunk, meta, unit_ref, piece_ref, tags_ref, before_ref, sums_ref, cols_ref, piece_unit):
    piece_unit[...] = normalised(piece_ref[:size, :])
    at = 0 if tags_ref.shape[0] == 8 else size
    column_tags = tags_ref[at : at + 8, :].astype(jnp.float32)[0:1, :]
    first = 0 if chunk == 2 else size if chunk == 1 else 0
    column_tags = column_tags[:, first : first + size]
    columns = None
    for start in range(0, blocks * BLOCK, STEP):
        cosine = products(unit_ref[start : start + STEP, :], piece_unit[...])
        for inner in range(0, STEP, BLOCK):
            block = (start + inner) // BLOCK
            bias = column_bias(meta[(2 + chunk) * blocks + block], column_tags)
            weight = jnp.exp2(cosine[inner : inner + BLOCK] * GAIN + bias)
            row = lax.broadcasted_iota(jnp.int32, weight.shape, 0)
            weight = jnp.where(row < meta[blocks + block], weight, 0.0)
            sums_ref[block : block + 1, :] = before_ref[block : block + 1, :] + lane_sums(weight)
            partial = weight[0:8]
            for down in range(8, BLOCK, 8):
                partial = partial + weight[down : down + 8]
            columns = partial if columns is None else columns + partial
    total = jnp.sum(columns, axis=0, keepdims=True)
    for k in range(size // BLOCK):
        cols_ref[k : k + 1, :] = total[:, k * BLOCK : (k + 1) * BLOCK]


def call(kernel, meta, operands, out_shapes, scratch, flops):
    vmem = pl.BlockSpec(memory_space=pltpu.VMEM)
    return pl.pallas_call(
        kernel,
        in_specs=[pl.BlockSpec(memory_space=pltpu.SMEM)] + [vmem] * len(operands),
        out_specs=jax.tree.map(lambda _: vmem, out_shapes),
        out_shape=out_shapes,
        scratch_shapes=scratch,
        compiler_params=pltpu.CompilerParams(vmem_limit_bytes=16 * 1024 * 1024),
        cost_estimate=pl.CostEstimate(flops=flops, bytes_accessed=1024 * 1024, transcendentals=flops // 2048),
    )(meta, *operands)


def every_pair(embeddings, cluster_ids):
    unit = normalised(embeddings)
    tags = cluster_ids + 1
    groups = lax.axis_size("sub")
    member = lax.axis_index("sub")
    owners = lax.axis_size("tile")
    place = lax.axis_index("tile")
    rows_here = unit.shape[0]
    width = rows_here // groups
    own_piece = lax.dynamic_slice_in_dim(unit, member * width, width, 0)
    own_tags = lax.dynamic_slice_in_dim(tags, member * width, width, 0)
    distance = place - jnp.arange(owners, dtype=jnp.int32)
    keep = (jnp.abs(distance) < SPAN) & (distance != 0)
    outgoing = jnp.where(keep[:, None, None], own_piece[None, :, :], jnp.zeros((), jnp.bfloat16))
    outgoing_tags = jnp.where(keep[:, None], own_tags[None, :], 0)
    arrived = lax.all_to_all(outgoing, "tile", split_axis=0, concat_axis=0, tiled=True)
    arrived_tags = lax.all_to_all(outgoing_tags, "tile", split_axis=0, concat_axis=0, tiled=True)
    local_rows = jnp.arange(rows_here, dtype=jnp.int32)[:, None]
    slice_rows = member * width + jnp.arange(width, dtype=jnp.int32)[None, :]
    total = jnp.zeros((rows_here,), jnp.float32)
    for offset in range(1 - SPAN, SPAN):
        if offset == 0:
            piece, piece_tags, order = own_piece, own_tags, local_rows != slice_rows
        else:
            source = place + offset
            valid = (source >= 0) & (source < owners)
            index = jnp.clip(source, 0, owners - 1)
            piece = lax.dynamic_index_in_dim(arrived, index, 0, keepdims=False)
            piece_tags = lax.dynamic_index_in_dim(arrived_tags, index, 0, keepdims=False)
            piece_tags = jnp.where(valid, piece_tags, 0)
            order = True
        same = (tags[:, None] == piece_tags[None, :]) & (tags[:, None] > 0) & order
        weight = jnp.where(same, jnp.exp(inverse_temp * (products(unit, piece) - 1.0)), 0.0)
        total = total + jnp.sum(weight, axis=1)
    return total


def uncovered(tag, blocks, tiles, place):
    half = blocks // 2
    part = place % QUAD
    quads = range(0, tiles, QUAD)
    edge = jnp.broadcast_to(jnp.where(part == 1, tag[half - 1], tag[half]), (BLOCK,))
    out = lax.ppermute(edge, "tile", [p for q in quads for p in ((q + 1, q), (q + 2, q + 3))])[0]
    over = lax.ppermute(edge, "tile", [p for q in quads for p in ((q + 1, q + 3), (q + 2, q))])[0]
    across = lax.ppermute(edge, "tile", [p for q in quads for p in ((q + 1, q + 2), (q + 2, q + 1))])[0]
    inner = (part == 1) | (part == 2)
    one = jnp.where(inner, edge[0], out)
    other = jnp.where(inner, across, over)
    bad = (one == other) & (one >= 0)
    if tiles > QUAD:
        last = jnp.broadcast_to(tag[blocks - 1], (BLOCK,))
        before = lax.ppermute(last, "tile", [(t, t + 1) for t in range(tiles - 1)])[0]
        bad = bad | ((part == 0) & (place > 0) & (before == tag[0]) & (before >= 0))
        bad = lax.pmax(bad.astype(jnp.int32), "tile") > 0
    return bad


def shards(embeddings, cluster_ids):
    tiles, subs = lax.axis_size("tile"), lax.axis_size("sub")
    place, member = lax.axis_index("tile"), lax.axis_index("sub")
    rows, depth = embeddings.shape
    blocks = rows // BLOCK
    width = blocks // subs
    share = width // 2
    size = share * BLOCK
    part = place % QUAD
    inner = (part == 1) | (part == 2)
    quads = range(0, tiles, QUAD)
    routes = [
        [p for q in quads for p in ((q, q + 1), (q + 3, q + 2), (q + 1, q + 3), (q + 2, q))],
        [p for q in quads for p in ((q, q + 1), (q + 3, q + 2))],
        [p for q in quads for p in ((q + 1, q + 2), (q + 2, q + 1))],
    ]
    back = [[(b, a) for a, b in route] for route in routes]

    first_at = BLOCK * jnp.where(
        part == 1, blocks // 2 + member * share, jnp.where(part == 2, member * share, member * width)
    )
    second_at = BLOCK * (member * width + share)
    carried = jnp.concatenate(
        [lax.dynamic_slice_in_dim(cluster_ids, at, size, 0) for at in (first_at, second_at)]
    ).astype(jnp.bfloat16)
    carried = jnp.broadcast_to(jnp.pad(carried, (0, depth - 2 * size))[None], (8, depth))
    first_out = jnp.concatenate([lax.dynamic_slice_in_dim(embeddings, first_at, size, 0), carried])
    second_out = lax.dynamic_slice_in_dim(embeddings, second_at, size, 0)
    first = lax.ppermute(first_out, "tile", routes[0])
    third = lax.ppermute(first_out, "tile", routes[2])
    second = lax.ppermute(second_out, "tile", routes[1])

    by_block = cluster_ids.reshape(blocks, BLOCK)
    tag = jnp.max(by_block, axis=1)
    used = jnp.sum((by_block >= 0).astype(jnp.int32), axis=1)
    far = (part == 1) & (jnp.arange(blocks) >= blocks // 2)
    from_outer = jnp.where(inner, tag, -2)
    meta = jnp.concatenate([tag, used, tag, from_outer, jnp.where(far, -2, from_outer), member[None]]).astype(jnp.int32)

    bad = uncovered(tag, blocks, tiles, place)
    extra = lax.cond(
        bad, lambda: every_pair(embeddings, cluster_ids), lambda: jnp.zeros((rows,), jnp.float32)
    )

    row_sums = jax.ShapeDtypeStruct((blocks, BLOCK), jnp.float32)
    unit, sums = call(
        functools.partial(self_kernel, blocks, width),
        meta,
        (embeddings, lax.dynamic_slice_in_dim(cluster_ids, member * width * BLOCK, width * BLOCK, 0)[None]),
        [jax.ShapeDtypeStruct((rows, depth), jnp.bfloat16), row_sums],
        [],
        2 * rows * width * BLOCK * depth,
    )

    def cross(chunk, piece, tags, before):
        return call(
            functools.partial(cross_kernel, blocks, size, chunk),
            meta,
            (unit, piece, tags, before),
            [row_sums, jax.ShapeDtypeStruct((share, BLOCK), jnp.float32)],
            [pltpu.VMEM((size, depth), jnp.bfloat16)],
            2 * rows * size * depth,
        )

    sums, first_cols = cross(0, first, first, sums)
    sums, third_cols = cross(2, third, third, sums)
    sums, second_cols = cross(1, second, first, sums)
    returned = lax.ppermute(first_cols, "tile", back[0]) + lax.ppermute(third_cols, "tile", back[2])
    outer = lax.ppermute(second_cols, "tile", back[1])

    partial = sums.reshape(-1)
    here = lax.dynamic_slice_in_dim(partial, first_at, size, 0) + returned.reshape(-1)
    partial = lax.dynamic_update_slice_in_dim(partial, here, first_at, 0)
    partial = jnp.where(bad, extra, partial)
    quarter = width * BLOCK

    def portion(shift):
        return lax.dynamic_slice_in_dim(partial, lax.rem(member + shift, subs) * quarter, quarter, 0)

    density = portion(0)
    for shift in range(1, subs):
        density = density + lax.ppermute(portion(shift), "sub", [(i, (i + shift) % subs) for i in range(subs)])
    outer = jnp.where(bad, 0.0, outer.reshape(-1))
    density = density + jnp.concatenate([jnp.zeros_like(outer), outer])
    return jnp.log(1.0 + density)


def solution(mesh):
    in_specs = (P(("groups", "tile"), None), P(("groups", "tile")))
    out_specs = P(("groups", "tile", "sub"))
    return jax.shard_map(shards, mesh=mesh, in_specs=in_specs, out_specs=out_specs, check_vma=False)
```

time: 150 us -> 54.6 us (0.36)
  waiting for transfers between devices: 85.5 us -> 5.38 us
  matrix products: 34.4 us -> 0 us
  Pallas kernels: 0 us -> 13.5 us
  starting transfers between devices: 11.5 us -> 23.1 us
  blocking collectives: 5.95 us -> 0 us
  other arithmetic: 8.38 us -> 2.56 us
  local copies, waits for them, and re-layouts: 2.86 us -> 7.79 us
    all_to_all x2 -> x0, waiting for transfers between devices: 85.5 us -> none  [the longest x1 85.5 us: shards(): lax.all_to_all(outgoing, 'tile', split_axis=0, concat_axis=0, tiled=True)]
    dot_general x7 -> x0, matrix products: 34.4 us -> none  [pair_terms(): lax.dot_general(unit, piece, (((1,), (1,)), ((), ())), preferred_element_...]
    ppermute x0 -> x12, starting transfers between devices: none -> 23.1 us  [the longest x1 5.87 us: shards(): first = lax.ppermute(first_out, 'tile', routes[0])]
    pallas_call x0 -> x4, Pallas kernels: none -> 13.5 us  [call(): pl.pallas_call(kernel, in_specs=[pl.BlockSpec(memory_space=pltpu.SMEM)] +...]
    all_to_all x2 -> x0, starting transfers between devices: 11.5 us -> none  [the longest x1 6.32 us: shards(): lax.all_to_all(outgoing_tags, 'tile', split_axis=0, concat_axis=0, tiled=...]
    unnamed x1 -> x0, blocking collectives: 5.95 us -> none
    ppermute x0 -> x12, waiting for transfers between devices: none -> 5.38 us  [the longest x1 3.22 us: uncovered(): lax.ppermute(edge, 'tile', [p for q in quads for p in ((q + 1, q + 3), (q...]
    select_n x3, other arithmetic: 3.02 us -> 0.02 us  [the longest x1 0.01 us: shards(): partial = jnp.where(bad, extra, partial)]
  transfers between devices with their start and end apart: 2 -> 12, of which waited for: 1 -> 3; matrix products, arithmetic and copies ran while one was open for 9% -> 5% of each run, Pallas kernels for 0% -> 25%
where the time goes in v3:
time: 54.6 us; the launch traced here: 54.1 us
  starting transfers between devices  23.1 us (42%)
  Pallas kernels  13.5 us (25%)
  local copies, waits for them, and re-layouts  7.79 us (14%)
  waiting for transfers between devices  5.38 us (10%)
  other arithmetic  2.56 us (5%)
  between operations  1.55 us (3%)
    pallas_call x4, Pallas kernels, call(): pl.pallas_call(kernel, in_specs=[pl.BlockSpec(memory_space=pltpu.SMEM)] +...  13.5 us
    ppermute x1, starting transfers between devices, shards(): first = lax.ppermute(first_out, 'tile', routes[0])  5.87 us
    ppermute x1, starting transfers between devices, shards(): second = lax.ppermute(second_out, 'tile', routes[1])  4.57 us
    unnamed x6, local copies, waits for them, and re-layouts  4.12 us
    ppermute x1, starting transfers between devices, shards(): lax.ppermute(first_cols, 'tile', back[0])  3.63 us
    ppermute x1, waiting for transfers between devices, uncovered(): lax.ppermute(edge, 'tile', [p for q in quads for p in ((q + 1, q + 3), (q...  3.22 us
    ppermute x3, starting transfers between devices, shards(): lax.ppermute(portion(shift), 'sub', [(i, (i + shift) % subs) for i in ran...  3.18 us
    dynamic_slice x1, local copies, waits for them, and re-layouts, shards(): lax.dynamic_slice_in_dim(embeddings, first_at, size, 0)  2.07 us
  transfers between devices with their start and end apart: 12, of which 3 were waited for; matrix products, arithmetic and copies ran while one was open for 5% of the time, Pallas kernels for 25%

profile of v3, /device:TPU:0, one launch (start us, length us, event | category | flops | bytes accessed | tf_op | source)
XLA Modules:
  0.0 54.1 jit_solution(7350521537189886581)
XLA Ops:
  0.0 0.8 %dynamic-slice_convert_fusion.1 = (bf16[256]{0:T(256)(128)(2,1)S(1)}, bf16[256]{0:T(256)(128)(2,1)S(1)}) fusion(s32[2048]{0:T(1024)} %param.5, s32[]{:T(128)S(6)} %select_n.227, s32[]{:T(128)S(6)} %select_n.224), kind=kLoop, calls=%fused_computation.67 | loop fusion | flops 512 | bytes 3080 | tf_op jit(solution)/shard_map/convert
  0.8 2.1 %constant_dynamic-slice_fusion.7 = (bf16[256,1024]{1,0:T(8,128)(2,1)S(1)}, bf16[256,1024]{1,0:T(8,128)(2,1)}) fusion(bf16[2048,1024]{1,0:T(8,128)(2,1)} %rows_ref.1, s32[]{:T(128)S(6)} %select_n.227, s32[]{:T(128)S(6)} %select_n.224), kind=kLoop, calls=%fused_computation.69 | loop fusion | bytes 2097160 | tf_op jit(solution)/shard_map/dynamic_slice | solution.py:187
  3.0 0.0 copy-start.5
  3.0 0.7 %collective-permute-start.5 = (bf16[264,1024]{1,0:T(8,128)(2,1)S(1)}, bf16[264,1024]{1,0:T(8,128)(2,1)S(1)}, u32[]{:S(2)}, u32[]{:S(2)}) collective-permute-start(bf16[264,1024]{1,0:T(8,128)(2,1)S(1)} %pad_maximum_fusion), channel_id=1, source_target_pairs={{4,8},{8,4},{5,9},{9,5},{6,10},{10,6},{7,11},{11,7},{20,24},{24,20... | collective-permute-start | bytes 1622024 | tf_op jit(solution)/shard_map/ppermute | solution.py:190
  3.7 5.9 %collective-permute-start.4 = (bf16[264,1024]{1,0:T(8,128)(2,1)S(1)}, bf16[264,1024]{1,0:T(8,128)(2,1)S(1)}, u32[]{:S(2)}, u32[]{:S(2)}) collective-permute-start(bf16[264,1024]{1,0:T(8,128)(2,1)S(1)} %pad_maximum_fusion), channel_id=1, source_target_pairs={{0,4},{12,8},{4,12},{8,0},{1,5},{13,9},{5,13},{9,1},{2,6},{14,10},... | collective-permute-start | bytes 1622024 | tf_op jit(solution)/shard_map/ppermute | solution.py:189
  9.6 0.8 %convert_reduce_fusion = (s32[16]{0:T(128)S(1)}, s32[16]{0:T(128)S(1)}) fusion(s32[2048]{0:T(1024)} %param.5), kind=kLoop, calls=%fused_computation.55 | loop fusion | flops 8160 | bytes 8320 | tf_op jit(solution)/shard_map/reduce_sum | solution.py:195
  10.4 0.7 %fusion.26 = (s32[1]{0:T(128)}, s32[1]{0:T(128)}) fusion(s32[16]{0:T(128)S(1)} %get-tuple-element.31), kind=kLoop, calls=%fused_computation.72 | loop fusion | bytes 16 | tf_op jit(solution)/shard_map/slice | solution.py:145
  12.3 1.3 %collective-permute-start.2 = (s32[128]{0:T(128)S(1)}, s32[128]{0:T(128)S(1)}, u32[]{:S(2)}, u32[]{:S(2)}) collective-permute-start(s32[128]{0:T(128)S(1)} %broadcast_in_dim.113), channel_id=1, source_target_pairs={{4,12},{8,0},{5,13},{9,1},{6,14},{10,2},{7,15},{11,3},{20,28},{24,... | collective-permute-start | bytes 1544 | tf_op jit(solution)/shard_map/ppermute | solution.py:147
  13.6 1.3 %collective-permute-start = (s32[128]{0:T(128)S(1)}, s32[128]{0:T(128)S(1)}, u32[]{:S(2)}, u32[]{:S(2)}) collective-permute-start(s32[128]{0:T(128)S(1)} %broadcast_in_dim.113), channel_id=1, source_target_pairs={{4,0},{8,12},{5,1},{9,13},{6,2},{10,14},{7,3},{11,15},{20,16},{24,... | collective-permute-start | bytes 1544 | tf_op jit(solution)/shard_map/ppermute | solution.py:146
  14.9 4.6 %collective-permute-start.3 = (bf16[256,1024]{1,0:T(8,128)(2,1)}, bf16[256,1024]{1,0:T(8,128)(2,1)S(1)}, u32[]{:S(2)}, u32[]{:S(2)}) collective-permute-start(bf16[256,1024]{1,0:T(8,128)(2,1)} %get-tuple-element.41), channel_id=1, source_target_pairs={{0,4},{12,8},{1,5},{13,9},{2,6},{14,10},{3,7},{15,11},{16,20},{28,... | collective-permute-start | bytes 1572872 | tf_op jit(solution)/shard_map/ppermute | solution.py:191
  19.5 0.8 %dynamic_slice.74 = s32[512]{0:T(512)S(1)} dynamic-slice(s32[2048]{0:T(1024)} %param.5, s32[]{:T(128)S(6)} %select_n.223), dynamic_slice_sizes={512} | dynamic-slice | bytes 4100 | tf_op jit(solution)/shard_map/dynamic_slice | solution.py:209
  20.3 0.1 concatenate.13.meta
  20.4 6.7 %shard_map.28 = (bf16[2048,1024]{1,0:T(8,128)(2,1)S(1)}, f32[16,128]{1,0:T(8,128)S(1)}) custom-call(s32[81]{0:T(128)S(1)} %concatenate.13.meta, bf16[2048,1024]{1,0:T(8,128)(2,1)} %rows_ref.1, s32[1,512]{1,0:T(1,128)S(1)} %bitcast.55), custom_call_target="tpu_custom_call" | custom-call | flops 2147483648 | bytes 1048576 | tf_op jit(solution)/shard_map/pallas_call | solution.py:93
  27.1 0.0 copy-start
  27.1 1.9 %copy-done = bf16[2048,1024]{1,0:T(8,128)(2,1)} copy-done((bf16[2048,1024]{1,0:T(8,128)(2,1)}, bf16[2048,1024]{1,0:T(8,128)(2,1)S(1)}, u32[]{:S(2)}) %copy-start) | copy-done | bytes 4194328
  29.0 0.0 collective-permute-done
  29.0 0.7 %collective-permute-start.1 = (s32[128]{0:T(128)S(1)}, s32[128]{0:T(128)S(1)}, u32[]{:S(2)}, u32[]{:S(2)}) collective-permute-start(s32[128]{0:T(128)S(1)} %broadcast_in_dim.113), channel_id=1, source_target_pairs={{4,8},{8,4},{5,9},{9,5},{6,10},{10,6},{7,11},{11,7},{20,24},{24,20... | collective-permute-start | bytes 1544 | tf_op jit(solution)/shard_map/ppermute | solution.py:148
  29.7 3.2 %collective-permute-done.2 = s32[128]{0:T(128)S(1)} collective-permute-done((s32[128]{0:T(128)S(1)}, s32[128]{0:T(128)S(1)}, u32[]{:S(2)}, u32[]{:S(2)}) %collective-permute-start.2) | collective-permute-done | bytes 544 | tf_op jit(solution)/shard_map/ppermute | solution.py:147
  33.0 0.0 collective-permute-done.1
  33.0 0.0 copy-done.5
  33.0 0.2 conditional.1
  33.3 0.0 collective-permute-done.4.piece_ref.tags_ref
  33.3 0.0 copy-start.1
  33.3 2.2 %copy-done.1 = bf16[2048,1024]{1,0:T(8,128)(2,1)S(1)} copy-done((bf16[2048,1024]{1,0:T(8,128)(2,1)S(1)}, bf16[2048,1024]{1,0:T(8,128)(2,1)}, u32[]{:S(2)}) %copy-start.1) | copy-done | bytes 4194328
  35.5 2.3 %shard_map.29 = (f32[16,128]{1,0:T(8,128)S(1)}, f32[2,128]{1,0:T(2,128)S(1)}) custom-call(s32[81]{0:T(128)S(1)} %concatenate.13.meta, bf16[2048,1024]{1,0:T(8,128)(2,1)S(1)} %copy-done.1, bf16[264,1024]{1,0:T(8,128)(2,1)S(1)} %collective-permute-done.4.piece_ref.tags_ref, bf16[264,1024]{1,0:T(8,128)(2,1)S(1)} %collective-permute-done.4.piece_ref.tags_ref, ...), custom_call_target="tpu_custom_call" | custom-call | flops 1073741824 | bytes 1048576 | tf_op jit(solution)/shard_map/pallas_call | solution.py:93
  37.7 0.0 collective-permute-done.5.piece_ref.tags_ref
  37.7 2.3 %shard_map.30 = (f32[16,128]{1,0:T(8,128)S(1)}, f32[2,128]{1,0:T(2,128)S(1)}) custom-call(s32[81]{0:T(128)S(1)} %concatenate.13.meta, bf16[2048,1024]{1,0:T(8,128)(2,1)S(1)} %copy-done.1, bf16[264,1024]{1,0:T(8,128)(2,1)S(1)} %collective-permute-done.5.piece_ref.tags_ref, bf16[264,1024]{1,0:T(8,128)(2,1)S(1)} %collective-permute-done.5.piece_ref.tags_ref, ...), custom_call_target="tpu_custom_call" | custom-call | flops 1073741824 | bytes 1048576 | tf_op jit(solution)/shard_map/pallas_call | solution.py:93
  40.0 0.7 %collective-permute-start.7 = (f32[2,128]{1,0:T(2,128)S(1)}, f32[2,128]{1,0:T(2,128)S(1)}, u32[]{:S(2)}, u32[]{:S(2)}) collective-permute-start(f32[2,128]{1,0:T(2,128)S(1)} %get-tuple-element.28), channel_id=1, source_target_pairs={{8,4},{4,8},{9,5},{5,9},{10,6},{6,10},{11,7},{7,11},{24,20},{20,24... | collective-permute-start | bytes 3080 | tf_op jit(solution)/shard_map/ppermute | solution.py:228
  40.7 3.6 %collective-permute-start.6 = (f32[2,128]{1,0:T(2,128)S(1)}, f32[2,128]{1,0:T(2,128)S(1)}, u32[]{:S(2)}, u32[]{:S(2)}) collective-permute-start(f32[2,128]{1,0:T(2,128)S(1)} %get-tuple-element.27), channel_id=1, source_target_pairs={{4,0},{8,12},{12,4},{0,8},{5,1},{9,13},{13,5},{1,9},{6,2},{10,14},... | collective-permute-start | bytes 3080 | tf_op jit(solution)/shard_map/ppermute | solution.py:228
  44.3 0.0 collective-permute-done.3.piece_ref
  44.3 2.3 %shard_map.31 = (f32[16,128]{1,0:T(8,128)S(1)}, f32[2,128]{1,0:T(2,128)S(1)}) custom-call(s32[81]{0:T(128)S(1)} %concatenate.13.meta, bf16[2048,1024]{1,0:T(8,128)(2,1)S(1)} %copy-done.1, bf16[256,1024]{1,0:T(8,128)(2,1)S(1)} %collective-permute-done.3.piece_ref, bf16[264,1024]{1,0:T(8,128)(2,1)S(1)} %collective-permute-done.4.piece_ref.tags_ref, ...), custom_call_target="tpu_custom_call" | custom-call | flops 1073741824 | bytes 1048576 | tf_op jit(solution)/shard_map/pallas_call | solution.py:93
  46.5 1.3 %collective-permute-start.11 = (f32[2,128]{1,0:T(2,128)S(1)}, f32[2,128]{1,0:T(2,128)S(1)}, u32[]{:S(2)}, u32[]{:S(2)}) collective-permute-start(f32[2,128]{1,0:T(2,128)S(1)} %get-tuple-element.29), channel_id=1, source_target_pairs={{4,0},{8,12},{5,1},{9,13},{6,2},{10,14},{7,3},{11,15},{20,16},{24,... | collective-permute-start | bytes 3080 | tf_op jit(solution)/shard_map/ppermute | solution.py:229
  47.8 0.0 collective-permute-done.7
  47.9 0.0 collective-permute-done.6
  47.9 0.2 fusion.24
  48.1 0.1 fusion.25
  48.1 0.0 collective-permute-start.8
  48.2 1.7 %collective-permute-start.10 = (f32[512]{0:T(512)S(1)}, f32[512]{0:T(512)S(1)}, u32[]{:S(2)}, u32[]{:S(2)}) collective-permute-start(f32[512]{0:T(512)S(1)} %get-tuple-element.43), channel_id=1, source_target_pairs={{0,3},{1,0},{2,1},{3,2},{4,7},{5,4},{6,5},{7,6},{8,11},{9,8},{10,9... | collective-permute-start | bytes 6152 | tf_op jit(solution)/shard_map/ppermute | solution.py:242
  49.9 1.4 %collective-permute-start.9 = (f32[512]{0:T(512)S(1)}, f32[512]{0:T(512)S(1)}, u32[]{:S(2)}, u32[]{:S(2)}) collective-permute-start(f32[512]{0:T(512)S(1)} %get-tuple-element.44), channel_id=1, source_target_pairs={{0,2},{1,3},{2,0},{3,1},{4,6},{5,7},{6,4},{7,5},{8,10},{9,11},{10,... | collective-permute-start | bytes 6152 | tf_op jit(solution)/shard_map/ppermute | solution.py:242
  51.3 0.7 %collective-permute-done.11 = f32[2,128]{1,0:T(2,128)S(1)} collective-permute-done((f32[2,128]{1,0:T(2,128)S(1)}, f32[2,128]{1,0:T(2,128)S(1)}, u32[]{:S(2)}, u32[]{:S(2)}) %collective-permute-start.11) | collective-permute-done | bytes 1056 | tf_op jit(solution)/shard_map/ppermute | solution.py:229
  52.0 0.0 collective-permute-done.8
  52.0 0.0 collective-permute-done.10
  52.0 1.5 %collective-permute-done.9 = f32[512]{0:T(512)S(1)} collective-permute-done((f32[512]{0:T(512)S(1)}, f32[512]{0:T(512)S(1)}, u32[]{:S(2)}, u32[]{:S(2)}) %collective-permute-start.9) | collective-permute-done | bytes 2080 | tf_op jit(solution)/shard_map/ppermute | solution.py:242
  53.5 0.7 %add_log_fusion = f32[512]{0:T(512)} fusion(f32[256]{0:T(256)S(1)} %select_bitcast_fusion, f32[512]{0:T(512)S(1)} %collective-permute-done.10, f32[512]{0:T(512)S(1)} %collective-permute-done.9, f32[512]{0:T(512)S(1)} %collective-permute-done.8, f32[2048]{0:T(1024)S(1)} %broadcast_select_fusion.8, s32[]{:T(128)S(6)} %select_n.229), kind=kLoop, calls=%fused_computation.61 | loop fusion | flops 2560 | bytes 11268 | tf_op jit(solution)/shard_map/log | solution.py:245
  (8 shorter events, 0.1 us)
Async XLA Ops:
  3.0 30.0 %copy-start.5 = (s32[2048]{0:T(1024)S(1)}, s32[2048]{0:T(1024)}, u32[]{:S(2)}) copy-start(s32[2048]{0:T(1024)} %param.5) | copy-start | bytes 24580
  3.0 34.7 %collective-permute-start.5 = (bf16[264,1024]{1,0:T(8,128)(2,1)S(1)}, bf16[264,1024]{1,0:T(8,128)(2,1)S(1)}, u32[]{:S(2)}, u32[]{:S(2)}) collective-permute-start(bf16[264,1024]{1,0:T(8,128)(2,1)S(1)} %pad_maximum_fusion), channel_id=1, source_target_pairs={{4,8},{8,4},{5,9},{9,5},{6,10},{10,6},{7,11},{11,7},{20,24},{24,20... | collective-permute-start | bytes 1622024 | tf_op jit(solution)/shard_map/ppermute | solution.py:190
  3.7 29.6 %collective-permute-start.4 = (bf16[264,1024]{1,0:T(8,128)(2,1)S(1)}, bf16[264,1024]{1,0:T(8,128)(2,1)S(1)}, u32[]{:S(2)}, u32[]{:S(2)}) collective-permute-start(bf16[264,1024]{1,0:T(8,128)(2,1)S(1)} %pad_maximum_fusion), channel_id=1, source_target_pairs={{0,4},{12,8},{4,12},{8,0},{1,5},{13,9},{5,13},{9,1},{2,6},{14,10},... | collective-permute-start | bytes 1622024 | tf_op jit(solution)/shard_map/ppermute | solution.py:189
  12.3 20.7 %collective-permute-start.2 = (s32[128]{0:T(128)S(1)}, s32[128]{0:T(128)S(1)}, u32[]{:S(2)}, u32[]{:S(2)}) collective-permute-start(s32[128]{0:T(128)S(1)} %broadcast_in_dim.113), channel_id=1, source_target_pairs={{4,12},{8,0},{5,13},{9,1},{6,14},{10,2},{7,15},{11,3},{20,28},{24,... | collective-permute-start | bytes 1544 | tf_op jit(solution)/shard_map/ppermute | solution.py:147
  13.6 15.4 %collective-permute-start = (s32[128]{0:T(128)S(1)}, s32[128]{0:T(128)S(1)}, u32[]{:S(2)}, u32[]{:S(2)}) collective-permute-start(s32[128]{0:T(128)S(1)} %broadcast_in_dim.113), channel_id=1, source_target_pairs={{4,0},{8,12},{5,1},{9,13},{6,2},{10,14},{7,3},{11,15},{20,16},{24,... | collective-permute-start | bytes 1544 | tf_op jit(solution)/shard_map/ppermute | solution.py:146
  14.9 29.4 %collective-permute-start.3 = (bf16[256,1024]{1,0:T(8,128)(2,1)}, bf16[256,1024]{1,0:T(8,128)(2,1)S(1)}, u32[]{:S(2)}, u32[]{:S(2)}) collective-permute-start(bf16[256,1024]{1,0:T(8,128)(2,1)} %get-tuple-element.41), channel_id=1, source_target_pairs={{0,4},{12,8},{1,5},{13,9},{2,6},{14,10},{3,7},{15,11},{16,20},{28,... | collective-permute-start | bytes 1572872 | tf_op jit(solution)/shard_map/ppermute | solution.py:191
  27.1 1.9 %copy-start = (bf16[2048,1024]{1,0:T(8,128)(2,1)}, bf16[2048,1024]{1,0:T(8,128)(2,1)S(1)}, u32[]{:S(2)}) copy-start(bf16[2048,1024]{1,0:T(8,128)(2,1)S(1)} %get-tuple-element.22.unit_ref) | copy-start | bytes 12582916
  29.0 3.9 %collective-permute-start.1 = (s32[128]{0:T(128)S(1)}, s32[128]{0:T(128)S(1)}, u32[]{:S(2)}, u32[]{:S(2)}) collective-permute-start(s32[128]{0:T(128)S(1)} %broadcast_in_dim.113), channel_id=1, source_target_pairs={{4,8},{8,4},{5,9},{9,5},{6,10},{10,6},{7,11},{11,7},{20,24},{24,20... | collective-permute-start | bytes 1544 | tf_op jit(solution)/shard_map/ppermute | solution.py:148
  33.3 2.2 %copy-start.1 = (bf16[2048,1024]{1,0:T(8,128)(2,1)S(1)}, bf16[2048,1024]{1,0:T(8,128)(2,1)}, u32[]{:S(2)}) copy-start(bf16[2048,1024]{1,0:T(8,128)(2,1)} %copy-done) | copy-start | bytes 12582916
  40.0 7.9 %collective-permute-start.7 = (f32[2,128]{1,0:T(2,128)S(1)}, f32[2,128]{1,0:T(2,128)S(1)}, u32[]{:S(2)}, u32[]{:S(2)}) collective-permute-start(f32[2,128]{1,0:T(2,128)S(1)} %get-tuple-element.28), channel_id=1, source_target_pairs={{8,4},{4,8},{9,5},{5,9},{10,6},{6,10},{11,7},{7,11},{24,20},{20,24... | collective-permute-start | bytes 3080 | tf_op jit(solution)/shard_map/ppermute | solution.py:228
  40.7 7.2 %collective-permute-start.6 = (f32[2,128]{1,0:T(2,128)S(1)}, f32[2,128]{1,0:T(2,128)S(1)}, u32[]{:S(2)}, u32[]{:S(2)}) collective-permute-start(f32[2,128]{1,0:T(2,128)S(1)} %get-tuple-element.27), channel_id=1, source_target_pairs={{4,0},{8,12},{12,4},{0,8},{5,1},{9,13},{13,5},{1,9},{6,2},{10,14},... | collective-permute-start | bytes 3080 | tf_op jit(solution)/shard_map/ppermute | solution.py:228
  46.5 5.5 %collective-permute-start.11 = (f32[2,128]{1,0:T(2,128)S(1)}, f32[2,128]{1,0:T(2,128)S(1)}, u32[]{:S(2)}, u32[]{:S(2)}) collective-permute-start(f32[2,128]{1,0:T(2,128)S(1)} %get-tuple-element.29), channel_id=1, source_target_pairs={{4,0},{8,12},{5,1},{9,13},{6,2},{10,14},{7,3},{11,15},{20,16},{24,... | collective-permute-start | bytes 3080 | tf_op jit(solution)/shard_map/ppermute | solution.py:229
  48.1 3.9 %collective-permute-start.8 = (f32[512]{0:T(512)S(1)}, f32[512]{0:T(512)S(1)}, u32[]{:S(2)}, u32[]{:S(2)}) collective-permute-start(f32[512]{0:T(512)S(1)} %get-tuple-element.42), channel_id=1, source_target_pairs={{0,1},{1,2},{2,3},{3,0},{4,5},{5,6},{6,7},{7,4},{8,9},{9,10},{10,1... | collective-permute-start | bytes 6152 | tf_op jit(solution)/shard_map/ppermute | solution.py:242
  48.2 3.9 %collective-permute-start.10 = (f32[512]{0:T(512)S(1)}, f32[512]{0:T(512)S(1)}, u32[]{:S(2)}, u32[]{:S(2)}) collective-permute-start(f32[512]{0:T(512)S(1)} %get-tuple-element.43), channel_id=1, source_target_pairs={{0,3},{1,0},{2,1},{3,2},{4,7},{5,4},{6,5},{7,6},{8,11},{9,8},{10,9... | collective-permute-start | bytes 6152 | tf_op jit(solution)/shard_map/ppermute | solution.py:242
  49.9 3.6 %collective-permute-start.9 = (f32[512]{0:T(512)S(1)}, f32[512]{0:T(512)S(1)}, u32[]{:S(2)}, u32[]{:S(2)}) collective-permute-start(f32[512]{0:T(512)S(1)} %get-tuple-element.44), channel_id=1, source_target_pairs={{0,2},{1,3},{2,0},{3,1},{4,6},{5,7},{6,4},{7,5},{8,10},{9,11},{10,... | collective-permute-start | bytes 6152 | tf_op jit(solution)/shard_map/ppermute | solution.py:242

commit v4 on v3

--- a/solution.py
+++ b/solution.py
@@ -42,6 +42,24 @@
     for start in range(BLOCK, weight.shape[1], BLOCK):
         total = total + weight[:, start : start + BLOCK]
     return jnp.sum(total.T, axis=0, keepdims=True)
+
+
+def pack_kernel(blocks, share, at, rows_ref, ids_ref, first_ref, second_ref, sems):
+    size = share * BLOCK
+    copies = []
+    for index, out in enumerate((first_ref.at[pl.ds(0, size), :], second_ref)):
+        start = pl.multiple_of(at[index] * BLOCK, BLOCK)
+        copies.append(pltpu.make_async_copy(rows_ref.at[pl.ds(start, size), :], out, sems.at[index]))
+        copies[-1].start()
+    depth = first_ref.shape[1]
+    parts = [ids_ref[pl.ds(at[index] + k, 1), :] for index in range(2) for k in range(share)]
+    edge = jnp.max(ids_ref[pl.ds(at[2], 1), :], axis=1, keepdims=True)
+    parts.append(jnp.broadcast_to(edge, (1, BLOCK)))
+    parts.append(jnp.zeros((1, depth - len(parts) * BLOCK), jnp.int32))
+    row = jnp.concatenate(parts, axis=1).astype(jnp.float32)
+    first_ref[size : size + 8, :] = jnp.broadcast_to(row, (8, depth)).astype(jnp.bfloat16)
+    for copy in copies:
+        copy.wait()
 
 
 def self_kernel(blocks, width, meta, rows_ref, tags_ref, unit_ref, sums_ref):
@@ -138,24 +156,11 @@
     return total
 
 
-def uncovered(tag, blocks, tiles, place):
-    half = blocks // 2
-    part = place % QUAD
-    quads = range(0, tiles, QUAD)
-    edge = jnp.broadcast_to(jnp.where(part == 1, tag[half - 1], tag[half]), (BLOCK,))
-    out = lax.ppermute(edge, "tile", [p for q in quads for p in ((q + 1, q), (q + 2, q + 3))])[0]
-    over = lax.ppermute(edge, "tile", [p for q in quads for p in ((q + 1, q + 3), (q + 2, q))])[0]
-    across = lax.ppermute(edge, "tile", [p for q in quads for p in ((q + 1, q + 2), (q + 2, q + 1))])[0]
-    inner = (part == 1) | (part == 2)
-    one = jnp.where(inner, edge[0], out)
-    other = jnp.where(inner, across, over)
-    bad = (one == other) & (one >= 0)
-    if tiles > QUAD:
-        last = jnp.broadcast_to(tag[blocks - 1], (BLOCK,))
-        before = lax.ppermute(last, "tile", [(t, t + 1) for t in range(tiles - 1)])[0]
-        bad = bad | ((part == 0) & (place > 0) & (before == tag[0]) & (before >= 0))
-        bad = lax.pmax(bad.astype(jnp.int32), "tile") > 0
-    return bad
+def quads_joined(tag, tiles, place):
+    last = jnp.broadcast_to(tag[-1], (BLOCK,))
+    before = lax.ppermute(last, "tile", [(t, t + 1) for t in range(tiles - 1)])[0]
+    joined = (place % QUAD == 0) & (place > 0) & (before == tag[0]) & (before >= 0)
+    return lax.pmax(joined.astype(jnp.int32), "tile") > 0
 
 
 def shards(embeddings, cluster_ids):
@@ -176,31 +181,36 @@
     ]
     back = [[(b, a) for a, b in route] for route in routes]
 
-    first_at = BLOCK * jnp.where(
+    first_block = jnp.where(
         part == 1, blocks // 2 + member * share, jnp.where(part == 2, member * share, member * width)
     )
-    second_at = BLOCK * (member * width + share)
-    carried = jnp.concatenate(
-        [lax.dynamic_slice_in_dim(cluster_ids, at, size, 0) for at in (first_at, second_at)]
-    ).astype(jnp.bfloat16)
-    carried = jnp.broadcast_to(jnp.pad(carried, (0, depth - 2 * size))[None], (8, depth))
-    first_out = jnp.concatenate([lax.dynamic_slice_in_dim(embeddings, first_at, size, 0), carried])
-    second_out = lax.dynamic_slice_in_dim(embeddings, second_at, size, 0)
+    first_at = first_block * BLOCK
+    edge_block = jnp.where(part == 1, blocks // 2 - 1, blocks // 2)
+    by_block = cluster_ids.reshape(blocks, BLOCK)
+    first_out, second_out = pl.pallas_call(
+        functools.partial(pack_kernel, blocks, share),
+        in_specs=[
+            pl.BlockSpec(memory_space=pltpu.SMEM),
+            pl.BlockSpec(memory_space=pl.ANY),
+            pl.BlockSpec(memory_space=pltpu.VMEM),
+        ],
+        out_specs=[pl.BlockSpec(memory_space=pltpu.VMEM)] * 2,
+        out_shape=[
+            jax.ShapeDtypeStruct((size + 8, depth), jnp.bfloat16),
+            jax.ShapeDtypeStruct((size, depth), jnp.bfloat16),
+        ],
+        scratch_shapes=[pltpu.SemaphoreType.DMA((2,))],
+        compiler_params=pltpu.CompilerParams(vmem_limit_bytes=8 * 1024 * 1024),
+    )(jnp.stack([first_block, member * width + share, edge_block]).astype(jnp.int32), embeddings, by_block)
     first = lax.ppermute(first_out, "tile", routes[0])
+    second = lax.ppermute(second_out, "tile", routes[1])
     third = lax.ppermute(first_out, "tile", routes[2])
-    second = lax.ppermute(second_out, "tile", routes[1])
-
-    by_block = cluster_ids.reshape(blocks, BLOCK)
+
     tag = jnp.max(by_block, axis=1)
     used = jnp.sum((by_block >= 0).astype(jnp.int32), axis=1)
     far = (part == 1) & (jnp.arange(blocks) >= blocks // 2)
     from_outer = jnp.where(inner, tag, -2)
     meta = jnp.concatenate([tag, used, tag, from_outer, jnp.where(far, -2, from_outer), member[None]]).astype(jnp.int32)
-
-    bad = uncovered(tag, blocks, tiles, place)
-    extra = lax.cond(
-        bad, lambda: every_pair(embeddings, cluster_ids), lambda: jnp.zeros((rows,), jnp.float32)
-    )
 
     row_sums = jax.ShapeDtypeStruct((blocks, BLOCK), jnp.float32)
     unit, sums = call(
@@ -225,8 +235,22 @@
     sums, first_cols = cross(0, first, first, sums)
     sums, third_cols = cross(2, third, third, sums)
     sums, second_cols = cross(1, second, first, sums)
-    returned = lax.ppermute(first_cols, "tile", back[0]) + lax.ppermute(third_cols, "tile", back[2])
+    edge = jnp.where(part == 1, tag[blocks // 2 - 1], tag[blocks // 2]).astype(jnp.float32)
+    first_cols = lax.ppermute(
+        jnp.concatenate([first_cols, jnp.broadcast_to(edge, (1, BLOCK))]), "tile", back[0]
+    )
+    returned = first_cols[:share] + lax.ppermute(third_cols, "tile", back[2])
     outer = lax.ppermute(second_cols, "tile", back[1])
+
+    one = jnp.where(inner, edge, first[size, 2 * size].astype(jnp.float32))
+    other = jnp.where(inner, third[size, 2 * size].astype(jnp.float32), first_cols[share, 0])
+    bad = (one == other) & (one >= 0)
+    if tiles > QUAD:
+        bad = lax.pmax(bad.astype(jnp.int32), "tile") > 0
+        bad = bad | quads_joined(tag, tiles, place)
+    extra = lax.cond(
+        bad, lambda: every_pair(embeddings, cluster_ids), lambda: jnp.zeros((rows,), jnp.float32)
+    )
 
     partial = sums.reshape(-1)
     here = lax.dynamic_slice_in_dim(partial, first_at, size, 0) + returned.reshape(-1)

time: 54.6 us -> 53.6 us (0.982)
  waiting for transfers between devices: 5.38 us -> 14.7 us
  starting transfers between devices: 23.1 us -> 16.1 us
  local copies, waits for them, and re-layouts: 7.79 us -> 2.49 us
  Pallas kernels: 13.5 us -> 15.4 us
  between operations: 1.55 us -> 3.32 us
  other arithmetic: 2.56 us -> 1.06 us
    ppermute x1, waiting for transfers between devices: 0.01 us -> 12.6 us  [shards(): first = lax.ppermute(first_out, 'tile', routes[0])]
    ppermute x5 -> x2, starting transfers between devices: 7.52 us -> 3.08 us  [the longest x1 2.42 us: shards(): lax.ppermute(jnp.concatenate([first_cols, jnp.broadcast_to(edge, (1, BLOC...]
    unnamed x6 -> x2, local copies, waits for them, and re-layouts: 4.12 us -> 0.01 us
    ppermute x5 -> x2, waiting for transfers between devices: 3.23 us -> 0.01 us  [the longest x1 0.01 us: shards(): returned = first_cols[:share] + lax.ppermute(third_cols, 'tile', back[2])]
    ppermute x1, starting transfers between devices: 4.57 us -> 1.95 us  [shards(): second = lax.ppermute(second_out, 'tile', routes[1])]
    dynamic_slice x1 -> x0, local copies, waits for them, and re-layouts: 2.07 us -> none  [shards(): lax.dynamic_slice_in_dim(embeddings, first_at, size, 0)]
    pallas_call x0 -> x1, Pallas kernels: none -> 1.93 us  [shards(): pl.pallas_call(functools.partial(pack_kernel, blocks, share), in_specs=[p...]
    slice x1 -> x4, local copies, waits for them, and re-layouts: 0.67 us -> 2.24 us  [the longest x1 0.62 us: shards(): tag[blocks // 2]]
  transfers between devices with their start and end apart: 12 -> 9, of which waited for: 3 -> 2; matrix products, arithmetic and copies ran while one was open for 5% -> 5% of each run, Pallas kernels for 25% -> 25%
where the time goes in v4:
time: 53.6 us; the launch traced here: 53.3 us
  starting transfers between devices  16.1 us (30%)
  Pallas kernels  15.4 us (29%)
  waiting for transfers between devices  14.7 us (27%)
  between operations  3.32 us (6%)
  local copies, waits for them, and re-layouts  2.49 us (5%)
  other arithmetic  1.06 us (2%)
    pallas_call x4, Pallas kernels, call(): pl.pallas_call(kernel, in_specs=[pl.BlockSpec(memory_space=pltpu.SMEM)] +...  13.5 us
    ppermute x1, waiting for transfers between devices, shards(): first = lax.ppermute(first_out, 'tile', routes[0])  12.6 us
    ppermute x1, starting transfers between devices, shards(): first = lax.ppermute(first_out, 'tile', routes[0])  5.87 us
    ppermute x3, starting transfers between devices, shards(): lax.ppermute(portion(shift), 'sub', [(i, (i + shift) % subs) for i in ran...  3.22 us
    ppermute x1, starting transfers between devices, shards(): lax.ppermute(jnp.concatenate([first_cols, jnp.broadcast_to(edge, (1, BLOC...  2.42 us
    ppermute x3, waiting for transfers between devices, shards(): lax.ppermute(portion(shift), 'sub', [(i, (i + shift) % subs) for i in ran...  2.09 us
    ppermute x1, starting transfers between devices, shards(): second = lax.ppermute(second_out, 'tile', routes[1])  1.95 us
    pallas_call x1, Pallas kernels, shards(): pl.pallas_call(functools.partial(pack_kernel, blocks, share), in_specs=[p...  1.93 us
  transfers between devices with their start and end apart: 9, of which 2 were waited for; matrix products, arithmetic and copies ran while one was open for 5% of the time, Pallas kernels for 25%

profile of v4, /device:TPU:0, one launch (start us, length us, event | category | flops | bytes accessed | tf_op | source)
XLA Modules:
  0.0 53.3 jit_solution(1490922277237723661)
XLA Ops:
  0.0 0.0 copy-start.3
  0.0 0.1 pad_add_fusion.at
  0.1 1.9 %shard_map.28 = (bf16[264,1024]{1,0:T(8,128)(2,1)S(1)}, bf16[256,1024]{1,0:T(8,128)(2,1)S(1)}) custom-call(s32[3]{0:T(128)S(1)} %pad_add_fusion.at, bf16[2048,1024]{1,0:T(8,128)(2,1)} %rows_ref.3, s32[16,128]{1,0:T(8,128)} %bitcast.56), custom_call_target="tpu_custom_call" | custom-call | tf_op jit(solution)/shard_map/pallas_call | solution.py:190
  2.0 0.7 %collective-permute-start.1 = (bf16[264,1024]{1,0:T(8,128)(2,1)S(1)}, bf16[264,1024]{1,0:T(8,128)(2,1)S(1)}, u32[]{:S(2)}, u32[]{:S(2)}) collective-permute-start(bf16[264,1024]{1,0:T(8,128)(2,1)S(1)} %get-tuple-element.24), channel_id=1, source_target_pairs={{4,8},{8,4},{5,9},{9,5},{6,10},{10,6},{7,11},{11,7},{20,24},{24,20... | collective-permute-start | bytes 1622024 | tf_op jit(solution)/shard_map/ppermute | solution.py:207
  2.7 5.9 %collective-permute-start = (bf16[264,1024]{1,0:T(8,128)(2,1)S(1)}, bf16[264,1024]{1,0:T(8,128)(2,1)S(1)}, u32[]{:S(2)}, u32[]{:S(2)}) collective-permute-start(bf16[264,1024]{1,0:T(8,128)(2,1)S(1)} %get-tuple-element.24), channel_id=1, source_target_pairs={{0,4},{12,8},{4,12},{8,0},{1,5},{13,9},{5,13},{9,1},{2,6},{14,10},... | collective-permute-start | bytes 1622024 | tf_op jit(solution)/shard_map/ppermute | solution.py:205
  8.6 1.9 %collective-permute-start.3 = (bf16[256,1024]{1,0:T(8,128)(2,1)S(1)}, bf16[256,1024]{1,0:T(8,128)(2,1)S(1)}, u32[]{:S(2)}, u32[]{:S(2)}) collective-permute-start(bf16[256,1024]{1,0:T(8,128)(2,1)S(1)} %get-tuple-element.28), channel_id=1, source_target_pairs={{0,4},{12,8},{1,5},{13,9},{2,6},{14,10},{3,7},{15,11},{16,20},{28,... | collective-permute-start | bytes 1572872 | tf_op jit(solution)/shard_map/ppermute | solution.py:206
  10.5 0.0 copy-done.3
  10.6 0.1 convert_reduce_fusion
  10.7 0.6 %fusion.23 = (s32[1]{0:T(128)}, s32[1]{0:T(128)}) fusion(s32[16]{0:T(128)S(1)} %get-tuple-element.35), kind=kLoop, calls=%fused_computation.63 | loop fusion | bytes 16 | tf_op jit(solution)/shard_map/slice | solution.py:238
  12.5 0.1 dynamic_slice.62
  12.6 0.1 concatenate.9.meta
  12.7 6.7 %shard_map.29 = (bf16[2048,1024]{1,0:T(8,128)(2,1)S(1)}, f32[16,128]{1,0:T(8,128)S(1)}) custom-call(s32[81]{0:T(128)S(1)} %concatenate.9.meta, bf16[2048,1024]{1,0:T(8,128)(2,1)} %rows_ref.3, s32[1,512]{1,0:T(1,128)S(1)} %bitcast.55), custom_call_target="tpu_custom_call" | custom-call | flops 2147483648 | bytes 1048576 | tf_op jit(solution)/shard_map/pallas_call | solution.py:111
  19.4 12.6 %collective-permute-done.piece_ref.tags_ref = bf16[264,1024]{1,0:T(8,128)(2,1)S(1)} collective-permute-done((bf16[264,1024]{1,0:T(8,128)(2,1)S(1)}, bf16[264,1024]{1,0:T(8,128)(2,1)S(1)}, u32[]{:S(2)}, u32[]{:S(2)}) %collective-permute-start) | collective-permute-done | bytes 540704 | tf_op jit(solution)/shard_map/ppermute | solution.py:205
  32.0 2.3 %shard_map.30 = (f32[16,128]{1,0:T(8,128)S(1)}, f32[2,128]{1,0:T(2,128)S(1)}) custom-call(s32[81]{0:T(128)S(1)} %concatenate.9.meta, bf16[2048,1024]{1,0:T(8,128)(2,1)S(1)} %get-tuple-element.25.unit_ref, bf16[264,1024]{1,0:T(8,128)(2,1)S(1)} %collective-permute-done.piece_ref.tags_ref, bf16[264,1024]{1,0:T(8,128)(2,1)S(1)} %collective-permute-done.piece_ref.tags_ref, ...), custom_call_target="tpu_custom_call" | custom-call | flops 1073741824 | bytes 1048576 | tf_op jit(solution)/shard_map/pallas_call | solution.py:111
  34.2 0.0 collective-permute-done.1.piece_ref.tags_ref
  34.2 2.3 %shard_map.31 = (f32[16,128]{1,0:T(8,128)S(1)}, f32[2,128]{1,0:T(2,128)S(1)}) custom-call(s32[81]{0:T(128)S(1)} %concatenate.9.meta, bf16[2048,1024]{1,0:T(8,128)(2,1)S(1)} %get-tuple-element.25.unit_ref, bf16[264,1024]{1,0:T(8,128)(2,1)S(1)} %collective-permute-done.1.piece_ref.tags_ref, bf16[264,1024]{1,0:T(8,128)(2,1)S(1)} %collective-permute-done.1.piece_ref.tags_ref, ...), custom_call_target="tpu_custom_call" | custom-call | flops 1073741824 | bytes 1048576 | tf_op jit(solution)/shard_map/pallas_call | solution.py:111
  36.5 0.7 %collective-permute-start.4 = (f32[2,128]{1,0:T(2,128)S(1)}, f32[2,128]{1,0:T(2,128)S(1)}, u32[]{:S(2)}, u32[]{:S(2)}) collective-permute-start(f32[2,128]{1,0:T(2,128)S(1)} %get-tuple-element.32), channel_id=1, source_target_pairs={{8,4},{4,8},{9,5},{5,9},{10,6},{6,10},{11,7},{7,11},{24,20},{20,24... | collective-permute-start | bytes 3080 | tf_op jit(solution)/shard_map/ppermute | solution.py:242
  37.2 2.4 %collective-permute-start.2 = (f32[3,128]{1,0:T(4,128)S(1)}, f32[3,128]{1,0:T(4,128)S(1)}, u32[]{:S(2)}, u32[]{:S(2)}) collective-permute-start(f32[3,128]{1,0:T(4,128)S(1)} %concatenate.10), channel_id=1, source_target_pairs={{4,0},{8,12},{12,4},{0,8},{5,1},{9,13},{13,5},{1,9},{6,2},{10,14},... | collective-permute-start | bytes 4616 | tf_op jit(solution)/shard_map/ppermute | solution.py:239
  39.6 0.0 collective-permute-done.3.piece_ref
  39.6 2.3 %shard_map.32 = (f32[16,128]{1,0:T(8,128)S(1)}, f32[2,128]{1,0:T(2,128)S(1)}) custom-call(s32[81]{0:T(128)S(1)} %concatenate.9.meta, bf16[2048,1024]{1,0:T(8,128)(2,1)S(1)} %get-tuple-element.25.unit_ref, bf16[256,1024]{1,0:T(8,128)(2,1)S(1)} %collective-permute-done.3.piece_ref, bf16[264,1024]{1,0:T(8,128)(2,1)S(1)} %collective-permute-done.piece_ref.tags_ref, ...), custom_call_target="tpu_custom_call" | custom-call | flops 1073741824 | bytes 1048576 | tf_op jit(solution)/shard_map/pallas_call | solution.py:111
  41.9 0.5 slice.24
  43.0 1.3 %collective-permute-start.8 = (f32[2,128]{1,0:T(2,128)S(1)}, f32[2,128]{1,0:T(2,128)S(1)}, u32[]{:S(2)}, u32[]{:S(2)}) collective-permute-start(f32[2,128]{1,0:T(2,128)S(1)} %get-tuple-element.33), channel_id=1, source_target_pairs={{4,0},{8,12},{5,1},{9,13},{6,2},{10,14},{7,3},{11,15},{20,16},{24,... | collective-permute-start | bytes 3080 | tf_op jit(solution)/shard_map/ppermute | solution.py:243
  44.3 0.5 slice.25
  44.8 0.0 collective-permute-done.2
  44.8 0.6 %slice.22 = f32[1,1]{1,0:T(1,128)} slice(f32[3,128]{1,0:T(4,128)S(1)} %collective-permute-done.2), slice={[2:3], [0:1]} | slice | bytes 8 | tf_op jit(solution)/shard_map/slice | solution.py:246
  46.8 0.2 conditional.1
  47.0 0.0 collective-permute-done.4
  47.1 0.2 fusion.21
  47.3 0.1 fusion.22
  47.3 0.0 collective-permute-start.5
  47.3 1.7 %collective-permute-start.7 = (f32[512]{0:T(512)S(1)}, f32[512]{0:T(512)S(1)}, u32[]{:S(2)}, u32[]{:S(2)}) collective-permute-start(f32[512]{0:T(512)S(1)} %get-tuple-element.45), channel_id=1, source_target_pairs={{0,3},{1,0},{2,1},{3,2},{4,7},{5,4},{6,5},{7,6},{8,11},{9,8},{10,9... | collective-permute-start | bytes 6152 | tf_op jit(solution)/shard_map/ppermute | solution.py:266
  49.1 1.5 %collective-permute-start.6 = (f32[512]{0:T(512)S(1)}, f32[512]{0:T(512)S(1)}, u32[]{:S(2)}, u32[]{:S(2)}) collective-permute-start(f32[512]{0:T(512)S(1)} %get-tuple-element.46), channel_id=1, source_target_pairs={{0,2},{1,3},{2,0},{3,1},{4,6},{5,7},{6,4},{7,5},{8,10},{9,11},{10,... | collective-permute-start | bytes 6152 | tf_op jit(solution)/shard_map/ppermute | solution.py:266
  50.6 0.0 collective-permute-done.8
  50.6 0.0 collective-permute-done.5
  50.6 0.0 collective-permute-done.7
  50.6 2.1 %collective-permute-done.6 = f32[512]{0:T(512)S(1)} collective-permute-done((f32[512]{0:T(512)S(1)}, f32[512]{0:T(512)S(1)}, u32[]{:S(2)}, u32[]{:S(2)}) %collective-permute-start.6) | collective-permute-done | bytes 2080 | tf_op jit(solution)/shard_map/ppermute | solution.py:266
  52.7 0.7 %add_log_fusion = f32[512]{0:T(512)} fusion(f32[256]{0:T(256)S(1)} %select_bitcast_fusion, f32[512]{0:T(512)S(1)} %collective-permute-done.7, f32[512]{0:T(512)S(1)} %collective-permute-done.6, f32[512]{0:T(512)S(1)} %collective-permute-done.5, f32[2048]{0:T(1024)S(1)} %broadcast_select_fusion.8, s32[]{:T(128)S(6)} %select_n.226), kind=kLoop, calls=%fused_computation.54 | loop fusion | flops 2560 | bytes 11268 | tf_op jit(solution)/shard_map/log | solution.py:269
  (5 shorter events, 0.0 us)
Async XLA Ops:
  0.0 10.5 %copy-start.3 = (s32[2048]{0:T(1024)S(1)}, s32[2048]{0:T(1024)}, u32[]{:S(2)}) copy-start(s32[2048]{0:T(1024)} %param.5) | copy-start | bytes 24580
  2.0 32.2 %collective-permute-start.1 = (bf16[264,1024]{1,0:T(8,128)(2,1)S(1)}, bf16[264,1024]{1,0:T(8,128)(2,1)S(1)}, u32[]{:S(2)}, u32[]{:S(2)}) collective-permute-start(bf16[264,1024]{1,0:T(8,128)(2,1)S(1)} %get-tuple-element.24), channel_id=1, source_target_pairs={{4,8},{8,4},{5,9},{9,5},{6,10},{10,6},{7,11},{11,7},{20,24},{24,20... | collective-permute-start | bytes 1622024 | tf_op jit(solution)/shard_map/ppermute | solution.py:207
  2.7 29.3 %collective-permute-start = (bf16[264,1024]{1,0:T(8,128)(2,1)S(1)}, bf16[264,1024]{1,0:T(8,128)(2,1)S(1)}, u32[]{:S(2)}, u32[]{:S(2)}) collective-permute-start(bf16[264,1024]{1,0:T(8,128)(2,1)S(1)} %get-tuple-element.24), channel_id=1, source_target_pairs={{0,4},{12,8},{4,12},{8,0},{1,5},{13,9},{5,13},{9,1},{2,6},{14,10},... | collective-permute-start | bytes 1622024 | tf_op jit(solution)/shard_map/ppermute | solution.py:205
  8.6 31.0 %collective-permute-start.3 = (bf16[256,1024]{1,0:T(8,128)(2,1)S(1)}, bf16[256,1024]{1,0:T(8,128)(2,1)S(1)}, u32[]{:S(2)}, u32[]{:S(2)}) collective-permute-start(bf16[256,1024]{1,0:T(8,128)(2,1)S(1)} %get-tuple-element.28), channel_id=1, source_target_pairs={{0,4},{12,8},{1,5},{13,9},{2,6},{14,10},{3,7},{15,11},{16,20},{28,... | collective-permute-start | bytes 1572872 | tf_op jit(solution)/shard_map/ppermute | solution.py:206
  36.5 10.6 %collective-permute-start.4 = (f32[2,128]{1,0:T(2,128)S(1)}, f32[2,128]{1,0:T(2,128)S(1)}, u32[]{:S(2)}, u32[]{:S(2)}) collective-permute-start(f32[2,128]{1,0:T(2,128)S(1)} %get-tuple-element.32), channel_id=1, source_target_pairs={{8,4},{4,8},{9,5},{5,9},{10,6},{6,10},{11,7},{7,11},{24,20},{20,24... | collective-permute-start | bytes 3080 | tf_op jit(solution)/shard_map/ppermute | solution.py:242
  37.2 7.7 %collective-permute-start.2 = (f32[3,128]{1,0:T(4,128)S(1)}, f32[3,128]{1,0:T(4,128)S(1)}, u32[]{:S(2)}, u32[]{:S(2)}) collective-permute-start(f32[3,128]{1,0:T(4,128)S(1)} %concatenate.10), channel_id=1, source_target_pairs={{4,0},{8,12},{12,4},{0,8},{5,1},{9,13},{13,5},{1,9},{6,2},{10,14},... | collective-permute-start | bytes 4616 | tf_op jit(solution)/shard_map/ppermute | solution.py:239
  43.0 7.5 %collective-permute-start.8 = (f32[2,128]{1,0:T(2,128)S(1)}, f32[2,128]{1,0:T(2,128)S(1)}, u32[]{:S(2)}, u32[]{:S(2)}) collective-permute-start(f32[2,128]{1,0:T(2,128)S(1)} %get-tuple-element.33), channel_id=1, source_target_pairs={{4,0},{8,12},{5,1},{9,13},{6,2},{10,14},{7,3},{11,15},{20,16},{24,... | collective-permute-start | bytes 3080 | tf_op jit(solution)/shard_map/ppermute | solution.py:243
  47.3 3.2 %collective-permute-start.5 = (f32[512]{0:T(512)S(1)}, f32[512]{0:T(512)S(1)}, u32[]{:S(2)}, u32[]{:S(2)}) collective-permute-start(f32[512]{0:T(512)S(1)} %get-tuple-element.44), channel_id=1, source_target_pairs={{0,1},{1,2},{2,3},{3,0},{4,5},{5,6},{6,7},{7,4},{8,9},{9,10},{10,1... | collective-permute-start | bytes 6152 | tf_op jit(solution)/shard_map/ppermute | solution.py:266
  47.3 3.2 %collective-permute-start.7 = (f32[512]{0:T(512)S(1)}, f32[512]{0:T(512)S(1)}, u32[]{:S(2)}, u32[]{:S(2)}) collective-permute-start(f32[512]{0:T(512)S(1)} %get-tuple-element.45), channel_id=1, source_target_pairs={{0,3},{1,0},{2,1},{3,2},{4,7},{5,4},{6,5},{7,6},{8,11},{9,8},{10,9... | collective-permute-start | bytes 6152 | tf_op jit(solution)/shard_map/ppermute | solution.py:266
  49.1 3.6 %collective-permute-start.6 = (f32[512]{0:T(512)S(1)}, f32[512]{0:T(512)S(1)}, u32[]{:S(2)}, u32[]{:S(2)}) collective-permute-start(f32[512]{0:T(512)S(1)} %get-tuple-element.46), channel_id=1, source_target_pairs={{0,2},{1,3},{2,0},{3,1},{4,6},{5,7},{6,4},{7,5},{8,10},{9,11},{10,... | collective-permute-start | bytes 6152 | tf_op jit(solution)/shard_map/ppermute | solution.py:266

commit v5 on v4

v5 whole, which is shorter than its diff:
```python
import functools
import math

import jax
import jax.numpy as jnp
import numpy as np
from jax import lax
from jax.experimental import pallas as pl
from jax.experimental.pallas import tpu as pltpu
from jax.sharding import PartitionSpec as P

BLOCK = 128
QUAD = 4
SPAN = 4

inverse_temp = 10.0
norm_eps = 1e-06
GAIN = inverse_temp * math.log2(math.e)
OFF = -1000.0

STEP = 512


def normalised(values):
    values = values.astype(jnp.float32)
    scale = lax.rsqrt(jnp.sum(values * values, axis=1, keepdims=True) + norm_eps)
    return (values * scale).astype(jnp.bfloat16)


def products(rows, columns):
    return lax.dot_general(
        rows, columns, (((1,), (1,)), ((), ())), preferred_element_type=jnp.float32
    )


def column_bias(tag, column_tags):
    return jnp.where(column_tags == tag.astype(jnp.float32), -GAIN, OFF)


def lane_sums(weight):
    total = weight[:, :BLOCK]
    for start in range(BLOCK, weight.shape[1], BLOCK):
        total = total + weight[:, start : start + BLOCK]
    return jnp.sum(total.T, axis=0, keepdims=True)


def pack_kernel(share, at, rows_ref, ids_ref, first_ref, second_ref, sems):
    size = share * BLOCK
    copies = []
    for index, out in enumerate((first_ref, second_ref)):
        start = pl.multiple_of(at[index] * BLOCK, BLOCK)
        copies.append(
            pltpu.make_async_copy(rows_ref.at[pl.ds(start, size), :], out.at[pl.ds(0, size), :], sems.at[index])
        )
        copies[-1].start()
    depth = first_ref.shape[1]
    edge = jnp.max(ids_ref[pl.ds(at[2], 1), :], axis=1, keepdims=True)
    rest = [jnp.broadcast_to(edge, (1, BLOCK)), jnp.zeros((1, depth - size - BLOCK), jnp.int32)]
    for index, out in enumerate((first_ref, second_ref)):
        row = jnp.concatenate([ids_ref[pl.ds(at[index] + k, 1), :] for k in range(share)] + rest, axis=1)
        out[size : size + 8, :] = jnp.broadcast_to(row.astype(jnp.float32), (8, depth)).astype(jnp.bfloat16)
    for copy in copies:
        copy.wait()


class Meta:
    def __init__(self, ref, blocks):
        self.ref, self.blocks = ref, blocks

    def tag(self, block, chunk=None):
        return self.ref[block + (0 if chunk is None else (2 + chunk) * self.blocks)]

    def used(self, block):
        return self.ref[self.blocks + block]

    def number(self, index):
        return self.ref[5 * self.blocks + index]


MEMBER, FIRST_BLOCK, EDGE = range(3)


def self_kernel(blocks, width, meta_ref, rows_ref, tags_ref, unit_ref, sums_ref):
    meta = Meta(meta_ref, blocks)
    for start in range(0, blocks * BLOCK, STEP):
        unit_ref[start : start + STEP, :] = normalised(rows_ref[start : start + STEP, :])
    first_col = meta.number(MEMBER) * width
    share = unit_ref[pl.ds(pl.multiple_of(first_col * BLOCK, width * BLOCK), width * BLOCK), :]
    column_tags = tags_ref[...].astype(jnp.float32)
    for start in range(0, blocks * BLOCK, STEP):
        cosine = products(unit_ref[start : start + STEP, :], share)
        for inner in range(0, STEP, BLOCK):
            block = (start + inner) // BLOCK
            bias = column_bias(meta.tag(block), column_tags)
            weight = jnp.exp2(cosine[inner : inner + BLOCK] * GAIN + bias)
            row = lax.broadcasted_iota(jnp.int32, weight.shape, 0)
            col = lax.broadcasted_iota(jnp.int32, weight.shape, 1)
            shift = (block - first_col) * BLOCK
            weight = jnp.where((row < meta.used(block)) & (col - row != shift), weight, 0.0)
            sums_ref[block : block + 1, :] = lane_sums(weight)


def chunk_tags(piece_ref, size):
    row = piece_ref[size : size + 8, :].astype(jnp.float32)[0:1, :]
    return row[:, :size], row[:, size : size + BLOCK]


def cross_terms(meta, chunks, column_tags, unit_ref, piece_unit, add_rows):
    size = column_tags[0].shape[1]
    columns = None
    for start in range(0, meta.blocks * BLOCK, STEP):
        cosine = products(unit_ref[start : start + STEP, :], piece_unit[...])
        for inner in range(0, STEP, BLOCK):
            block = (start + inner) // BLOCK
            bias = [column_bias(meta.tag(block, chunk), tags) for chunk, tags in zip(chunks, column_tags)]
            bias = jnp.concatenate(bias, axis=1) if len(bias) > 1 else bias[0]
            weight = jnp.exp2(cosine[inner : inner + BLOCK] * GAIN + bias)
            row = lax.broadcasted_iota(jnp.int32, weight.shape, 0)
            weight = jnp.where(row < meta.used(block), weight, 0.0)
            add_rows(block, lane_sums(weight))
            partial = weight[0:8]
            for down in range(8, BLOCK, 8):
                partial = partial + weight[down : down + 8]
            columns = partial if columns is None else columns + partial
    total = jnp.sum(columns, axis=0, keepdims=True)
    return [
        [total[:, at + down : at + down + BLOCK] for down in range(0, size, BLOCK)]
        for at in range(0, total.shape[1], size)
    ]


def middle_kernel(
    blocks, share, meta_ref, unit_ref, outer_ref, swap_ref, before_ref, sums_ref, outer_cols_ref, swap_cols_ref,
    piece_unit,
):
    meta = Meta(meta_ref, blocks)
    size = share * BLOCK
    piece_unit[:size, :] = normalised(outer_ref[:size, :])
    piece_unit[size:, :] = normalised(swap_ref[:size, :])
    outer_tags, _ = chunk_tags(outer_ref, size)
    swap_tags, edge = chunk_tags(swap_ref, size)

    def add_rows(block, value):
        sums_ref[block : block + 1, :] = before_ref[block : block + 1, :] + value

    outer, swap = cross_terms(meta, (0, 1), (outer_tags, swap_tags), unit_ref, piece_unit, add_rows)
    for k in range(share):
        outer_cols_ref[k : k + 1, :] = outer[k]
        swap_cols_ref[k : k + 1, :] = swap[k]
    mine = meta.number(EDGE).astype(jnp.float32)
    outer_cols_ref[share : share + 1, :] = jnp.where((edge == mine) & (edge >= 0), 1.0, 0.0)


def last_kernel(
    blocks, share, width, meta_ref, unit_ref, piece_ref, before_ref, outer_back_ref, swap_back_ref,
    keep_ref, send_ref, cols_ref, piece_unit, sums,
):
    meta = Meta(meta_ref, blocks)
    size = share * BLOCK
    piece_unit[...] = normalised(piece_ref[:size, :])
    tags, _ = chunk_tags(piece_ref, size)

    def place(block):
        owner = block // width
        return owner % 2 * (blocks // 2) + owner // 2 * width + block % width

    def add_rows(block, value):
        at = place(block)
        sums[at : at + 1, :] = before_ref[block : block + 1, :] + value

    (cols,) = cross_terms(meta, (2,), (tags,), unit_ref, piece_unit, add_rows)
    for k in range(share):
        cols_ref[k : k + 1, :] = cols[k]
        at = place(meta.number(FIRST_BLOCK) + k)
        sums[pl.ds(at, 1), :] += outer_back_ref[k : k + 1, :] + swap_back_ref[k : k + 1, :]
    parity = meta.number(MEMBER) % 2
    heap = blocks // 2
    keep_ref[...] = sums[pl.ds(pl.multiple_of(parity * heap, heap), heap), :]
    send_ref[...] = sums[pl.ds(pl.multiple_of((1 - parity) * heap, heap), heap), :]


def call(kernel, meta, operands, out_shapes, scratch, flops):
    vmem = pl.BlockSpec(memory_space=pltpu.VMEM)
    return pl.pallas_call(
        kernel,
        in_specs=[pl.BlockSpec(memory_space=pltpu.SMEM)] + [vmem] * len(operands),
        out_specs=jax.tree.map(lambda _: vmem, out_shapes),
        out_shape=out_shapes,
        scratch_shapes=scratch,
        compiler_params=pltpu.CompilerParams(vmem_limit_bytes=16 * 1024 * 1024),
        cost_estimate=pl.CostEstimate(flops=flops, bytes_accessed=1024 * 1024, transcendentals=flops // 2048),
    )(meta, *operands)


def every_pair(embeddings, cluster_ids):
    unit = normalised(embeddings)
    tags = cluster_ids + 1
    groups = lax.axis_size("sub")
    member = lax.axis_index("sub")
    owners = lax.axis_size("tile")
    place = lax.axis_index("tile")
    rows_here = unit.shape[0]
    width = rows_here // groups
    own_piece = lax.dynamic_slice_in_dim(unit, member * width, width, 0)
    own_tags = lax.dynamic_slice_in_dim(tags, member * width, width, 0)
    distance = place - jnp.arange(owners, dtype=jnp.int32)
    keep = (jnp.abs(distance) < SPAN) & (distance != 0)
    outgoing = jnp.where(keep[:, None, None], own_piece[None, :, :], jnp.zeros((), jnp.bfloat16))
    outgoing_tags = jnp.where(keep[:, None], own_tags[None, :], 0)
    arrived = lax.all_to_all(outgoing, "tile", split_axis=0, concat_axis=0, tiled=True)
    arrived_tags = lax.all_to_all(outgoing_tags, "tile", split_axis=0, concat_axis=0, tiled=True)
    local_rows = jnp.arange(rows_here, dtype=jnp.int32)[:, None]
    slice_rows = member * width + jnp.arange(width, dtype=jnp.int32)[None, :]
    total = jnp.zeros((rows_here,), jnp.float32)
    for offset in range(1 - SPAN, SPAN):
        if offset == 0:
            piece, piece_tags, order = own_piece, own_tags, local_rows != slice_rows
        else:
            source = place + offset
            valid = (source >= 0) & (source < owners)
            index = jnp.clip(source, 0, owners - 1)
            piece = lax.dynamic_index_in_dim(arrived, index, 0, keepdims=False)
            piece_tags = lax.dynamic_index_in_dim(arrived_tags, index, 0, keepdims=False)
            piece_tags = jnp.where(valid, piece_tags, 0)
            order = True
        same = (tags[:, None] == piece_tags[None, :]) & (tags[:, None] > 0) & order
        weight = jnp.where(same, jnp.exp(inverse_temp * (products(unit, piece) - 1.0)), 0.0)
        total = total + jnp.sum(weight, axis=1)
    return jnp.log(1.0 + lax.psum_scatter(total, "sub", scatter_dimension=0, tiled=True))


def quads_joined(tag, tiles, place):
    last = jnp.broadcast_to(tag[-1], (BLOCK,))
    before = lax.ppermute(last, "tile", [(t, t + 1) for t in range(tiles - 1)])[0]
    joined = (place % QUAD == 0) & (place > 0) & (before == tag[0]) & (before >= 0)
    return lax.pmax(joined.astype(jnp.int32), "tile") > 0


def shards(embeddings, cluster_ids):
    tiles, subs = lax.axis_size("tile"), lax.axis_size("sub")
    place, member = lax.axis_index("tile"), lax.axis_index("sub")
    rows, depth = embeddings.shape
    blocks = rows // BLOCK
    width = blocks // subs
    share = width // 2
    size = share * BLOCK
    part = place % QUAD
    inner = (part == 1) | (part == 2)
    quads = range(0, tiles, QUAD)
    inward = [p for q in quads for p in ((q, q + 1), (q + 3, q + 2))]
    swap = [p for q in quads for p in ((q + 1, q + 2), (q + 2, q + 1))]
    around = [p for q in quads for p in ((q, q + 1), (q + 3, q + 2), (q + 1, q + 3), (q + 2, q))]

    def turned(route):
        return [(b, a) for a, b in route]

    dealt = member // 2 * share
    near = (dealt // width * 2 + member % 2) * width + dealt % width
    near = jnp.where(part == 1, blocks // 2, 0) + near
    first_block = jnp.where(inner, near, member * width)
    second_block = jnp.where(inner, near, member * width + share)
    edge_block = jnp.where(part == 1, blocks // 2 - 1, blocks // 2)
    by_block = cluster_ids.reshape(blocks, BLOCK)
    vmem = pl.BlockSpec(memory_space=pltpu.VMEM)
    first_out, second_out = pl.pallas_call(
        functools.partial(pack_kernel, share),
        in_specs=[pl.BlockSpec(memory_space=pltpu.SMEM), pl.BlockSpec(memory_space=pl.ANY), vmem],
        out_specs=[vmem] * 2,
        out_shape=[jax.ShapeDtypeStruct((size + 8, depth), jnp.bfloat16)] * 2,
        scratch_shapes=[pltpu.SemaphoreType.DMA((2,))],
        compiler_params=pltpu.CompilerParams(vmem_limit_bytes=8 * 1024 * 1024),
    )(jnp.stack([first_block, second_block, edge_block]).astype(jnp.int32), embeddings, by_block)
    from_outer = lax.ppermute(first_out, "tile", inward)
    from_inner = lax.ppermute(first_out, "tile", swap)

    tag = jnp.max(by_block, axis=1)
    used = jnp.sum((by_block >= 0).astype(jnp.int32), axis=1)
    edge = jnp.where(part == 1, tag[blocks // 2 - 1], tag[blocks // 2])
    far = (part == 1) & (jnp.arange(blocks) >= blocks // 2)
    seen = jnp.where(inner, tag, -2)
    meta = jnp.concatenate(
        [tag, used, seen, jnp.where(far, -2, seen), tag, jnp.stack([member, first_block, edge])]
    ).astype(jnp.int32)

    row_sums = jax.ShapeDtypeStruct((blocks, BLOCK), jnp.float32)
    col_sums = jax.ShapeDtypeStruct((share, BLOCK), jnp.float32)
    unit, sums = call(
        functools.partial(self_kernel, blocks, width),
        meta,
        (embeddings, lax.dynamic_slice_in_dim(cluster_ids, member * width * BLOCK, width * BLOCK, 0)[None]),
        [jax.ShapeDtypeStruct((rows, depth), jnp.bfloat16), row_sums],
        [],
        2 * rows * width * BLOCK * depth,
    )
    second_out, sums = lax.optimization_barrier((second_out, sums))
    last = lax.ppermute(second_out, "tile", around)
    sums, outer_cols, swap_cols = call(
        functools.partial(middle_kernel, blocks, share),
        meta,
        (unit, from_outer, from_inner, sums),
        [row_sums, jax.ShapeDtypeStruct((share + 1, BLOCK), jnp.float32), col_sums],
        [pltpu.VMEM((2 * size, depth), jnp.bfloat16)],
        4 * rows * size * depth,
    )
    outer_back = lax.ppermute(outer_cols, "tile", turned(inward))
    swap_back = lax.ppermute(swap_cols, "tile", turned(swap))

    bad = jnp.where(inner, outer_cols[share, 0], outer_back[share, 0]) > 0
    if tiles > QUAD:
        bad = lax.pmax(bad.astype(jnp.int32), "tile") > 0
        bad = bad | quads_joined(tag, tiles, place)

    half = jax.ShapeDtypeStruct((blocks // 2, BLOCK), jnp.float32)
    held, leaving, cols = call(
        functools.partial(last_kernel, blocks, share, width),
        meta,
        (unit, last, sums, outer_back, swap_back),
        [half, half, col_sums],
        [pltpu.VMEM((size, depth), jnp.bfloat16), pltpu.VMEM((blocks, BLOCK), jnp.float32)],
        2 * rows * size * depth,
    )

    came = lax.ppermute(leaving, "sub", [(i, i ^ 1) for i in range(subs)])
    home = lax.ppermute(cols, "tile", turned(around))
    owner = second_block // width
    home_at = owner // 2 * width + second_block % width
    held = held + came
    held = lax.dynamic_update_slice_in_dim(
        held, lax.dynamic_slice_in_dim(held, home_at, share, 0) + home, home_at, 0
    )
    bit = 1
    while 1 << bit < subs:
        pairs = held.reshape(-1, 2, width, BLOCK)
        own = (member >> bit) & 1
        leaving = lax.dynamic_index_in_dim(pairs, 1 - own, 1, keepdims=False)
        came = lax.ppermute(leaving, "sub", [(i, i ^ (1 << bit)) for i in range(subs)])
        held = lax.dynamic_index_in_dim(pairs, own, 1, keepdims=False) + came
        bit += 1
    scores = jnp.log(1.0 + held.reshape(-1))
    return lax.cond(bad, lambda: every_pair(embeddings, cluster_ids), lambda: scores)


def solution(mesh):
    in_specs = (P(("groups", "tile"), None), P(("groups", "tile")))
    out_specs = P(("groups", "tile", "sub"))
    return jax.shard_map(shards, mesh=mesh, in_specs=in_specs, out_specs=out_specs, check_vma=False)
```

time: 53.6 us -> 45.4 us (0.85)
  waiting for transfers between devices: 14.7 us -> 10.4 us
  starting transfers between devices: 16.1 us -> 14.4 us
  Pallas kernels: 15.4 us -> 14.5 us
  other arithmetic: 1.06 us -> 0.22 us
  between operations: 3.32 us -> 2.76 us
    ppermute x9 -> x8, waiting for transfers between devices: 14.7 us -> 10.4 us  [the longest x1 5.08 us: shards(): last = lax.ppermute(second_out, 'tile', around)]
    ppermute x9 -> x8, starting transfers between devices: 16.1 us -> 14.4 us  [the longest x1 7.75 us: shards(): from_outer = lax.ppermute(first_out, 'tile', inward)]
    pallas_call x4 -> x3, Pallas kernels: 13.5 us -> 12.6 us  [call(): pl.pallas_call(kernel, in_specs=[pl.BlockSpec(memory_space=pltpu.SMEM)] +...]
    log x1, other arithmetic: 0.66 us -> 0.01 us  [shards(): scores = jnp.log(1.0 + held.reshape(-1))]
    unnamed x2 -> x4, local copies, waits for them, and re-layouts: 0.01 us -> 0.58 us
    slice x4 -> x3, local copies, waits for them, and re-layouts: 2.24 us -> 1.75 us  [the longest x2 1.11 us: shards(): bad = jnp.where(inner, outer_cols[share, 0], outer_back[share, 0]) > 0]
  transfers between devices with their start and end apart: 9 -> 8, of which waited for: 2 -> 3; matrix products, arithmetic and copies ran while one was open for 5% -> 5% of each run, Pallas kernels for 25% -> 23%
where the time goes in v5:
time: 45.4 us; the launch traced here: 45.1 us
  Pallas kernels  14.5 us (32%)
  starting transfers between devices  14.4 us (32%)
  waiting for transfers between devices  10.4 us (23%)
  between operations  2.76 us (6%)
  local copies, waits for them, and re-layouts  2.59 us (6%)
    pallas_call x3, Pallas kernels, call(): pl.pallas_call(kernel, in_specs=[pl.BlockSpec(memory_space=pltpu.SMEM)] +...  12.6 us
    ppermute x1, starting transfers between devices, shards(): from_outer = lax.ppermute(first_out, 'tile', inward)  7.75 us
    ppermute x1, waiting for transfers between devices, shards(): last = lax.ppermute(second_out, 'tile', around)  5.08 us
    ppermute x1, waiting for transfers between devices, shards(): from_outer = lax.ppermute(first_out, 'tile', inward)  3.69 us
    ppermute x1, starting transfers between devices, shards(): home = lax.ppermute(cols, 'tile', turned(around))  2.35 us
    pallas_call x1, Pallas kernels, shards(): pl.pallas_call(functools.partial(pack_kernel, share), in_specs=[pl.BlockS...  1.93 us
    ppermute x1, waiting for transfers between devices, shards(): home = lax.ppermute(cols, 'tile', turned(around))  1.6 us
    ppermute x1, starting transfers between devices, shards(): lax.ppermute(leaving, 'sub', [(i, i ^ 1 << bit) for i in range(subs)])  1.55 us
  transfers between devices with their start and end apart: 8, of which 3 were waited for; matrix products, arithmetic and copies ran while one was open for 5% of the time, Pallas kernels for 23%

profile of v5, /device:TPU:0, one launch (start us, length us, event | category | flops | bytes accessed | tf_op | source)
XLA Modules:
  0.0 45.1 jit_solution(9686249207809454150)
XLA Ops:
  0.0 0.0 copy-start.3
  0.0 0.1 pad_add_fusion.at
  0.1 1.9 %shard_map.31 = (bf16[264,1024]{1,0:T(8,128)(2,1)S(1)}, bf16[264,1024]{1,0:T(8,128)(2,1)S(1)}) custom-call(s32[3]{0:T(128)S(1)} %pad_add_fusion.at, bf16[2048,1024]{1,0:T(8,128)(2,1)} %rows_ref.3, s32[16,128]{1,0:T(8,128)} %bitcast.60), custom_call_target="tpu_custom_call" | custom-call | tf_op jit(solution)/shard_map/pallas_call | solution.py:265
  2.0 0.7 %collective-permute-start.1 = (bf16[264,1024]{1,0:T(8,128)(2,1)S(1)}, bf16[264,1024]{1,0:T(8,128)(2,1)S(1)}, u32[]{:S(2)}, u32[]{:S(2)}) collective-permute-start(bf16[264,1024]{1,0:T(8,128)(2,1)S(1)} %get-tuple-element.53), channel_id=1, source_target_pairs={{4,8},{8,4},{5,9},{9,5},{6,10},{10,6},{7,11},{11,7},{20,24},{24,20... | collective-permute-start | bytes 1622024 | tf_op jit(solution)/shard_map/ppermute | solution.py:274
  2.7 7.8 %collective-permute-start = (bf16[264,1024]{1,0:T(8,128)(2,1)S(1)}, bf16[264,1024]{1,0:T(8,128)(2,1)S(1)}, u32[]{:S(2)}, u32[]{:S(2)}) collective-permute-start(bf16[264,1024]{1,0:T(8,128)(2,1)S(1)} %get-tuple-element.53), channel_id=1, source_target_pairs={{0,4},{12,8},{1,5},{13,9},{2,6},{14,10},{3,7},{15,11},{16,20},{28,... | collective-permute-start | bytes 1622024 | tf_op jit(solution)/shard_map/ppermute | solution.py:273
  10.5 0.0 copy-done.3
  10.5 0.1 convert_reduce_fusion
  10.6 0.6 %fusion.25 = (s32[1]{0:T(128)}, s32[1]{0:T(128)}) fusion(s32[16]{0:T(128)S(1)} %get-tuple-element.66), kind=kLoop, calls=%fused_computation.65 | loop fusion | bytes 16 | tf_op jit(solution)/shard_map/slice | solution.py:278
  11.3 0.1 dynamic_slice.59
  12.6 0.1 concatenate.3.meta_ref
  12.7 6.7 %shard_map.30 = (bf16[2048,1024]{1,0:T(8,128)(2,1)S(1)}, f32[16,128]{1,0:T(8,128)S(1)}) custom-call(s32[83]{0:T(128)S(1)} %concatenate.3.meta_ref, bf16[2048,1024]{1,0:T(8,128)(2,1)} %rows_ref.3, s32[1,512]{1,0:T(1,128)S(1)} %bitcast.59), custom_call_target="tpu_custom_call" | custom-call | flops 2147483648 | bytes 1048576 | tf_op jit(solution)/shard_map/pallas_call | solution.py:184
  19.4 0.1 collective-permute-start.3
  19.4 0.0 collective-permute-done.1.swap_ref
  19.5 3.7 %collective-permute-done.outer_ref = bf16[264,1024]{1,0:T(8,128)(2,1)S(1)} collective-permute-done((bf16[264,1024]{1,0:T(8,128)(2,1)S(1)}, bf16[264,1024]{1,0:T(8,128)(2,1)S(1)}, u32[]{:S(2)}, u32[]{:S(2)}) %collective-permute-start) | collective-permute-done | bytes 540704 | tf_op jit(solution)/shard_map/ppermute | solution.py:273
  23.1 3.6 %shard_map.32 = (f32[16,128]{1,0:T(8,128)S(1)}, f32[3,128]{1,0:T(4,128)S(1)}, f32[2,128]{1,0:T(2,128)S(1)}) custom-call(s32[83]{0:T(128)S(1)} %concatenate.3.meta_ref, bf16[2048,1024]{1,0:T(8,128)(2,1)S(1)} %get-tuple-element.52.unit_ref, bf16[264,1024]{1,0:T(8,128)(2,1)S(1)} %collective-permute-done.outer_ref, ...), custom_call_target="tpu_custom_call" | custom-call | flops 2147483648 | bytes 1048576 | tf_op jit(solution)/shard_map/pallas_call | solution.py:184
  26.8 1.3 %collective-permute-start.2 = (f32[3,128]{1,0:T(4,128)S(1)}, f32[3,128]{1,0:T(4,128)S(1)}, u32[]{:S(2)}, u32[]{:S(2)}) collective-permute-start(f32[3,128]{1,0:T(4,128)S(1)} %get-tuple-element.57), channel_id=1, source_target_pairs={{4,0},{8,12},{5,1},{9,13},{6,2},{10,14},{7,3},{11,15},{20,16},{24,... | collective-permute-start | bytes 4616 | tf_op jit(solution)/shard_map/ppermute | solution.py:305
  28.1 0.7 %collective-permute-start.4 = (f32[2,128]{1,0:T(2,128)S(1)}, f32[2,128]{1,0:T(2,128)S(1)}, u32[]{:S(2)}, u32[]{:S(2)}) collective-permute-start(f32[2,128]{1,0:T(2,128)S(1)} %get-tuple-element.60), channel_id=1, source_target_pairs={{8,4},{4,8},{9,5},{5,9},{10,6},{6,10},{11,7},{7,11},{24,20},{20,24... | collective-permute-start | bytes 3080 | tf_op jit(solution)/shard_map/ppermute | solution.py:306
  28.7 5.1 %collective-permute-done.3.piece_ref = bf16[264,1024]{1,0:T(8,128)(2,1)S(1)} collective-permute-done((bf16[264,1024]{1,0:T(8,128)(2,1)S(1)}, bf16[264,1024]{1,0:T(8,128)(2,1)S(1)}, u32[]{:S(2)}, u32[]{:S(2)}) %collective-permute-start.3) | collective-permute-done | bytes 540704 | tf_op jit(solution)/shard_map/ppermute | solution.py:296
  33.8 0.0 collective-permute-done.4.swap_back_ref
  33.8 0.0 collective-permute-done.2.outer_back_ref
  33.8 2.3 %shard_map.33 = (f32[8,128]{1,0:T(8,128)S(1)}, f32[8,128]{1,0:T(8,128)S(1)}, f32[2,128]{1,0:T(2,128)S(1)}) custom-call(s32[83]{0:T(128)S(1)} %concatenate.3.meta_ref, bf16[2048,1024]{1,0:T(8,128)(2,1)S(1)} %get-tuple-element.52.unit_ref, bf16[264,1024]{1,0:T(8,128)(2,1)S(1)} %collective-permute-done.3.piece_ref, f32[16,128]{1,0:T(8,128)S(1)} %get-tuple-element.59.before_ref, ...), custom_call_target="tpu_custom_call" | custom-call | flops 1073741824 | bytes 1048576 | tf_op jit(solution)/shard_map/pallas_call | solution.py:184
  36.1 0.1 collective-permute-start.5
  36.2 2.3 %collective-permute-start.6 = (f32[2,128]{1,0:T(2,128)S(1)}, f32[2,128]{1,0:T(2,128)S(1)}, u32[]{:S(2)}, u32[]{:S(2)}) collective-permute-start(f32[2,128]{1,0:T(2,128)S(1)} %get-tuple-element.63), channel_id=1, source_target_pairs={{4,0},{8,12},{12,4},{0,8},{5,1},{9,13},{13,5},{1,9},{6,2},{10,14},... | collective-permute-start | bytes 3080 | tf_op jit(solution)/shard_map/ppermute | solution.py:324
  38.6 0.0 collective-permute-done.5
  38.6 1.6 %collective-permute-done.6 = f32[2,128]{1,0:T(2,128)S(1)} collective-permute-done((f32[2,128]{1,0:T(2,128)S(1)}, f32[2,128]{1,0:T(2,128)S(1)}, u32[]{:S(2)}, u32[]{:S(2)}) %collective-permute-start.6) | collective-permute-done | bytes 1056 | tf_op jit(solution)/shard_map/ppermute | solution.py:324
  40.2 0.1 dynamic_update_slice.3
  40.3 1.6 %collective-permute-start.7 = (f32[1,4,128]{2,1,0:T(4,128)S(1)}, f32[1,4,128]{2,1,0:T(4,128)S(1)}, u32[]{:S(2)}, u32[]{:S(2)}) collective-permute-start(f32[1,4,128]{2,1,0:T(4,128)S(1)} %dynamic-slice_bitcast_fusion), channel_id=1, source_target_pairs={{0,2},{1,3},{2,0},{3,1},{4,6},{5,7},{6,4},{7,5},{8,10},{9,11},{10,... | collective-permute-start | bytes 6152 | tf_op jit(solution)/shard_map/ppermute | solution.py:336
  41.8 0.5 %slice.14 = f32[1,1]{1,0:T(1,128)} slice(f32[3,128]{1,0:T(4,128)S(1)} %get-tuple-element.57), slice={[2:3], [0:1]} | slice | bytes 8 | tf_op jit(solution)/shard_map/slice | solution.py:308
  42.3 0.6 %slice.15 = f32[1,1]{1,0:T(1,128)} slice(f32[3,128]{1,0:T(4,128)S(1)} %collective-permute-done.2.outer_back_ref), slice={[2:3], [0:1]} | slice | bytes 8 | tf_op jit(solution)/shard_map/slice | solution.py:308
  44.3 0.0 collective-permute-done.7
  44.3 0.3 conditional.1
  44.6 0.0 copy-start.4
  44.6 0.6 %copy-done.4 = f32[512]{0:T(512)} copy-done((f32[512]{0:T(512)}, f32[512]{0:T(512)S(1)}, u32[]{:S(2)}) %copy-start.4) | copy-done | bytes 2072
  (5 shorter events, 0.0 us)
Async XLA Ops:
  0.0 10.5 %copy-start.3 = (s32[2048]{0:T(1024)S(1)}, s32[2048]{0:T(1024)}, u32[]{:S(2)}) copy-start(s32[2048]{0:T(1024)} %param.5) | copy-start | bytes 24580
  2.0 17.4 %collective-permute-start.1 = (bf16[264,1024]{1,0:T(8,128)(2,1)S(1)}, bf16[264,1024]{1,0:T(8,128)(2,1)S(1)}, u32[]{:S(2)}, u32[]{:S(2)}) collective-permute-start(bf16[264,1024]{1,0:T(8,128)(2,1)S(1)} %get-tuple-element.53), channel_id=1, source_target_pairs={{4,8},{8,4},{5,9},{9,5},{6,10},{10,6},{7,11},{11,7},{20,24},{24,20... | collective-permute-start | bytes 1622024 | tf_op jit(solution)/shard_map/ppermute | solution.py:274
  2.7 20.4 %collective-permute-start = (bf16[264,1024]{1,0:T(8,128)(2,1)S(1)}, bf16[264,1024]{1,0:T(8,128)(2,1)S(1)}, u32[]{:S(2)}, u32[]{:S(2)}) collective-permute-start(bf16[264,1024]{1,0:T(8,128)(2,1)S(1)} %get-tuple-element.53), channel_id=1, source_target_pairs={{0,4},{12,8},{1,5},{13,9},{2,6},{14,10},{3,7},{15,11},{16,20},{28,... | collective-permute-start | bytes 1622024 | tf_op jit(solution)/shard_map/ppermute | solution.py:273
  19.4 14.4 %collective-permute-start.3 = (bf16[264,1024]{1,0:T(8,128)(2,1)S(1)}, bf16[264,1024]{1,0:T(8,128)(2,1)S(1)}, u32[]{:S(2)}, u32[]{:S(2)}) collective-permute-start(bf16[264,1024]{1,0:T(8,128)(2,1)S(1)} %get-tuple-element.58), channel_id=1, source_target_pairs={{0,4},{12,8},{4,12},{8,0},{1,5},{13,9},{5,13},{9,1},{2,6},{14,10},... | collective-permute-start | bytes 1622024 | tf_op jit(solution)/shard_map/ppermute | solution.py:296
  26.8 7.1 %collective-permute-start.2 = (f32[3,128]{1,0:T(4,128)S(1)}, f32[3,128]{1,0:T(4,128)S(1)}, u32[]{:S(2)}, u32[]{:S(2)}) collective-permute-start(f32[3,128]{1,0:T(4,128)S(1)} %get-tuple-element.57), channel_id=1, source_target_pairs={{4,0},{8,12},{5,1},{9,13},{6,2},{10,14},{7,3},{11,15},{20,16},{24,... | collective-permute-start | bytes 4616 | tf_op jit(solution)/shard_map/ppermute | solution.py:305
  28.1 5.8 %collective-permute-start.4 = (f32[2,128]{1,0:T(2,128)S(1)}, f32[2,128]{1,0:T(2,128)S(1)}, u32[]{:S(2)}, u32[]{:S(2)}) collective-permute-start(f32[2,128]{1,0:T(2,128)S(1)} %get-tuple-element.60), channel_id=1, source_target_pairs={{8,4},{4,8},{9,5},{5,9},{10,6},{6,10},{11,7},{7,11},{24,20},{20,24... | collective-permute-start | bytes 3080 | tf_op jit(solution)/shard_map/ppermute | solution.py:306
  36.1 2.5 %collective-permute-start.5 = (f32[8,128]{1,0:T(8,128)S(1)}, f32[8,128]{1,0:T(8,128)S(1)}, u32[]{:S(2)}, u32[]{:S(2)}) collective-permute-start(f32[8,128]{1,0:T(8,128)S(1)} %get-tuple-element.62), channel_id=1, source_target_pairs={{0,1},{1,0},{2,3},{3,2},{4,5},{5,4},{6,7},{7,6},{8,9},{9,8},{10,11... | collective-permute-start | bytes 12296 | tf_op jit(solution)/shard_map/ppermute | solution.py:323
  36.2 3.9 %collective-permute-start.6 = (f32[2,128]{1,0:T(2,128)S(1)}, f32[2,128]{1,0:T(2,128)S(1)}, u32[]{:S(2)}, u32[]{:S(2)}) collective-permute-start(f32[2,128]{1,0:T(2,128)S(1)} %get-tuple-element.63), channel_id=1, source_target_pairs={{4,0},{8,12},{12,4},{0,8},{5,1},{9,13},{13,5},{1,9},{6,2},{10,14},... | collective-permute-start | bytes 3080 | tf_op jit(solution)/shard_map/ppermute | solution.py:324
  40.3 4.0 %collective-permute-start.7 = (f32[1,4,128]{2,1,0:T(4,128)S(1)}, f32[1,4,128]{2,1,0:T(4,128)S(1)}, u32[]{:S(2)}, u32[]{:S(2)}) collective-permute-start(f32[1,4,128]{2,1,0:T(4,128)S(1)} %dynamic-slice_bitcast_fusion), channel_id=1, source_target_pairs={{0,2},{1,3},{2,0},{3,1},{4,6},{5,7},{6,4},{7,5},{8,10},{9,11},{10,... | collective-permute-start | bytes 6152 | tf_op jit(solution)/shard_map/ppermute | solution.py:336
  44.6 0.6 %copy-start.4 = (f32[512]{0:T(512)}, f32[512]{0:T(512)S(1)}, u32[]{:S(2)}) copy-start(f32[512]{0:T(512)S(1)} %get-tuple-element.97) | copy-start | bytes 6148

commit v6 on v5

--- a/solution.py
+++ b/solution.py
@@ -44,23 +44,31 @@
     return jnp.sum(total.T, axis=0, keepdims=True)
 
 
-def pack_kernel(share, at, rows_ref, ids_ref, first_ref, second_ref, sems):
+def pack_kernel(share, at, rows_ref, ids_ref, out_ref, sem):
     size = share * BLOCK
-    copies = []
-    for index, out in enumerate((first_ref, second_ref)):
-        start = pl.multiple_of(at[index] * BLOCK, BLOCK)
-        copies.append(
-            pltpu.make_async_copy(rows_ref.at[pl.ds(start, size), :], out.at[pl.ds(0, size), :], sems.at[index])
-        )
-        copies[-1].start()
-    depth = first_ref.shape[1]
-    edge = jnp.max(ids_ref[pl.ds(at[2], 1), :], axis=1, keepdims=True)
-    rest = [jnp.broadcast_to(edge, (1, BLOCK)), jnp.zeros((1, depth - size - BLOCK), jnp.int32)]
-    for index, out in enumerate((first_ref, second_ref)):
-        row = jnp.concatenate([ids_ref[pl.ds(at[index] + k, 1), :] for k in range(share)] + rest, axis=1)
-        out[size : size + 8, :] = jnp.broadcast_to(row.astype(jnp.float32), (8, depth)).astype(jnp.bfloat16)
-    for copy in copies:
-        copy.wait()
+    start = pl.multiple_of(at[0] * BLOCK, BLOCK)
+    copy = pltpu.make_async_copy(rows_ref.at[pl.ds(start, size), :], out_ref.at[pl.ds(0, size), :], sem)
+    copy.start()
+    depth = out_ref.shape[1]
+    edge = jnp.max(ids_ref[pl.ds(at[1], 1), :], axis=1, keepdims=True)
+    row = [ids_ref[pl.ds(at[0] + k, 1), :] for k in range(share)]
+    row += [jnp.broadcast_to(edge, (1, BLOCK)), jnp.zeros((1, depth - size - BLOCK), jnp.int32)]
+    row = jnp.concatenate(row, axis=1).astype(jnp.float32)
+    out_ref[size : size + 8, :] = jnp.broadcast_to(row, (8, depth)).astype(jnp.bfloat16)
+    copy.wait()
+
+
+def pack(share, block, edge_block, embeddings, by_block):
+    vmem = pl.BlockSpec(memory_space=pltpu.VMEM)
+    return pl.pallas_call(
+        functools.partial(pack_kernel, share),
+        in_specs=[pl.BlockSpec(memory_space=pltpu.SMEM), pl.BlockSpec(memory_space=pl.ANY), vmem],
+        out_specs=vmem,
+        out_shape=jax.ShapeDtypeStruct((share * BLOCK + 8, embeddings.shape[1]), jnp.bfloat16),
+        scratch_shapes=[pltpu.SemaphoreType.DMA],
+        compiler_params=pltpu.CompilerParams(vmem_limit_bytes=8 * 1024 * 1024),
+        cost_estimate=pl.CostEstimate(flops=0, bytes_accessed=1024, transcendentals=0),
+    )(jnp.stack([block, edge_block]).astype(jnp.int32), embeddings, by_block)
 
 
 class Meta:
@@ -80,24 +88,28 @@
 MEMBER, FIRST_BLOCK, EDGE = range(3)
 
 
-def self_kernel(blocks, width, meta_ref, rows_ref, tags_ref, unit_ref, sums_ref):
+def self_kernel(blocks, width, meta_ref, rows_ref, piece_ref, tags_ref, unit_ref, sums_ref, piece_unit):
     meta = Meta(meta_ref, blocks)
-    for start in range(0, blocks * BLOCK, STEP):
-        unit_ref[start : start + STEP, :] = normalised(rows_ref[start : start + STEP, :])
+    step = pl.program_id(0)
+
+    @pl.when(step == 0)
+    def _():
+        piece_unit[...] = normalised(piece_ref[...])
+
+    unit = normalised(rows_ref[...])
+    unit_ref[pl.ds(pl.multiple_of(step * STEP, STEP), STEP), :] = unit
     first_col = meta.number(MEMBER) * width
-    share = unit_ref[pl.ds(pl.multiple_of(first_col * BLOCK, width * BLOCK), width * BLOCK), :]
     column_tags = tags_ref[...].astype(jnp.float32)
-    for start in range(0, blocks * BLOCK, STEP):
-        cosine = products(unit_ref[start : start + STEP, :], share)
-        for inner in range(0, STEP, BLOCK):
-            block = (start + inner) // BLOCK
-            bias = column_bias(meta.tag(block), column_tags)
-            weight = jnp.exp2(cosine[inner : inner + BLOCK] * GAIN + bias)
-            row = lax.broadcasted_iota(jnp.int32, weight.shape, 0)
-            col = lax.broadcasted_iota(jnp.int32, weight.shape, 1)
-            shift = (block - first_col) * BLOCK
-            weight = jnp.where((row < meta.used(block)) & (col - row != shift), weight, 0.0)
-            sums_ref[block : block + 1, :] = lane_sums(weight)
+    cosine = products(unit, piece_unit[...])
+    for inner in range(0, STEP, BLOCK):
+        block = step * (STEP // BLOCK) + inner // BLOCK
+        bias = column_bias(meta.tag(block), column_tags)
+        weight = jnp.exp2(cosine[inner : inner + BLOCK] * GAIN + bias)
+        row = lax.broadcasted_iota(jnp.int32, weight.shape, 0)
+        col = lax.broadcasted_iota(jnp.int32, weight.shape, 1)
+        shift = (block - first_col) * BLOCK
+        weight = jnp.where((row < meta.used(block)) & (col - row != shift), weight, 0.0)
+        sums_ref[pl.ds(block, 1), :] = lane_sums(weight)
 
 
 def chunk_tags(piece_ref, size):
@@ -130,7 +142,7 @@
 
 
 def middle_kernel(
-    blocks, share, meta_ref, unit_ref, outer_ref, swap_ref, before_ref, sums_ref, outer_cols_ref, swap_cols_ref,
+    blocks, share, meta_ref, unit_ref, swap_ref, outer_ref, before_ref, sums_ref, outer_cols_ref, swap_cols_ref,
     piece_unit,
 ):
     meta = Meta(meta_ref, blocks)
@@ -188,7 +200,7 @@
         out_shape=out_shapes,
         scratch_shapes=scratch,
         compiler_params=pltpu.CompilerParams(vmem_limit_bytes=16 * 1024 * 1024),
-        cost_estimate=pl.CostEstimate(flops=flops, bytes_accessed=1024 * 1024, transcendentals=flops // 2048),
+        cost_estimate=pl.CostEstimate(flops=flops, bytes_accessed=1024, transcendentals=0),
     )(meta, *operands)
 
 
@@ -261,17 +273,9 @@
     second_block = jnp.where(inner, near, member * width + share)
     edge_block = jnp.where(part == 1, blocks // 2 - 1, blocks // 2)
     by_block = cluster_ids.reshape(blocks, BLOCK)
-    vmem = pl.BlockSpec(memory_space=pltpu.VMEM)
-    first_out, second_out = pl.pallas_call(
-        functools.partial(pack_kernel, share),
-        in_specs=[pl.BlockSpec(memory_space=pltpu.SMEM), pl.BlockSpec(memory_space=pl.ANY), vmem],
-        out_specs=[vmem] * 2,
-        out_shape=[jax.ShapeDtypeStruct((size + 8, depth), jnp.bfloat16)] * 2,
-        scratch_shapes=[pltpu.SemaphoreType.DMA((2,))],
-        compiler_params=pltpu.CompilerParams(vmem_limit_bytes=8 * 1024 * 1024),
-    )(jnp.stack([first_block, second_block, edge_block]).astype(jnp.int32), embeddings, by_block)
+    first_out = pack(share, first_block, edge_block, embeddings, by_block)
+    from_inner = lax.ppermute(first_out, "tile", swap)
     from_outer = lax.ppermute(first_out, "tile", inward)
-    from_inner = lax.ppermute(first_out, "tile", swap)
 
     tag = jnp.max(by_block, axis=1)
     used = jnp.sum((by_block >= 0).astype(jnp.int32), axis=1)
@@ -282,22 +286,35 @@
         [tag, used, seen, jnp.where(far, -2, seen), tag, jnp.stack([member, first_block, edge])]
     ).astype(jnp.int32)
 
+    second_block, meta = lax.optimization_barrier((second_block, meta))
+    second_out = pack(share, second_block, edge_block, embeddings, by_block)
+
     row_sums = jax.ShapeDtypeStruct((blocks, BLOCK), jnp.float32)
     col_sums = jax.ShapeDtypeStruct((share, BLOCK), jnp.float32)
-    unit, sums = call(
+    quarter = width * BLOCK
+    unit, sums = pl.pallas_call(
         functools.partial(self_kernel, blocks, width),
-        meta,
-        (embeddings, lax.dynamic_slice_in_dim(cluster_ids, member * width * BLOCK, width * BLOCK, 0)[None]),
-        [jax.ShapeDtypeStruct((rows, depth), jnp.bfloat16), row_sums],
-        [],
-        2 * rows * width * BLOCK * depth,
-    )
+        grid_spec=pltpu.PrefetchScalarGridSpec(
+            num_scalar_prefetch=1,
+            grid=(rows // STEP,),
+            in_specs=[
+                pl.BlockSpec((STEP, depth), lambda i, _: (i, 0)),
+                pl.BlockSpec((quarter, depth), lambda i, m: (m[5 * blocks + MEMBER], 0)),
+                pl.BlockSpec((1, quarter), lambda i, _: (0, 0)),
+            ],
+            out_specs=[pl.BlockSpec((rows, depth), lambda i, _: (0, 0)), pl.BlockSpec((blocks, BLOCK), lambda i, _: (0, 0))],
+            scratch_shapes=[pltpu.VMEM((quarter, depth), jnp.bfloat16)],
+        ),
+        out_shape=[jax.ShapeDtypeStruct((rows, depth), jnp.bfloat16), row_sums],
+        compiler_params=pltpu.CompilerParams(vmem_limit_bytes=32 * 1024 * 1024),
+        cost_estimate=pl.CostEstimate(flops=0, bytes_accessed=1024, transcendentals=0),
+    )(meta, embeddings, embeddings, lax.dynamic_slice_in_dim(cluster_ids, member * quarter, quarter, 0)[None])
     second_out, sums = lax.optimization_barrier((second_out, sums))
     last = lax.ppermute(second_out, "tile", around)
     sums, outer_cols, swap_cols = call(
         functools.partial(middle_kernel, blocks, share),
         meta,
-        (unit, from_outer, from_inner, sums),
+        (unit, from_inner, from_outer, sums),
         [row_sums, jax.ShapeDtypeStruct((share + 1, BLOCK), jnp.float32), col_sums],
         [pltpu.VMEM((2 * size, depth), jnp.bfloat16)],
         4 * rows * size * depth,
@@ -309,6 +326,7 @@
     if tiles > QUAD:
         bad = lax.pmax(bad.astype(jnp.int32), "tile") > 0
         bad = bad | quads_joined(tag, tiles, place)
+    sums, bad = lax.optimization_barrier((sums, bad.astype(jnp.int32)))
 
     half = jax.ShapeDtypeStruct((blocks // 2, BLOCK), jnp.float32)
     held, leaving, cols = call(
@@ -320,14 +338,21 @@
         2 * rows * size * depth,
     )
 
+    def owners(turn):
+        pairs = [(b * subs + s, a * subs + s) for a, b in inward for s in range(subs) if turn == 0]
+        for a, b in around:
+            if (a, b) not in inward:
+                for s in range(subs):
+                    dealt = s // 2 * share
+                    if dealt % width == turn * share:
+                        near = (subs // 2 if a % QUAD == 1 else 0) + dealt // width * 2 + s % 2
+                        pairs.append((b * subs + s, a * subs + near))
+        return pairs
+
+    home = [lax.ppermute(cols, ("tile", "sub"), owners(turn)) for turn in range(2)]
+
     came = lax.ppermute(leaving, "sub", [(i, i ^ 1) for i in range(subs)])
-    home = lax.ppermute(cols, "tile", turned(around))
-    owner = second_block // width
-    home_at = owner // 2 * width + second_block % width
     held = held + came
-    held = lax.dynamic_update_slice_in_dim(
-        held, lax.dynamic_slice_in_dim(held, home_at, share, 0) + home, home_at, 0
-    )
     bit = 1
     while 1 << bit < subs:
         pairs = held.reshape(-1, 2, width, BLOCK)
@@ -336,8 +361,10 @@
         came = lax.ppermute(leaving, "sub", [(i, i ^ (1 << bit)) for i in range(subs)])
         held = lax.dynamic_index_in_dim(pairs, own, 1, keepdims=False) + came
         bit += 1
-    scores = jnp.log(1.0 + held.reshape(-1))
-    return lax.cond(bad, lambda: every_pair(embeddings, cluster_ids), lambda: scores)
+    held, *home = lax.optimization_barrier((held, *home))
+    home = jnp.concatenate([jnp.where(inner, home[0], 0.0), jnp.where(inner, home[1], home[0])])
+    scores = jnp.log(1.0 + (held.reshape(width, BLOCK) + home).reshape(-1))
+    return lax.cond(bad > 0, lambda: every_pair(embeddings, cluster_ids), lambda: scores)
 
 
 def solution(mesh):

time: 45.4 us -> 50.9 us (1.12)
  the two profiles are of different devices: /device:TPU:0 before, /device:TPU:2 now
where the time goes in v6:
time: 50.9 us; the launch traced here: 50.5 us
  starting transfers between devices  15.9 us (31%)
  Pallas kernels  14.9 us (29%)
  waiting for transfers between devices  9.55 us (19%)
  local copies, waits for them, and re-layouts  6.83 us (13%)
  between operations  2.69 us (5%)
    ppermute x2, starting transfers between devices, shards(): lax.ppermute(cols, ('tile', 'sub'), owners(turn))  6.98 us
    pallas_call x2, Pallas kernels, call(): pl.pallas_call(kernel, in_specs=[pl.BlockSpec(memory_space=pltpu.SMEM)] +...  5.9 us
    pallas_call x1, Pallas kernels, shards(): pl.pallas_call(functools.partial(self_kernel, blocks, width), grid_spec=p...  5.33 us
    unnamed x10, local copies, waits for them, and re-layouts  4.94 us
    ppermute x1, waiting for transfers between devices, shards(): outer_back = lax.ppermute(outer_cols, 'tile', turned(inward))  4.27 us
    ppermute x2, waiting for transfers between devices, shards(): lax.ppermute(cols, ('tile', 'sub'), owners(turn))  4.12 us
    pallas_call x2, Pallas kernels, pack(): pl.pallas_call(functools.partial(pack_kernel, share), in_specs=[pl.BlockS...  3.7 us
    ppermute x1, starting transfers between devices, shards(): from_outer = lax.ppermute(first_out, 'tile', inward)  3.51 us
  transfers between devices with their start and end apart: 9, of which 3 were waited for; matrix products, arithmetic and copies ran while one was open for 4% of the time, Pallas kernels for 22%

profile of v6, /device:TPU:2, one launch (start us, length us, event | category | flops | bytes accessed | tf_op | source)
XLA Modules:
  0.0 50.5 jit_solution(14479809424315710451)
XLA Ops:
  0.0 0.0 copy-start.6
  0.0 0.1 pad_add_fusion.at
  0.1 1.8 %shard_map.31 = bf16[264,1024]{1,0:T(8,128)(2,1)S(1)} custom-call(s32[2]{0:T(128)S(1)} %pad_add_fusion.at, bf16[2048,1024]{1,0:T(8,128)(2,1)} %rows_ref.5, s32[16,128]{1,0:T(8,128)} %bitcast.60), custom_call_target="tpu_custom_call" | custom-call | bytes 1024 | tf_op jit(solution)/shard_map/pallas_call | solution.py:63
  1.8 3.5 %collective-permute-start.1 = (bf16[264,1024]{1,0:T(8,128)(2,1)S(1)}, bf16[264,1024]{1,0:T(8,128)(2,1)S(1)}, u32[]{:S(2)}, u32[]{:S(2)}) collective-permute-start(bf16[264,1024]{1,0:T(8,128)(2,1)S(1)} %shard_map.31), channel_id=1, source_target_pairs={{0,4},{12,8},{1,5},{13,9},{2,6},{14,10},{3,7},{15,11},{16,20},{28,... | collective-permute-start | bytes 1622024 | tf_op jit(solution)/shard_map/ppermute | solution.py:278
  5.4 0.7 %collective-permute-start = (bf16[264,1024]{1,0:T(8,128)(2,1)S(1)}, bf16[264,1024]{1,0:T(8,128)(2,1)S(1)}, u32[]{:S(2)}, u32[]{:S(2)}) collective-permute-start(bf16[264,1024]{1,0:T(8,128)(2,1)S(1)} %shard_map.31), channel_id=1, source_target_pairs={{4,8},{8,4},{5,9},{9,5},{6,10},{10,6},{7,11},{11,7},{20,24},{24,20... | collective-permute-start | bytes 1622024 | tf_op jit(solution)/shard_map/ppermute | solution.py:277
  6.1 0.0 copy-done.6
  6.1 0.1 convert_reduce_fusion
  6.2 0.6 %fusion.24 = (s32[1]{0:T(128)}, s32[1]{0:T(128)}) fusion(s32[16]{0:T(128)S(1)} %get-tuple-element.64), kind=kLoop, calls=%fused_computation.68 | loop fusion | bytes 16 | tf_op jit(solution)/shard_map/slice | solution.py:282
  8.0 0.1 concatenate.8.meta_ref
  8.1 0.0 copy-start.2
  8.1 0.1 dynamic_slice.54
  8.2 0.1 pad_add_fusion.1.at
  8.2 1.9 %shard_map.32 = bf16[264,1024]{1,0:T(8,128)(2,1)S(1)} custom-call(s32[2]{0:T(128)S(1)} %pad_add_fusion.1.at, bf16[2048,1024]{1,0:T(8,128)(2,1)} %rows_ref.5, s32[16,128]{1,0:T(8,128)S(1)} %bitcast.61), custom_call_target="tpu_custom_call" | custom-call | bytes 1024 | tf_op jit(solution)/shard_map/pallas_call | solution.py:63
  10.2 0.2 copy-done.2
  10.4 5.3 %shard_map.30 = (bf16[2048,1024]{1,0:T(8,128)(2,1)S(1)}, f32[16,128]{1,0:T(8,128)S(1)}) custom-call(s32[83]{0:T(128)S(1)} %concatenate.8.meta_ref, bf16[2048,1024]{1,0:T(8,128)(2,1)S(1)} %copy-done.2, bf16[2048,1024]{1,0:T(8,128)(2,1)S(1)} %copy-done.2, s32[1,512]{1,0:T(1,128)S(1)} %bitcast.59), custom_call_target="tpu_custom_call" | custom-call | bytes 1024 | tf_op jit(solution)/shard_map/pallas_call | solution.py:295
  15.8 2.2 %collective-permute-start.3 = (bf16[264,1024]{1,0:T(8,128)(2,1)S(1)}, bf16[264,1024]{1,0:T(8,128)(2,1)S(1)}, u32[]{:S(2)}, u32[]{:S(2)}) collective-permute-start(bf16[264,1024]{1,0:T(8,128)(2,1)S(1)} %shard_map.32), channel_id=1, source_target_pairs={{0,4},{12,8},{4,12},{8,0},{1,5},{13,9},{5,13},{9,1},{2,6},{14,10},... | collective-permute-start | bytes 1622024 | tf_op jit(solution)/shard_map/ppermute | solution.py:313
  18.0 0.0 collective-permute-done.1.outer_ref
  18.0 0.0 collective-permute-done.swap_ref
  18.0 3.6 %shard_map.33 = (f32[16,128]{1,0:T(8,128)S(1)}, f32[3,128]{1,0:T(4,128)S(1)}, f32[2,128]{1,0:T(2,128)S(1)}) custom-call(s32[83]{0:T(128)S(1)} %concatenate.8.meta_ref, bf16[2048,1024]{1,0:T(8,128)(2,1)S(1)} %get-tuple-element.46.unit_ref, bf16[264,1024]{1,0:T(8,128)(2,1)S(1)} %collective-permute-done.swap_ref, ...), custom_call_target="tpu_custom_call" | custom-call | flops 2147483648 | bytes 1024 | tf_op jit(solution)/shard_map/pallas_call | solution.py:196
  21.6 0.0 copy-start
  21.6 1.9 %copy-done = bf16[2048,1024]{1,0:T(8,128)(2,1)} copy-done((bf16[2048,1024]{1,0:T(8,128)(2,1)}, bf16[2048,1024]{1,0:T(8,128)(2,1)S(1)}, u32[]{:S(2)}) %copy-start) | copy-done | bytes 4194328
  23.6 1.3 %collective-permute-start.2 = (f32[3,128]{1,0:T(4,128)S(1)}, f32[3,128]{1,0:T(4,128)S(1)}, u32[]{:S(2)}, u32[]{:S(2)}) collective-permute-start(f32[3,128]{1,0:T(4,128)S(1)} %get-tuple-element.51), channel_id=1, source_target_pairs={{4,0},{8,12},{5,1},{9,13},{6,2},{10,14},{7,3},{11,15},{20,16},{24,... | collective-permute-start | bytes 4616 | tf_op jit(solution)/shard_map/ppermute | solution.py:322
  24.8 0.7 %collective-permute-start.4 = (f32[2,128]{1,0:T(2,128)S(1)}, f32[2,128]{1,0:T(2,128)S(1)}, u32[]{:S(2)}, u32[]{:S(2)}) collective-permute-start(f32[2,128]{1,0:T(2,128)S(1)} %get-tuple-element.55), channel_id=1, source_target_pairs={{8,4},{4,8},{9,5},{5,9},{10,6},{6,10},{11,7},{7,11},{24,20},{20,24... | collective-permute-start | bytes 3080 | tf_op jit(solution)/shard_map/ppermute | solution.py:323
  25.5 0.5 %slice.14 = f32[1,1]{1,0:T(1,128)} slice(f32[3,128]{1,0:T(4,128)S(1)} %get-tuple-element.51), slice={[2:3], [0:1]} | slice | bytes 8 | tf_op jit(solution)/shard_map/slice | solution.py:325
  26.1 4.3 %collective-permute-done.2.outer_back_ref = f32[3,128]{1,0:T(4,128)S(1)} collective-permute-done((f32[3,128]{1,0:T(4,128)S(1)}, f32[3,128]{1,0:T(4,128)S(1)}, u32[]{:S(2)}, u32[]{:S(2)}) %collective-permute-start.2) | collective-permute-done | bytes 1568 | tf_op jit(solution)/shard_map/ppermute | solution.py:322
  30.3 0.6 %slice.15 = f32[1,1]{1,0:T(1,128)} slice(f32[3,128]{1,0:T(4,128)S(1)} %collective-permute-done.2.outer_back_ref), slice={[2:3], [0:1]} | slice | bytes 8 | tf_op jit(solution)/shard_map/slice | solution.py:325
  32.2 0.0 collective-permute-done.3.piece_ref
  32.2 0.0 collective-permute-done.4.swap_back_ref
  32.2 0.0 copy-start.1
  32.3 2.2 %copy-done.1 = bf16[2048,1024]{1,0:T(8,128)(2,1)S(1)} copy-done((bf16[2048,1024]{1,0:T(8,128)(2,1)S(1)}, bf16[2048,1024]{1,0:T(8,128)(2,1)}, u32[]{:S(2)}) %copy-start.1) | copy-done | bytes 4194328
  34.4 2.3 %shard_map.34 = (f32[8,128]{1,0:T(8,128)S(1)}, f32[8,128]{1,0:T(8,128)S(1)}, f32[2,128]{1,0:T(2,128)S(1)}) custom-call(s32[83]{0:T(128)S(1)} %concatenate.8.meta_ref, bf16[2048,1024]{1,0:T(8,128)(2,1)S(1)} %copy-done.1, bf16[264,1024]{1,0:T(8,128)(2,1)S(1)} %collective-permute-done.3.piece_ref, f32[16,128]{1,0:T(8,128)S(1)} %get-tuple-element.54.before_ref, ...), custom_call_target="tpu_custom_call" | custom-call | flops 1073741824 | bytes 1024 | tf_op jit(solution)/shard_map/pallas_call | solution.py:196
  36.7 0.1 collective-permute-start.5
  36.8 1.1 %collective-permute-done.5 = f32[8,128]{1,0:T(8,128)S(1)} collective-permute-done((f32[8,128]{1,0:T(8,128)S(1)}, f32[8,128]{1,0:T(8,128)S(1)}, u32[]{:S(2)}, u32[]{:S(2)}) %collective-permute-start.5) | collective-permute-done | bytes 4128 | tf_op jit(solution)/shard_map/ppermute | solution.py:354
  37.9 0.5 %collective-permute-start.6 = (f32[1,4,128]{2,1,0:T(4,128)S(1)}, f32[1,4,128]{2,1,0:T(4,128)S(1)}, u32[]{:S(2)}, u32[]{:S(2)}) collective-permute-start(f32[1,4,128]{2,1,0:T(4,128)S(1)} %dynamic-slice_bitcast_fusion), channel_id=1, source_target_pairs={{0,2},{1,3},{2,0},{3,1},{4,6},{5,7},{6,4},{7,5},{8,10},{9,11},{10,... | collective-permute-start | bytes 6152 | tf_op jit(solution)/shard_map/ppermute | solution.py:361
  38.5 5.7 %collective-permute-start.8 = (f32[2,128]{1,0:T(2,128)S(1)}, f32[2,128]{1,0:T(2,128)S(1)}, u32[]{:S(2)}, u32[]{:S(2)}) collective-permute-start(f32[2,128]{1,0:T(2,128)S(1)} %get-tuple-element.58), channel_id=1, source_target_pairs={{14,6},{15,7},{2,8},{3,9},{30,22},{31,23},{18,24},{19,25}} | collective-permute-start | bytes 3080 | tf_op jit(solution)/shard_map/ppermute | solution.py:352
  44.2 1.3 %collective-permute-start.7 = (f32[2,128]{1,0:T(2,128)S(1)}, f32[2,128]{1,0:T(2,128)S(1)}, u32[]{:S(2)}, u32[]{:S(2)}) collective-permute-start(f32[2,128]{1,0:T(2,128)S(1)} %get-tuple-element.58), channel_id=1, source_target_pairs={{4,0},{5,1},{6,2},{7,3},{8,12},{9,13},{10,14},{11,15},{12,6},{13,7... | collective-permute-start | bytes 3080 | tf_op jit(solution)/shard_map/ppermute | solution.py:352
  45.5 0.0 collective-permute-done.6
  45.5 0.0 collective-permute-done.8
  45.5 4.1 %collective-permute-done.7 = f32[2,128]{1,0:T(2,128)S(1)} collective-permute-done((f32[2,128]{1,0:T(2,128)S(1)}, f32[2,128]{1,0:T(2,128)S(1)}, u32[]{:S(2)}, u32[]{:S(2)}) %collective-permute-start.7) | collective-permute-done | bytes 1056 | tf_op jit(solution)/shard_map/ppermute | solution.py:352
  49.7 0.2 conditional.1
  49.9 0.0 copy-start.7
  49.9 0.6 %copy-done.7 = f32[512]{0:T(512)} copy-done((f32[512]{0:T(512)}, f32[512]{0:T(512)S(1)}, u32[]{:S(2)}) %copy-start.7) | copy-done | bytes 2072
  (7 shorter events, 0.0 us)
Async XLA Ops:
  0.0 6.1 %copy-start.6 = (s32[2048]{0:T(1024)S(1)}, s32[2048]{0:T(1024)}, u32[]{:S(2)}) copy-start(s32[2048]{0:T(1024)} %param.5) | copy-start | bytes 24580
  1.8 16.1 %collective-permute-start.1 = (bf16[264,1024]{1,0:T(8,128)(2,1)S(1)}, bf16[264,1024]{1,0:T(8,128)(2,1)S(1)}, u32[]{:S(2)}, u32[]{:S(2)}) collective-permute-start(bf16[264,1024]{1,0:T(8,128)(2,1)S(1)} %shard_map.31), channel_id=1, source_target_pairs={{0,4},{12,8},{1,5},{13,9},{2,6},{14,10},{3,7},{15,11},{16,20},{28,... | collective-permute-start | bytes 1622024 | tf_op jit(solution)/shard_map/ppermute | solution.py:278
  5.4 12.6 %collective-permute-start = (bf16[264,1024]{1,0:T(8,128)(2,1)S(1)}, bf16[264,1024]{1,0:T(8,128)(2,1)S(1)}, u32[]{:S(2)}, u32[]{:S(2)}) collective-permute-start(bf16[264,1024]{1,0:T(8,128)(2,1)S(1)} %shard_map.31), channel_id=1, source_target_pairs={{4,8},{8,4},{5,9},{9,5},{6,10},{10,6},{7,11},{11,7},{20,24},{24,20... | collective-permute-start | bytes 1622024 | tf_op jit(solution)/shard_map/ppermute | solution.py:277
  8.1 2.3 %copy-start.2 = (bf16[2048,1024]{1,0:T(8,128)(2,1)S(1)}, bf16[2048,1024]{1,0:T(8,128)(2,1)}, u32[]{:S(2)}) copy-start(bf16[2048,1024]{1,0:T(8,128)(2,1)} %rows_ref.5) | copy-start | bytes 12582916
  15.8 16.5 %collective-permute-start.3 = (bf16[264,1024]{1,0:T(8,128)(2,1)S(1)}, bf16[264,1024]{1,0:T(8,128)(2,1)S(1)}, u32[]{:S(2)}, u32[]{:S(2)}) collective-permute-start(bf16[264,1024]{1,0:T(8,128)(2,1)S(1)} %shard_map.32), channel_id=1, source_target_pairs={{0,4},{12,8},{4,12},{8,0},{1,5},{13,9},{5,13},{9,1},{2,6},{14,10},... | collective-permute-start | bytes 1622024 | tf_op jit(solution)/shard_map/ppermute | solution.py:313
  21.6 1.9 %copy-start = (bf16[2048,1024]{1,0:T(8,128)(2,1)}, bf16[2048,1024]{1,0:T(8,128)(2,1)S(1)}, u32[]{:S(2)}) copy-start(bf16[2048,1024]{1,0:T(8,128)(2,1)S(1)} %get-tuple-element.46.unit_ref) | copy-start | bytes 12582916
  23.6 6.8 %collective-permute-start.2 = (f32[3,128]{1,0:T(4,128)S(1)}, f32[3,128]{1,0:T(4,128)S(1)}, u32[]{:S(2)}, u32[]{:S(2)}) collective-permute-start(f32[3,128]{1,0:T(4,128)S(1)} %get-tuple-element.51), channel_id=1, source_target_pairs={{4,0},{8,12},{5,1},{9,13},{6,2},{10,14},{7,3},{11,15},{20,16},{24,... | collective-permute-start | bytes 4616 | tf_op jit(solution)/shard_map/ppermute | solution.py:322
  24.8 7.4 %collective-permute-start.4 = (f32[2,128]{1,0:T(2,128)S(1)}, f32[2,128]{1,0:T(2,128)S(1)}, u32[]{:S(2)}, u32[]{:S(2)}) collective-permute-start(f32[2,128]{1,0:T(2,128)S(1)} %get-tuple-element.55), channel_id=1, source_target_pairs={{8,4},{4,8},{9,5},{5,9},{10,6},{6,10},{11,7},{7,11},{24,20},{20,24... | collective-permute-start | bytes 3080 | tf_op jit(solution)/shard_map/ppermute | solution.py:323
  32.2 2.2 %copy-start.1 = (bf16[2048,1024]{1,0:T(8,128)(2,1)S(1)}, bf16[2048,1024]{1,0:T(8,128)(2,1)}, u32[]{:S(2)}) copy-start(bf16[2048,1024]{1,0:T(8,128)(2,1)} %copy-done) | copy-start | bytes 12582916
  36.7 1.2 %collective-permute-start.5 = (f32[8,128]{1,0:T(8,128)S(1)}, f32[8,128]{1,0:T(8,128)S(1)}, u32[]{:S(2)}, u32[]{:S(2)}) collective-permute-start(f32[8,128]{1,0:T(8,128)S(1)} %get-tuple-element.57), channel_id=1, source_target_pairs={{0,1},{1,0},{2,3},{3,2},{4,5},{5,4},{6,7},{7,6},{8,9},{9,8},{10,11... | collective-permute-start | bytes 12296 | tf_op jit(solution)/shard_map/ppermute | solution.py:354
  37.9 7.6 %collective-permute-start.6 = (f32[1,4,128]{2,1,0:T(4,128)S(1)}, f32[1,4,128]{2,1,0:T(4,128)S(1)}, u32[]{:S(2)}, u32[]{:S(2)}) collective-permute-start(f32[1,4,128]{2,1,0:T(4,128)S(1)} %dynamic-slice_bitcast_fusion), channel_id=1, source_target_pairs={{0,2},{1,3},{2,0},{3,1},{4,6},{5,7},{6,4},{7,5},{8,10},{9,11},{10,... | collective-permute-start | bytes 6152 | tf_op jit(solution)/shard_map/ppermute | solution.py:361
  38.5 7.0 %collective-permute-start.8 = (f32[2,128]{1,0:T(2,128)S(1)}, f32[2,128]{1,0:T(2,128)S(1)}, u32[]{:S(2)}, u32[]{:S(2)}) collective-permute-start(f32[2,128]{1,0:T(2,128)S(1)} %get-tuple-element.58), channel_id=1, source_target_pairs={{14,6},{15,7},{2,8},{3,9},{30,22},{31,23},{18,24},{19,25}} | collective-permute-start | bytes 3080 | tf_op jit(solution)/shard_map/ppermute | solution.py:352
  44.2 5.5 %collective-permute-start.7 = (f32[2,128]{1,0:T(2,128)S(1)}, f32[2,128]{1,0:T(2,128)S(1)}, u32[]{:S(2)}, u32[]{:S(2)}) collective-permute-start(f32[2,128]{1,0:T(2,128)S(1)} %get-tuple-element.58), channel_id=1, source_target_pairs={{4,0},{5,1},{6,2},{7,3},{8,12},{9,13},{10,14},{11,15},{12,6},{13,7... | collective-permute-start | bytes 3080 | tf_op jit(solution)/shard_map/ppermute | solution.py:352
  49.9 0.6 %copy-start.7 = (f32[512]{0:T(512)}, f32[512]{0:T(512)S(1)}, u32[]{:S(2)}) copy-start(f32[512]{0:T(512)S(1)} %get-tuple-element.96) | copy-start | bytes 6148

commit v7 on v6

--- a/solution.py
+++ b/solution.py
@@ -19,6 +19,7 @@
 OFF = -1000.0
 
 STEP = 512
+COPY = 64
 
 
 def normalised(values):
@@ -44,31 +45,56 @@
     return jnp.sum(total.T, axis=0, keepdims=True)
 
 
-def pack_kernel(share, at, rows_ref, ids_ref, out_ref, sem):
-    size = share * BLOCK
-    start = pl.multiple_of(at[0] * BLOCK, BLOCK)
-    copy = pltpu.make_async_copy(rows_ref.at[pl.ds(start, size), :], out_ref.at[pl.ds(0, size), :], sem)
-    copy.start()
-    depth = out_ref.shape[1]
-    edge = jnp.max(ids_ref[pl.ds(at[1], 1), :], axis=1, keepdims=True)
-    row = [ids_ref[pl.ds(at[0] + k, 1), :] for k in range(share)]
-    row += [jnp.broadcast_to(edge, (1, BLOCK)), jnp.zeros((1, depth - size - BLOCK), jnp.int32)]
-    row = jnp.concatenate(row, axis=1).astype(jnp.float32)
-    out_ref[size : size + 8, :] = jnp.broadcast_to(row, (8, depth)).astype(jnp.bfloat16)
-    copy.wait()
-
-
-def pack(share, block, edge_block, embeddings, by_block):
-    vmem = pl.BlockSpec(memory_space=pltpu.VMEM)
+class Plan:
+    def __init__(self, blocks, subs, place, member):
+        width = blocks // subs
+        share = width // 2
+        part = place % QUAD
+        self.inner = (part == 1) | (part == 2)
+        self.far = part == 1
+        dealt = member // 2 * share
+        near = (dealt // width * 2 + member % 2) * width + dealt % width
+        near = jnp.where(part == 1, blocks // 2, 0) + near
+        self.first = jnp.where(self.inner, near, member * width)
+        self.second = jnp.where(self.inner, near, member * width + share)
+        self.edge = jnp.where(part == 1, blocks // 2 - 1, blocks // 2)
+        self.width, self.share = width, share
+
+
+def pack_kernel(blocks, subs, rows_ref, ids_ref, first_ref, second_ref, ids, sems):
+    plan = Plan(blocks, subs, lax.axis_index("tile"), lax.axis_index("sub"))
+    share, size = plan.share, plan.share * BLOCK
+    copies = []
+    for block, out in ((plan.first, first_ref), (plan.second, second_ref)):
+        for down in range(0, size, COPY):
+            start = pl.multiple_of(block * BLOCK + down, COPY)
+            copies.append((rows_ref.at[pl.ds(start, COPY), :], out.at[pl.ds(down, COPY), :]))
+    copies.append((ids_ref, ids))
+    copies = [pltpu.make_async_copy(*ends, sems.at[index]) for index, ends in enumerate(copies)]
+    for copy in copies:
+        copy.start()
+    copies[-1].wait()
+    depth = first_ref.shape[1]
+    edge = jnp.max(ids[pl.ds(plan.edge, 1), :], axis=1, keepdims=True)
+    rest = [jnp.broadcast_to(edge, (1, BLOCK)), jnp.zeros((1, depth - size - BLOCK), jnp.int32)]
+    for block, out in ((plan.first, first_ref), (plan.second, second_ref)):
+        row = jnp.concatenate([ids[pl.ds(block + k, 1), :] for k in range(share)] + rest, axis=1)
+        out[size : size + 8, :] = jnp.broadcast_to(row.astype(jnp.float32), (8, depth)).astype(jnp.bfloat16)
+    for copy in copies[:-1]:
+        copy.wait()
+
+
+def pack(size, subs, embeddings, by_block):
+    blocks, depth = by_block.shape[0], embeddings.shape[1]
     return pl.pallas_call(
-        functools.partial(pack_kernel, share),
-        in_specs=[pl.BlockSpec(memory_space=pltpu.SMEM), pl.BlockSpec(memory_space=pl.ANY), vmem],
-        out_specs=vmem,
-        out_shape=jax.ShapeDtypeStruct((share * BLOCK + 8, embeddings.shape[1]), jnp.bfloat16),
-        scratch_shapes=[pltpu.SemaphoreType.DMA],
+        functools.partial(pack_kernel, blocks, subs),
+        in_specs=[pl.BlockSpec(memory_space=pl.ANY)] * 2,
+        out_specs=[pl.BlockSpec(memory_space=pltpu.VMEM)] * 2,
+        out_shape=[jax.ShapeDtypeStruct((size + 8, depth), jnp.bfloat16)] * 2,
+        scratch_shapes=[pltpu.VMEM(by_block.shape, jnp.int32), pltpu.SemaphoreType.DMA((2 * size // COPY + 1,))],
         compiler_params=pltpu.CompilerParams(vmem_limit_bytes=8 * 1024 * 1024),
         cost_estimate=pl.CostEstimate(flops=0, bytes_accessed=1024, transcendentals=0),
-    )(jnp.stack([block, edge_block]).astype(jnp.int32), embeddings, by_block)
+    )(embeddings, by_block)
 
 
 class Meta:
@@ -85,7 +111,7 @@
         return self.ref[5 * self.blocks + index]
 
 
-MEMBER, FIRST_BLOCK, EDGE = range(3)
+MEMBER, FIRST_BLOCK, EDGE, INNER = range(4)
 
 
 def self_kernel(blocks, width, meta_ref, rows_ref, piece_ref, tags_ref, unit_ref, sums_ref, piece_unit):
@@ -159,13 +185,14 @@
     for k in range(share):
         outer_cols_ref[k : k + 1, :] = outer[k]
         swap_cols_ref[k : k + 1, :] = swap[k]
-    mine = meta.number(EDGE).astype(jnp.float32)
-    outer_cols_ref[share : share + 1, :] = jnp.where((edge == mine) & (edge >= 0), 1.0, 0.0)
+    mine = meta.tag(meta.number(EDGE)).astype(jnp.float32)
+    joined = (edge == mine) & (edge >= 0) & (meta.number(INNER) > 0)
+    outer_cols_ref[share : share + 1, :] = jnp.where(joined, 1.0, 0.0)
 
 
 def last_kernel(
-    blocks, share, width, meta_ref, unit_ref, piece_ref, before_ref, outer_back_ref, swap_back_ref,
-    keep_ref, send_ref, cols_ref, piece_unit, sums,
+    blocks, share, width, meta_ref, unit_ref, piece_ref, before_ref, outer_cols_ref, outer_back_ref, swap_back_ref,
+    keep_ref, send_ref, cols_ref, flag_ref, piece_unit, sums,
 ):
     meta = Meta(meta_ref, blocks)
     size = share * BLOCK
@@ -180,6 +207,8 @@
         at = place(block)
         sums[at : at + 1, :] = before_ref[block : block + 1, :] + value
 
+    flags = jnp.maximum(outer_cols_ref[share : share + 1, :], outer_back_ref[share : share + 1, :])
+    flag_ref[0] = jnp.max(flags).astype(jnp.int32)
     (cols,) = cross_terms(meta, (2,), (tags,), unit_ref, piece_unit, add_rows)
     for k in range(share):
         cols_ref[k : k + 1, :] = cols[k]
@@ -192,11 +221,11 @@
 
 
 def call(kernel, meta, operands, out_shapes, scratch, flops):
-    vmem = pl.BlockSpec(memory_space=pltpu.VMEM)
+    vmem, smem = pl.BlockSpec(memory_space=pltpu.VMEM), pl.BlockSpec(memory_space=pltpu.SMEM)
     return pl.pallas_call(
         kernel,
-        in_specs=[pl.BlockSpec(memory_space=pltpu.SMEM)] + [vmem] * len(operands),
-        out_specs=jax.tree.map(lambda _: vmem, out_shapes),
+        in_specs=[smem] + [vmem] * len(operands),
+        out_specs=[vmem if len(shape.shape) > 1 else smem for shape in out_shapes],
         out_shape=out_shapes,
         scratch_shapes=scratch,
         compiler_params=pltpu.CompilerParams(vmem_limit_bytes=16 * 1024 * 1024),
@@ -253,11 +282,9 @@
     place, member = lax.axis_index("tile"), lax.axis_index("sub")
     rows, depth = embeddings.shape
     blocks = rows // BLOCK
-    width = blocks // subs
-    share = width // 2
+    plan = Plan(blocks, subs, place, member)
+    width, share, inner = plan.width, plan.share, plan.inner
     size = share * BLOCK
-    part = place % QUAD
-    inner = (part == 1) | (part == 2)
     quads = range(0, tiles, QUAD)
     inward = [p for q in quads for p in ((q, q + 1), (q + 3, q + 2))]
     swap = [p for q in quads for p in ((q + 1, q + 2), (q + 2, q + 1))]
@@ -266,28 +293,17 @@
     def turned(route):
         return [(b, a) for a, b in route]
 
-    dealt = member // 2 * share
-    near = (dealt // width * 2 + member % 2) * width + dealt % width
-    near = jnp.where(part == 1, blocks // 2, 0) + near
-    first_block = jnp.where(inner, near, member * width)
-    second_block = jnp.where(inner, near, member * width + share)
-    edge_block = jnp.where(part == 1, blocks // 2 - 1, blocks // 2)
     by_block = cluster_ids.reshape(blocks, BLOCK)
-    first_out = pack(share, first_block, edge_block, embeddings, by_block)
+    first_out, second_out = pack(size, subs, embeddings, by_block)
     from_inner = lax.ppermute(first_out, "tile", swap)
     from_outer = lax.ppermute(first_out, "tile", inward)
 
     tag = jnp.max(by_block, axis=1)
     used = jnp.sum((by_block >= 0).astype(jnp.int32), axis=1)
-    edge = jnp.where(part == 1, tag[blocks // 2 - 1], tag[blocks // 2])
-    far = (part == 1) & (jnp.arange(blocks) >= blocks // 2)
     seen = jnp.where(inner, tag, -2)
-    meta = jnp.concatenate(
-        [tag, used, seen, jnp.where(far, -2, seen), tag, jnp.stack([member, first_block, edge])]
-    ).astype(jnp.int32)
-
-    second_block, meta = lax.optimization_barrier((second_block, meta))
-    second_out = pack(share, second_block, edge_block, embeddings, by_block)
+    swapped = jnp.where(plan.far & (jnp.arange(blocks) >= blocks // 2), -2, seen)
+    numbers = jnp.stack([member, plan.first, plan.edge, inner])
+    meta = jnp.concatenate([tag, used, seen, swapped, tag, numbers]).astype(jnp.int32)
 
     row_sums = jax.ShapeDtypeStruct((blocks, BLOCK), jnp.float32)
     col_sums = jax.ShapeDtypeStruct((share, BLOCK), jnp.float32)
@@ -322,37 +338,23 @@
     outer_back = lax.ppermute(outer_cols, "tile", turned(inward))
     swap_back = lax.ppermute(swap_cols, "tile", turned(swap))
 
-    bad = jnp.where(inner, outer_cols[share, 0], outer_back[share, 0]) > 0
-    if tiles > QUAD:
-        bad = lax.pmax(bad.astype(jnp.int32), "tile") > 0
-        bad = bad | quads_joined(tag, tiles, place)
-    sums, bad = lax.optimization_barrier((sums, bad.astype(jnp.int32)))
-
     half = jax.ShapeDtypeStruct((blocks // 2, BLOCK), jnp.float32)
-    held, leaving, cols = call(
+    held, leaving, cols, flag = call(
         functools.partial(last_kernel, blocks, share, width),
         meta,
-        (unit, last, sums, outer_back, swap_back),
-        [half, half, col_sums],
+        (unit, last, sums, outer_cols, outer_back, swap_back),
+        [half, half, col_sums, jax.ShapeDtypeStruct((1,), jnp.int32)],
         [pltpu.VMEM((size, depth), jnp.bfloat16), pltpu.VMEM((blocks, BLOCK), jnp.float32)],
         2 * rows * size * depth,
     )
 
-    def owners(turn):
-        pairs = [(b * subs + s, a * subs + s) for a, b in inward for s in range(subs) if turn == 0]
-        for a, b in around:
-            if (a, b) not in inward:
-                for s in range(subs):
-                    dealt = s // 2 * share
-                    if dealt % width == turn * share:
-                        near = (subs // 2 if a % QUAD == 1 else 0) + dealt // width * 2 + s % 2
-                        pairs.append((b * subs + s, a * subs + near))
-        return pairs
-
-    home = [lax.ppermute(cols, ("tile", "sub"), owners(turn)) for turn in range(2)]
-
-    came = lax.ppermute(leaving, "sub", [(i, i ^ 1) for i in range(subs)])
-    held = held + came
+    home = lax.ppermute(cols, "tile", turned(around))
+    owner = plan.second // width
+    home_at = owner // 2 * width + plan.second % width
+    held = lax.dynamic_update_slice_in_dim(
+        held, lax.dynamic_slice_in_dim(held, home_at, share, 0) + home, home_at, 0
+    )
+    held = held + lax.ppermute(leaving, "sub", [(i, i ^ 1) for i in range(subs)])
     bit = 1
     while 1 << bit < subs:
         pairs = held.reshape(-1, 2, width, BLOCK)
@@ -361,10 +363,13 @@
         came = lax.ppermute(leaving, "sub", [(i, i ^ (1 << bit)) for i in range(subs)])
         held = lax.dynamic_index_in_dim(pairs, own, 1, keepdims=False) + came
         bit += 1
-    held, *home = lax.optimization_barrier((held, *home))
-    home = jnp.concatenate([jnp.where(inner, home[0], 0.0), jnp.where(inner, home[1], home[0])])
-    scores = jnp.log(1.0 + (held.reshape(width, BLOCK) + home).reshape(-1))
-    return lax.cond(bad > 0, lambda: every_pair(embeddings, cluster_ids), lambda: scores)
+    scores = jnp.log(1.0 + held.reshape(-1))
+
+    bad = flag[0] > 0
+    if tiles > QUAD:
+        bad = lax.pmax(bad.astype(jnp.int32), "tile") > 0
+        bad = bad | quads_joined(tag, tiles, place)
+    return lax.cond(bad, lambda: every_pair(embeddings, cluster_ids), lambda: scores)
 
 
 def solution(mesh):

time: 50.9 us -> 47.4 us (0.931)
  the two profiles are of different devices: /device:TPU:2 before, /device:TPU:0 now
where the time goes in v7:
time: 47.4 us; the launch traced here: 47 us
  starting transfers between devices  15.2 us (32%)
  Pallas kernels  15 us (32%)
  waiting for transfers between devices  8.68 us (18%)
  local copies, waits for them, and re-layouts  7.11 us (15%)
  between operations  0.92 us (2%)
    pallas_call x1, Pallas kernels, shards(): pl.pallas_call(functools.partial(self_kernel, blocks, width), grid_spec=p...  7.31 us
    unnamed x10, local copies, waits for them, and re-layouts  6.87 us
    pallas_call x2, Pallas kernels, call(): pl.pallas_call(kernel, in_specs=[smem] + [vmem] * len(operands), out_spec...  6.32 us
    ppermute x1, waiting for transfers between devices, shards(): last = lax.ppermute(second_out, 'tile', around)  5.97 us
    ppermute x1, starting transfers between devices, shards(): from_outer = lax.ppermute(first_out, 'tile', inward)  4.96 us
    ppermute x1, starting transfers between devices, shards(): home = lax.ppermute(cols, 'tile', turned(around))  3.8 us
    ppermute x1, starting transfers between devices, shards(): last = lax.ppermute(second_out, 'tile', around)  2.18 us
    ppermute x1, starting transfers between devices, shards(): lax.ppermute(leaving, 'sub', [(i, i ^ 1 << bit) for i in range(subs)])  1.59 us
  transfers between devices with their start and end apart: 8, of which 3 were waited for; matrix products, arithmetic and copies ran while one was open for 1% of the time, Pallas kernels for 23%

profile of v7, /device:TPU:0, one launch (start us, length us, event | category | flops | bytes accessed | tf_op | source)
XLA Modules:
  0.0 47.0 jit_solution(15839127488341678565)
XLA Ops:
  0.0 0.0 copy-start.6
  0.0 1.4 %shard_map.31 = (bf16[264,1024]{1,0:T(8,128)(2,1)S(1)}, bf16[264,1024]{1,0:T(8,128)(2,1)S(1)}) custom-call(bf16[2048,1024]{1,0:T(8,128)(2,1)} %rows_ref.3, s32[16,128]{1,0:T(8,128)} %bitcast.56), custom_call_target="tpu_custom_call" | custom-call | bytes 1024 | tf_op jit(solution)/shard_map/pallas_call | solution.py:89
  1.4 5.0 %collective-permute-start.2 = (bf16[264,1024]{1,0:T(8,128)(2,1)S(1)}, bf16[264,1024]{1,0:T(8,128)(2,1)S(1)}, u32[]{:S(2)}, u32[]{:S(2)}) collective-permute-start(bf16[264,1024]{1,0:T(8,128)(2,1)S(1)} %get-tuple-element.57), channel_id=1, source_target_pairs={{0,4},{12,8},{1,5},{13,9},{2,6},{14,10},{3,7},{15,11},{16,20},{28,... | collective-permute-start | bytes 1622024 | tf_op jit(solution)/shard_map/ppermute | solution.py:299
  6.3 0.7 %collective-permute-start.1 = (bf16[264,1024]{1,0:T(8,128)(2,1)S(1)}, bf16[264,1024]{1,0:T(8,128)(2,1)S(1)}, u32[]{:S(2)}, u32[]{:S(2)}) collective-permute-start(bf16[264,1024]{1,0:T(8,128)(2,1)S(1)} %get-tuple-element.57), channel_id=1, source_target_pairs={{4,8},{8,4},{5,9},{9,5},{6,10},{10,6},{7,11},{11,7},{20,24},{24,20... | collective-permute-start | bytes 1622024 | tf_op jit(solution)/shard_map/ppermute | solution.py:298
  7.1 0.0 copy-done.6
  7.1 0.1 convert_reduce_fusion
  7.3 0.1 dynamic_slice.59
  7.4 0.1 concatenate.3.meta_ref
  7.4 7.3 %shard_map.30 = (bf16[2048,1024]{1,0:T(8,128)(2,1)S(1)}, f32[16,128]{1,0:T(8,128)S(1)}) custom-call(s32[84]{0:T(128)S(1)} %concatenate.3.meta_ref, bf16[2048,1024]{1,0:T(8,128)(2,1)} %rows_ref.3, bf16[2048,1024]{1,0:T(8,128)(2,1)} %rows_ref.3, s32[1,512]{1,0:T(1,128)S(1)} %bitcast.55), custom_call_target="tpu_custom_call" | custom-call | bytes 1024 | tf_op jit(solution)/shard_map/pallas_call | solution.py:311
  14.8 0.0 copy-start
  14.8 1.9 %copy-done = bf16[2048,1024]{1,0:T(8,128)(2,1)} copy-done((bf16[2048,1024]{1,0:T(8,128)(2,1)}, bf16[2048,1024]{1,0:T(8,128)(2,1)S(1)}, u32[]{:S(2)}) %copy-start) | copy-done | bytes 4194328
  16.7 2.2 %collective-permute-start = (bf16[264,1024]{1,0:T(8,128)(2,1)S(1)}, bf16[264,1024]{1,0:T(8,128)(2,1)S(1)}, u32[]{:S(2)}, u32[]{:S(2)}) collective-permute-start(bf16[264,1024]{1,0:T(8,128)(2,1)S(1)} %get-tuple-element.56), channel_id=1, source_target_pairs={{0,4},{12,8},{4,12},{8,0},{1,5},{13,9},{5,13},{9,1},{2,6},{14,10},... | collective-permute-start | bytes 1622024 | tf_op jit(solution)/shard_map/ppermute | solution.py:329
  18.9 0.0 collective-permute-done.2.outer_ref
  18.9 0.0 collective-permute-done.1.swap_ref
  18.9 0.0 copy-start.1
  18.9 2.2 %copy-done.1 = bf16[2048,1024]{1,0:T(8,128)(2,1)S(1)} copy-done((bf16[2048,1024]{1,0:T(8,128)(2,1)S(1)}, bf16[2048,1024]{1,0:T(8,128)(2,1)}, u32[]{:S(2)}) %copy-start.1) | copy-done | bytes 4194328
  21.1 3.6 %shard_map.32 = (f32[16,128]{1,0:T(8,128)S(1)}, f32[3,128]{1,0:T(4,128)S(1)}, f32[2,128]{1,0:T(2,128)S(1)}) custom-call(s32[84]{0:T(128)S(1)} %concatenate.3.meta_ref, bf16[2048,1024]{1,0:T(8,128)(2,1)S(1)} %copy-done.1, bf16[264,1024]{1,0:T(8,128)(2,1)S(1)} %collective-permute-done.1.swap_ref, bf16[264,1024]{1,0:T(8,128)(2,1)S(1)} %collective-permute-done.2.outer_ref, ...), custom_call_target="tpu_custom_call" | custom-call | flops 2147483648 | bytes 1024 | tf_op jit(solution)/shard_map/pallas_call | solution.py:225
  24.7 1.3 %collective-permute-start.3 = (f32[3,128]{1,0:T(4,128)S(1)}, f32[3,128]{1,0:T(4,128)S(1)}, u32[]{:S(2)}, u32[]{:S(2)}) collective-permute-start(f32[3,128]{1,0:T(4,128)S(1)} %get-tuple-element.60.outer_cols_ref), channel_id=1, source_target_pairs={{4,0},{8,12},{5,1},{9,13},{6,2},{10,14},{7,3},{11,15},{20,16},{24,... | collective-permute-start | bytes 4616 | tf_op jit(solution)/shard_map/ppermute | solution.py:338
  26.0 0.7 %collective-permute-start.4 = (f32[2,128]{1,0:T(2,128)S(1)}, f32[2,128]{1,0:T(2,128)S(1)}, u32[]{:S(2)}, u32[]{:S(2)}) collective-permute-start(f32[2,128]{1,0:T(2,128)S(1)} %get-tuple-element.61), channel_id=1, source_target_pairs={{8,4},{4,8},{9,5},{5,9},{10,6},{6,10},{11,7},{7,11},{24,20},{20,24... | collective-permute-start | bytes 3080 | tf_op jit(solution)/shard_map/ppermute | solution.py:339
  26.7 6.0 %collective-permute-done.piece_ref = bf16[264,1024]{1,0:T(8,128)(2,1)S(1)} collective-permute-done((bf16[264,1024]{1,0:T(8,128)(2,1)S(1)}, bf16[264,1024]{1,0:T(8,128)(2,1)S(1)}, u32[]{:S(2)}, u32[]{:S(2)}) %collective-permute-start) | collective-permute-done | bytes 540704 | tf_op jit(solution)/shard_map/ppermute | solution.py:329
  32.7 0.0 collective-permute-done.4.swap_back_ref
  32.7 0.0 collective-permute-done.3.outer_back_ref
  32.7 0.0 copy-start.2
  32.7 2.2 %copy-done.2 = bf16[2048,1024]{1,0:T(8,128)(2,1)S(1)} copy-done((bf16[2048,1024]{1,0:T(8,128)(2,1)S(1)}, bf16[2048,1024]{1,0:T(8,128)(2,1)}, u32[]{:S(2)}) %copy-start.2) | copy-done | bytes 4194328
  34.9 2.7 %shard_map.33 = (f32[8,128]{1,0:T(8,128)S(1)}, f32[8,128]{1,0:T(8,128)S(1)}, f32[2,128]{1,0:T(2,128)S(1)}, s32[1]{0:T(128)}) custom-call(s32[84]{0:T(128)S(1)} %concatenate.3.meta_ref, bf16[2048,1024]{1,0:T(8,128)(2,1)S(1)} %copy-done.2, bf16[264,1024]{1,0:T(8,128)(2,1)S(1)} %collective-permute-done.piece_ref, f32[16,128]{1,0:T(8,128)S(1)} %get-tuple-element.59.before_ref, ...), custom_call_target="tpu_custom_call" | custom-call | flops 1073741824 | bytes 1024 | tf_op jit(solution)/shard_map/pallas_call | solution.py:225
  37.6 3.8 %collective-permute-start.5 = (f32[2,128]{1,0:T(2,128)S(1)}, f32[2,128]{1,0:T(2,128)S(1)}, u32[]{:S(2)}, u32[]{:S(2)}) collective-permute-start(f32[2,128]{1,0:T(2,128)S(1)} %get-tuple-element.64), channel_id=1, source_target_pairs={{4,0},{8,12},{12,4},{0,8},{5,1},{9,13},{13,5},{1,9},{6,2},{10,14},... | collective-permute-start | bytes 3080 | tf_op jit(solution)/shard_map/ppermute | solution.py:351
  41.4 0.0 collective-permute-start.6
  41.4 1.3 %collective-permute-done.5 = f32[2,128]{1,0:T(2,128)S(1)} collective-permute-done((f32[2,128]{1,0:T(2,128)S(1)}, f32[2,128]{1,0:T(2,128)S(1)}, u32[]{:S(2)}, u32[]{:S(2)}) %collective-permute-start.5) | collective-permute-done | bytes 1056 | tf_op jit(solution)/shard_map/ppermute | solution.py:351
  42.7 0.1 dynamic_update_slice.3
  42.8 0.0 collective-permute-done.6
  42.8 1.6 %collective-permute-start.7 = (f32[1,4,128]{2,1,0:T(4,128)S(1)}, f32[1,4,128]{2,1,0:T(4,128)S(1)}, u32[]{:S(2)}, u32[]{:S(2)}) collective-permute-start(f32[1,4,128]{2,1,0:T(4,128)S(1)} %dynamic-slice_bitcast_fusion), channel_id=1, source_target_pairs={{0,2},{1,3},{2,0},{3,1},{4,6},{5,7},{6,4},{7,5},{8,10},{9,11},{10,... | collective-permute-start | bytes 6152 | tf_op jit(solution)/shard_map/ppermute | solution.py:363
  45.0 1.4 %collective-permute-done.7 = f32[1,4,128]{2,1,0:T(4,128)S(1)} collective-permute-done((f32[1,4,128]{2,1,0:T(4,128)S(1)}, f32[1,4,128]{2,1,0:T(4,128)S(1)}, u32[]{:S(2)}, u32[]{:S(2)}) %collective-permute-start.7) | collective-permute-done | bytes 2080 | tf_op jit(solution)/shard_map/ppermute | solution.py:363
  46.5 0.0 copy-start.7
  46.5 0.6 %copy-done.7 = f32[512]{0:T(512)} copy-done((f32[512]{0:T(512)}, f32[512]{0:T(512)S(1)}, u32[]{:S(2)}) %copy-start.7) | copy-done | bytes 2072
  (6 shorter events, 0.0 us)
Async XLA Ops:
  0.0 7.1 %copy-start.6 = (s32[2048]{0:T(1024)S(1)}, s32[2048]{0:T(1024)}, u32[]{:S(2)}) copy-start(s32[2048]{0:T(1024)} %param.5) | copy-start | bytes 24580
  1.4 17.5 %collective-permute-start.2 = (bf16[264,1024]{1,0:T(8,128)(2,1)S(1)}, bf16[264,1024]{1,0:T(8,128)(2,1)S(1)}, u32[]{:S(2)}, u32[]{:S(2)}) collective-permute-start(bf16[264,1024]{1,0:T(8,128)(2,1)S(1)} %get-tuple-element.57), channel_id=1, source_target_pairs={{0,4},{12,8},{1,5},{13,9},{2,6},{14,10},{3,7},{15,11},{16,20},{28,... | collective-permute-start | bytes 1622024 | tf_op jit(solution)/shard_map/ppermute | solution.py:299
  6.3 12.5 %collective-permute-start.1 = (bf16[264,1024]{1,0:T(8,128)(2,1)S(1)}, bf16[264,1024]{1,0:T(8,128)(2,1)S(1)}, u32[]{:S(2)}, u32[]{:S(2)}) collective-permute-start(bf16[264,1024]{1,0:T(8,128)(2,1)S(1)} %get-tuple-element.57), channel_id=1, source_target_pairs={{4,8},{8,4},{5,9},{9,5},{6,10},{10,6},{7,11},{11,7},{20,24},{24,20... | collective-permute-start | bytes 1622024 | tf_op jit(solution)/shard_map/ppermute | solution.py:298
  14.8 1.9 %copy-start = (bf16[2048,1024]{1,0:T(8,128)(2,1)}, bf16[2048,1024]{1,0:T(8,128)(2,1)S(1)}, u32[]{:S(2)}) copy-start(bf16[2048,1024]{1,0:T(8,128)(2,1)S(1)} %get-tuple-element.53.unit_ref) | copy-start | bytes 12582916
  16.7 16.0 %collective-permute-start = (bf16[264,1024]{1,0:T(8,128)(2,1)S(1)}, bf16[264,1024]{1,0:T(8,128)(2,1)S(1)}, u32[]{:S(2)}, u32[]{:S(2)}) collective-permute-start(bf16[264,1024]{1,0:T(8,128)(2,1)S(1)} %get-tuple-element.56), channel_id=1, source_target_pairs={{0,4},{12,8},{4,12},{8,0},{1,5},{13,9},{5,13},{9,1},{2,6},{14,10},... | collective-permute-start | bytes 1622024 | tf_op jit(solution)/shard_map/ppermute | solution.py:329
  18.9 2.2 %copy-start.1 = (bf16[2048,1024]{1,0:T(8,128)(2,1)S(1)}, bf16[2048,1024]{1,0:T(8,128)(2,1)}, u32[]{:S(2)}) copy-start(bf16[2048,1024]{1,0:T(8,128)(2,1)} %copy-done) | copy-start | bytes 12582916
  24.7 8.0 %collective-permute-start.3 = (f32[3,128]{1,0:T(4,128)S(1)}, f32[3,128]{1,0:T(4,128)S(1)}, u32[]{:S(2)}, u32[]{:S(2)}) collective-permute-start(f32[3,128]{1,0:T(4,128)S(1)} %get-tuple-element.60.outer_cols_ref), channel_id=1, source_target_pairs={{4,0},{8,12},{5,1},{9,13},{6,2},{10,14},{7,3},{11,15},{20,16},{24,... | collective-permute-start | bytes 4616 | tf_op jit(solution)/shard_map/ppermute | solution.py:338
  26.0 6.7 %collective-permute-start.4 = (f32[2,128]{1,0:T(2,128)S(1)}, f32[2,128]{1,0:T(2,128)S(1)}, u32[]{:S(2)}, u32[]{:S(2)}) collective-permute-start(f32[2,128]{1,0:T(2,128)S(1)} %get-tuple-element.61), channel_id=1, source_target_pairs={{8,4},{4,8},{9,5},{5,9},{10,6},{6,10},{11,7},{7,11},{24,20},{20,24... | collective-permute-start | bytes 3080 | tf_op jit(solution)/shard_map/ppermute | solution.py:339
  32.7 2.2 %copy-start.2 = (bf16[2048,1024]{1,0:T(8,128)(2,1)S(1)}, bf16[2048,1024]{1,0:T(8,128)(2,1)}, u32[]{:S(2)}) copy-start(bf16[2048,1024]{1,0:T(8,128)(2,1)} %copy-done) | copy-start | bytes 12582916
  37.6 5.1 %collective-permute-start.5 = (f32[2,128]{1,0:T(2,128)S(1)}, f32[2,128]{1,0:T(2,128)S(1)}, u32[]{:S(2)}, u32[]{:S(2)}) collective-permute-start(f32[2,128]{1,0:T(2,128)S(1)} %get-tuple-element.64), channel_id=1, source_target_pairs={{4,0},{8,12},{12,4},{0,8},{5,1},{9,13},{13,5},{1,9},{6,2},{10,14},... | collective-permute-start | bytes 3080 | tf_op jit(solution)/shard_map/ppermute | solution.py:351
  41.4 1.4 %collective-permute-start.6 = (f32[8,128]{1,0:T(8,128)S(1)}, f32[8,128]{1,0:T(8,128)S(1)}, u32[]{:S(2)}, u32[]{:S(2)}) collective-permute-start(f32[8,128]{1,0:T(8,128)S(1)} %get-tuple-element.65), channel_id=1, source_target_pairs={{0,1},{1,0},{2,3},{3,2},{4,5},{5,4},{6,7},{7,6},{8,9},{9,8},{10,11... | collective-permute-start | bytes 12296 | tf_op jit(solution)/shard_map/ppermute | solution.py:357
  42.8 3.7 %collective-permute-start.7 = (f32[1,4,128]{2,1,0:T(4,128)S(1)}, f32[1,4,128]{2,1,0:T(4,128)S(1)}, u32[]{:S(2)}, u32[]{:S(2)}) collective-permute-start(f32[1,4,128]{2,1,0:T(4,128)S(1)} %dynamic-slice_bitcast_fusion), channel_id=1, source_target_pairs={{0,2},{1,3},{2,0},{3,1},{4,6},{5,7},{6,4},{7,5},{8,10},{9,11},{10,... | collective-permute-start | bytes 6152 | tf_op jit(solution)/shard_map/ppermute | solution.py:363
  46.5 0.6 %copy-start.7 = (f32[512]{0:T(512)}, f32[512]{0:T(512)S(1)}, u32[]{:S(2)}) copy-start(f32[512]{0:T(512)S(1)} %get-tuple-element.97) | copy-start | bytes 6148

commit v8 on v7

--- a/solution.py
+++ b/solution.py
@@ -190,9 +190,14 @@
     outer_cols_ref[share : share + 1, :] = jnp.where(joined, 1.0, 0.0)
 
 
+def flag_kernel(share, outer_cols_ref, outer_back_ref, flag_ref):
+    flags = jnp.maximum(outer_cols_ref[share : share + 1, :], outer_back_ref[share : share + 1, :])
+    flag_ref[0] = jnp.max(flags).astype(jnp.int32)
+
+
 def last_kernel(
-    blocks, share, width, meta_ref, unit_ref, piece_ref, before_ref, outer_cols_ref, outer_back_ref, swap_back_ref,
-    keep_ref, send_ref, cols_ref, flag_ref, piece_unit, sums,
+    blocks, share, width, meta_ref, unit_ref, piece_ref, before_ref, outer_back_ref, swap_back_ref,
+    keep_ref, send_ref, cols_ref, piece_unit, sums,
 ):
     meta = Meta(meta_ref, blocks)
     size = share * BLOCK
@@ -207,8 +212,6 @@
         at = place(block)
         sums[at : at + 1, :] = before_ref[block : block + 1, :] + value
 
-    flags = jnp.maximum(outer_cols_ref[share : share + 1, :], outer_back_ref[share : share + 1, :])
-    flag_ref[0] = jnp.max(flags).astype(jnp.int32)
     (cols,) = cross_terms(meta, (2,), (tags,), unit_ref, piece_unit, add_rows)
     for k in range(share):
         cols_ref[k : k + 1, :] = cols[k]
@@ -305,6 +308,16 @@
     numbers = jnp.stack([member, plan.first, plan.edge, inner])
     meta = jnp.concatenate([tag, used, seen, swapped, tag, numbers]).astype(jnp.int32)
 
+    heap = blocks // 2
+    owner = plan.second // width
+    home_row = jnp.arange(heap)[:, None] - (owner // 2 * width + plan.second % width)
+    home_row = jnp.broadcast_to(home_row, (heap, BLOCK)).astype(jnp.int32)
+    upper = [
+        jnp.broadcast_to((member >> bit) & 1, (heap >> bit, BLOCK)).astype(jnp.int32)
+        for bit in range(1, subs.bit_length() - 1)
+    ]
+    meta, home_row, *upper = lax.optimization_barrier((meta, home_row, *upper))
+
     row_sums = jax.ShapeDtypeStruct((blocks, BLOCK), jnp.float32)
     col_sums = jax.ShapeDtypeStruct((share, BLOCK), jnp.float32)
     quarter = width * BLOCK
@@ -338,31 +351,33 @@
     outer_back = lax.ppermute(outer_cols, "tile", turned(inward))
     swap_back = lax.ppermute(swap_cols, "tile", turned(swap))
 
-    half = jax.ShapeDtypeStruct((blocks // 2, BLOCK), jnp.float32)
-    held, leaving, cols, flag = call(
+    flag = pl.pallas_call(
+        functools.partial(flag_kernel, share),
+        out_specs=pl.BlockSpec(memory_space=pltpu.SMEM),
+        out_shape=jax.ShapeDtypeStruct((1,), jnp.int32),
+        compiler_params=pltpu.CompilerParams(vmem_limit_bytes=4 * 1024 * 1024),
+    )(outer_cols, outer_back)
+    sums, flag = lax.optimization_barrier((sums, flag))
+    half = jax.ShapeDtypeStruct((heap, BLOCK), jnp.float32)
+    held, leaving, cols = call(
         functools.partial(last_kernel, blocks, share, width),
         meta,
-        (unit, last, sums, outer_cols, outer_back, swap_back),
-        [half, half, col_sums, jax.ShapeDtypeStruct((1,), jnp.int32)],
+        (unit, last, sums, outer_back, swap_back),
+        [half, half, col_sums],
         [pltpu.VMEM((size, depth), jnp.bfloat16), pltpu.VMEM((blocks, BLOCK), jnp.float32)],
         2 * rows * size * depth,
     )
 
     home = lax.ppermute(cols, "tile", turned(around))
-    owner = plan.second // width
-    home_at = owner // 2 * width + plan.second % width
-    held = lax.dynamic_update_slice_in_dim(
-        held, lax.dynamic_slice_in_dim(held, home_at, share, 0) + home, home_at, 0
-    )
+    for k in range(share):
+        held = held + jnp.where(home_row == k, home[k : k + 1], 0.0)
     held = held + lax.ppermute(leaving, "sub", [(i, i ^ 1) for i in range(subs)])
-    bit = 1
-    while 1 << bit < subs:
+    for bit, mine in enumerate(upper, 1):
         pairs = held.reshape(-1, 2, width, BLOCK)
-        own = (member >> bit) & 1
-        leaving = lax.dynamic_index_in_dim(pairs, 1 - own, 1, keepdims=False)
-        came = lax.ppermute(leaving, "sub", [(i, i ^ (1 << bit)) for i in range(subs)])
-        held = lax.dynamic_index_in_dim(pairs, own, 1, keepdims=False) + came
-        bit += 1
+        low, high = pairs[:, 0].reshape(mine.shape), pairs[:, 1].reshape(mine.shape)
+        leaving = jnp.where(mine > 0, low, high)
+        held = jnp.where(mine > 0, high, low)
+        held = held + lax.ppermute(leaving, "sub", [(i, i ^ (1 << bit)) for i in range(subs)])
     scores = jnp.log(1.0 + held.reshape(-1))
 
     bad = flag[0] > 0

time: 47.4 us -> 43.1 us (0.909)
  local copies, waits for them, and re-layouts: 7.11 us -> 0.81 us
  waiting for transfers between devices: 8.68 us -> 12.7 us
  starting transfers between devices: 15.2 us -> 13.1 us
    unnamed x10 -> x4, local copies, waits for them, and re-layouts: 6.87 us -> 0.58 us
    ppermute x1, waiting for transfers between devices: 0.01 us -> 4.79 us  [shards(): outer_back = lax.ppermute(outer_cols, 'tile', turned(inward))]
    ppermute x1, waiting for transfers between devices: 5.97 us -> 2.66 us  [shards(): last = lax.ppermute(second_out, 'tile', around)]
    ppermute x1, starting transfers between devices: 3.8 us -> 1.59 us  [shards(): home = lax.ppermute(cols, 'tile', turned(around))]
    ppermute x1, waiting for transfers between devices: 0.01 us -> 1.84 us  [shards(): from_outer = lax.ppermute(first_out, 'tile', inward)]
    ppermute x1, waiting for transfers between devices: 1.41 us -> 2.09 us  [shards(): lax.ppermute(leaving, 'sub', [(i, i ^ 1 << bit) for i in range(subs)])]
    pallas_call x0 -> x1, Pallas kernels: none -> 0.64 us  [shards(): pl.pallas_call(functools.partial(flag_kernel, share), out_specs=pl.BlockS...]
  transfers between devices with their start and end apart: 8 -> 8, of which waited for: 3 -> 5; matrix products, arithmetic and copies ran while one was open for 1% -> 1% of each run, Pallas kernels for 23% -> 27%
where the time goes in v8:
time: 43.1 us; the launch traced here: 42.8 us
  Pallas kernels  15.2 us (35%)
  starting transfers between devices  13.1 us (30%)
  waiting for transfers between devices  12.7 us (29%)
  between operations  0.91 us (2%)
  local copies, waits for them, and re-layouts  0.81 us (2%)
    pallas_call x1, Pallas kernels, shards(): pl.pallas_call(functools.partial(self_kernel, blocks, width), grid_spec=p...  7.31 us
    pallas_call x2, Pallas kernels, call(): pl.pallas_call(kernel, in_specs=[smem] + [vmem] * len(operands), out_spec...  5.89 us
    ppermute x1, starting transfers between devices, shards(): from_outer = lax.ppermute(first_out, 'tile', inward)  4.96 us
    ppermute x1, waiting for transfers between devices, shards(): outer_back = lax.ppermute(outer_cols, 'tile', turned(inward))  4.79 us
    ppermute x1, waiting for transfers between devices, shards(): last = lax.ppermute(second_out, 'tile', around)  2.66 us
    ppermute x1, starting transfers between devices, shards(): last = lax.ppermute(second_out, 'tile', around)  2.24 us
    ppermute x1, waiting for transfers between devices, shards(): lax.ppermute(leaving, 'sub', [(i, i ^ 1 << bit) for i in range(subs)])  2.09 us
    ppermute x1, waiting for transfers between devices, shards(): from_outer = lax.ppermute(first_out, 'tile', inward)  1.84 us
  transfers between devices with their start and end apart: 8, of which 5 were waited for; matrix products, arithmetic and copies ran while one was open for 1% of the time, Pallas kernels for 27%

profile of v8, /device:TPU:0, one launch (start us, length us, event | category | flops | bytes accessed | tf_op | source)
XLA Modules:
  0.0 42.8 jit_solution(3785220274041472549)
XLA Ops:
  0.0 0.0 copy-start.3
  0.0 1.4 %shard_map.31 = (bf16[264,1024]{1,0:T(8,128)(2,1)S(1)}, bf16[264,1024]{1,0:T(8,128)(2,1)S(1)}) custom-call(bf16[2048,1024]{1,0:T(8,128)(2,1)} %rows_ref.3, s32[16,128]{1,0:T(8,128)} %bitcast.58), custom_call_target="tpu_custom_call" | custom-call | bytes 1024 | tf_op jit(solution)/shard_map/pallas_call | solution.py:89
  1.4 5.0 %collective-permute-start.1 = (bf16[264,1024]{1,0:T(8,128)(2,1)S(1)}, bf16[264,1024]{1,0:T(8,128)(2,1)S(1)}, u32[]{:S(2)}, u32[]{:S(2)}) collective-permute-start(bf16[264,1024]{1,0:T(8,128)(2,1)S(1)} %get-tuple-element.53), channel_id=1, source_target_pairs={{0,4},{12,8},{1,5},{13,9},{2,6},{14,10},{3,7},{15,11},{16,20},{28,... | collective-permute-start | bytes 1622024 | tf_op jit(solution)/shard_map/ppermute | solution.py:302
  6.3 0.7 %collective-permute-start = (bf16[264,1024]{1,0:T(8,128)(2,1)S(1)}, bf16[264,1024]{1,0:T(8,128)(2,1)S(1)}, u32[]{:S(2)}, u32[]{:S(2)}) collective-permute-start(bf16[264,1024]{1,0:T(8,128)(2,1)S(1)} %get-tuple-element.53), channel_id=1, source_target_pairs={{4,8},{8,4},{5,9},{9,5},{6,10},{10,6},{7,11},{11,7},{20,24},{24,20... | collective-permute-start | bytes 1622024 | tf_op jit(solution)/shard_map/ppermute | solution.py:301
  7.1 0.0 copy-done.3
  7.1 0.1 convert_reduce_fusion
  7.3 0.1 dynamic_slice.47
  7.4 0.1 concatenate.3.meta_ref
  7.5 0.1 broadcast_in_dim.128
  7.6 7.3 %shard_map.30 = (bf16[2048,1024]{1,0:T(8,128)(2,1)S(1)}, f32[16,128]{1,0:T(8,128)S(1)}) custom-call(s32[84]{0:T(128)S(1)} %concatenate.3.meta_ref, bf16[2048,1024]{1,0:T(8,128)(2,1)} %rows_ref.3, bf16[2048,1024]{1,0:T(8,128)(2,1)} %rows_ref.3, s32[1,512]{1,0:T(1,128)S(1)} %bitcast.57), custom_call_target="tpu_custom_call" | custom-call | bytes 1024 | tf_op jit(solution)/shard_map/pallas_call | solution.py:324
  14.9 2.2 %collective-permute-start.3 = (bf16[264,1024]{1,0:T(8,128)(2,1)S(1)}, bf16[264,1024]{1,0:T(8,128)(2,1)S(1)}, u32[]{:S(2)}, u32[]{:S(2)}) collective-permute-start(bf16[264,1024]{1,0:T(8,128)(2,1)S(1)} %get-tuple-element.61), channel_id=1, source_target_pairs={{0,4},{12,8},{4,12},{8,0},{1,5},{13,9},{5,13},{9,1},{2,6},{14,10},... | collective-permute-start | bytes 1622024 | tf_op jit(solution)/shard_map/ppermute | solution.py:342
  17.1 1.8 %collective-permute-done.1.outer_ref = bf16[264,1024]{1,0:T(8,128)(2,1)S(1)} collective-permute-done((bf16[264,1024]{1,0:T(8,128)(2,1)S(1)}, bf16[264,1024]{1,0:T(8,128)(2,1)S(1)}, u32[]{:S(2)}, u32[]{:S(2)}) %collective-permute-start.1) | collective-permute-done | bytes 540704 | tf_op jit(solution)/shard_map/ppermute | solution.py:302
  19.0 0.0 collective-permute-done.swap_ref
  19.0 3.6 %shard_map.32 = (f32[16,128]{1,0:T(8,128)S(1)}, f32[3,128]{1,0:T(4,128)S(1)}, f32[2,128]{1,0:T(2,128)S(1)}) custom-call(s32[84]{0:T(128)S(1)} %concatenate.3.meta_ref, bf16[2048,1024]{1,0:T(8,128)(2,1)S(1)} %get-tuple-element.52.unit_ref, bf16[264,1024]{1,0:T(8,128)(2,1)S(1)} %collective-permute-done.swap_ref, ...), custom_call_target="tpu_custom_call" | custom-call | flops 2147483648 | bytes 1024 | tf_op jit(solution)/shard_map/pallas_call | solution.py:228
  22.6 1.3 %collective-permute-start.2 = (f32[3,128]{1,0:T(4,128)S(1)}, f32[3,128]{1,0:T(4,128)S(1)}, u32[]{:S(2)}, u32[]{:S(2)}) collective-permute-start(f32[3,128]{1,0:T(4,128)S(1)} %get-tuple-element.58.outer_cols_ref), channel_id=1, source_target_pairs={{4,0},{8,12},{5,1},{9,13},{6,2},{10,14},{7,3},{11,15},{20,16},{24,... | collective-permute-start | bytes 4616 | tf_op jit(solution)/shard_map/ppermute | solution.py:351
  23.9 0.7 %collective-permute-start.4 = (f32[2,128]{1,0:T(2,128)S(1)}, f32[2,128]{1,0:T(2,128)S(1)}, u32[]{:S(2)}, u32[]{:S(2)}) collective-permute-start(f32[2,128]{1,0:T(2,128)S(1)} %get-tuple-element.63), channel_id=1, source_target_pairs={{8,4},{4,8},{9,5},{5,9},{10,6},{6,10},{11,7},{7,11},{24,20},{20,24... | collective-permute-start | bytes 3080 | tf_op jit(solution)/shard_map/ppermute | solution.py:352
  24.6 4.8 %collective-permute-done.2.outer_back_ref = f32[3,128]{1,0:T(4,128)S(1)} collective-permute-done((f32[3,128]{1,0:T(4,128)S(1)}, f32[3,128]{1,0:T(4,128)S(1)}, u32[]{:S(2)}, u32[]{:S(2)}) %collective-permute-start.2) | collective-permute-done | bytes 1568 | tf_op jit(solution)/shard_map/ppermute | solution.py:351
  29.4 0.6 %shard_map.33 = s32[1]{0:T(128)} custom-call(f32[3,128]{1,0:T(4,128)S(1)} %get-tuple-element.58.outer_cols_ref, f32[3,128]{1,0:T(4,128)S(1)} %collective-permute-done.2.outer_back_ref), custom_call_target="tpu_custom_call" | custom-call | tf_op jit(solution)/shard_map/pallas_call | solution.py:354
  30.0 2.7 %collective-permute-done.3.piece_ref = bf16[264,1024]{1,0:T(8,128)(2,1)S(1)} collective-permute-done((bf16[264,1024]{1,0:T(8,128)(2,1)S(1)}, bf16[264,1024]{1,0:T(8,128)(2,1)S(1)}, u32[]{:S(2)}, u32[]{:S(2)}) %collective-permute-start.3) | collective-permute-done | bytes 540704 | tf_op jit(solution)/shard_map/ppermute | solution.py:342
  32.7 0.0 collective-permute-done.4.swap_back_ref
  32.7 2.3 %shard_map.34 = (f32[8,128]{1,0:T(8,128)S(1)}, f32[8,128]{1,0:T(8,128)S(1)}, f32[2,128]{1,0:T(2,128)S(1)}) custom-call(s32[84]{0:T(128)S(1)} %concatenate.3.meta_ref, bf16[2048,1024]{1,0:T(8,128)(2,1)S(1)} %get-tuple-element.52.unit_ref, bf16[264,1024]{1,0:T(8,128)(2,1)S(1)} %collective-permute-done.3.piece_ref, f32[16,128]{1,0:T(8,128)S(1)} %get-tuple-element.62.before_ref, ...), custom_call_target="tpu_custom_call" | custom-call | flops 1073741824 | bytes 1024 | tf_op jit(solution)/shard_map/pallas_call | solution.py:228
  34.9 1.6 %collective-permute-start.5 = (f32[2,128]{1,0:T(2,128)S(1)}, f32[2,128]{1,0:T(2,128)S(1)}, u32[]{:S(2)}, u32[]{:S(2)}) collective-permute-start(f32[2,128]{1,0:T(2,128)S(1)} %get-tuple-element.66), channel_id=1, source_target_pairs={{4,0},{8,12},{12,4},{0,8},{5,1},{9,13},{13,5},{1,9},{6,2},{10,14},... | collective-permute-start | bytes 3080 | tf_op jit(solution)/shard_map/ppermute | solution.py:371
  37.2 0.1 collective-permute-start.6
  37.3 1.3 %collective-permute-done.5 = f32[2,128]{1,0:T(2,128)S(1)} collective-permute-done((f32[2,128]{1,0:T(2,128)S(1)}, f32[2,128]{1,0:T(2,128)S(1)}, u32[]{:S(2)}, u32[]{:S(2)}) %collective-permute-start.5) | collective-permute-done | bytes 1056 | tf_op jit(solution)/shard_map/ppermute | solution.py:371
  38.6 0.0 collective-permute-done.6
  38.6 1.6 %collective-permute-start.7 = (f32[4,128]{1,0:T(4,128)S(1)}, f32[4,128]{1,0:T(4,128)S(1)}, u32[]{:S(2)}, u32[]{:S(2)}) collective-permute-start(f32[4,128]{1,0:T(4,128)S(1)} %get-tuple-element.71), channel_id=1, source_target_pairs={{0,2},{1,3},{2,0},{3,1},{4,6},{5,7},{6,4},{7,5},{8,10},{9,11},{10,... | collective-permute-start | bytes 6152 | tf_op jit(solution)/shard_map/ppermute | solution.py:380
  40.2 2.1 %collective-permute-done.7 = f32[4,128]{1,0:T(4,128)S(1)} collective-permute-done((f32[4,128]{1,0:T(4,128)S(1)}, f32[4,128]{1,0:T(4,128)S(1)}, u32[]{:S(2)}, u32[]{:S(2)}) %collective-permute-start.7) | collective-permute-done | bytes 2080 | tf_op jit(solution)/shard_map/ppermute | solution.py:380
  42.3 0.0 copy-start.4
  42.3 0.6 %copy-done.4 = f32[512]{0:T(512)} copy-done((f32[512]{0:T(512)}, f32[512]{0:T(512)S(1)}, u32[]{:S(2)}) %copy-start.4) | copy-done | bytes 2072
  (9 shorter events, 0.0 us)
Async XLA Ops:
  0.0 7.1 %copy-start.3 = (s32[2048]{0:T(1024)S(1)}, s32[2048]{0:T(1024)}, u32[]{:S(2)}) copy-start(s32[2048]{0:T(1024)} %param.5) | copy-start | bytes 24580
  1.4 17.6 %collective-permute-start.1 = (bf16[264,1024]{1,0:T(8,128)(2,1)S(1)}, bf16[264,1024]{1,0:T(8,128)(2,1)S(1)}, u32[]{:S(2)}, u32[]{:S(2)}) collective-permute-start(bf16[264,1024]{1,0:T(8,128)(2,1)S(1)} %get-tuple-element.53), channel_id=1, source_target_pairs={{0,4},{12,8},{1,5},{13,9},{2,6},{14,10},{3,7},{15,11},{16,20},{28,... | collective-permute-start | bytes 1622024 | tf_op jit(solution)/shard_map/ppermute | solution.py:302
  6.3 12.6 %collective-permute-start = (bf16[264,1024]{1,0:T(8,128)(2,1)S(1)}, bf16[264,1024]{1,0:T(8,128)(2,1)S(1)}, u32[]{:S(2)}, u32[]{:S(2)}) collective-permute-start(bf16[264,1024]{1,0:T(8,128)(2,1)S(1)} %get-tuple-element.53), channel_id=1, source_target_pairs={{4,8},{8,4},{5,9},{9,5},{6,10},{10,6},{7,11},{11,7},{20,24},{24,20... | collective-permute-start | bytes 1622024 | tf_op jit(solution)/shard_map/ppermute | solution.py:301
  14.9 17.8 %collective-permute-start.3 = (bf16[264,1024]{1,0:T(8,128)(2,1)S(1)}, bf16[264,1024]{1,0:T(8,128)(2,1)S(1)}, u32[]{:S(2)}, u32[]{:S(2)}) collective-permute-start(bf16[264,1024]{1,0:T(8,128)(2,1)S(1)} %get-tuple-element.61), channel_id=1, source_target_pairs={{0,4},{12,8},{4,12},{8,0},{1,5},{13,9},{5,13},{9,1},{2,6},{14,10},... | collective-permute-start | bytes 1622024 | tf_op jit(solution)/shard_map/ppermute | solution.py:342
  22.6 6.8 %collective-permute-start.2 = (f32[3,128]{1,0:T(4,128)S(1)}, f32[3,128]{1,0:T(4,128)S(1)}, u32[]{:S(2)}, u32[]{:S(2)}) collective-permute-start(f32[3,128]{1,0:T(4,128)S(1)} %get-tuple-element.58.outer_cols_ref), channel_id=1, source_target_pairs={{4,0},{8,12},{5,1},{9,13},{6,2},{10,14},{7,3},{11,15},{20,16},{24,... | collective-permute-start | bytes 4616 | tf_op jit(solution)/shard_map/ppermute | solution.py:351
  23.9 8.8 %collective-permute-start.4 = (f32[2,128]{1,0:T(2,128)S(1)}, f32[2,128]{1,0:T(2,128)S(1)}, u32[]{:S(2)}, u32[]{:S(2)}) collective-permute-start(f32[2,128]{1,0:T(2,128)S(1)} %get-tuple-element.63), channel_id=1, source_target_pairs={{8,4},{4,8},{9,5},{5,9},{10,6},{6,10},{11,7},{7,11},{24,20},{20,24... | collective-permute-start | bytes 3080 | tf_op jit(solution)/shard_map/ppermute | solution.py:352
  34.9 3.6 %collective-permute-start.5 = (f32[2,128]{1,0:T(2,128)S(1)}, f32[2,128]{1,0:T(2,128)S(1)}, u32[]{:S(2)}, u32[]{:S(2)}) collective-permute-start(f32[2,128]{1,0:T(2,128)S(1)} %get-tuple-element.66), channel_id=1, source_target_pairs={{4,0},{8,12},{12,4},{0,8},{5,1},{9,13},{13,5},{1,9},{6,2},{10,14},... | collective-permute-start | bytes 3080 | tf_op jit(solution)/shard_map/ppermute | solution.py:371
  37.2 1.4 %collective-permute-start.6 = (f32[8,128]{1,0:T(8,128)S(1)}, f32[8,128]{1,0:T(8,128)S(1)}, u32[]{:S(2)}, u32[]{:S(2)}) collective-permute-start(f32[8,128]{1,0:T(8,128)S(1)} %get-tuple-element.67), channel_id=1, source_target_pairs={{0,1},{1,0},{2,3},{3,2},{4,5},{5,4},{6,7},{7,6},{8,9},{9,8},{10,11... | collective-permute-start | bytes 12296 | tf_op jit(solution)/shard_map/ppermute | solution.py:374
  38.6 3.7 %collective-permute-start.7 = (f32[4,128]{1,0:T(4,128)S(1)}, f32[4,128]{1,0:T(4,128)S(1)}, u32[]{:S(2)}, u32[]{:S(2)}) collective-permute-start(f32[4,128]{1,0:T(4,128)S(1)} %get-tuple-element.71), channel_id=1, source_target_pairs={{0,2},{1,3},{2,0},{3,1},{4,6},{5,7},{6,4},{7,5},{8,10},{9,11},{10,... | collective-permute-start | bytes 6152 | tf_op jit(solution)/shard_map/ppermute | solution.py:380
  42.3 0.6 %copy-start.4 = (f32[512]{0:T(512)}, f32[512]{0:T(512)S(1)}, u32[]{:S(2)}) copy-start(f32[512]{0:T(512)S(1)} %get-tuple-element.105) | copy-start | bytes 6148

commit v9 on v8

--- a/solution.py
+++ b/solution.py
@@ -61,36 +61,39 @@
         self.width, self.share = width, share
 
 
-def pack_kernel(blocks, subs, rows_ref, ids_ref, first_ref, second_ref, ids, sems):
+def pack_kernel(blocks, subs, rows_ref, ids_ref, *refs):
+    outs, (ids, sems) = refs[:4], refs[4:]
     plan = Plan(blocks, subs, lax.axis_index("tile"), lax.axis_index("sub"))
-    share, size = plan.share, plan.share * BLOCK
+    share, half = plan.share, plan.share * BLOCK // 2
     copies = []
-    for block, out in ((plan.first, first_ref), (plan.second, second_ref)):
-        for down in range(0, size, COPY):
-            start = pl.multiple_of(block * BLOCK + down, COPY)
+    for index, out in enumerate(outs):
+        block = plan.first if index < 2 else plan.second
+        for down in range(0, half, COPY):
+            start = pl.multiple_of(block * BLOCK + index % 2 * half + down, COPY)
             copies.append((rows_ref.at[pl.ds(start, COPY), :], out.at[pl.ds(down, COPY), :]))
     copies.append((ids_ref, ids))
     copies = [pltpu.make_async_copy(*ends, sems.at[index]) for index, ends in enumerate(copies)]
     for copy in copies:
         copy.start()
     copies[-1].wait()
-    depth = first_ref.shape[1]
+    depth = outs[1].shape[1]
     edge = jnp.max(ids[pl.ds(plan.edge, 1), :], axis=1, keepdims=True)
-    rest = [jnp.broadcast_to(edge, (1, BLOCK)), jnp.zeros((1, depth - size - BLOCK), jnp.int32)]
-    for block, out in ((plan.first, first_ref), (plan.second, second_ref)):
+    rest = [jnp.broadcast_to(edge, (1, BLOCK)), jnp.zeros((1, depth - 2 * half - BLOCK), jnp.int32)]
+    for block, out in ((plan.first, outs[1]), (plan.second, outs[3])):
         row = jnp.concatenate([ids[pl.ds(block + k, 1), :] for k in range(share)] + rest, axis=1)
-        out[size : size + 8, :] = jnp.broadcast_to(row.astype(jnp.float32), (8, depth)).astype(jnp.bfloat16)
+        out[half : half + 8, :] = jnp.broadcast_to(row.astype(jnp.float32), (8, depth)).astype(jnp.bfloat16)
     for copy in copies[:-1]:
         copy.wait()
 
 
 def pack(size, subs, embeddings, by_block):
     blocks, depth = by_block.shape[0], embeddings.shape[1]
+    halves = [jax.ShapeDtypeStruct((size // 2 + more, depth), jnp.bfloat16) for more in (0, 8)]
     return pl.pallas_call(
         functools.partial(pack_kernel, blocks, subs),
         in_specs=[pl.BlockSpec(memory_space=pl.ANY)] * 2,
-        out_specs=[pl.BlockSpec(memory_space=pltpu.VMEM)] * 2,
-        out_shape=[jax.ShapeDtypeStruct((size + 8, depth), jnp.bfloat16)] * 2,
+        out_specs=[pl.BlockSpec(memory_space=pltpu.VMEM)] * 4,
+        out_shape=halves * 2,
         scratch_shapes=[pltpu.VMEM(by_block.shape, jnp.int32), pltpu.SemaphoreType.DMA((2 * size // COPY + 1,))],
         compiler_params=pltpu.CompilerParams(vmem_limit_bytes=8 * 1024 * 1024),
         cost_estimate=pl.CostEstimate(flops=0, bytes_accessed=1024, transcendentals=0),
@@ -114,32 +117,44 @@
 MEMBER, FIRST_BLOCK, EDGE, INNER = range(4)
 
 
-def self_kernel(blocks, width, meta_ref, rows_ref, piece_ref, tags_ref, unit_ref, sums_ref, piece_unit):
+def self_kernel(blocks, subs, meta_ref, rows_ref, tags_ref, unit_ref, sums_ref, held, sems):
     meta = Meta(meta_ref, blocks)
-    step = pl.program_id(0)
-
-    @pl.when(step == 0)
-    def _():
-        piece_unit[...] = normalised(piece_ref[...])
-
-    unit = normalised(rows_ref[...])
-    unit_ref[pl.ds(pl.multiple_of(step * STEP, STEP), STEP), :] = unit
-    first_col = meta.number(MEMBER) * width
+    width = blocks // subs
+    quarter = width * BLOCK
+    member = meta.number(MEMBER)
+    owners = [lax.rem(member + turn, subs) for turn in range(subs)]
+    spans = [pl.ds(pl.multiple_of(owner * quarter, quarter), quarter) for owner in owners]
+    copies = []
+    for turn, span in enumerate(spans):
+        copies.append(pltpu.make_async_copy(rows_ref.at[span, :], held.at[turn], sems.at[turn]))
+        copies[-1].start()
     column_tags = tags_ref[...].astype(jnp.float32)
-    cosine = products(unit, piece_unit[...])
-    for inner in range(0, STEP, BLOCK):
-        block = step * (STEP // BLOCK) + inner // BLOCK
-        bias = column_bias(meta.tag(block), column_tags)
-        weight = jnp.exp2(cosine[inner : inner + BLOCK] * GAIN + bias)
-        row = lax.broadcasted_iota(jnp.int32, weight.shape, 0)
-        col = lax.broadcasted_iota(jnp.int32, weight.shape, 1)
-        shift = (block - first_col) * BLOCK
-        weight = jnp.where((row < meta.used(block)) & (col - row != shift), weight, 0.0)
-        sums_ref[pl.ds(block, 1), :] = lane_sums(weight)
-
-
-def chunk_tags(piece_ref, size):
-    row = piece_ref[size : size + 8, :].astype(jnp.float32)[0:1, :]
+    for turn in range(subs):
+        copies[turn].wait()
+        unit = normalised(held[turn])
+        unit_ref[spans[turn], :] = unit
+        if turn == 0:
+            share = unit
+        cosine = products(unit, share)
+        for inner in range(width):
+            block = owners[turn] * width + inner
+            bias = column_bias(meta.tag(block), column_tags)
+            weight = jnp.exp2(cosine[inner * BLOCK : (inner + 1) * BLOCK] * GAIN + bias)
+            row = lax.broadcasted_iota(jnp.int32, weight.shape, 0)
+            keep = row < meta.used(block)
+            if turn == 0:
+                keep = keep & (lax.broadcasted_iota(jnp.int32, weight.shape, 1) - row != inner * BLOCK)
+            sums_ref[pl.ds(block, 1), :] = lane_sums(jnp.where(keep, weight, 0.0))
+
+
+def whole_chunk(low_ref, high_ref, piece_unit, at):
+    half = low_ref.shape[0]
+    piece_unit[at : at + half, :] = normalised(low_ref[...])
+    piece_unit[at + half : at + 2 * half, :] = normalised(high_ref[:half, :])
+
+
+def chunk_tags(high_ref, size):
+    row = high_ref[size // 2 : size // 2 + 8, :].astype(jnp.float32)[0:1, :]
     return row[:, :size], row[:, size : size + BLOCK]
 
 
@@ -168,15 +183,15 @@
 
 
 def middle_kernel(
-    blocks, share, meta_ref, unit_ref, swap_ref, outer_ref, before_ref, sums_ref, outer_cols_ref, swap_cols_ref,
-    piece_unit,
+    blocks, share, meta_ref, unit_ref, swap_low_ref, swap_high_ref, outer_low_ref, outer_high_ref, before_ref,
+    sums_ref, outer_cols_ref, swap_cols_ref, piece_unit,
 ):
     meta = Meta(meta_ref, blocks)
     size = share * BLOCK
-    piece_unit[:size, :] = normalised(outer_ref[:size, :])
-    piece_unit[size:, :] = normalised(swap_ref[:size, :])
-    outer_tags, _ = chunk_tags(outer_ref, size)
-    swap_tags, edge = chunk_tags(swap_ref, size)
+    whole_chunk(outer_low_ref, outer_high_ref, piece_unit, 0)
+    whole_chunk(swap_low_ref, swap_high_ref, piece_unit, size)
+    outer_tags, _ = chunk_tags(outer_high_ref, size)
+    swap_tags, edge = chunk_tags(swap_high_ref, size)
 
     def add_rows(block, value):
         sums_ref[block : block + 1, :] = before_ref[block : block + 1, :] + value
@@ -196,13 +211,13 @@
 
 
 def last_kernel(
-    blocks, share, width, meta_ref, unit_ref, piece_ref, before_ref, outer_back_ref, swap_back_ref,
+    blocks, share, width, meta_ref, unit_ref, low_ref, high_ref, before_ref, outer_back_ref,
     keep_ref, send_ref, cols_ref, piece_unit, sums,
 ):
     meta = Meta(meta_ref, blocks)
     size = share * BLOCK
-    piece_unit[...] = normalised(piece_ref[:size, :])
-    tags, _ = chunk_tags(piece_ref, size)
+    whole_chunk(low_ref, high_ref, piece_unit, 0)
+    tags, _ = chunk_tags(high_ref, size)
 
     def place(block):
         owner = block // width
@@ -216,7 +231,7 @@
     for k in range(share):
         cols_ref[k : k + 1, :] = cols[k]
         at = place(meta.number(FIRST_BLOCK) + k)
-        sums[pl.ds(at, 1), :] += outer_back_ref[k : k + 1, :] + swap_back_ref[k : k + 1, :]
+        sums[pl.ds(at, 1), :] += outer_back_ref[k : k + 1, :]
     parity = meta.number(MEMBER) % 2
     heap = blocks // 2
     keep_ref[...] = sums[pl.ds(pl.multiple_of(parity * heap, heap), heap), :]
@@ -297,9 +312,9 @@
         return [(b, a) for a, b in route]
 
     by_block = cluster_ids.reshape(blocks, BLOCK)
-    first_out, second_out = pack(size, subs, embeddings, by_block)
-    from_inner = lax.ppermute(first_out, "tile", swap)
-    from_outer = lax.ppermute(first_out, "tile", inward)
+    *first_out, second_low, second_high = pack(size, subs, embeddings, by_block)
+    from_inner = [lax.ppermute(out, "tile", swap) for out in first_out]
+    from_outer = [lax.ppermute(out, "tile", inward) for out in first_out]
 
     tag = jnp.max(by_block, axis=1)
     used = jnp.sum((by_block >= 0).astype(jnp.int32), axis=1)
@@ -321,29 +336,22 @@
     row_sums = jax.ShapeDtypeStruct((blocks, BLOCK), jnp.float32)
     col_sums = jax.ShapeDtypeStruct((share, BLOCK), jnp.float32)
     quarter = width * BLOCK
+    vmem, smem = pl.BlockSpec(memory_space=pltpu.VMEM), pl.BlockSpec(memory_space=pltpu.SMEM)
     unit, sums = pl.pallas_call(
-        functools.partial(self_kernel, blocks, width),
-        grid_spec=pltpu.PrefetchScalarGridSpec(
-            num_scalar_prefetch=1,
-            grid=(rows // STEP,),
-            in_specs=[
-                pl.BlockSpec((STEP, depth), lambda i, _: (i, 0)),
-                pl.BlockSpec((quarter, depth), lambda i, m: (m[5 * blocks + MEMBER], 0)),
-                pl.BlockSpec((1, quarter), lambda i, _: (0, 0)),
-            ],
-            out_specs=[pl.BlockSpec((rows, depth), lambda i, _: (0, 0)), pl.BlockSpec((blocks, BLOCK), lambda i, _: (0, 0))],
-            scratch_shapes=[pltpu.VMEM((quarter, depth), jnp.bfloat16)],
-        ),
+        functools.partial(self_kernel, blocks, subs),
+        in_specs=[smem, pl.BlockSpec(memory_space=pl.ANY), vmem],
+        out_specs=[vmem, vmem],
         out_shape=[jax.ShapeDtypeStruct((rows, depth), jnp.bfloat16), row_sums],
-        compiler_params=pltpu.CompilerParams(vmem_limit_bytes=32 * 1024 * 1024),
+        scratch_shapes=[pltpu.VMEM((subs, quarter, depth), jnp.bfloat16), pltpu.SemaphoreType.DMA((subs,))],
+        compiler_params=pltpu.CompilerParams(vmem_limit_bytes=24 * 1024 * 1024),
         cost_estimate=pl.CostEstimate(flops=0, bytes_accessed=1024, transcendentals=0),
-    )(meta, embeddings, embeddings, lax.dynamic_slice_in_dim(cluster_ids, member * quarter, quarter, 0)[None])
-    second_out, sums = lax.optimization_barrier((second_out, sums))
-    last = lax.ppermute(second_out, "tile", around)
+    )(meta, embeddings, lax.dynamic_slice_in_dim(cluster_ids, member * quarter, quarter, 0)[None])
+    second_low, second_high, sums = lax.optimization_barrier((second_low, second_high, sums))
+    last = [lax.ppermute(out, "tile", around) for out in (second_low, second_high)]
     sums, outer_cols, swap_cols = call(
         functools.partial(middle_kernel, blocks, share),
         meta,
-        (unit, from_inner, from_outer, sums),
+        (unit, *from_inner, *from_outer, sums),
         [row_sums, jax.ShapeDtypeStruct((share + 1, BLOCK), jnp.float32), col_sums],
         [pltpu.VMEM((2 * size, depth), jnp.bfloat16)],
         4 * rows * size * depth,
@@ -362,16 +370,17 @@
     held, leaving, cols = call(
         functools.partial(last_kernel, blocks, share, width),
         meta,
-        (unit, last, sums, outer_back, swap_back),
+        (unit, *last, sums, outer_back),
         [half, half, col_sums],
         [pltpu.VMEM((size, depth), jnp.bfloat16), pltpu.VMEM((blocks, BLOCK), jnp.float32)],
         2 * rows * size * depth,
     )
 
-    home = lax.ppermute(cols, "tile", turned(around))
+    home = lax.ppermute(cols, "tile", turned(around)) + swap_back
     for k in range(share):
         held = held + jnp.where(home_row == k, home[k : k + 1], 0.0)
     held = held + lax.ppermute(leaving, "sub", [(i, i ^ 1) for i in range(subs)])
+    held, flag = lax.optimization_barrier((held, flag))
     for bit, mine in enumerate(upper, 1):
         pairs = held.reshape(-1, 2, width, BLOCK)
         low, high = pairs[:, 0].reshape(mine.shape), pairs[:, 1].reshape(mine.shape)

time: 43.1 us -> 43.3 us (level)
  starting transfers between devices: 13.1 us -> 17.2 us
  waiting for transfers between devices: 12.7 us -> 9.95 us
  Pallas kernels: 15.2 us -> 13.9 us
    ppermute x4 -> x7, starting transfers between devices: 9.49 us -> 13.7 us  [the longest x2 9.06 us: shards(): from_outer = [lax.ppermute(out, 'tile', inward) for out in first_out]]
    pallas_call x1, Pallas kernels: 7.31 us -> 6.05 us  [shards(): pl.pallas_call(functools.partial(self_kernel, blocks, subs), in_specs=[sm...]
    ppermute x1, waiting for transfers between devices: 4.79 us -> 3.65 us  [shards(): outer_back = lax.ppermute(outer_cols, 'tile', turned(inward))]
    ppermute x4 -> x7, waiting for transfers between devices: 5.8 us -> 4.85 us  [the longest x1 2.43 us: shards(): home = lax.ppermute(cols, 'tile', turned(around)) + swap_back]
    ppermute x1, waiting for transfers between devices: 2.09 us -> 1.44 us  [shards(): lax.ppermute(leaving, 'sub', [(i, i ^ 1 << bit) for i in range(subs)])]
  transfers between devices with their start and end apart: 8 -> 11, of which waited for: 5 -> 4; matrix products, arithmetic and copies ran while one was open for 1% -> 1% of each run, Pallas kernels for 27% -> 29%
where the time goes in v9:
time: 43.3 us; the launch traced here: 43 us
  starting transfers between devices  17.2 us (40%)
  Pallas kernels  13.9 us (32%)
  waiting for transfers between devices  9.95 us (23%)
  between operations  0.93 us (2%)
  local copies, waits for them, and re-layouts  0.82 us (2%)
    ppermute x2, starting transfers between devices, shards(): from_outer = [lax.ppermute(out, 'tile', inward) for out in first_out]  9.06 us
    pallas_call x1, Pallas kernels, shards(): pl.pallas_call(functools.partial(self_kernel, blocks, subs), in_specs=[sm...  6.05 us
    pallas_call x2, Pallas kernels, call(): pl.pallas_call(kernel, in_specs=[smem] + [vmem] * len(operands), out_spec...  5.89 us
    ppermute x1, waiting for transfers between devices, shards(): outer_back = lax.ppermute(outer_cols, 'tile', turned(inward))  3.65 us
    ppermute x1, waiting for transfers between devices, shards(): home = lax.ppermute(cols, 'tile', turned(around)) + swap_back  2.43 us
    ppermute x2, waiting for transfers between devices, shards(): lax.ppermute(out, 'tile', around)  2.41 us
    ppermute x2, starting transfers between devices, shards(): lax.ppermute(out, 'tile', around)  2.11 us
    ppermute x1, starting transfers between devices, shards(): lax.ppermute(leaving, 'sub', [(i, i ^ 1 << bit) for i in range(subs)])  1.55 us
  transfers between devices with their start and end apart: 11, of which 4 were waited for; matrix products, arithmetic and copies ran while one was open for 1% of the time, Pallas kernels for 29%

profile of v9, /device:TPU:0, one launch (start us, length us, event | category | flops | bytes accessed | tf_op | source)
XLA Modules:
  0.0 43.0 jit_solution(3865834473511311515)
XLA Ops:
  0.0 0.0 copy-start.3
  0.0 1.4 %shard_map.31 = (bf16[128,1024]{1,0:T(8,128)(2,1)S(1)}, bf16[136,1024]{1,0:T(8,128)(2,1)S(1)}, bf16[128,1024]{1,0:T(8,128)(2,1)S(1)}, bf16[136,1024]{1,0:T(8,128)(2,1)S(1)}) custom-call(bf16[2048,1024]{1,0:T(8,128)(2,1)} %rows_ref.3, s32[16,128]{1,0:T(8,128)} %bitcast.58), custom_call_target="tpu_custom_call" | custom-call | bytes 1024 | tf_op jit(solution)/shard_map/pallas_call | solution.py:92
  1.4 5.1 %collective-permute-start.4 = (bf16[128,1024]{1,0:T(8,128)(2,1)S(1)}, bf16[128,1024]{1,0:T(8,128)(2,1)S(1)}, u32[]{:S(2)}, u32[]{:S(2)}) collective-permute-start(bf16[128,1024]{1,0:T(8,128)(2,1)S(1)} %get-tuple-element.63), channel_id=1, source_target_pairs={{0,4},{12,8},{1,5},{13,9},{2,6},{14,10},{3,7},{15,11},{16,20},{28,... | collective-permute-start | bytes 786440 | tf_op jit(solution)/shard_map/ppermute | solution.py:317
  6.5 0.7 %collective-permute-start.2 = (bf16[128,1024]{1,0:T(8,128)(2,1)S(1)}, bf16[128,1024]{1,0:T(8,128)(2,1)S(1)}, u32[]{:S(2)}, u32[]{:S(2)}) collective-permute-start(bf16[128,1024]{1,0:T(8,128)(2,1)S(1)} %get-tuple-element.63), channel_id=1, source_target_pairs={{4,8},{8,4},{5,9},{9,5},{6,10},{10,6},{7,11},{11,7},{20,24},{24,20... | collective-permute-start | bytes 786440 | tf_op jit(solution)/shard_map/ppermute | solution.py:316
  7.2 3.9 %collective-permute-start.5 = (bf16[136,1024]{1,0:T(8,128)(2,1)S(1)}, bf16[136,1024]{1,0:T(8,128)(2,1)S(1)}, u32[]{:S(2)}, u32[]{:S(2)}) collective-permute-start(bf16[136,1024]{1,0:T(8,128)(2,1)S(1)} %get-tuple-element.64), channel_id=1, source_target_pairs={{0,4},{12,8},{1,5},{13,9},{2,6},{14,10},{3,7},{15,11},{16,20},{28,... | collective-permute-start | bytes 835592 | tf_op jit(solution)/shard_map/ppermute | solution.py:317
  11.1 0.7 %collective-permute-start.3 = (bf16[136,1024]{1,0:T(8,128)(2,1)S(1)}, bf16[136,1024]{1,0:T(8,128)(2,1)S(1)}, u32[]{:S(2)}, u32[]{:S(2)}) collective-permute-start(bf16[136,1024]{1,0:T(8,128)(2,1)S(1)} %get-tuple-element.64), channel_id=1, source_target_pairs={{4,8},{8,4},{5,9},{9,5},{6,10},{10,6},{7,11},{11,7},{20,24},{24,20... | collective-permute-start | bytes 835592 | tf_op jit(solution)/shard_map/ppermute | solution.py:316
  11.8 0.0 copy-done.3
  11.8 0.1 convert_reduce_fusion
  12.1 0.1 dynamic_slice.47
  12.2 0.1 concatenate.3.meta_ref
  12.3 0.1 broadcast_in_dim.128
  12.3 6.1 %shard_map.30 = (bf16[2048,1024]{1,0:T(8,128)(2,1)S(1)}, f32[16,128]{1,0:T(8,128)S(1)}) custom-call(s32[84]{0:T(128)S(1)} %concatenate.3.meta_ref, bf16[2048,1024]{1,0:T(8,128)(2,1)} %rows_ref.3, s32[1,512]{1,0:T(1,128)S(1)} %bitcast.57), custom_call_target="tpu_custom_call" | custom-call | bytes 1024 | tf_op jit(solution)/shard_map/pallas_call | solution.py:340
  18.4 1.3 %collective-permute-start.1 = (bf16[136,1024]{1,0:T(8,128)(2,1)S(1)}, bf16[136,1024]{1,0:T(8,128)(2,1)S(1)}, u32[]{:S(2)}, u32[]{:S(2)}) collective-permute-start(bf16[136,1024]{1,0:T(8,128)(2,1)S(1)} %get-tuple-element.62), channel_id=1, source_target_pairs={{0,4},{12,8},{4,12},{8,0},{1,5},{13,9},{5,13},{9,1},{2,6},{14,10},... | collective-permute-start | bytes 835592 | tf_op jit(solution)/shard_map/ppermute | solution.py:350
  19.7 0.0 collective-permute-done.4.outer_low_ref
  19.7 0.9 %collective-permute-start = (bf16[128,1024]{1,0:T(8,128)(2,1)S(1)}, bf16[128,1024]{1,0:T(8,128)(2,1)S(1)}, u32[]{:S(2)}, u32[]{:S(2)}) collective-permute-start(bf16[128,1024]{1,0:T(8,128)(2,1)S(1)} %get-tuple-element.61), channel_id=1, source_target_pairs={{0,4},{12,8},{4,12},{8,0},{1,5},{13,9},{5,13},{9,1},{2,6},{14,10},... | collective-permute-start | bytes 786440 | tf_op jit(solution)/shard_map/ppermute | solution.py:350
  20.5 0.0 collective-permute-done.2.swap_low_ref
  20.5 0.0 collective-permute-done.5.outer_high_ref
  20.5 0.0 collective-permute-done.3.swap_high_ref
  20.5 3.6 %shard_map.32 = (f32[16,128]{1,0:T(8,128)S(1)}, f32[3,128]{1,0:T(4,128)S(1)}, f32[2,128]{1,0:T(2,128)S(1)}) custom-call(s32[84]{0:T(128)S(1)} %concatenate.3.meta_ref, bf16[2048,1024]{1,0:T(8,128)(2,1)S(1)} %get-tuple-element.57.unit_ref, bf16[128,1024]{1,0:T(8,128)(2,1)S(1)} %collective-permute-done.2.swap_low_ref, ...), custom_call_target="tpu_custom_call" | custom-call | flops 2147483648 | bytes 1024 | tf_op jit(solution)/shard_map/pallas_call | solution.py:243
  24.2 1.3 %collective-permute-start.6 = (f32[3,128]{1,0:T(4,128)S(1)}, f32[3,128]{1,0:T(4,128)S(1)}, u32[]{:S(2)}, u32[]{:S(2)}) collective-permute-start(f32[3,128]{1,0:T(4,128)S(1)} %get-tuple-element.67.outer_cols_ref), channel_id=1, source_target_pairs={{4,0},{8,12},{5,1},{9,13},{6,2},{10,14},{7,3},{11,15},{20,16},{24,... | collective-permute-start | bytes 4616 | tf_op jit(solution)/shard_map/ppermute | solution.py:359
  25.5 0.7 %collective-permute-start.8 = (f32[2,128]{1,0:T(2,128)S(1)}, f32[2,128]{1,0:T(2,128)S(1)}, u32[]{:S(2)}, u32[]{:S(2)}) collective-permute-start(f32[2,128]{1,0:T(2,128)S(1)} %get-tuple-element.72), channel_id=1, source_target_pairs={{8,4},{4,8},{9,5},{5,9},{10,6},{6,10},{11,7},{7,11},{24,20},{20,24... | collective-permute-start | bytes 3080 | tf_op jit(solution)/shard_map/ppermute | solution.py:360
  26.1 3.7 %collective-permute-done.6.outer_back_ref = f32[3,128]{1,0:T(4,128)S(1)} collective-permute-done((f32[3,128]{1,0:T(4,128)S(1)}, f32[3,128]{1,0:T(4,128)S(1)}, u32[]{:S(2)}, u32[]{:S(2)}) %collective-permute-start.6) | collective-permute-done | bytes 1568 | tf_op jit(solution)/shard_map/ppermute | solution.py:359
  29.8 0.6 %shard_map.33 = s32[1]{0:T(128)} custom-call(f32[3,128]{1,0:T(4,128)S(1)} %get-tuple-element.67.outer_cols_ref, f32[3,128]{1,0:T(4,128)S(1)} %collective-permute-done.6.outer_back_ref), custom_call_target="tpu_custom_call" | custom-call | tf_op jit(solution)/shard_map/pallas_call | solution.py:362
  30.4 2.4 %collective-permute-done.low_ref = bf16[128,1024]{1,0:T(8,128)(2,1)S(1)} collective-permute-done((bf16[128,1024]{1,0:T(8,128)(2,1)S(1)}, bf16[128,1024]{1,0:T(8,128)(2,1)S(1)}, u32[]{:S(2)}, u32[]{:S(2)}) %collective-permute-start) | collective-permute-done | bytes 262176 | tf_op jit(solution)/shard_map/ppermute | solution.py:350
  32.8 0.0 collective-permute-done.1.high_ref
  32.8 2.3 %shard_map.34 = (f32[8,128]{1,0:T(8,128)S(1)}, f32[8,128]{1,0:T(8,128)S(1)}, f32[2,128]{1,0:T(2,128)S(1)}) custom-call(s32[84]{0:T(128)S(1)} %concatenate.3.meta_ref, bf16[2048,1024]{1,0:T(8,128)(2,1)S(1)} %get-tuple-element.57.unit_ref, bf16[128,1024]{1,0:T(8,128)(2,1)S(1)} %collective-permute-done.low_ref, ...), custom_call_target="tpu_custom_call" | custom-call | flops 1073741824 | bytes 1024 | tf_op jit(solution)/shard_map/pallas_call | solution.py:243
  35.1 1.2 %collective-permute-start.7 = (f32[2,128]{1,0:T(2,128)S(1)}, f32[2,128]{1,0:T(2,128)S(1)}, u32[]{:S(2)}, u32[]{:S(2)}) collective-permute-start(f32[2,128]{1,0:T(2,128)S(1)} %get-tuple-element.71), channel_id=1, source_target_pairs={{4,0},{8,12},{12,4},{0,8},{5,1},{9,13},{13,5},{1,9},{6,2},{10,14},... | collective-permute-start | bytes 3080 | tf_op jit(solution)/shard_map/ppermute | solution.py:379
  36.3 0.0 collective-permute-start.9
  36.3 0.0 collective-permute-done.8
  36.3 2.4 %collective-permute-done.7 = f32[2,128]{1,0:T(2,128)S(1)} collective-permute-done((f32[2,128]{1,0:T(2,128)S(1)}, f32[2,128]{1,0:T(2,128)S(1)}, u32[]{:S(2)}, u32[]{:S(2)}) %collective-permute-start.7) | collective-permute-done | bytes 1056 | tf_op jit(solution)/shard_map/ppermute | solution.py:379
  38.7 0.0 collective-permute-done.9
  38.8 1.6 %collective-permute-start.10 = (f32[4,128]{1,0:T(4,128)S(1)}, f32[4,128]{1,0:T(4,128)S(1)}, u32[]{:S(2)}, u32[]{:S(2)}) collective-permute-start(f32[4,128]{1,0:T(4,128)S(1)} %get-tuple-element.81), channel_id=1, source_target_pairs={{0,2},{1,3},{2,0},{3,1},{4,6},{5,7},{6,4},{7,5},{8,10},{9,11},{10,... | collective-permute-start | bytes 6152 | tf_op jit(solution)/shard_map/ppermute | solution.py:389
  41.0 1.4 %collective-permute-done.10 = f32[4,128]{1,0:T(4,128)S(1)} collective-permute-done((f32[4,128]{1,0:T(4,128)S(1)}, f32[4,128]{1,0:T(4,128)S(1)}, u32[]{:S(2)}, u32[]{:S(2)}) %collective-permute-start.10) | collective-permute-done | bytes 2080 | tf_op jit(solution)/shard_map/ppermute | solution.py:389
  42.4 0.0 copy-start.4
  42.4 0.6 %copy-done.4 = f32[512]{0:T(512)} copy-done((f32[512]{0:T(512)}, f32[512]{0:T(512)S(1)}, u32[]{:S(2)}) %copy-start.4) | copy-done | bytes 2072
  (10 shorter events, 0.1 us)
Async XLA Ops:
  0.0 11.8 %copy-start.3 = (s32[2048]{0:T(1024)S(1)}, s32[2048]{0:T(1024)}, u32[]{:S(2)}) copy-start(s32[2048]{0:T(1024)} %param.5) | copy-start | bytes 24580
  1.4 18.3 %collective-permute-start.4 = (bf16[128,1024]{1,0:T(8,128)(2,1)S(1)}, bf16[128,1024]{1,0:T(8,128)(2,1)S(1)}, u32[]{:S(2)}, u32[]{:S(2)}) collective-permute-start(bf16[128,1024]{1,0:T(8,128)(2,1)S(1)} %get-tuple-element.63), channel_id=1, source_target_pairs={{0,4},{12,8},{1,5},{13,9},{2,6},{14,10},{3,7},{15,11},{16,20},{28,... | collective-permute-start | bytes 786440 | tf_op jit(solution)/shard_map/ppermute | solution.py:317
  6.5 14.0 %collective-permute-start.2 = (bf16[128,1024]{1,0:T(8,128)(2,1)S(1)}, bf16[128,1024]{1,0:T(8,128)(2,1)S(1)}, u32[]{:S(2)}, u32[]{:S(2)}) collective-permute-start(bf16[128,1024]{1,0:T(8,128)(2,1)S(1)} %get-tuple-element.63), channel_id=1, source_target_pairs={{4,8},{8,4},{5,9},{9,5},{6,10},{10,6},{7,11},{11,7},{20,24},{24,20... | collective-permute-start | bytes 786440 | tf_op jit(solution)/shard_map/ppermute | solution.py:316
  7.2 13.3 %collective-permute-start.5 = (bf16[136,1024]{1,0:T(8,128)(2,1)S(1)}, bf16[136,1024]{1,0:T(8,128)(2,1)S(1)}, u32[]{:S(2)}, u32[]{:S(2)}) collective-permute-start(bf16[136,1024]{1,0:T(8,128)(2,1)S(1)} %get-tuple-element.64), channel_id=1, source_target_pairs={{0,4},{12,8},{1,5},{13,9},{2,6},{14,10},{3,7},{15,11},{16,20},{28,... | collective-permute-start | bytes 835592 | tf_op jit(solution)/shard_map/ppermute | solution.py:317
  11.1 9.4 %collective-permute-start.3 = (bf16[136,1024]{1,0:T(8,128)(2,1)S(1)}, bf16[136,1024]{1,0:T(8,128)(2,1)S(1)}, u32[]{:S(2)}, u32[]{:S(2)}) collective-permute-start(bf16[136,1024]{1,0:T(8,128)(2,1)S(1)} %get-tuple-element.64), channel_id=1, source_target_pairs={{4,8},{8,4},{5,9},{9,5},{6,10},{10,6},{7,11},{11,7},{20,24},{24,20... | collective-permute-start | bytes 835592 | tf_op jit(solution)/shard_map/ppermute | solution.py:316
  18.4 14.4 %collective-permute-start.1 = (bf16[136,1024]{1,0:T(8,128)(2,1)S(1)}, bf16[136,1024]{1,0:T(8,128)(2,1)S(1)}, u32[]{:S(2)}, u32[]{:S(2)}) collective-permute-start(bf16[136,1024]{1,0:T(8,128)(2,1)S(1)} %get-tuple-element.62), channel_id=1, source_target_pairs={{0,4},{12,8},{4,12},{8,0},{1,5},{13,9},{5,13},{9,1},{2,6},{14,10},... | collective-permute-start | bytes 835592 | tf_op jit(solution)/shard_map/ppermute | solution.py:350
  19.7 13.2 %collective-permute-start = (bf16[128,1024]{1,0:T(8,128)(2,1)S(1)}, bf16[128,1024]{1,0:T(8,128)(2,1)S(1)}, u32[]{:S(2)}, u32[]{:S(2)}) collective-permute-start(bf16[128,1024]{1,0:T(8,128)(2,1)S(1)} %get-tuple-element.61), channel_id=1, source_target_pairs={{0,4},{12,8},{4,12},{8,0},{1,5},{13,9},{5,13},{9,1},{2,6},{14,10},... | collective-permute-start | bytes 786440 | tf_op jit(solution)/shard_map/ppermute | solution.py:350
  24.2 5.6 %collective-permute-start.6 = (f32[3,128]{1,0:T(4,128)S(1)}, f32[3,128]{1,0:T(4,128)S(1)}, u32[]{:S(2)}, u32[]{:S(2)}) collective-permute-start(f32[3,128]{1,0:T(4,128)S(1)} %get-tuple-element.67.outer_cols_ref), channel_id=1, source_target_pairs={{4,0},{8,12},{5,1},{9,13},{6,2},{10,14},{7,3},{11,15},{20,16},{24,... | collective-permute-start | bytes 4616 | tf_op jit(solution)/shard_map/ppermute | solution.py:359
  25.5 10.8 %collective-permute-start.8 = (f32[2,128]{1,0:T(2,128)S(1)}, f32[2,128]{1,0:T(2,128)S(1)}, u32[]{:S(2)}, u32[]{:S(2)}) collective-permute-start(f32[2,128]{1,0:T(2,128)S(1)} %get-tuple-element.72), channel_id=1, source_target_pairs={{8,4},{4,8},{9,5},{5,9},{10,6},{6,10},{11,7},{7,11},{24,20},{20,24... | collective-permute-start | bytes 3080 | tf_op jit(solution)/shard_map/ppermute | solution.py:360
  35.1 3.6 %collective-permute-start.7 = (f32[2,128]{1,0:T(2,128)S(1)}, f32[2,128]{1,0:T(2,128)S(1)}, u32[]{:S(2)}, u32[]{:S(2)}) collective-permute-start(f32[2,128]{1,0:T(2,128)S(1)} %get-tuple-element.71), channel_id=1, source_target_pairs={{4,0},{8,12},{12,4},{0,8},{5,1},{9,13},{13,5},{1,9},{6,2},{10,14},... | collective-permute-start | bytes 3080 | tf_op jit(solution)/shard_map/ppermute | solution.py:379
  36.3 2.5 %collective-permute-start.9 = (f32[8,128]{1,0:T(8,128)S(1)}, f32[8,128]{1,0:T(8,128)S(1)}, u32[]{:S(2)}, u32[]{:S(2)}) collective-permute-start(f32[8,128]{1,0:T(8,128)S(1)} %get-tuple-element.73), channel_id=1, source_target_pairs={{0,1},{1,0},{2,3},{3,2},{4,5},{5,4},{6,7},{7,6},{8,9},{9,8},{10,11... | collective-permute-start | bytes 12296 | tf_op jit(solution)/shard_map/ppermute | solution.py:382
  38.8 3.7 %collective-permute-start.10 = (f32[4,128]{1,0:T(4,128)S(1)}, f32[4,128]{1,0:T(4,128)S(1)}, u32[]{:S(2)}, u32[]{:S(2)}) collective-permute-start(f32[4,128]{1,0:T(4,128)S(1)} %get-tuple-element.81), channel_id=1, source_target_pairs={{0,2},{1,3},{2,0},{3,1},{4,6},{5,7},{6,4},{7,5},{8,10},{9,11},{10,... | collective-permute-start | bytes 6152 | tf_op jit(solution)/shard_map/ppermute | solution.py:389
  42.4 0.6 %copy-start.4 = (f32[512]{0:T(512)}, f32[512]{0:T(512)S(1)}, u32[]{:S(2)}) copy-start(f32[512]{0:T(512)S(1)} %get-tuple-element.120) | copy-start | bytes 6148

commit v10 on v9

--- a/solution.py
+++ b/solution.py
@@ -62,38 +62,75 @@
 
 
 def pack_kernel(blocks, subs, rows_ref, ids_ref, *refs):
-    outs, (ids, sems) = refs[:4], refs[4:]
+    outs, (ids, sems) = refs[:5], refs[5:]
     plan = Plan(blocks, subs, lax.axis_index("tile"), lax.axis_index("sub"))
-    share, half = plan.share, plan.share * BLOCK // 2
-    copies = []
-    for index, out in enumerate(outs):
-        block = plan.first if index < 2 else plan.second
-        for down in range(0, half, COPY):
-            start = pl.multiple_of(block * BLOCK + index % 2 * half + down, COPY)
-            copies.append((rows_ref.at[pl.ds(start, COPY), :], out.at[pl.ds(down, COPY), :]))
-    copies.append((ids_ref, ids))
-    copies = [pltpu.make_async_copy(*ends, sems.at[index]) for index, ends in enumerate(copies)]
-    for copy in copies:
+    share, size = plan.share, plan.share * BLOCK
+    first_low, first_high, swapped, second_low, second_high = outs
+    ids_copy = pltpu.make_async_copy(ids_ref, ids, sems.at[0])
+    ids_copy.start()
+
+    def copies(block, parts, sem):
+        made, down = [], 0
+        for part, count in parts:
+            for at in range(0, count, COPY):
+                start = pl.multiple_of(block * BLOCK + down, COPY)
+                made.append(
+                    pltpu.make_async_copy(
+                        rows_ref.at[pl.ds(start, COPY), :], part.at[pl.ds(at, COPY), :], sems.at[sem + len(made)]
+                    )
+                )
+                down += COPY
+        return made
+
+    count = size // COPY
+    first = copies(plan.first, ((first_low, size // 2), (first_high, size // 2)), 1)
+    swap = copies(plan.first, ((swapped, size),), 1)
+    second = copies(plan.second, ((second_low, size // 2), (second_high, size // 2)), 1 + count)
+
+    @pl.when(plan.inner)
+    def _():
+        for copy in swap:
+            copy.start()
+
+    @pl.when(jnp.logical_not(plan.inner))
+    def _():
+        for copy in first:
+            copy.start()
+
+    for copy in second:
         copy.start()
-    copies[-1].wait()
-    depth = outs[1].shape[1]
+    ids_copy.wait()
+    depth = swapped.shape[1]
     edge = jnp.max(ids[pl.ds(plan.edge, 1), :], axis=1, keepdims=True)
-    rest = [jnp.broadcast_to(edge, (1, BLOCK)), jnp.zeros((1, depth - 2 * half - BLOCK), jnp.int32)]
-    for block, out in ((plan.first, outs[1]), (plan.second, outs[3])):
+    rest = [jnp.broadcast_to(edge, (1, BLOCK)), jnp.zeros((1, depth - size - BLOCK), jnp.int32)]
+    for block, parts in ((plan.first, (first_high, swapped)), (plan.second, (second_high,))):
         row = jnp.concatenate([ids[pl.ds(block + k, 1), :] for k in range(share)] + rest, axis=1)
-        out[half : half + 8, :] = jnp.broadcast_to(row.astype(jnp.float32), (8, depth)).astype(jnp.bfloat16)
-    for copy in copies[:-1]:
+        row = jnp.broadcast_to(row.astype(jnp.float32), (8, depth)).astype(jnp.bfloat16)
+        for part in parts:
+            part[part.shape[0] - 8 :, :] = row
+
+    @pl.when(plan.inner)
+    def _():
+        for copy in swap:
+            copy.wait()
+
+    @pl.when(jnp.logical_not(plan.inner))
+    def _():
+        for copy in first:
+            copy.wait()
+
+    for copy in second:
         copy.wait()
 
 
 def pack(size, subs, embeddings, by_block):
-    blocks, depth = by_block.shape[0], embeddings.shape[1]
-    halves = [jax.ShapeDtypeStruct((size // 2 + more, depth), jnp.bfloat16) for more in (0, 8)]
+    depth = embeddings.shape[1]
+    parts = (size // 2, size // 2 + 8, size + 8, size // 2, size // 2 + 8)
     return pl.pallas_call(
-        functools.partial(pack_kernel, blocks, subs),
+        functools.partial(pack_kernel, by_block.shape[0], subs),
         in_specs=[pl.BlockSpec(memory_space=pl.ANY)] * 2,
-        out_specs=[pl.BlockSpec(memory_space=pltpu.VMEM)] * 4,
-        out_shape=halves * 2,
+        out_specs=[pl.BlockSpec(memory_space=pltpu.VMEM)] * 5,
+        out_shape=[jax.ShapeDtypeStruct((count, depth), jnp.bfloat16) for count in parts],
         scratch_shapes=[pltpu.VMEM(by_block.shape, jnp.int32), pltpu.SemaphoreType.DMA((2 * size // COPY + 1,))],
         compiler_params=pltpu.CompilerParams(vmem_limit_bytes=8 * 1024 * 1024),
         cost_estimate=pl.CostEstimate(flops=0, bytes_accessed=1024, transcendentals=0),
@@ -147,26 +184,25 @@
             sums_ref[pl.ds(block, 1), :] = lane_sums(jnp.where(keep, weight, 0.0))
 
 
-def whole_chunk(low_ref, high_ref, piece_unit, at):
-    half = low_ref.shape[0]
-    piece_unit[at : at + half, :] = normalised(low_ref[...])
-    piece_unit[at + half : at + 2 * half, :] = normalised(high_ref[:half, :])
-
-
-def chunk_tags(high_ref, size):
-    row = high_ref[size // 2 : size // 2 + 8, :].astype(jnp.float32)[0:1, :]
+def unit_chunk(parts, piece_unit):
+    size = piece_unit.shape[0]
+    down = 0
+    for part in parts:
+        count = part.shape[0] // 16 * 16
+        piece_unit[down : down + count, :] = normalised(part[:count, :])
+        down += count
+    row = parts[-1][count : count + 8, :].astype(jnp.float32)[0:1, :]
     return row[:, :size], row[:, size : size + BLOCK]
 
 
-def cross_terms(meta, chunks, column_tags, unit_ref, piece_unit, add_rows):
-    size = column_tags[0].shape[1]
+def cross_terms(meta, chunk, column_tags, unit_ref, piece_unit, add_rows):
+    size = column_tags.shape[1]
     columns = None
     for start in range(0, meta.blocks * BLOCK, STEP):
         cosine = products(unit_ref[start : start + STEP, :], piece_unit[...])
         for inner in range(0, STEP, BLOCK):
             block = (start + inner) // BLOCK
-            bias = [column_bias(meta.tag(block, chunk), tags) for chunk, tags in zip(chunks, column_tags)]
-            bias = jnp.concatenate(bias, axis=1) if len(bias) > 1 else bias[0]
+            bias = column_bias(meta.tag(block, chunk), column_tags)
             weight = jnp.exp2(cosine[inner : inner + BLOCK] * GAIN + bias)
             row = lax.broadcasted_iota(jnp.int32, weight.shape, 0)
             weight = jnp.where(row < meta.used(block), weight, 0.0)
@@ -176,48 +212,31 @@
                 partial = partial + weight[down : down + 8]
             columns = partial if columns is None else columns + partial
     total = jnp.sum(columns, axis=0, keepdims=True)
-    return [
-        [total[:, at + down : at + down + BLOCK] for down in range(0, size, BLOCK)]
-        for at in range(0, total.shape[1], size)
-    ]
-
-
-def middle_kernel(
-    blocks, share, meta_ref, unit_ref, swap_low_ref, swap_high_ref, outer_low_ref, outer_high_ref, before_ref,
-    sums_ref, outer_cols_ref, swap_cols_ref, piece_unit,
-):
+    return [total[:, at : at + BLOCK] for at in range(0, size, BLOCK)]
+
+
+def middle_kernel(blocks, share, chunk, meta_ref, unit_ref, *refs):
+    *parts, before_ref, sums_ref, cols_ref, piece_unit = refs
     meta = Meta(meta_ref, blocks)
-    size = share * BLOCK
-    whole_chunk(outer_low_ref, outer_high_ref, piece_unit, 0)
-    whole_chunk(swap_low_ref, swap_high_ref, piece_unit, size)
-    outer_tags, _ = chunk_tags(outer_high_ref, size)
-    swap_tags, edge = chunk_tags(swap_high_ref, size)
+    tags, edge = unit_chunk(parts, piece_unit)
 
     def add_rows(block, value):
         sums_ref[block : block + 1, :] = before_ref[block : block + 1, :] + value
 
-    outer, swap = cross_terms(meta, (0, 1), (outer_tags, swap_tags), unit_ref, piece_unit, add_rows)
+    cols = cross_terms(meta, chunk, tags, unit_ref, piece_unit, add_rows)
     for k in range(share):
-        outer_cols_ref[k : k + 1, :] = outer[k]
-        swap_cols_ref[k : k + 1, :] = swap[k]
+        cols_ref[k : k + 1, :] = cols[k]
     mine = meta.tag(meta.number(EDGE)).astype(jnp.float32)
     joined = (edge == mine) & (edge >= 0) & (meta.number(INNER) > 0)
-    outer_cols_ref[share : share + 1, :] = jnp.where(joined, 1.0, 0.0)
-
-
-def flag_kernel(share, outer_cols_ref, outer_back_ref, flag_ref):
-    flags = jnp.maximum(outer_cols_ref[share : share + 1, :], outer_back_ref[share : share + 1, :])
-    flag_ref[0] = jnp.max(flags).astype(jnp.int32)
+    cols_ref[share : share + 1, :] = jnp.where(joined, 1.0, 0.0)
 
 
 def last_kernel(
-    blocks, share, width, meta_ref, unit_ref, low_ref, high_ref, before_ref, outer_back_ref,
+    blocks, share, width, meta_ref, unit_ref, low_ref, high_ref, before_ref, outer_back_ref, swap_cols_ref,
     keep_ref, send_ref, cols_ref, piece_unit, sums,
 ):
     meta = Meta(meta_ref, blocks)
-    size = share * BLOCK
-    whole_chunk(low_ref, high_ref, piece_unit, 0)
-    tags, _ = chunk_tags(high_ref, size)
+    tags, _ = unit_chunk((low_ref, high_ref), piece_unit)
 
     def place(block):
         owner = block // width
@@ -227,15 +246,21 @@
         at = place(block)
         sums[at : at + 1, :] = before_ref[block : block + 1, :] + value
 
-    (cols,) = cross_terms(meta, (2,), (tags,), unit_ref, piece_unit, add_rows)
+    cols = cross_terms(meta, 2, tags, unit_ref, piece_unit, add_rows)
     for k in range(share):
         cols_ref[k : k + 1, :] = cols[k]
         at = place(meta.number(FIRST_BLOCK) + k)
         sums[pl.ds(at, 1), :] += outer_back_ref[k : k + 1, :]
+    cols_ref[share : share + 1, :] = swap_cols_ref[share : share + 1, :]
     parity = meta.number(MEMBER) % 2
     heap = blocks // 2
     keep_ref[...] = sums[pl.ds(pl.multiple_of(parity * heap, heap), heap), :]
     send_ref[...] = sums[pl.ds(pl.multiple_of((1 - parity) * heap, heap), heap), :]
+
+
+def flag_kernel(share, here_ref, home_ref, flag_ref):
+    flags = jnp.maximum(here_ref[share : share + 1, :], home_ref[share : share + 1, :])
+    flag_ref[0] = jnp.max(flags).astype(jnp.int32)
 
 
 def call(kernel, meta, operands, out_shapes, scratch, flops):
@@ -312,9 +337,9 @@
         return [(b, a) for a, b in route]
 
     by_block = cluster_ids.reshape(blocks, BLOCK)
-    *first_out, second_low, second_high = pack(size, subs, embeddings, by_block)
-    from_inner = [lax.ppermute(out, "tile", swap) for out in first_out]
-    from_outer = [lax.ppermute(out, "tile", inward) for out in first_out]
+    first_low, first_high, swapped, second_low, second_high = pack(size, subs, embeddings, by_block)
+    from_inner = lax.ppermute(swapped, "tile", swap)
+    from_outer = [lax.ppermute(out, "tile", inward) for out in (first_high, first_low)][::-1]
 
     tag = jnp.max(by_block, axis=1)
     used = jnp.sum((by_block >= 0).astype(jnp.int32), axis=1)
@@ -334,7 +359,7 @@
     meta, home_row, *upper = lax.optimization_barrier((meta, home_row, *upper))
 
     row_sums = jax.ShapeDtypeStruct((blocks, BLOCK), jnp.float32)
-    col_sums = jax.ShapeDtypeStruct((share, BLOCK), jnp.float32)
+    col_sums = jax.ShapeDtypeStruct((share + 1, BLOCK), jnp.float32)
     quarter = width * BLOCK
     vmem, smem = pl.BlockSpec(memory_space=pltpu.VMEM), pl.BlockSpec(memory_space=pltpu.SMEM)
     unit, sums = pl.pallas_call(
@@ -348,39 +373,36 @@
     )(meta, embeddings, lax.dynamic_slice_in_dim(cluster_ids, member * quarter, quarter, 0)[None])
     second_low, second_high, sums = lax.optimization_barrier((second_low, second_high, sums))
     last = [lax.ppermute(out, "tile", around) for out in (second_low, second_high)]
-    sums, outer_cols, swap_cols = call(
-        functools.partial(middle_kernel, blocks, share),
-        meta,
-        (unit, *from_inner, *from_outer, sums),
-        [row_sums, jax.ShapeDtypeStruct((share + 1, BLOCK), jnp.float32), col_sums],
-        [pltpu.VMEM((2 * size, depth), jnp.bfloat16)],
-        4 * rows * size * depth,
-    )
+
+    def middle(chunk, parts, before):
+        return call(
+            functools.partial(middle_kernel, blocks, share, chunk),
+            meta,
+            (unit, *parts, before),
+            [row_sums, col_sums],
+            [pltpu.VMEM((size, depth), jnp.bfloat16)],
+            2 * rows * size * depth,
+        )
+
+    sums, outer_cols = middle(0, from_outer, sums)
     outer_back = lax.ppermute(outer_cols, "tile", turned(inward))
+    sums, swap_cols = middle(1, (from_inner,), sums)
     swap_back = lax.ppermute(swap_cols, "tile", turned(swap))
-
-    flag = pl.pallas_call(
-        functools.partial(flag_kernel, share),
-        out_specs=pl.BlockSpec(memory_space=pltpu.SMEM),
-        out_shape=jax.ShapeDtypeStruct((1,), jnp.int32),
-        compiler_params=pltpu.CompilerParams(vmem_limit_bytes=4 * 1024 * 1024),
-    )(outer_cols, outer_back)
-    sums, flag = lax.optimization_barrier((sums, flag))
     half = jax.ShapeDtypeStruct((heap, BLOCK), jnp.float32)
     held, leaving, cols = call(
         functools.partial(last_kernel, blocks, share, width),
         meta,
-        (unit, *last, sums, outer_back),
+        (unit, *last, sums, outer_back, swap_cols),
         [half, half, col_sums],
         [pltpu.VMEM((size, depth), jnp.bfloat16), pltpu.VMEM((blocks, BLOCK), jnp.float32)],
         2 * rows * size * depth,
     )
 
-    home = lax.ppermute(cols, "tile", turned(around)) + swap_back
+    home = lax.ppermute(cols, "tile", turned(around))
     for k in range(share):
-        held = held + jnp.where(home_row == k, home[k : k + 1], 0.0)
+        held = held + jnp.where(home_row == k, home[k : k + 1] + swap_back[k : k + 1], 0.0)
     held = held + lax.ppermute(leaving, "sub", [(i, i ^ 1) for i in range(subs)])
-    held, flag = lax.optimization_barrier((held, flag))
+    home, held = lax.optimization_barrier((home, held))
     for bit, mine in enumerate(upper, 1):
         pairs = held.reshape(-1, 2, width, BLOCK)
         low, high = pairs[:, 0].reshape(mine.shape), pairs[:, 1].reshape(mine.shape)
@@ -389,6 +411,12 @@
         held = held + lax.ppermute(leaving, "sub", [(i, i ^ (1 << bit)) for i in range(subs)])
     scores = jnp.log(1.0 + held.reshape(-1))
 
+    flag = pl.pallas_call(
+        functools.partial(flag_kernel, share),
+        out_specs=pl.BlockSpec(memory_space=pltpu.SMEM),
+        out_shape=jax.ShapeDtypeStruct((1,), jnp.int32),
+        compiler_params=pltpu.CompilerParams(vmem_limit_bytes=4 * 1024 * 1024),
+    )(swap_cols, home)
     bad = flag[0] > 0
     if tiles > QUAD:
         bad = lax.pmax(bad.astype(jnp.int32), "tile") > 0

time: 43.3 us -> 44.4 us (1.025)
  waiting for transfers between devices: 9.95 us -> 13.8 us
  starting transfers between devices: 17.2 us -> 13.7 us
  Pallas kernels: 13.9 us -> 14.8 us
    ppermute x2, waiting for transfers between devices: 2.41 us -> 8.7 us  [shards(): lax.ppermute(out, 'tile', around)]
    ppermute x5 -> x4, starting transfers between devices: 11.6 us -> 7 us  [the longest x2 6.25 us: shards(): lax.ppermute(out, 'tile', inward)]
    ppermute x1, waiting for transfers between devices: 3.65 us -> 0.01 us  [shards(): outer_back = lax.ppermute(outer_cols, 'tile', turned(inward))]
    ppermute x5 -> x4, waiting for transfers between devices: 2.44 us -> 4.27 us  [the longest x1 3.48 us: shards(): home = lax.ppermute(cols, 'tile', turned(around))]
    ppermute x2, starting transfers between devices: 2.11 us -> 3.1 us  [shards(): lax.ppermute(out, 'tile', around)]
    pallas_call x2 -> x3, Pallas kernels: 5.89 us -> 6.77 us  [call(): pl.pallas_call(kernel, in_specs=[smem] + [vmem] * len(operands), out_spec...]
    ppermute x1, waiting for transfers between devices: 1.44 us -> 0.81 us  [shards(): lax.ppermute(leaving, 'sub', [(i, i ^ 1 << bit) for i in range(subs)])]
  transfers between devices with their start and end apart: 11 -> 10, of which waited for: 4 -> 4; matrix products, arithmetic and copies ran while one was open for 1% -> 1% of each run, Pallas kernels for 29% -> 30%
where the time goes in v10:
time: 44.4 us; the launch traced here: 44.2 us
  Pallas kernels  14.8 us (33%)
  waiting for transfers between devices  13.8 us (31%)
  starting transfers between devices  13.7 us (31%)
  between operations  0.93 us (2%)
  local copies, waits for them, and re-layouts  0.81 us (2%)
    ppermute x2, waiting for transfers between devices, shards(): lax.ppermute(out, 'tile', around)  8.7 us
    pallas_call x3, Pallas kernels, call(): pl.pallas_call(kernel, in_specs=[smem] + [vmem] * len(operands), out_spec...  6.77 us
    ppermute x2, starting transfers between devices, shards(): lax.ppermute(out, 'tile', inward)  6.25 us
    pallas_call x1, Pallas kernels, shards(): pl.pallas_call(functools.partial(self_kernel, blocks, subs), in_specs=[sm...  6.05 us
    ppermute x1, waiting for transfers between devices, shards(): home = lax.ppermute(cols, 'tile', turned(around))  3.48 us
    ppermute x2, starting transfers between devices, shards(): lax.ppermute(out, 'tile', around)  3.1 us
    ppermute x1, starting transfers between devices, shards(): lax.ppermute(leaving, 'sub', [(i, i ^ 1 << bit) for i in range(subs)])  1.54 us
    pallas_call x1, Pallas kernels, pack(): pl.pallas_call(functools.partial(pack_kernel, by_block.shape[0], subs), i...  1.38 us
  transfers between devices with their start and end apart: 10, of which 4 were waited for; matrix products, arithmetic and copies ran while one was open for 1% of the time, Pallas kernels for 30%

profile of v10, /device:TPU:0, one launch (start us, length us, event | category | flops | bytes accessed | tf_op | source)
XLA Modules:
  0.0 44.2 jit_solution(12092287428106836525)
XLA Ops:
  0.0 0.0 copy-start.3
  0.0 1.4 %shard_map.31 = (bf16[128,1024]{1,0:T(8,128)(2,1)S(1)}, bf16[136,1024]{1,0:T(8,128)(2,1)S(1)}, bf16[264,1024]{1,0:T(8,128)(2,1)S(1)}, bf16[128,1024]{1,0:T(8,128)(2,1)S(1)}, bf16[136,1024]{1,0:T(8,128)(2,1)S(1)}) custom-call(bf16[2048,1024]{1,0:T(8,128)(2,1)} %rows_ref.3, s32[16,128]{1,0:T(8,128)} %bitcast.58), custom_call_target="tpu_custom_call" | custom-call | bytes 1024 | tf_op jit(solution)/shard_map/pallas_call | solution.py:129
  1.4 4.9 %collective-permute-start.1 = (bf16[128,1024]{1,0:T(8,128)(2,1)S(1)}, bf16[128,1024]{1,0:T(8,128)(2,1)S(1)}, u32[]{:S(2)}, u32[]{:S(2)}) collective-permute-start(bf16[128,1024]{1,0:T(8,128)(2,1)S(1)} %get-tuple-element.59), channel_id=1, source_target_pairs={{0,4},{12,8},{1,5},{13,9},{2,6},{14,10},{3,7},{15,11},{16,20},{28,... | collective-permute-start | bytes 786440 | tf_op jit(solution)/shard_map/ppermute | solution.py:342
  6.3 1.3 %collective-permute-start.2 = (bf16[136,1024]{1,0:T(8,128)(2,1)S(1)}, bf16[136,1024]{1,0:T(8,128)(2,1)S(1)}, u32[]{:S(2)}, u32[]{:S(2)}) collective-permute-start(bf16[136,1024]{1,0:T(8,128)(2,1)S(1)} %get-tuple-element.60), channel_id=1, source_target_pairs={{0,4},{12,8},{1,5},{13,9},{2,6},{14,10},{3,7},{15,11},{16,20},{28,... | collective-permute-start | bytes 835592 | tf_op jit(solution)/shard_map/ppermute | solution.py:342
  7.7 0.7 %collective-permute-start = (bf16[264,1024]{1,0:T(8,128)(2,1)S(1)}, bf16[264,1024]{1,0:T(8,128)(2,1)S(1)}, u32[]{:S(2)}, u32[]{:S(2)}) collective-permute-start(bf16[264,1024]{1,0:T(8,128)(2,1)S(1)} %get-tuple-element.58), channel_id=1, source_target_pairs={{4,8},{8,4},{5,9},{9,5},{6,10},{10,6},{7,11},{11,7},{20,24},{24,20... | collective-permute-start | bytes 1622024 | tf_op jit(solution)/shard_map/ppermute | solution.py:341
  8.4 0.0 copy-done.3
  8.4 0.1 convert_reduce_fusion
  8.6 0.1 dynamic_slice.47
  8.7 0.1 concatenate.3.meta_ref
  8.8 0.1 broadcast_in_dim.128
  8.9 6.0 %shard_map.30 = (bf16[2048,1024]{1,0:T(8,128)(2,1)S(1)}, f32[16,128]{1,0:T(8,128)S(1)}) custom-call(s32[84]{0:T(128)S(1)} %concatenate.3.meta_ref, bf16[2048,1024]{1,0:T(8,128)(2,1)} %rows_ref.3, s32[1,512]{1,0:T(1,128)S(1)} %bitcast.57), custom_call_target="tpu_custom_call" | custom-call | bytes 1024 | tf_op jit(solution)/shard_map/pallas_call | solution.py:365
  14.9 2.2 %collective-permute-start.4 = (bf16[136,1024]{1,0:T(8,128)(2,1)S(1)}, bf16[136,1024]{1,0:T(8,128)(2,1)S(1)}, u32[]{:S(2)}, u32[]{:S(2)}) collective-permute-start(bf16[136,1024]{1,0:T(8,128)(2,1)S(1)} %get-tuple-element.68), channel_id=1, source_target_pairs={{0,4},{12,8},{4,12},{8,0},{1,5},{13,9},{5,13},{9,1},{2,6},{14,10},... | collective-permute-start | bytes 835592 | tf_op jit(solution)/shard_map/ppermute | solution.py:375
  17.1 0.9 %collective-permute-start.3 = (bf16[128,1024]{1,0:T(8,128)(2,1)S(1)}, bf16[128,1024]{1,0:T(8,128)(2,1)S(1)}, u32[]{:S(2)}, u32[]{:S(2)}) collective-permute-start(bf16[128,1024]{1,0:T(8,128)(2,1)S(1)} %get-tuple-element.67), channel_id=1, source_target_pairs={{0,4},{12,8},{4,12},{8,0},{1,5},{13,9},{5,13},{9,1},{2,6},{14,10},... | collective-permute-start | bytes 786440 | tf_op jit(solution)/shard_map/ppermute | solution.py:375
  18.0 0.0 collective-permute-done.1.refs_0_
  18.0 0.8 %collective-permute-done.2.refs_1_ = bf16[136,1024]{1,0:T(8,128)(2,1)S(1)} collective-permute-done((bf16[136,1024]{1,0:T(8,128)(2,1)S(1)}, bf16[136,1024]{1,0:T(8,128)(2,1)S(1)}, u32[]{:S(2)}, u32[]{:S(2)}) %collective-permute-start.2) | collective-permute-done | bytes 278560 | tf_op jit(solution)/shard_map/ppermute | solution.py:342
  18.8 2.3 %shard_map.32 = (f32[16,128]{1,0:T(8,128)S(1)}, f32[3,128]{1,0:T(4,128)S(1)}) custom-call(s32[84]{0:T(128)S(1)} %concatenate.3.meta_ref, bf16[2048,1024]{1,0:T(8,128)(2,1)S(1)} %get-tuple-element.57.unit_ref, bf16[128,1024]{1,0:T(8,128)(2,1)S(1)} %collective-permute-done.1.refs_0_, bf16[136,1024]{1,0:T(8,128)(2,1)S(1)} %collective-permute-done.2.refs_1_, ...), custom_call_target="tpu_custom_call" | custom-call | flops 1073741824 | bytes 1024 | tf_op jit(solution)/shard_map/pallas_call | solution.py:268
  21.1 1.3 %collective-permute-start.5 = (f32[3,128]{1,0:T(4,128)S(1)}, f32[3,128]{1,0:T(4,128)S(1)}, u32[]{:S(2)}, u32[]{:S(2)}) collective-permute-start(f32[3,128]{1,0:T(4,128)S(1)} %get-tuple-element.70), channel_id=1, source_target_pairs={{4,0},{8,12},{5,1},{9,13},{6,2},{10,14},{7,3},{11,15},{20,16},{24,... | collective-permute-start | bytes 4616 | tf_op jit(solution)/shard_map/ppermute | solution.py:388
  22.4 0.0 collective-permute-done.refs_0_
  22.4 2.2 %shard_map.33 = (f32[16,128]{1,0:T(8,128)S(1)}, f32[3,128]{1,0:T(4,128)S(1)}) custom-call(s32[84]{0:T(128)S(1)} %concatenate.3.meta_ref, bf16[2048,1024]{1,0:T(8,128)(2,1)S(1)} %get-tuple-element.57.unit_ref, bf16[264,1024]{1,0:T(8,128)(2,1)S(1)} %collective-permute-done.refs_0_, f32[16,128]{1,0:T(8,128)S(1)} %get-tuple-element.65.refs_1_), custom_call_target="tpu_custom_call" | custom-call | flops 1073741824 | bytes 1024 | tf_op jit(solution)/shard_map/pallas_call | solution.py:268
  24.6 0.7 %collective-permute-start.7 = (f32[3,128]{1,0:T(4,128)S(1)}, f32[3,128]{1,0:T(4,128)S(1)}, u32[]{:S(2)}, u32[]{:S(2)}) collective-permute-start(f32[3,128]{1,0:T(4,128)S(1)} %get-tuple-element.66.swap_cols_ref.here_ref), channel_id=1, source_target_pairs={{8,4},{4,8},{9,5},{5,9},{10,6},{6,10},{11,7},{7,11},{24,20},{20,24... | collective-permute-start | bytes 4616 | tf_op jit(solution)/shard_map/ppermute | solution.py:390
  25.3 8.7 %collective-permute-done.3.low_ref = bf16[128,1024]{1,0:T(8,128)(2,1)S(1)} collective-permute-done((bf16[128,1024]{1,0:T(8,128)(2,1)S(1)}, bf16[128,1024]{1,0:T(8,128)(2,1)S(1)}, u32[]{:S(2)}, u32[]{:S(2)}) %collective-permute-start.3) | collective-permute-done | bytes 262176 | tf_op jit(solution)/shard_map/ppermute | solution.py:375
  34.0 0.0 collective-permute-done.4.high_ref
  34.0 0.0 collective-permute-done.5.outer_back_ref
  34.0 2.3 %shard_map.34 = (f32[8,128]{1,0:T(8,128)S(1)}, f32[8,128]{1,0:T(8,128)S(1)}, f32[3,128]{1,0:T(4,128)S(1)}) custom-call(s32[84]{0:T(128)S(1)} %concatenate.3.meta_ref, bf16[2048,1024]{1,0:T(8,128)(2,1)S(1)} %get-tuple-element.57.unit_ref, bf16[128,1024]{1,0:T(8,128)(2,1)S(1)} %collective-permute-done.3.low_ref, ...), custom_call_target="tpu_custom_call" | custom-call | flops 1073741824 | bytes 1024 | tf_op jit(solution)/shard_map/pallas_call | solution.py:268
  36.3 0.1 collective-permute-start.6
  36.3 0.1 collective-permute-start.8
  36.4 0.0 collective-permute-done.7
  36.4 3.5 %collective-permute-done.6.home_ref = f32[3,128]{1,0:T(4,128)S(1)} collective-permute-done((f32[3,128]{1,0:T(4,128)S(1)}, f32[3,128]{1,0:T(4,128)S(1)}, u32[]{:S(2)}, u32[]{:S(2)}) %collective-permute-start.6) | collective-permute-done | bytes 1568 | tf_op jit(solution)/shard_map/ppermute | solution.py:401
  39.9 0.0 collective-permute-done.8
  39.9 1.5 %collective-permute-start.9 = (f32[4,128]{1,0:T(4,128)S(1)}, f32[4,128]{1,0:T(4,128)S(1)}, u32[]{:S(2)}, u32[]{:S(2)}) collective-permute-start(f32[4,128]{1,0:T(4,128)S(1)} %get-tuple-element.81), channel_id=1, source_target_pairs={{0,2},{1,3},{2,0},{3,1},{4,6},{5,7},{6,4},{7,5},{8,10},{9,11},{10,... | collective-permute-start | bytes 6152 | tf_op jit(solution)/shard_map/ppermute | solution.py:411
  41.5 0.6 %shard_map.35 = s32[1]{0:T(128)} custom-call(f32[3,128]{1,0:T(4,128)S(1)} %get-tuple-element.66.swap_cols_ref.here_ref, f32[3,128]{1,0:T(4,128)S(1)} %collective-permute-done.6.home_ref), custom_call_target="tpu_custom_call" | custom-call | tf_op jit(solution)/shard_map/pallas_call | solution.py:414
  42.8 0.8 %collective-permute-done.9 = f32[4,128]{1,0:T(4,128)S(1)} collective-permute-done((f32[4,128]{1,0:T(4,128)S(1)}, f32[4,128]{1,0:T(4,128)S(1)}, u32[]{:S(2)}, u32[]{:S(2)}) %collective-permute-start.9) | collective-permute-done | bytes 2080 | tf_op jit(solution)/shard_map/ppermute | solution.py:411
  43.6 0.0 copy-start.4
  43.6 0.6 %copy-done.4 = f32[512]{0:T(512)} copy-done((f32[512]{0:T(512)}, f32[512]{0:T(512)S(1)}, u32[]{:S(2)}) %copy-start.4) | copy-done | bytes 2072
  (9 shorter events, 0.0 us)
Async XLA Ops:
  0.0 8.4 %copy-start.3 = (s32[2048]{0:T(1024)S(1)}, s32[2048]{0:T(1024)}, u32[]{:S(2)}) copy-start(s32[2048]{0:T(1024)} %param.5) | copy-start | bytes 24580
  1.4 16.6 %collective-permute-start.1 = (bf16[128,1024]{1,0:T(8,128)(2,1)S(1)}, bf16[128,1024]{1,0:T(8,128)(2,1)S(1)}, u32[]{:S(2)}, u32[]{:S(2)}) collective-permute-start(bf16[128,1024]{1,0:T(8,128)(2,1)S(1)} %get-tuple-element.59), channel_id=1, source_target_pairs={{0,4},{12,8},{1,5},{13,9},{2,6},{14,10},{3,7},{15,11},{16,20},{28,... | collective-permute-start | bytes 786440 | tf_op jit(solution)/shard_map/ppermute | solution.py:342
  6.3 12.5 %collective-permute-start.2 = (bf16[136,1024]{1,0:T(8,128)(2,1)S(1)}, bf16[136,1024]{1,0:T(8,128)(2,1)S(1)}, u32[]{:S(2)}, u32[]{:S(2)}) collective-permute-start(bf16[136,1024]{1,0:T(8,128)(2,1)S(1)} %get-tuple-element.60), channel_id=1, source_target_pairs={{0,4},{12,8},{1,5},{13,9},{2,6},{14,10},{3,7},{15,11},{16,20},{28,... | collective-permute-start | bytes 835592 | tf_op jit(solution)/shard_map/ppermute | solution.py:342
  7.7 14.7 %collective-permute-start = (bf16[264,1024]{1,0:T(8,128)(2,1)S(1)}, bf16[264,1024]{1,0:T(8,128)(2,1)S(1)}, u32[]{:S(2)}, u32[]{:S(2)}) collective-permute-start(bf16[264,1024]{1,0:T(8,128)(2,1)S(1)} %get-tuple-element.58), channel_id=1, source_target_pairs={{4,8},{8,4},{5,9},{9,5},{6,10},{10,6},{7,11},{11,7},{20,24},{24,20... | collective-permute-start | bytes 1622024 | tf_op jit(solution)/shard_map/ppermute | solution.py:341
  14.9 19.1 %collective-permute-start.4 = (bf16[136,1024]{1,0:T(8,128)(2,1)S(1)}, bf16[136,1024]{1,0:T(8,128)(2,1)S(1)}, u32[]{:S(2)}, u32[]{:S(2)}) collective-permute-start(bf16[136,1024]{1,0:T(8,128)(2,1)S(1)} %get-tuple-element.68), channel_id=1, source_target_pairs={{0,4},{12,8},{4,12},{8,0},{1,5},{13,9},{5,13},{9,1},{2,6},{14,10},... | collective-permute-start | bytes 835592 | tf_op jit(solution)/shard_map/ppermute | solution.py:375
  17.1 16.9 %collective-permute-start.3 = (bf16[128,1024]{1,0:T(8,128)(2,1)S(1)}, bf16[128,1024]{1,0:T(8,128)(2,1)S(1)}, u32[]{:S(2)}, u32[]{:S(2)}) collective-permute-start(bf16[128,1024]{1,0:T(8,128)(2,1)S(1)} %get-tuple-element.67), channel_id=1, source_target_pairs={{0,4},{12,8},{4,12},{8,0},{1,5},{13,9},{5,13},{9,1},{2,6},{14,10},... | collective-permute-start | bytes 786440 | tf_op jit(solution)/shard_map/ppermute | solution.py:375
  21.1 12.9 %collective-permute-start.5 = (f32[3,128]{1,0:T(4,128)S(1)}, f32[3,128]{1,0:T(4,128)S(1)}, u32[]{:S(2)}, u32[]{:S(2)}) collective-permute-start(f32[3,128]{1,0:T(4,128)S(1)} %get-tuple-element.70), channel_id=1, source_target_pairs={{4,0},{8,12},{5,1},{9,13},{6,2},{10,14},{7,3},{11,15},{20,16},{24,... | collective-permute-start | bytes 4616 | tf_op jit(solution)/shard_map/ppermute | solution.py:388
  24.6 11.8 %collective-permute-start.7 = (f32[3,128]{1,0:T(4,128)S(1)}, f32[3,128]{1,0:T(4,128)S(1)}, u32[]{:S(2)}, u32[]{:S(2)}) collective-permute-start(f32[3,128]{1,0:T(4,128)S(1)} %get-tuple-element.66.swap_cols_ref.here_ref), channel_id=1, source_target_pairs={{8,4},{4,8},{9,5},{5,9},{10,6},{6,10},{11,7},{7,11},{24,20},{20,24... | collective-permute-start | bytes 4616 | tf_op jit(solution)/shard_map/ppermute | solution.py:390
  36.3 3.6 %collective-permute-start.6 = (f32[3,128]{1,0:T(4,128)S(1)}, f32[3,128]{1,0:T(4,128)S(1)}, u32[]{:S(2)}, u32[]{:S(2)}) collective-permute-start(f32[3,128]{1,0:T(4,128)S(1)} %get-tuple-element.71), channel_id=1, source_target_pairs={{4,0},{8,12},{12,4},{0,8},{5,1},{9,13},{13,5},{1,9},{6,2},{10,14},... | collective-permute-start | bytes 4616 | tf_op jit(solution)/shard_map/ppermute | solution.py:401
  36.3 3.6 %collective-permute-start.8 = (f32[8,128]{1,0:T(8,128)S(1)}, f32[8,128]{1,0:T(8,128)S(1)}, u32[]{:S(2)}, u32[]{:S(2)}) collective-permute-start(f32[8,128]{1,0:T(8,128)S(1)} %get-tuple-element.74), channel_id=1, source_target_pairs={{0,1},{1,0},{2,3},{3,2},{4,5},{5,4},{6,7},{7,6},{8,9},{9,8},{10,11... | collective-permute-start | bytes 12296 | tf_op jit(solution)/shard_map/ppermute | solution.py:404
  39.9 3.7 %collective-permute-start.9 = (f32[4,128]{1,0:T(4,128)S(1)}, f32[4,128]{1,0:T(4,128)S(1)}, u32[]{:S(2)}, u32[]{:S(2)}) collective-permute-start(f32[4,128]{1,0:T(4,128)S(1)} %get-tuple-element.81), channel_id=1, source_target_pairs={{0,2},{1,3},{2,0},{3,1},{4,6},{5,7},{6,4},{7,5},{8,10},{9,11},{10,... | collective-permute-start | bytes 6152 | tf_op jit(solution)/shard_map/ppermute | solution.py:411
  43.6 0.6 %copy-start.4 = (f32[512]{0:T(512)}, f32[512]{0:T(512)S(1)}, u32[]{:S(2)}) copy-start(f32[512]{0:T(512)S(1)} %get-tuple-element.119) | copy-start | bytes 6148

commit v11 on v10

--- a/solution.py
+++ b/solution.py
@@ -61,76 +61,50 @@
         self.width, self.share = width, share
 
 
-def pack_kernel(blocks, subs, rows_ref, ids_ref, *refs):
-    outs, (ids, sems) = refs[:5], refs[5:]
+def pack_kernel(blocks, subs, rows_ref, ids_ref, first_ref, second_ref, ids, sems):
     plan = Plan(blocks, subs, lax.axis_index("tile"), lax.axis_index("sub"))
     share, size = plan.share, plan.share * BLOCK
-    first_low, first_high, swapped, second_low, second_high = outs
     ids_copy = pltpu.make_async_copy(ids_ref, ids, sems.at[0])
-    ids_copy.start()
-
-    def copies(block, parts, sem):
-        made, down = [], 0
-        for part, count in parts:
-            for at in range(0, count, COPY):
-                start = pl.multiple_of(block * BLOCK + down, COPY)
-                made.append(
-                    pltpu.make_async_copy(
-                        rows_ref.at[pl.ds(start, COPY), :], part.at[pl.ds(at, COPY), :], sems.at[sem + len(made)]
-                    )
-                )
-                down += COPY
-        return made
-
-    count = size // COPY
-    first = copies(plan.first, ((first_low, size // 2), (first_high, size // 2)), 1)
-    swap = copies(plan.first, ((swapped, size),), 1)
-    second = copies(plan.second, ((second_low, size // 2), (second_high, size // 2)), 1 + count)
-
-    @pl.when(plan.inner)
-    def _():
-        for copy in swap:
-            copy.start()
+
+    def copies(block, out, sem):
+        for down in range(0, size, COPY):
+            start = pl.multiple_of(block * BLOCK + down, COPY)
+            yield pltpu.make_async_copy(
+                rows_ref.at[pl.ds(start, COPY), :], out.at[pl.ds(down, COPY), :], sems.at[sem + down // COPY]
+            )
+
+    first = list(copies(plan.first, first_ref, 1))
+    second = list(copies(plan.second, second_ref, 1 + size // COPY))
+    for copy in [ids_copy] + first:
+        copy.start()
 
     @pl.when(jnp.logical_not(plan.inner))
     def _():
-        for copy in first:
+        for copy in second:
             copy.start()
 
-    for copy in second:
-        copy.start()
     ids_copy.wait()
-    depth = swapped.shape[1]
+    depth = first_ref.shape[1]
     edge = jnp.max(ids[pl.ds(plan.edge, 1), :], axis=1, keepdims=True)
     rest = [jnp.broadcast_to(edge, (1, BLOCK)), jnp.zeros((1, depth - size - BLOCK), jnp.int32)]
-    for block, parts in ((plan.first, (first_high, swapped)), (plan.second, (second_high,))):
+    for block, out in ((plan.first, first_ref), (plan.second, second_ref)):
         row = jnp.concatenate([ids[pl.ds(block + k, 1), :] for k in range(share)] + rest, axis=1)
-        row = jnp.broadcast_to(row.astype(jnp.float32), (8, depth)).astype(jnp.bfloat16)
-        for part in parts:
-            part[part.shape[0] - 8 :, :] = row
-
-    @pl.when(plan.inner)
-    def _():
-        for copy in swap:
-            copy.wait()
+        out[size:, :] = jnp.broadcast_to(row.astype(jnp.float32), (8, depth)).astype(jnp.bfloat16)
+    for copy in first:
+        copy.wait()
 
     @pl.when(jnp.logical_not(plan.inner))
     def _():
-        for copy in first:
+        for copy in second:
             copy.wait()
 
-    for copy in second:
-        copy.wait()
-
 
 def pack(size, subs, embeddings, by_block):
-    depth = embeddings.shape[1]
-    parts = (size // 2, size // 2 + 8, size + 8, size // 2, size // 2 + 8)
     return pl.pallas_call(
         functools.partial(pack_kernel, by_block.shape[0], subs),
         in_specs=[pl.BlockSpec(memory_space=pl.ANY)] * 2,
-        out_specs=[pl.BlockSpec(memory_space=pltpu.VMEM)] * 5,
-        out_shape=[jax.ShapeDtypeStruct((count, depth), jnp.bfloat16) for count in parts],
+        out_specs=[pl.BlockSpec(memory_space=pltpu.VMEM)] * 2,
+        out_shape=[jax.ShapeDtypeStruct((size + 8, embeddings.shape[1]), jnp.bfloat16)] * 2,
         scratch_shapes=[pltpu.VMEM(by_block.shape, jnp.int32), pltpu.SemaphoreType.DMA((2 * size // COPY + 1,))],
         compiler_params=pltpu.CompilerParams(vmem_limit_bytes=8 * 1024 * 1024),
         cost_estimate=pl.CostEstimate(flops=0, bytes_accessed=1024, transcendentals=0),
@@ -184,14 +158,8 @@
             sums_ref[pl.ds(block, 1), :] = lane_sums(jnp.where(keep, weight, 0.0))
 
 
-def unit_chunk(parts, piece_unit):
-    size = piece_unit.shape[0]
-    down = 0
-    for part in parts:
-        count = part.shape[0] // 16 * 16
-        piece_unit[down : down + count, :] = normalised(part[:count, :])
-        down += count
-    row = parts[-1][count : count + 8, :].astype(jnp.float32)[0:1, :]
+def chunk_tags(piece_ref, size):
+    row = piece_ref[size:, :].astype(jnp.float32)[0:1, :]
     return row[:, :size], row[:, size : size + BLOCK]
 
 
@@ -215,10 +183,13 @@
     return [total[:, at : at + BLOCK] for at in range(0, size, BLOCK)]
 
 
-def middle_kernel(blocks, share, chunk, meta_ref, unit_ref, *refs):
-    *parts, before_ref, sums_ref, cols_ref, piece_unit = refs
+def middle_kernel(
+    blocks, share, chunk, meta_ref, unit_ref, piece_ref, before_ref, sums_ref, cols_ref, piece_unit
+):
     meta = Meta(meta_ref, blocks)
-    tags, edge = unit_chunk(parts, piece_unit)
+    size = share * BLOCK
+    piece_unit[...] = normalised(piece_ref[:size, :])
+    tags, edge = chunk_tags(piece_ref, size)
 
     def add_rows(block, value):
         sums_ref[block : block + 1, :] = before_ref[block : block + 1, :] + value
@@ -232,11 +203,22 @@
 
 
 def last_kernel(
-    blocks, share, width, meta_ref, unit_ref, low_ref, high_ref, before_ref, outer_back_ref, swap_cols_ref,
+    blocks, share, width, meta_ref, unit_ref, inward_ref, relayed_ref, before_ref, outer_back_ref, swap_cols_ref,
     keep_ref, send_ref, cols_ref, piece_unit, sums,
 ):
     meta = Meta(meta_ref, blocks)
-    tags, _ = unit_chunk((low_ref, high_ref), piece_unit)
+    size = share * BLOCK
+    is_inner = meta.number(INNER) > 0
+
+    @pl.when(is_inner)
+    def _():
+        piece_unit[...] = normalised(inward_ref[:size, :])
+
+    @pl.when(jnp.logical_not(is_inner))
+    def _():
+        piece_unit[...] = normalised(relayed_ref[:size, :])
+
+    tags = jnp.where(is_inner, chunk_tags(inward_ref, size)[0], chunk_tags(relayed_ref, size)[0])
 
     def place(block):
         owner = block // width
@@ -337,9 +319,10 @@
         return [(b, a) for a, b in route]
 
     by_block = cluster_ids.reshape(blocks, BLOCK)
-    first_low, first_high, swapped, second_low, second_high = pack(size, subs, embeddings, by_block)
-    from_inner = lax.ppermute(swapped, "tile", swap)
-    from_outer = [lax.ppermute(out, "tile", inward) for out in (first_high, first_low)][::-1]
+    first_out, second_out = pack(size, subs, embeddings, by_block)
+    from_outer = lax.ppermute(first_out, "tile", inward)
+    from_inner = lax.ppermute(first_out, "tile", swap)
+    relayed = lax.ppermute(from_inner, "tile", turned(inward))
 
     tag = jnp.max(by_block, axis=1)
     used = jnp.sum((by_block >= 0).astype(jnp.int32), axis=1)
@@ -371,28 +354,28 @@
         compiler_params=pltpu.CompilerParams(vmem_limit_bytes=24 * 1024 * 1024),
         cost_estimate=pl.CostEstimate(flops=0, bytes_accessed=1024, transcendentals=0),
     )(meta, embeddings, lax.dynamic_slice_in_dim(cluster_ids, member * quarter, quarter, 0)[None])
-    second_low, second_high, sums = lax.optimization_barrier((second_low, second_high, sums))
-    last = [lax.ppermute(out, "tile", around) for out in (second_low, second_high)]
-
-    def middle(chunk, parts, before):
+    second_out, sums = lax.optimization_barrier((second_out, sums))
+    last = lax.ppermute(second_out, "tile", inward)
+
+    def middle(chunk, piece, before):
         return call(
             functools.partial(middle_kernel, blocks, share, chunk),
             meta,
-            (unit, *parts, before),
+            (unit, piece, before),
             [row_sums, col_sums],
             [pltpu.VMEM((size, depth), jnp.bfloat16)],
             2 * rows * size * depth,
         )
 
+    sums, swap_cols = middle(1, from_inner, sums)
     sums, outer_cols = middle(0, from_outer, sums)
     outer_back = lax.ppermute(outer_cols, "tile", turned(inward))
-    sums, swap_cols = middle(1, (from_inner,), sums)
     swap_back = lax.ppermute(swap_cols, "tile", turned(swap))
     half = jax.ShapeDtypeStruct((heap, BLOCK), jnp.float32)
     held, leaving, cols = call(
         functools.partial(last_kernel, blocks, share, width),
         meta,
-        (unit, *last, sums, outer_back, swap_cols),
+        (unit, last, relayed, sums, outer_back, swap_cols),
         [half, half, col_sums],
         [pltpu.VMEM((size, depth), jnp.bfloat16), pltpu.VMEM((blocks, BLOCK), jnp.float32)],
         2 * rows * size * depth,

time: 44.4 us -> 43.5 us (0.980)
  waiting for transfers between devices: 13.8 us -> 10.1 us
  starting transfers between devices: 13.7 us -> 16.3 us
    ppermute x5 -> x4, waiting for transfers between devices: 9.49 us -> 7.1 us  [the longest x1 5.9 us: shards(): last = lax.ppermute(second_out, 'tile', inward)]
    ppermute x1, starting transfers between devices: 0.05 us -> 1.9 us  [shards(): home = lax.ppermute(cols, 'tile', turned(around))]
    ppermute x1, waiting for transfers between devices: 3.48 us -> 1.73 us  [shards(): home = lax.ppermute(cols, 'tile', turned(around))]
    ppermute x5 -> x4, starting transfers between devices: 10 us -> 10.9 us  [the longest x1 7.57 us: shards(): from_outer = lax.ppermute(first_out, 'tile', inward)]
    ppermute x1, waiting for transfers between devices: 0.01 us -> 0.52 us  [shards(): outer_back = lax.ppermute(outer_cols, 'tile', turned(inward))]
  transfers between devices with their start and end apart: 10 -> 9, of which waited for: 4 -> 5; matrix products, arithmetic and copies ran while one was open for 1% -> 1% of each run, Pallas kernels for 30% -> 31%
where the time goes in v11:
time: 43.5 us; the launch traced here: 43.2 us
  starting transfers between devices  16.3 us (37%)
  Pallas kernels  14.9 us (34%)
  waiting for transfers between devices  10.1 us (23%)
  between operations  0.91 us (2%)
  local copies, waits for them, and re-layouts  0.82 us (2%)
    ppermute x1, starting transfers between devices, shards(): from_outer = lax.ppermute(first_out, 'tile', inward)  7.57 us
    pallas_call x3, Pallas kernels, call(): pl.pallas_call(kernel, in_specs=[smem] + [vmem] * len(operands), out_spec...  6.84 us
    pallas_call x1, Pallas kernels, shards(): pl.pallas_call(functools.partial(self_kernel, blocks, subs), in_specs=[sm...  6.05 us
    ppermute x1, waiting for transfers between devices, shards(): last = lax.ppermute(second_out, 'tile', inward)  5.9 us
    ppermute x1, starting transfers between devices, shards(): home = lax.ppermute(cols, 'tile', turned(around))  1.9 us
    ppermute x1, waiting for transfers between devices, shards(): home = lax.ppermute(cols, 'tile', turned(around))  1.73 us
    ppermute x1, starting transfers between devices, shards(): lax.ppermute(leaving, 'sub', [(i, i ^ 1 << bit) for i in range(subs)])  1.57 us
    pallas_call x1, Pallas kernels, pack(): pl.pallas_call(functools.partial(pack_kernel, by_block.shape[0], subs), i...  1.38 us
  transfers between devices with their start and end apart: 9, of which 5 were waited for; matrix products, arithmetic and copies ran while one was open for 1% of the time, Pallas kernels for 31%

profile of v11, /device:TPU:0, one launch (start us, length us, event | category | flops | bytes accessed | tf_op | source)
XLA Modules:
  0.0 43.2 jit_solution(13459310144352777621)
XLA Ops:
  0.0 0.0 copy-start.3
  0.0 1.4 %shard_map.31 = (bf16[264,1024]{1,0:T(8,128)(2,1)S(1)}, bf16[264,1024]{1,0:T(8,128)(2,1)S(1)}) custom-call(bf16[2048,1024]{1,0:T(8,128)(2,1)} %rows_ref.3, s32[16,128]{1,0:T(8,128)} %bitcast.58), custom_call_target="tpu_custom_call" | custom-call | bytes 1024 | tf_op jit(solution)/shard_map/pallas_call | solution.py:103
  1.4 0.7 %collective-permute-start = (bf16[264,1024]{1,0:T(8,128)(2,1)S(1)}, bf16[264,1024]{1,0:T(8,128)(2,1)S(1)}, u32[]{:S(2)}, u32[]{:S(2)}) collective-permute-start(bf16[264,1024]{1,0:T(8,128)(2,1)S(1)} %get-tuple-element.54), channel_id=1, source_target_pairs={{4,8},{8,4},{5,9},{9,5},{6,10},{10,6},{7,11},{11,7},{20,24},{24,20... | collective-permute-start | bytes 1622024 | tf_op jit(solution)/shard_map/ppermute | solution.py:324
  2.1 7.6 %collective-permute-start.3 = (bf16[264,1024]{1,0:T(8,128)(2,1)S(1)}, bf16[264,1024]{1,0:T(8,128)(2,1)S(1)}, u32[]{:S(2)}, u32[]{:S(2)}) collective-permute-start(bf16[264,1024]{1,0:T(8,128)(2,1)S(1)} %get-tuple-element.54), channel_id=1, source_target_pairs={{0,4},{12,8},{1,5},{13,9},{2,6},{14,10},{3,7},{15,11},{16,20},{28,... | collective-permute-start | bytes 1622024 | tf_op jit(solution)/shard_map/ppermute | solution.py:323
  9.8 0.0 copy-done.3
  9.8 0.1 dynamic_slice.47
  9.9 0.1 convert_reduce_fusion
  10.0 0.1 concatenate.3.meta_ref
  10.1 0.1 broadcast_in_dim.128
  10.2 6.0 %shard_map.30 = (bf16[2048,1024]{1,0:T(8,128)(2,1)S(1)}, f32[16,128]{1,0:T(8,128)S(1)}) custom-call(s32[84]{0:T(128)S(1)} %concatenate.3.meta_ref, bf16[2048,1024]{1,0:T(8,128)(2,1)} %rows_ref.3, s32[1,512]{1,0:T(1,128)S(1)} %bitcast.57), custom_call_target="tpu_custom_call" | custom-call | bytes 1024 | tf_op jit(solution)/shard_map/pallas_call | solution.py:348
  16.2 1.3 %collective-permute-start.1 = (bf16[264,1024]{1,0:T(8,128)(2,1)S(1)}, bf16[264,1024]{1,0:T(8,128)(2,1)S(1)}, u32[]{:S(2)}, u32[]{:S(2)}) collective-permute-start(bf16[264,1024]{1,0:T(8,128)(2,1)S(1)} %get-tuple-element.59), channel_id=1, source_target_pairs={{0,4},{12,8},{1,5},{13,9},{2,6},{14,10},{3,7},{15,11},{16,20},{28,... | collective-permute-start | bytes 1622024 | tf_op jit(solution)/shard_map/ppermute | solution.py:358
  17.6 0.0 collective-permute-done.piece_ref
  17.6 1.3 %collective-permute-start.2 = (bf16[264,1024]{1,0:T(8,128)(2,1)S(1)}, bf16[264,1024]{1,0:T(8,128)(2,1)S(1)}, u32[]{:S(2)}, u32[]{:S(2)}) collective-permute-start(bf16[264,1024]{1,0:T(8,128)(2,1)S(1)} %collective-permute-done.piece_ref), channel_id=1, source_target_pairs={{4,0},{8,12},{5,1},{9,13},{6,2},{10,14},{7,3},{11,15},{20,16},{24,... | collective-permute-start | bytes 1622024 | tf_op jit(solution)/shard_map/ppermute | solution.py:325
  18.9 2.3 %shard_map.32 = (f32[16,128]{1,0:T(8,128)S(1)}, f32[3,128]{1,0:T(4,128)S(1)}) custom-call(s32[84]{0:T(128)S(1)} %concatenate.3.meta_ref, bf16[2048,1024]{1,0:T(8,128)(2,1)S(1)} %get-tuple-element.53.unit_ref, bf16[264,1024]{1,0:T(8,128)(2,1)S(1)} %collective-permute-done.piece_ref, f32[16,128]{1,0:T(8,128)S(1)} %get-tuple-element.57.before_ref), custom_call_target="tpu_custom_call" | custom-call | flops 1073741824 | bytes 1024 | tf_op jit(solution)/shard_map/pallas_call | solution.py:250
  21.1 1.2 %collective-permute-done.3.piece_ref = bf16[264,1024]{1,0:T(8,128)(2,1)S(1)} collective-permute-done((bf16[264,1024]{1,0:T(8,128)(2,1)S(1)}, bf16[264,1024]{1,0:T(8,128)(2,1)S(1)}, u32[]{:S(2)}, u32[]{:S(2)}) %collective-permute-start.3) | collective-permute-done | bytes 540704 | tf_op jit(solution)/shard_map/ppermute | solution.py:323
  22.3 2.2 %shard_map.33 = (f32[16,128]{1,0:T(8,128)S(1)}, f32[3,128]{1,0:T(4,128)S(1)}) custom-call(s32[84]{0:T(128)S(1)} %concatenate.3.meta_ref, bf16[2048,1024]{1,0:T(8,128)(2,1)S(1)} %get-tuple-element.53.unit_ref, bf16[264,1024]{1,0:T(8,128)(2,1)S(1)} %collective-permute-done.3.piece_ref, f32[16,128]{1,0:T(8,128)S(1)} %get-tuple-element.60.before_ref), custom_call_target="tpu_custom_call" | custom-call | flops 1073741824 | bytes 1024 | tf_op jit(solution)/shard_map/pallas_call | solution.py:250
  24.6 1.3 %collective-permute-start.4 = (f32[3,128]{1,0:T(4,128)S(1)}, f32[3,128]{1,0:T(4,128)S(1)}, u32[]{:S(2)}, u32[]{:S(2)}) collective-permute-start(f32[3,128]{1,0:T(4,128)S(1)} %get-tuple-element.62), channel_id=1, source_target_pairs={{4,0},{8,12},{5,1},{9,13},{6,2},{10,14},{7,3},{11,15},{20,16},{24,... | collective-permute-start | bytes 4616 | tf_op jit(solution)/shard_map/ppermute | solution.py:372
  25.9 0.7 %collective-permute-start.6 = (f32[3,128]{1,0:T(4,128)S(1)}, f32[3,128]{1,0:T(4,128)S(1)}, u32[]{:S(2)}, u32[]{:S(2)}) collective-permute-start(f32[3,128]{1,0:T(4,128)S(1)} %get-tuple-element.58.swap_cols_ref.here_ref), channel_id=1, source_target_pairs={{8,4},{4,8},{9,5},{5,9},{10,6},{6,10},{11,7},{7,11},{24,20},{20,24... | collective-permute-start | bytes 4616 | tf_op jit(solution)/shard_map/ppermute | solution.py:373
  26.6 5.9 %collective-permute-done.1.inward_ref = bf16[264,1024]{1,0:T(8,128)(2,1)S(1)} collective-permute-done((bf16[264,1024]{1,0:T(8,128)(2,1)S(1)}, bf16[264,1024]{1,0:T(8,128)(2,1)S(1)}, u32[]{:S(2)}, u32[]{:S(2)}) %collective-permute-start.1) | collective-permute-done | bytes 540704 | tf_op jit(solution)/shard_map/ppermute | solution.py:358
  32.5 0.5 %collective-permute-done.4.outer_back_ref = f32[3,128]{1,0:T(4,128)S(1)} collective-permute-done((f32[3,128]{1,0:T(4,128)S(1)}, f32[3,128]{1,0:T(4,128)S(1)}, u32[]{:S(2)}, u32[]{:S(2)}) %collective-permute-start.4) | collective-permute-done | bytes 1568 | tf_op jit(solution)/shard_map/ppermute | solution.py:372
  33.0 0.0 collective-permute-done.2.relayed_ref
  33.0 2.3 %shard_map.34 = (f32[8,128]{1,0:T(8,128)S(1)}, f32[8,128]{1,0:T(8,128)S(1)}, f32[3,128]{1,0:T(4,128)S(1)}) custom-call(s32[84]{0:T(128)S(1)} %concatenate.3.meta_ref, bf16[2048,1024]{1,0:T(8,128)(2,1)S(1)} %get-tuple-element.53.unit_ref, bf16[264,1024]{1,0:T(8,128)(2,1)S(1)} %collective-permute-done.1.inward_ref, ...), custom_call_target="tpu_custom_call" | custom-call | flops 1073741824 | bytes 1024 | tf_op jit(solution)/shard_map/pallas_call | solution.py:250
  35.3 1.9 %collective-permute-start.5 = (f32[3,128]{1,0:T(4,128)S(1)}, f32[3,128]{1,0:T(4,128)S(1)}, u32[]{:S(2)}, u32[]{:S(2)}) collective-permute-start(f32[3,128]{1,0:T(4,128)S(1)} %get-tuple-element.63), channel_id=1, source_target_pairs={{4,0},{8,12},{12,4},{0,8},{5,1},{9,13},{13,5},{1,9},{6,2},{10,14},... | collective-permute-start | bytes 4616 | tf_op jit(solution)/shard_map/ppermute | solution.py:384
  37.2 0.0 collective-permute-start.7
  37.2 0.0 collective-permute-done.6
  37.2 1.7 %collective-permute-done.5.home_ref = f32[3,128]{1,0:T(4,128)S(1)} collective-permute-done((f32[3,128]{1,0:T(4,128)S(1)}, f32[3,128]{1,0:T(4,128)S(1)}, u32[]{:S(2)}, u32[]{:S(2)}) %collective-permute-start.5) | collective-permute-done | bytes 1568 | tf_op jit(solution)/shard_map/ppermute | solution.py:384
  39.0 0.0 collective-permute-done.7
  39.0 1.6 %collective-permute-start.8 = (f32[4,128]{1,0:T(4,128)S(1)}, f32[4,128]{1,0:T(4,128)S(1)}, u32[]{:S(2)}, u32[]{:S(2)}) collective-permute-start(f32[4,128]{1,0:T(4,128)S(1)} %get-tuple-element.73), channel_id=1, source_target_pairs={{0,2},{1,3},{2,0},{3,1},{4,6},{5,7},{6,4},{7,5},{8,10},{9,11},{10,... | collective-permute-start | bytes 6152 | tf_op jit(solution)/shard_map/ppermute | solution.py:394
  40.6 0.6 %shard_map.35 = s32[1]{0:T(128)} custom-call(f32[3,128]{1,0:T(4,128)S(1)} %get-tuple-element.58.swap_cols_ref.here_ref, f32[3,128]{1,0:T(4,128)S(1)} %collective-permute-done.5.home_ref), custom_call_target="tpu_custom_call" | custom-call | tf_op jit(solution)/shard_map/pallas_call | solution.py:397
  41.9 0.8 %collective-permute-done.8 = f32[4,128]{1,0:T(4,128)S(1)} collective-permute-done((f32[4,128]{1,0:T(4,128)S(1)}, f32[4,128]{1,0:T(4,128)S(1)}, u32[]{:S(2)}, u32[]{:S(2)}) %collective-permute-start.8) | collective-permute-done | bytes 2080 | tf_op jit(solution)/shard_map/ppermute | solution.py:394
  42.7 0.0 copy-start.4
  42.7 0.6 %copy-done.4 = f32[512]{0:T(512)} copy-done((f32[512]{0:T(512)}, f32[512]{0:T(512)S(1)}, u32[]{:S(2)}) %copy-start.4) | copy-done | bytes 2072
  (9 shorter events, 0.1 us)
Async XLA Ops:
  0.0 9.8 %copy-start.3 = (s32[2048]{0:T(1024)S(1)}, s32[2048]{0:T(1024)}, u32[]{:S(2)}) copy-start(s32[2048]{0:T(1024)} %param.5) | copy-start | bytes 24580
  1.4 16.2 %collective-permute-start = (bf16[264,1024]{1,0:T(8,128)(2,1)S(1)}, bf16[264,1024]{1,0:T(8,128)(2,1)S(1)}, u32[]{:S(2)}, u32[]{:S(2)}) collective-permute-start(bf16[264,1024]{1,0:T(8,128)(2,1)S(1)} %get-tuple-element.54), channel_id=1, source_target_pairs={{4,8},{8,4},{5,9},{9,5},{6,10},{10,6},{7,11},{11,7},{20,24},{24,20... | collective-permute-start | bytes 1622024 | tf_op jit(solution)/shard_map/ppermute | solution.py:324
  2.1 20.2 %collective-permute-start.3 = (bf16[264,1024]{1,0:T(8,128)(2,1)S(1)}, bf16[264,1024]{1,0:T(8,128)(2,1)S(1)}, u32[]{:S(2)}, u32[]{:S(2)}) collective-permute-start(bf16[264,1024]{1,0:T(8,128)(2,1)S(1)} %get-tuple-element.54), channel_id=1, source_target_pairs={{0,4},{12,8},{1,5},{13,9},{2,6},{14,10},{3,7},{15,11},{16,20},{28,... | collective-permute-start | bytes 1622024 | tf_op jit(solution)/shard_map/ppermute | solution.py:323
  16.2 16.2 %collective-permute-start.1 = (bf16[264,1024]{1,0:T(8,128)(2,1)S(1)}, bf16[264,1024]{1,0:T(8,128)(2,1)S(1)}, u32[]{:S(2)}, u32[]{:S(2)}) collective-permute-start(bf16[264,1024]{1,0:T(8,128)(2,1)S(1)} %get-tuple-element.59), channel_id=1, source_target_pairs={{0,4},{12,8},{1,5},{13,9},{2,6},{14,10},{3,7},{15,11},{16,20},{28,... | collective-permute-start | bytes 1622024 | tf_op jit(solution)/shard_map/ppermute | solution.py:358
  17.6 15.4 %collective-permute-start.2 = (bf16[264,1024]{1,0:T(8,128)(2,1)S(1)}, bf16[264,1024]{1,0:T(8,128)(2,1)S(1)}, u32[]{:S(2)}, u32[]{:S(2)}) collective-permute-start(bf16[264,1024]{1,0:T(8,128)(2,1)S(1)} %collective-permute-done.piece_ref), channel_id=1, source_target_pairs={{4,0},{8,12},{5,1},{9,13},{6,2},{10,14},{7,3},{11,15},{20,16},{24,... | collective-permute-start | bytes 1622024 | tf_op jit(solution)/shard_map/ppermute | solution.py:325
  24.6 8.4 %collective-permute-start.4 = (f32[3,128]{1,0:T(4,128)S(1)}, f32[3,128]{1,0:T(4,128)S(1)}, u32[]{:S(2)}, u32[]{:S(2)}) collective-permute-start(f32[3,128]{1,0:T(4,128)S(1)} %get-tuple-element.62), channel_id=1, source_target_pairs={{4,0},{8,12},{5,1},{9,13},{6,2},{10,14},{7,3},{11,15},{20,16},{24,... | collective-permute-start | bytes 4616 | tf_op jit(solution)/shard_map/ppermute | solution.py:372
  25.9 11.3 %collective-permute-start.6 = (f32[3,128]{1,0:T(4,128)S(1)}, f32[3,128]{1,0:T(4,128)S(1)}, u32[]{:S(2)}, u32[]{:S(2)}) collective-permute-start(f32[3,128]{1,0:T(4,128)S(1)} %get-tuple-element.58.swap_cols_ref.here_ref), channel_id=1, source_target_pairs={{8,4},{4,8},{9,5},{5,9},{10,6},{6,10},{11,7},{7,11},{24,20},{20,24... | collective-permute-start | bytes 4616 | tf_op jit(solution)/shard_map/ppermute | solution.py:373
  35.3 3.6 %collective-permute-start.5 = (f32[3,128]{1,0:T(4,128)S(1)}, f32[3,128]{1,0:T(4,128)S(1)}, u32[]{:S(2)}, u32[]{:S(2)}) collective-permute-start(f32[3,128]{1,0:T(4,128)S(1)} %get-tuple-element.63), channel_id=1, source_target_pairs={{4,0},{8,12},{12,4},{0,8},{5,1},{9,13},{13,5},{1,9},{6,2},{10,14},... | collective-permute-start | bytes 4616 | tf_op jit(solution)/shard_map/ppermute | solution.py:384
  37.2 1.7 %collective-permute-start.7 = (f32[8,128]{1,0:T(8,128)S(1)}, f32[8,128]{1,0:T(8,128)S(1)}, u32[]{:S(2)}, u32[]{:S(2)}) collective-permute-start(f32[8,128]{1,0:T(8,128)S(1)} %get-tuple-element.66), channel_id=1, source_target_pairs={{0,1},{1,0},{2,3},{3,2},{4,5},{5,4},{6,7},{7,6},{8,9},{9,8},{10,11... | collective-permute-start | bytes 12296 | tf_op jit(solution)/shard_map/ppermute | solution.py:387
  39.0 3.7 %collective-permute-start.8 = (f32[4,128]{1,0:T(4,128)S(1)}, f32[4,128]{1,0:T(4,128)S(1)}, u32[]{:S(2)}, u32[]{:S(2)}) collective-permute-start(f32[4,128]{1,0:T(4,128)S(1)} %get-tuple-element.73), channel_id=1, source_target_pairs={{0,2},{1,3},{2,0},{3,1},{4,6},{5,7},{6,4},{7,5},{8,10},{9,11},{10,... | collective-permute-start | bytes 6152 | tf_op jit(solution)/shard_map/ppermute | solution.py:394
  42.7 0.6 %copy-start.4 = (f32[512]{0:T(512)}, f32[512]{0:T(512)S(1)}, u32[]{:S(2)}) copy-start(f32[512]{0:T(512)S(1)} %get-tuple-element.109) | copy-start | bytes 6148

commit v12 on v11

--- a/solution.py
+++ b/solution.py
@@ -18,7 +18,7 @@
 GAIN = inverse_temp * math.log2(math.e)
 OFF = -1000.0
 
-STEP = 512
+STEPS = (512, 256, 1024)
 COPY = 64
 
 
@@ -75,14 +75,8 @@
 
     first = list(copies(plan.first, first_ref, 1))
     second = list(copies(plan.second, second_ref, 1 + size // COPY))
-    for copy in [ids_copy] + first:
+    for copy in [ids_copy] + first + second:
         copy.start()
-
-    @pl.when(jnp.logical_not(plan.inner))
-    def _():
-        for copy in second:
-            copy.start()
-
     ids_copy.wait()
     depth = first_ref.shape[1]
     edge = jnp.max(ids[pl.ds(plan.edge, 1), :], axis=1, keepdims=True)
@@ -90,13 +84,8 @@
     for block, out in ((plan.first, first_ref), (plan.second, second_ref)):
         row = jnp.concatenate([ids[pl.ds(block + k, 1), :] for k in range(share)] + rest, axis=1)
         out[size:, :] = jnp.broadcast_to(row.astype(jnp.float32), (8, depth)).astype(jnp.bfloat16)
-    for copy in first:
+    for copy in first + second:
         copy.wait()
-
-    @pl.when(jnp.logical_not(plan.inner))
-    def _():
-        for copy in second:
-            copy.wait()
 
 
 def pack(size, subs, embeddings, by_block):
@@ -163,12 +152,12 @@
     return row[:, :size], row[:, size : size + BLOCK]
 
 
-def cross_terms(meta, chunk, column_tags, unit_ref, piece_unit, add_rows):
+def cross_terms(meta, chunk, column_tags, unit_ref, piece_unit, add_rows, step):
     size = column_tags.shape[1]
     columns = None
-    for start in range(0, meta.blocks * BLOCK, STEP):
-        cosine = products(unit_ref[start : start + STEP, :], piece_unit[...])
-        for inner in range(0, STEP, BLOCK):
+    for start in range(0, meta.blocks * BLOCK, step):
+        cosine = products(unit_ref[start : start + step, :], piece_unit[...])
+        for inner in range(0, step, BLOCK):
             block = (start + inner) // BLOCK
             bias = column_bias(meta.tag(block, chunk), column_tags)
             weight = jnp.exp2(cosine[inner : inner + BLOCK] * GAIN + bias)
@@ -194,7 +183,7 @@
     def add_rows(block, value):
         sums_ref[block : block + 1, :] = before_ref[block : block + 1, :] + value
 
-    cols = cross_terms(meta, chunk, tags, unit_ref, piece_unit, add_rows)
+    cols = cross_terms(meta, chunk, tags, unit_ref, piece_unit, add_rows, STEPS[chunk])
     for k in range(share):
         cols_ref[k : k + 1, :] = cols[k]
     mine = meta.tag(meta.number(EDGE)).astype(jnp.float32)
@@ -203,22 +192,13 @@
 
 
 def last_kernel(
-    blocks, share, width, meta_ref, unit_ref, inward_ref, relayed_ref, before_ref, outer_back_ref, swap_cols_ref,
+    blocks, share, width, meta_ref, unit_ref, piece_ref, before_ref, outer_back_ref, swap_cols_ref,
     keep_ref, send_ref, cols_ref, piece_unit, sums,
 ):
     meta = Meta(meta_ref, blocks)
     size = share * BLOCK
-    is_inner = meta.number(INNER) > 0
-
-    @pl.when(is_inner)
-    def _():
-        piece_unit[...] = normalised(inward_ref[:size, :])
-
-    @pl.when(jnp.logical_not(is_inner))
-    def _():
-        piece_unit[...] = normalised(relayed_ref[:size, :])
-
-    tags = jnp.where(is_inner, chunk_tags(inward_ref, size)[0], chunk_tags(relayed_ref, size)[0])
+    piece_unit[...] = normalised(piece_ref[:size, :])
+    tags, _ = chunk_tags(piece_ref, size)
 
     def place(block):
         owner = block // width
@@ -228,7 +208,7 @@
         at = place(block)
         sums[at : at + 1, :] = before_ref[block : block + 1, :] + value
 
-    cols = cross_terms(meta, 2, tags, unit_ref, piece_unit, add_rows)
+    cols = cross_terms(meta, 2, tags, unit_ref, piece_unit, add_rows, STEPS[2])
     for k in range(share):
         cols_ref[k : k + 1, :] = cols[k]
         at = place(meta.number(FIRST_BLOCK) + k)
@@ -320,9 +300,8 @@
 
     by_block = cluster_ids.reshape(blocks, BLOCK)
     first_out, second_out = pack(size, subs, embeddings, by_block)
+    from_inner = lax.ppermute(first_out, "tile", swap)
     from_outer = lax.ppermute(first_out, "tile", inward)
-    from_inner = lax.ppermute(first_out, "tile", swap)
-    relayed = lax.ppermute(from_inner, "tile", turned(inward))
 
     tag = jnp.max(by_block, axis=1)
     used = jnp.sum((by_block >= 0).astype(jnp.int32), axis=1)
@@ -355,7 +334,7 @@
         cost_estimate=pl.CostEstimate(flops=0, bytes_accessed=1024, transcendentals=0),
     )(meta, embeddings, lax.dynamic_slice_in_dim(cluster_ids, member * quarter, quarter, 0)[None])
     second_out, sums = lax.optimization_barrier((second_out, sums))
-    last = lax.ppermute(second_out, "tile", inward)
+    last = lax.ppermute(second_out, "tile", around)
 
     def middle(chunk, piece, before):
         return call(
@@ -367,15 +346,15 @@
             2 * rows * size * depth,
         )
 
-    sums, swap_cols = middle(1, from_inner, sums)
     sums, outer_cols = middle(0, from_outer, sums)
     outer_back = lax.ppermute(outer_cols, "tile", turned(inward))
+    sums, swap_cols = middle(1, from_inner, sums)
     swap_back = lax.ppermute(swap_cols, "tile", turned(swap))
     half = jax.ShapeDtypeStruct((heap, BLOCK), jnp.float32)
     held, leaving, cols = call(
         functools.partial(last_kernel, blocks, share, width),
         meta,
-        (unit, last, relayed, sums, outer_back, swap_cols),
+        (unit, last, sums, outer_back, swap_cols),
         [half, half, col_sums],
         [pltpu.VMEM((size, depth), jnp.bfloat16), pltpu.VMEM((blocks, BLOCK), jnp.float32)],
         2 * rows * size * depth,

time: 43.5 us -> 43.1 us (level)
  starting transfers between devices: 16.3 us -> 11.6 us
  waiting for transfers between devices: 10.1 us -> 14.6 us
    ppermute x1, starting transfers between devices: 7.57 us -> 4.96 us  [shards(): from_outer = lax.ppermute(first_out, 'tile', inward)]
    ppermute x1, waiting for transfers between devices: 1.19 us -> 3.15 us  [shards(): from_outer = lax.ppermute(first_out, 'tile', inward)]
    ppermute x1, starting transfers between devices: 1.9 us -> 0.28 us  [shards(): home = lax.ppermute(cols, 'tile', turned(around))]
    ppermute x1, waiting for transfers between devices: 1.73 us -> 3.35 us  [shards(): home = lax.ppermute(cols, 'tile', turned(around))]
    ppermute x2 -> x1, waiting for transfers between devices: 5.91 us -> 7.26 us  [shards(): last = lax.ppermute(second_out, 'tile', around)]
    ppermute x1, waiting for transfers between devices: 0.52 us -> 0.01 us  [shards(): outer_back = lax.ppermute(outer_cols, 'tile', turned(inward))]
    ppermute x2 -> x1, starting transfers between devices: 2.62 us -> 2.2 us  [shards(): last = lax.ppermute(second_out, 'tile', around)]
  transfers between devices with their start and end apart: 9 -> 8, of which waited for: 5 -> 4; matrix products, arithmetic and copies ran while one was open for 1% -> 1% of each run, Pallas kernels for 31% -> 31%
where the time goes in v12:
time: 43.1 us; the launch traced here: 42.9 us
  Pallas kernels  14.8 us (34%)
  waiting for transfers between devices  14.6 us (34%)
  starting transfers between devices  11.6 us (27%)
  between operations  0.91 us (2%)
  local copies, waits for them, and re-layouts  0.81 us (2%)
    ppermute x1, waiting for transfers between devices, shards(): last = lax.ppermute(second_out, 'tile', around)  7.26 us
    pallas_call x3, Pallas kernels, call(): pl.pallas_call(kernel, in_specs=[smem] + [vmem] * len(operands), out_spec...  6.78 us
    pallas_call x1, Pallas kernels, shards(): pl.pallas_call(functools.partial(self_kernel, blocks, subs), in_specs=[sm...  6.05 us
    ppermute x1, starting transfers between devices, shards(): from_outer = lax.ppermute(first_out, 'tile', inward)  4.96 us
    ppermute x1, waiting for transfers between devices, shards(): home = lax.ppermute(cols, 'tile', turned(around))  3.35 us
    ppermute x1, waiting for transfers between devices, shards(): from_outer = lax.ppermute(first_out, 'tile', inward)  3.15 us
    ppermute x1, starting transfers between devices, shards(): last = lax.ppermute(second_out, 'tile', around)  2.2 us
    ppermute x1, starting transfers between devices, shards(): lax.ppermute(leaving, 'sub', [(i, i ^ 1 << bit) for i in range(subs)])  1.55 us
  transfers between devices with their start and end apart: 8, of which 4 were waited for; matrix products, arithmetic and copies ran while one was open for 1% of the time, Pallas kernels for 31%

profile of v12, /device:TPU:0, one launch (start us, length us, event | category | flops | bytes accessed | tf_op | source)
XLA Modules:
  0.0 42.9 jit_solution(2283239107697099023)
XLA Ops:
  0.0 0.0 copy-start.3
  0.0 1.4 %shard_map.31 = (bf16[264,1024]{1,0:T(8,128)(2,1)S(1)}, bf16[264,1024]{1,0:T(8,128)(2,1)S(1)}) custom-call(bf16[2048,1024]{1,0:T(8,128)(2,1)} %rows_ref.3, s32[16,128]{1,0:T(8,128)} %bitcast.58), custom_call_target="tpu_custom_call" | custom-call | bytes 1024 | tf_op jit(solution)/shard_map/pallas_call | solution.py:92
  1.4 5.0 %collective-permute-start.1 = (bf16[264,1024]{1,0:T(8,128)(2,1)S(1)}, bf16[264,1024]{1,0:T(8,128)(2,1)S(1)}, u32[]{:S(2)}, u32[]{:S(2)}) collective-permute-start(bf16[264,1024]{1,0:T(8,128)(2,1)S(1)} %get-tuple-element.54), channel_id=1, source_target_pairs={{0,4},{12,8},{1,5},{13,9},{2,6},{14,10},{3,7},{15,11},{16,20},{28,... | collective-permute-start | bytes 1622024 | tf_op jit(solution)/shard_map/ppermute | solution.py:304
  6.4 0.7 %collective-permute-start = (bf16[264,1024]{1,0:T(8,128)(2,1)S(1)}, bf16[264,1024]{1,0:T(8,128)(2,1)S(1)}, u32[]{:S(2)}, u32[]{:S(2)}) collective-permute-start(bf16[264,1024]{1,0:T(8,128)(2,1)S(1)} %get-tuple-element.54), channel_id=1, source_target_pairs={{4,8},{8,4},{5,9},{9,5},{6,10},{10,6},{7,11},{11,7},{20,24},{24,20... | collective-permute-start | bytes 1622024 | tf_op jit(solution)/shard_map/ppermute | solution.py:303
  7.1 0.0 copy-done.3
  7.1 0.1 convert_reduce_fusion
  7.3 0.1 dynamic_slice.47
  7.4 0.1 concatenate.3.meta_ref
  7.5 0.1 broadcast_in_dim.128
  7.6 6.0 %shard_map.30 = (bf16[2048,1024]{1,0:T(8,128)(2,1)S(1)}, f32[16,128]{1,0:T(8,128)S(1)}) custom-call(s32[84]{0:T(128)S(1)} %concatenate.3.meta_ref, bf16[2048,1024]{1,0:T(8,128)(2,1)} %rows_ref.3, s32[1,512]{1,0:T(1,128)S(1)} %bitcast.57), custom_call_target="tpu_custom_call" | custom-call | bytes 1024 | tf_op jit(solution)/shard_map/pallas_call | solution.py:327
  13.6 2.2 %collective-permute-start.2 = (bf16[264,1024]{1,0:T(8,128)(2,1)S(1)}, bf16[264,1024]{1,0:T(8,128)(2,1)S(1)}, u32[]{:S(2)}, u32[]{:S(2)}) collective-permute-start(bf16[264,1024]{1,0:T(8,128)(2,1)S(1)} %get-tuple-element.60), channel_id=1, source_target_pairs={{0,4},{12,8},{4,12},{8,0},{1,5},{13,9},{5,13},{9,1},{2,6},{14,10},... | collective-permute-start | bytes 1622024 | tf_op jit(solution)/shard_map/ppermute | solution.py:337
  15.8 3.1 %collective-permute-done.1.piece_ref = bf16[264,1024]{1,0:T(8,128)(2,1)S(1)} collective-permute-done((bf16[264,1024]{1,0:T(8,128)(2,1)S(1)}, bf16[264,1024]{1,0:T(8,128)(2,1)S(1)}, u32[]{:S(2)}, u32[]{:S(2)}) %collective-permute-start.1) | collective-permute-done | bytes 540704 | tf_op jit(solution)/shard_map/ppermute | solution.py:304
  19.0 2.2 %shard_map.32 = (f32[16,128]{1,0:T(8,128)S(1)}, f32[3,128]{1,0:T(4,128)S(1)}) custom-call(s32[84]{0:T(128)S(1)} %concatenate.3.meta_ref, bf16[2048,1024]{1,0:T(8,128)(2,1)S(1)} %get-tuple-element.53.unit_ref, bf16[264,1024]{1,0:T(8,128)(2,1)S(1)} %collective-permute-done.1.piece_ref, f32[16,128]{1,0:T(8,128)S(1)} %get-tuple-element.57.before_ref), custom_call_target="tpu_custom_call" | custom-call | flops 1073741824 | bytes 1024 | tf_op jit(solution)/shard_map/pallas_call | solution.py:230
  21.2 1.3 %collective-permute-start.3 = (f32[3,128]{1,0:T(4,128)S(1)}, f32[3,128]{1,0:T(4,128)S(1)}, u32[]{:S(2)}, u32[]{:S(2)}) collective-permute-start(f32[3,128]{1,0:T(4,128)S(1)} %get-tuple-element.62), channel_id=1, source_target_pairs={{4,0},{8,12},{5,1},{9,13},{6,2},{10,14},{7,3},{11,15},{20,16},{24,... | collective-permute-start | bytes 4616 | tf_op jit(solution)/shard_map/ppermute | solution.py:350
  22.5 0.0 collective-permute-done.piece_ref
  22.5 2.2 %shard_map.33 = (f32[16,128]{1,0:T(8,128)S(1)}, f32[3,128]{1,0:T(4,128)S(1)}) custom-call(s32[84]{0:T(128)S(1)} %concatenate.3.meta_ref, bf16[2048,1024]{1,0:T(8,128)(2,1)S(1)} %get-tuple-element.53.unit_ref, bf16[264,1024]{1,0:T(8,128)(2,1)S(1)} %collective-permute-done.piece_ref, f32[16,128]{1,0:T(8,128)S(1)} %get-tuple-element.58.before_ref), custom_call_target="tpu_custom_call" | custom-call | flops 1073741824 | bytes 1024 | tf_op jit(solution)/shard_map/pallas_call | solution.py:230
  24.8 0.7 %collective-permute-start.5 = (f32[3,128]{1,0:T(4,128)S(1)}, f32[3,128]{1,0:T(4,128)S(1)}, u32[]{:S(2)}, u32[]{:S(2)}) collective-permute-start(f32[3,128]{1,0:T(4,128)S(1)} %get-tuple-element.59.swap_cols_ref.here_ref), channel_id=1, source_target_pairs={{8,4},{4,8},{9,5},{5,9},{10,6},{6,10},{11,7},{7,11},{24,20},{20,24... | collective-permute-start | bytes 4616 | tf_op jit(solution)/shard_map/ppermute | solution.py:352
  25.4 7.3 %collective-permute-done.2.piece_ref = bf16[264,1024]{1,0:T(8,128)(2,1)S(1)} collective-permute-done((bf16[264,1024]{1,0:T(8,128)(2,1)S(1)}, bf16[264,1024]{1,0:T(8,128)(2,1)S(1)}, u32[]{:S(2)}, u32[]{:S(2)}) %collective-permute-start.2) | collective-permute-done | bytes 540704 | tf_op jit(solution)/shard_map/ppermute | solution.py:337
  32.7 0.0 collective-permute-done.3.outer_back_ref
  32.7 2.3 %shard_map.34 = (f32[8,128]{1,0:T(8,128)S(1)}, f32[8,128]{1,0:T(8,128)S(1)}, f32[3,128]{1,0:T(4,128)S(1)}) custom-call(s32[84]{0:T(128)S(1)} %concatenate.3.meta_ref, bf16[2048,1024]{1,0:T(8,128)(2,1)S(1)} %get-tuple-element.53.unit_ref, bf16[264,1024]{1,0:T(8,128)(2,1)S(1)} %collective-permute-done.2.piece_ref, f32[16,128]{1,0:T(8,128)S(1)} %get-tuple-element.61.before_ref, ...), custom_call_target="tpu_custom_call" | custom-call | flops 1073741824 | bytes 1024 | tf_op jit(solution)/shard_map/pallas_call | solution.py:230
  35.0 0.3 collective-permute-start.4
  35.3 0.0 collective-permute-start.6
  35.3 0.0 collective-permute-done.5
  35.3 3.3 %collective-permute-done.4.home_ref = f32[3,128]{1,0:T(4,128)S(1)} collective-permute-done((f32[3,128]{1,0:T(4,128)S(1)}, f32[3,128]{1,0:T(4,128)S(1)}, u32[]{:S(2)}, u32[]{:S(2)}) %collective-permute-start.4) | collective-permute-done | bytes 1568 | tf_op jit(solution)/shard_map/ppermute | solution.py:363
  38.7 0.0 collective-permute-done.6
  38.7 1.6 %collective-permute-start.7 = (f32[4,128]{1,0:T(4,128)S(1)}, f32[4,128]{1,0:T(4,128)S(1)}, u32[]{:S(2)}, u32[]{:S(2)}) collective-permute-start(f32[4,128]{1,0:T(4,128)S(1)} %get-tuple-element.73), channel_id=1, source_target_pairs={{0,2},{1,3},{2,0},{3,1},{4,6},{5,7},{6,4},{7,5},{8,10},{9,11},{10,... | collective-permute-start | bytes 6152 | tf_op jit(solution)/shard_map/ppermute | solution.py:373
  40.2 0.6 %shard_map.35 = s32[1]{0:T(128)} custom-call(f32[3,128]{1,0:T(4,128)S(1)} %get-tuple-element.59.swap_cols_ref.here_ref, f32[3,128]{1,0:T(4,128)S(1)} %collective-permute-done.4.home_ref), custom_call_target="tpu_custom_call" | custom-call | tf_op jit(solution)/shard_map/pallas_call | solution.py:376
  41.5 0.8 %collective-permute-done.7 = f32[4,128]{1,0:T(4,128)S(1)} collective-permute-done((f32[4,128]{1,0:T(4,128)S(1)}, f32[4,128]{1,0:T(4,128)S(1)}, u32[]{:S(2)}, u32[]{:S(2)}) %collective-permute-start.7) | collective-permute-done | bytes 2080 | tf_op jit(solution)/shard_map/ppermute | solution.py:373
  42.4 0.0 copy-start.4
  42.4 0.6 %copy-done.4 = f32[512]{0:T(512)} copy-done((f32[512]{0:T(512)}, f32[512]{0:T(512)S(1)}, u32[]{:S(2)}) %copy-start.4) | copy-done | bytes 2072
  (9 shorter events, 0.0 us)
Async XLA Ops:
  0.0 7.1 %copy-start.3 = (s32[2048]{0:T(1024)S(1)}, s32[2048]{0:T(1024)}, u32[]{:S(2)}) copy-start(s32[2048]{0:T(1024)} %param.5) | copy-start | bytes 24580
  1.4 17.6 %collective-permute-start.1 = (bf16[264,1024]{1,0:T(8,128)(2,1)S(1)}, bf16[264,1024]{1,0:T(8,128)(2,1)S(1)}, u32[]{:S(2)}, u32[]{:S(2)}) collective-permute-start(bf16[264,1024]{1,0:T(8,128)(2,1)S(1)} %get-tuple-element.54), channel_id=1, source_target_pairs={{0,4},{12,8},{1,5},{13,9},{2,6},{14,10},{3,7},{15,11},{16,20},{28,... | collective-permute-start | bytes 1622024 | tf_op jit(solution)/shard_map/ppermute | solution.py:304
  6.4 16.2 %collective-permute-start = (bf16[264,1024]{1,0:T(8,128)(2,1)S(1)}, bf16[264,1024]{1,0:T(8,128)(2,1)S(1)}, u32[]{:S(2)}, u32[]{:S(2)}) collective-permute-start(bf16[264,1024]{1,0:T(8,128)(2,1)S(1)} %get-tuple-element.54), channel_id=1, source_target_pairs={{4,8},{8,4},{5,9},{9,5},{6,10},{10,6},{7,11},{11,7},{20,24},{24,20... | collective-permute-start | bytes 1622024 | tf_op jit(solution)/shard_map/ppermute | solution.py:303
  13.6 19.0 %collective-permute-start.2 = (bf16[264,1024]{1,0:T(8,128)(2,1)S(1)}, bf16[264,1024]{1,0:T(8,128)(2,1)S(1)}, u32[]{:S(2)}, u32[]{:S(2)}) collective-permute-start(bf16[264,1024]{1,0:T(8,128)(2,1)S(1)} %get-tuple-element.60), channel_id=1, source_target_pairs={{0,4},{12,8},{4,12},{8,0},{1,5},{13,9},{5,13},{9,1},{2,6},{14,10},... | collective-permute-start | bytes 1622024 | tf_op jit(solution)/shard_map/ppermute | solution.py:337
  21.2 11.5 %collective-permute-start.3 = (f32[3,128]{1,0:T(4,128)S(1)}, f32[3,128]{1,0:T(4,128)S(1)}, u32[]{:S(2)}, u32[]{:S(2)}) collective-permute-start(f32[3,128]{1,0:T(4,128)S(1)} %get-tuple-element.62), channel_id=1, source_target_pairs={{4,0},{8,12},{5,1},{9,13},{6,2},{10,14},{7,3},{11,15},{20,16},{24,... | collective-permute-start | bytes 4616 | tf_op jit(solution)/shard_map/ppermute | solution.py:350
  24.8 10.5 %collective-permute-start.5 = (f32[3,128]{1,0:T(4,128)S(1)}, f32[3,128]{1,0:T(4,128)S(1)}, u32[]{:S(2)}, u32[]{:S(2)}) collective-permute-start(f32[3,128]{1,0:T(4,128)S(1)} %get-tuple-element.59.swap_cols_ref.here_ref), channel_id=1, source_target_pairs={{8,4},{4,8},{9,5},{5,9},{10,6},{6,10},{11,7},{7,11},{24,20},{20,24... | collective-permute-start | bytes 4616 | tf_op jit(solution)/shard_map/ppermute | solution.py:352
  35.0 3.6 %collective-permute-start.4 = (f32[3,128]{1,0:T(4,128)S(1)}, f32[3,128]{1,0:T(4,128)S(1)}, u32[]{:S(2)}, u32[]{:S(2)}) collective-permute-start(f32[3,128]{1,0:T(4,128)S(1)} %get-tuple-element.63), channel_id=1, source_target_pairs={{4,0},{8,12},{12,4},{0,8},{5,1},{9,13},{13,5},{1,9},{6,2},{10,14},... | collective-permute-start | bytes 4616 | tf_op jit(solution)/shard_map/ppermute | solution.py:363
  35.3 3.4 %collective-permute-start.6 = (f32[8,128]{1,0:T(8,128)S(1)}, f32[8,128]{1,0:T(8,128)S(1)}, u32[]{:S(2)}, u32[]{:S(2)}) collective-permute-start(f32[8,128]{1,0:T(8,128)S(1)} %get-tuple-element.66), channel_id=1, source_target_pairs={{0,1},{1,0},{2,3},{3,2},{4,5},{5,4},{6,7},{7,6},{8,9},{9,8},{10,11... | collective-permute-start | bytes 12296 | tf_op jit(solution)/shard_map/ppermute | solution.py:366
  38.7 3.7 %collective-permute-start.7 = (f32[4,128]{1,0:T(4,128)S(1)}, f32[4,128]{1,0:T(4,128)S(1)}, u32[]{:S(2)}, u32[]{:S(2)}) collective-permute-start(f32[4,128]{1,0:T(4,128)S(1)} %get-tuple-element.73), channel_id=1, source_target_pairs={{0,2},{1,3},{2,0},{3,1},{4,6},{5,7},{6,4},{7,5},{8,10},{9,11},{10,... | collective-permute-start | bytes 6152 | tf_op jit(solution)/shard_map/ppermute | solution.py:373
  42.4 0.6 %copy-start.4 = (f32[512]{0:T(512)}, f32[512]{0:T(512)S(1)}, u32[]{:S(2)}) copy-start(f32[512]{0:T(512)S(1)} %get-tuple-element.107) | copy-start | bytes 6148

commit v13 on v10

--- a/solution.py
+++ b/solution.py
@@ -56,81 +56,70 @@
         near = (dealt // width * 2 + member % 2) * width + dealt % width
         near = jnp.where(part == 1, blocks // 2, 0) + near
         self.first = jnp.where(self.inner, near, member * width)
-        self.second = jnp.where(self.inner, near, member * width + share)
+        self.second = member * width + share
         self.edge = jnp.where(part == 1, blocks // 2 - 1, blocks // 2)
         self.width, self.share = width, share
 
 
-def pack_kernel(blocks, subs, rows_ref, ids_ref, *refs):
-    outs, (ids, sems) = refs[:5], refs[5:]
+def pack_kernel(blocks, subs, rows_ref, ids_ref, first_ref, second_ref, low_ref, high_ref, ids, sems):
     plan = Plan(blocks, subs, lax.axis_index("tile"), lax.axis_index("sub"))
     share, size = plan.share, plan.share * BLOCK
-    first_low, first_high, swapped, second_low, second_high = outs
     ids_copy = pltpu.make_async_copy(ids_ref, ids, sems.at[0])
     ids_copy.start()
 
     def copies(block, parts, sem):
-        made, down = [], 0
+        down = 0
         for part, count in parts:
             for at in range(0, count, COPY):
                 start = pl.multiple_of(block * BLOCK + down, COPY)
-                made.append(
-                    pltpu.make_async_copy(
-                        rows_ref.at[pl.ds(start, COPY), :], part.at[pl.ds(at, COPY), :], sems.at[sem + len(made)]
-                    )
+                yield pltpu.make_async_copy(
+                    rows_ref.at[pl.ds(start, COPY), :], part.at[pl.ds(at, COPY), :], sems.at[sem + down // COPY]
                 )
                 down += COPY
-        return made
-
-    count = size // COPY
-    first = copies(plan.first, ((first_low, size // 2), (first_high, size // 2)), 1)
-    swap = copies(plan.first, ((swapped, size),), 1)
-    second = copies(plan.second, ((second_low, size // 2), (second_high, size // 2)), 1 + count)
+
+    near = list(copies(plan.first, ((low_ref, size // 2), (high_ref, size // 2)), 1))
+    outer = list(copies(plan.first, ((first_ref, size),), 1))
+    outer += list(copies(plan.second, ((second_ref, size),), 1 + size // COPY))
 
     @pl.when(plan.inner)
     def _():
-        for copy in swap:
+        for copy in near:
             copy.start()
 
     @pl.when(jnp.logical_not(plan.inner))
     def _():
-        for copy in first:
+        for copy in outer:
             copy.start()
 
-    for copy in second:
-        copy.start()
     ids_copy.wait()
-    depth = swapped.shape[1]
+    depth = first_ref.shape[1]
     edge = jnp.max(ids[pl.ds(plan.edge, 1), :], axis=1, keepdims=True)
     rest = [jnp.broadcast_to(edge, (1, BLOCK)), jnp.zeros((1, depth - size - BLOCK), jnp.int32)]
-    for block, parts in ((plan.first, (first_high, swapped)), (plan.second, (second_high,))):
+    for block, outs in ((plan.first, (first_ref, high_ref)), (plan.second, (second_ref,))):
         row = jnp.concatenate([ids[pl.ds(block + k, 1), :] for k in range(share)] + rest, axis=1)
         row = jnp.broadcast_to(row.astype(jnp.float32), (8, depth)).astype(jnp.bfloat16)
-        for part in parts:
-            part[part.shape[0] - 8 :, :] = row
+        for out in outs:
+            out[out.shape[0] - 8 :, :] = row
 
     @pl.when(plan.inner)
     def _():
-        for copy in swap:
+        for copy in near:
             copy.wait()
 
     @pl.when(jnp.logical_not(plan.inner))
     def _():
-        for copy in first:
+        for copy in outer:
             copy.wait()
-
-    for copy in second:
-        copy.wait()
 
 
 def pack(size, subs, embeddings, by_block):
     depth = embeddings.shape[1]
-    parts = (size // 2, size // 2 + 8, size + 8, size // 2, size // 2 + 8)
+    counts = (size + 8, size + 8, size // 2, size // 2 + 8)
     return pl.pallas_call(
         functools.partial(pack_kernel, by_block.shape[0], subs),
         in_specs=[pl.BlockSpec(memory_space=pl.ANY)] * 2,
-        out_specs=[pl.BlockSpec(memory_space=pltpu.VMEM)] * 5,
-        out_shape=[jax.ShapeDtypeStruct((count, depth), jnp.bfloat16) for count in parts],
+        out_specs=[pl.BlockSpec(memory_space=pltpu.VMEM)] * len(counts),
+        out_shape=[jax.ShapeDtypeStruct((count, depth), jnp.bfloat16) for count in counts],
         scratch_shapes=[pltpu.VMEM(by_block.shape, jnp.int32), pltpu.SemaphoreType.DMA((2 * size // COPY + 1,))],
         compiler_params=pltpu.CompilerParams(vmem_limit_bytes=8 * 1024 * 1024),
         cost_estimate=pl.CostEstimate(flops=0, bytes_accessed=1024, transcendentals=0),
@@ -151,7 +140,7 @@
         return self.ref[5 * self.blocks + index]
 
 
-MEMBER, FIRST_BLOCK, EDGE, INNER = range(4)
+MEMBER, EDGE, INNER = range(3)
 
 
 def self_kernel(blocks, subs, meta_ref, rows_ref, tags_ref, unit_ref, sums_ref, held, sems):
@@ -184,14 +173,16 @@
             sums_ref[pl.ds(block, 1), :] = lane_sums(jnp.where(keep, weight, 0.0))
 
 
-def unit_chunk(parts, piece_unit):
-    size = piece_unit.shape[0]
+def take_chunk(parts, piece_unit):
     down = 0
     for part in parts:
         count = part.shape[0] // 16 * 16
         piece_unit[down : down + count, :] = normalised(part[:count, :])
         down += count
-    row = parts[-1][count : count + 8, :].astype(jnp.float32)[0:1, :]
+
+
+def chunk_tags(parts, size):
+    row = parts[-1][parts[-1].shape[0] - 8 :, :].astype(jnp.float32)[0:1, :]
     return row[:, :size], row[:, size : size + BLOCK]
 
 
@@ -218,7 +209,8 @@
 def middle_kernel(blocks, share, chunk, meta_ref, unit_ref, *refs):
     *parts, before_ref, sums_ref, cols_ref, piece_unit = refs
     meta = Meta(meta_ref, blocks)
-    tags, edge = unit_chunk(parts, piece_unit)
+    take_chunk(parts, piece_unit)
+    tags, edge = chunk_tags(parts, share * BLOCK)
 
     def add_rows(block, value):
         sums_ref[block : block + 1, :] = before_ref[block : block + 1, :] + value
@@ -232,11 +224,22 @@
 
 
 def last_kernel(
-    blocks, share, width, meta_ref, unit_ref, low_ref, high_ref, before_ref, outer_back_ref, swap_cols_ref,
+    blocks, share, width, meta_ref, unit_ref, inward_ref, low_ref, high_ref, before_ref, outer_cols_ref, swap_cols_ref,
     keep_ref, send_ref, cols_ref, piece_unit, sums,
 ):
     meta = Meta(meta_ref, blocks)
-    tags, _ = unit_chunk((low_ref, high_ref), piece_unit)
+    size = share * BLOCK
+    is_inner = meta.number(INNER) > 0
+
+    @pl.when(is_inner)
+    def _():
+        take_chunk((inward_ref,), piece_unit)
+
+    @pl.when(jnp.logical_not(is_inner))
+    def _():
+        take_chunk((low_ref, high_ref), piece_unit)
+
+    tags = jnp.where(is_inner, chunk_tags((inward_ref,), size)[0], chunk_tags((low_ref, high_ref), size)[0])
 
     def place(block):
         owner = block // width
@@ -248,10 +251,9 @@
 
     cols = cross_terms(meta, 2, tags, unit_ref, piece_unit, add_rows)
     for k in range(share):
-        cols_ref[k : k + 1, :] = cols[k]
-        at = place(meta.number(FIRST_BLOCK) + k)
-        sums[pl.ds(at, 1), :] += outer_back_ref[k : k + 1, :]
-    cols_ref[share : share + 1, :] = swap_cols_ref[share : share + 1, :]
+        cols_ref[k : k + 1, :] = jnp.where(is_inner, outer_cols_ref[k : k + 1, :], cols[k])
+        cols_ref[share + k : share + k + 1, :] = jnp.where(is_inner, cols[k], 0.0)
+    cols_ref[2 * share : 2 * share + 1, :] = swap_cols_ref[share : share + 1, :]
     parity = meta.number(MEMBER) % 2
     heap = blocks // 2
     keep_ref[...] = sums[pl.ds(pl.multiple_of(parity * heap, heap), heap), :]
@@ -259,11 +261,11 @@
 
 
 def flag_kernel(share, here_ref, home_ref, flag_ref):
-    flags = jnp.maximum(here_ref[share : share + 1, :], home_ref[share : share + 1, :])
+    flags = jnp.maximum(here_ref[share : share + 1, :], home_ref[2 * share : 2 * share + 1, :])
     flag_ref[0] = jnp.max(flags).astype(jnp.int32)
 
 
-def call(kernel, meta, operands, out_shapes, scratch, flops):
+def call(kernel, meta, operands, out_shapes, scratch):
     vmem, smem = pl.BlockSpec(memory_space=pltpu.VMEM), pl.BlockSpec(memory_space=pltpu.SMEM)
     return pl.pallas_call(
         kernel,
@@ -272,7 +274,7 @@
         out_shape=out_shapes,
         scratch_shapes=scratch,
         compiler_params=pltpu.CompilerParams(vmem_limit_bytes=16 * 1024 * 1024),
-        cost_estimate=pl.CostEstimate(flops=flops, bytes_accessed=1024, transcendentals=0),
+        cost_estimate=pl.CostEstimate(flops=0, bytes_accessed=1024, transcendentals=0),
     )(meta, *operands)
 
 
@@ -337,26 +339,27 @@
         return [(b, a) for a, b in route]
 
     by_block = cluster_ids.reshape(blocks, BLOCK)
-    first_low, first_high, swapped, second_low, second_high = pack(size, subs, embeddings, by_block)
-    from_inner = lax.ppermute(swapped, "tile", swap)
-    from_outer = [lax.ppermute(out, "tile", inward) for out in (first_high, first_low)][::-1]
+    first_out, second_out, low_out, high_out = pack(size, subs, embeddings, by_block)
+    from_outer = lax.ppermute(first_out, "tile", inward)
 
     tag = jnp.max(by_block, axis=1)
     used = jnp.sum((by_block >= 0).astype(jnp.int32), axis=1)
     seen = jnp.where(inner, tag, -2)
     swapped = jnp.where(plan.far & (jnp.arange(blocks) >= blocks // 2), -2, seen)
-    numbers = jnp.stack([member, plan.first, plan.edge, inner])
+    numbers = jnp.stack([member, plan.edge, inner])
     meta = jnp.concatenate([tag, used, seen, swapped, tag, numbers]).astype(jnp.int32)
 
     heap = blocks // 2
-    owner = plan.second // width
-    home_row = jnp.arange(heap)[:, None] - (owner // 2 * width + plan.second % width)
+    owner = plan.first // width
+    home_row = jnp.arange(heap)[:, None] - (owner // 2 * width + plan.first % width)
     home_row = jnp.broadcast_to(home_row, (heap, BLOCK)).astype(jnp.int32)
     upper = [
         jnp.broadcast_to((member >> bit) & 1, (heap >> bit, BLOCK)).astype(jnp.int32)
         for bit in range(1, subs.bit_length() - 1)
     ]
-    meta, home_row, *upper = lax.optimization_barrier((meta, home_row, *upper))
+    meta, home_row, low_out, high_out, *upper = lax.optimization_barrier((meta, home_row, low_out, high_out, *upper))
+    near_high = lax.ppermute(high_out, "tile", swap)
+    near_low = lax.ppermute(low_out, "tile", swap)
 
     row_sums = jax.ShapeDtypeStruct((blocks, BLOCK), jnp.float32)
     col_sums = jax.ShapeDtypeStruct((share + 1, BLOCK), jnp.float32)
@@ -371,8 +374,9 @@
         compiler_params=pltpu.CompilerParams(vmem_limit_bytes=24 * 1024 * 1024),
         cost_estimate=pl.CostEstimate(flops=0, bytes_accessed=1024, transcendentals=0),
     )(meta, embeddings, lax.dynamic_slice_in_dim(cluster_ids, member * quarter, quarter, 0)[None])
-    second_low, second_high, sums = lax.optimization_barrier((second_low, second_high, sums))
-    last = [lax.ppermute(out, "tile", around) for out in (second_low, second_high)]
+    second_out, near_low, sums = lax.optimization_barrier((second_out, near_low, sums))
+    relayed_low = lax.ppermute(near_low, "tile", turned(inward))
+    last = lax.ppermute(second_out, "tile", inward)
 
     def middle(chunk, parts, before):
         return call(
@@ -381,26 +385,27 @@
             (unit, *parts, before),
             [row_sums, col_sums],
             [pltpu.VMEM((size, depth), jnp.bfloat16)],
-            2 * rows * size * depth,
         )
 
-    sums, outer_cols = middle(0, from_outer, sums)
-    outer_back = lax.ppermute(outer_cols, "tile", turned(inward))
-    sums, swap_cols = middle(1, (from_inner,), sums)
+    sums, outer_cols = middle(0, (from_outer,), sums)
+    near_high, relayed_low, sums = lax.optimization_barrier((near_high, relayed_low, sums))
+    relayed_high = lax.ppermute(near_high, "tile", turned(inward))
+    sums, swap_cols = middle(1, (near_low, near_high), sums)
     swap_back = lax.ppermute(swap_cols, "tile", turned(swap))
+    swap_back, sums = lax.optimization_barrier((swap_back, sums))
     half = jax.ShapeDtypeStruct((heap, BLOCK), jnp.float32)
     held, leaving, cols = call(
         functools.partial(last_kernel, blocks, share, width),
         meta,
-        (unit, *last, sums, outer_back, swap_cols),
-        [half, half, col_sums],
+        (unit, last, relayed_low, relayed_high, sums, outer_cols, swap_cols),
+        [half, half, jax.ShapeDtypeStruct((2 * share + 1, BLOCK), jnp.float32)],
         [pltpu.VMEM((size, depth), jnp.bfloat16), pltpu.VMEM((blocks, BLOCK), jnp.float32)],
-        2 * rows * size * depth,
     )
 
     home = lax.ppermute(cols, "tile", turned(around))
-    for k in range(share):
-        held = held + jnp.where(home_row == k, home[k : k + 1] + swap_back[k : k + 1], 0.0)
+    for k in range(2 * share):
+        came = home[k : k + 1] + swap_back[k : k + 1] if k < share else home[k : k + 1]
+        held = held + jnp.where(home_row == k, came, 0.0)
     held = held + lax.ppermute(leaving, "sub", [(i, i ^ 1) for i in range(subs)])
     home, held = lax.optimization_barrier((home, held))
     for bit, mine in enumerate(upper, 1):

time: 44.4 us -> 45.9 us (1.034)
  starting transfers between devices: 13.7 us -> 20.4 us
  waiting for transfers between devices: 13.8 us -> 8.48 us
    ppermute x1, starting transfers between devices: 0.05 us -> 3.65 us  [shards(): home = lax.ppermute(cols, 'tile', turned(around))]
    ppermute x6, starting transfers between devices: 11.3 us -> 14.5 us  [the longest x1 5.79 us: shards(): last = lax.ppermute(second_out, 'tile', inward)]
    ppermute x6, waiting for transfers between devices: 9.49 us -> 6.36 us  [the longest x1 2.93 us: shards(): last = lax.ppermute(second_out, 'tile', inward)]
    ppermute x1, waiting for transfers between devices: 3.48 us -> 1.33 us  [shards(): home = lax.ppermute(cols, 'tile', turned(around))]
  transfers between devices with their start and end apart: 10 -> 10, of which waited for: 4 -> 5; matrix products, arithmetic and copies ran while one was open for 1% -> 1% of each run, Pallas kernels for 30% -> 25%
where the time goes in v13:
time: 45.9 us; the launch traced here: 45.7 us
  starting transfers between devices  20.4 us (44%)
  Pallas kernels  14.9 us (32%)
  waiting for transfers between devices  8.48 us (18%)
  between operations  0.97 us (2%)
  local copies, waits for them, and re-layouts  0.81 us (2%)
    pallas_call x3, Pallas kernels, call(): pl.pallas_call(kernel, in_specs=[smem] + [vmem] * len(operands), out_spec...  6.84 us
    pallas_call x1, Pallas kernels, shards(): pl.pallas_call(functools.partial(self_kernel, blocks, subs), in_specs=[sm...  6.05 us
    ppermute x1, starting transfers between devices, shards(): last = lax.ppermute(second_out, 'tile', inward)  5.79 us
    ppermute x1, starting transfers between devices, shards(): from_outer = lax.ppermute(first_out, 'tile', inward)  4.78 us
    ppermute x1, starting transfers between devices, shards(): home = lax.ppermute(cols, 'tile', turned(around))  3.65 us
    ppermute x1, waiting for transfers between devices, shards(): last = lax.ppermute(second_out, 'tile', inward)  2.93 us
    ppermute x1, waiting for transfers between devices, shards(): relayed_high = lax.ppermute(near_high, 'tile', turned(inward))  1.93 us
    ppermute x1, starting transfers between devices, shards(): lax.ppermute(leaving, 'sub', [(i, i ^ 1 << bit) for i in range(subs)])  1.57 us
  transfers between devices with their start and end apart: 10, of which 5 were waited for; matrix products, arithmetic and copies ran while one was open for 1% of the time, Pallas kernels for 25%

profile of v13, /device:TPU:0, one launch (start us, length us, event | category | flops | bytes accessed | tf_op | source)
XLA Modules:
  0.0 45.7 jit_solution(14323991901367859653)
XLA Ops:
  0.0 0.0 copy-start.3
  0.0 1.4 %shard_map.30 = (bf16[264,1024]{1,0:T(8,128)(2,1)S(1)}, bf16[264,1024]{1,0:T(8,128)(2,1)S(1)}, bf16[128,1024]{1,0:T(8,128)(2,1)S(1)}, bf16[136,1024]{1,0:T(8,128)(2,1)S(1)}) custom-call(bf16[2048,1024]{1,0:T(8,128)(2,1)} %rows_ref.3, s32[16,128]{1,0:T(8,128)} %bitcast.61), custom_call_target="tpu_custom_call" | custom-call | bytes 1024 | tf_op jit(solution)/shard_map/pallas_call | solution.py:118
  1.4 4.8 %collective-permute-start.3 = (bf16[264,1024]{1,0:T(8,128)(2,1)S(1)}, bf16[264,1024]{1,0:T(8,128)(2,1)S(1)}, u32[]{:S(2)}, u32[]{:S(2)}) collective-permute-start(bf16[264,1024]{1,0:T(8,128)(2,1)S(1)} %get-tuple-element.71), channel_id=1, source_target_pairs={{0,4},{12,8},{1,5},{13,9},{2,6},{14,10},{3,7},{15,11},{16,20},{28,... | collective-permute-start | bytes 1622024 | tf_op jit(solution)/shard_map/ppermute | solution.py:343
  6.3 0.0 copy-done.3
  6.3 0.1 convert_reduce_fusion
  6.5 0.1 concatenate.3.meta_ref
  6.6 0.1 broadcast_in_dim.144
  6.6 0.7 %collective-permute-start = (bf16[128,1024]{1,0:T(8,128)(2,1)S(1)}, bf16[128,1024]{1,0:T(8,128)(2,1)S(1)}, u32[]{:S(2)}, u32[]{:S(2)}) collective-permute-start(bf16[128,1024]{1,0:T(8,128)(2,1)S(1)} %get-tuple-element.67), channel_id=1, source_target_pairs={{4,8},{8,4},{5,9},{9,5},{6,10},{10,6},{7,11},{11,7},{20,24},{24,20... | collective-permute-start | bytes 786440 | tf_op jit(solution)/shard_map/ppermute | solution.py:362
  7.3 0.7 %collective-permute-start.1 = (bf16[136,1024]{1,0:T(8,128)(2,1)S(1)}, bf16[136,1024]{1,0:T(8,128)(2,1)S(1)}, u32[]{:S(2)}, u32[]{:S(2)}) collective-permute-start(bf16[136,1024]{1,0:T(8,128)(2,1)S(1)} %get-tuple-element.70), channel_id=1, source_target_pairs={{4,8},{8,4},{5,9},{9,5},{6,10},{10,6},{7,11},{11,7},{20,24},{24,20... | collective-permute-start | bytes 835592 | tf_op jit(solution)/shard_map/ppermute | solution.py:361
  8.0 0.1 dynamic_slice.47
  8.1 6.1 %shard_map.31 = (bf16[2048,1024]{1,0:T(8,128)(2,1)S(1)}, f32[16,128]{1,0:T(8,128)S(1)}) custom-call(s32[83]{0:T(128)S(1)} %concatenate.3.meta_ref, bf16[2048,1024]{1,0:T(8,128)(2,1)} %rows_ref.3, s32[1,512]{1,0:T(1,128)S(1)} %bitcast.60), custom_call_target="tpu_custom_call" | custom-call | bytes 1024 | tf_op jit(solution)/shard_map/pallas_call | solution.py:368
  14.1 0.0 collective-permute-done.refs_0_
  14.2 1.3 %collective-permute-start.2 = (bf16[128,1024]{1,0:T(8,128)(2,1)S(1)}, bf16[128,1024]{1,0:T(8,128)(2,1)S(1)}, u32[]{:S(2)}, u32[]{:S(2)}) collective-permute-start(bf16[128,1024]{1,0:T(8,128)(2,1)S(1)} %collective-permute-done.refs_0_), channel_id=1, source_target_pairs={{4,0},{8,12},{5,1},{9,13},{6,2},{10,14},{7,3},{11,15},{20,16},{24,... | collective-permute-start | bytes 786440 | tf_op jit(solution)/shard_map/ppermute | solution.py:378
  15.5 5.8 %collective-permute-start.4 = (bf16[264,1024]{1,0:T(8,128)(2,1)S(1)}, bf16[264,1024]{1,0:T(8,128)(2,1)S(1)}, u32[]{:S(2)}, u32[]{:S(2)}) collective-permute-start(bf16[264,1024]{1,0:T(8,128)(2,1)S(1)} %get-tuple-element.77), channel_id=1, source_target_pairs={{0,4},{12,8},{1,5},{13,9},{2,6},{14,10},{3,7},{15,11},{16,20},{28,... | collective-permute-start | bytes 1622024 | tf_op jit(solution)/shard_map/ppermute | solution.py:379
  21.2 0.0 collective-permute-done.3.refs_0_
  21.3 2.3 %shard_map.32 = (f32[16,128]{1,0:T(8,128)S(1)}, f32[3,128]{1,0:T(4,128)S(1)}) custom-call(s32[83]{0:T(128)S(1)} %concatenate.3.meta_ref, bf16[2048,1024]{1,0:T(8,128)(2,1)S(1)} %get-tuple-element.65.unit_ref, bf16[264,1024]{1,0:T(8,128)(2,1)S(1)} %collective-permute-done.3.refs_0_, f32[16,128]{1,0:T(8,128)S(1)} %get-tuple-element.72.refs_1_), custom_call_target="tpu_custom_call" | custom-call | bytes 1024 | tf_op jit(solution)/shard_map/pallas_call | solution.py:270
  23.5 0.0 collective-permute-done.1.refs_1_
  23.5 1.5 %collective-permute-done.2.low_ref = bf16[128,1024]{1,0:T(8,128)(2,1)S(1)} collective-permute-done((bf16[128,1024]{1,0:T(8,128)(2,1)S(1)}, bf16[128,1024]{1,0:T(8,128)(2,1)S(1)}, u32[]{:S(2)}, u32[]{:S(2)}) %collective-permute-start.2) | collective-permute-done | bytes 262176 | tf_op jit(solution)/shard_map/ppermute | solution.py:378
  25.0 1.3 %collective-permute-start.5 = (bf16[136,1024]{1,0:T(8,128)(2,1)S(1)}, bf16[136,1024]{1,0:T(8,128)(2,1)S(1)}, u32[]{:S(2)}, u32[]{:S(2)}) collective-permute-start(bf16[136,1024]{1,0:T(8,128)(2,1)S(1)} %collective-permute-done.1.refs_1_), channel_id=1, source_target_pairs={{4,0},{8,12},{5,1},{9,13},{6,2},{10,14},{7,3},{11,15},{20,16},{24,... | collective-permute-start | bytes 835592 | tf_op jit(solution)/shard_map/ppermute | solution.py:392
  26.3 2.3 %shard_map.33 = (f32[16,128]{1,0:T(8,128)S(1)}, f32[3,128]{1,0:T(4,128)S(1)}) custom-call(s32[83]{0:T(128)S(1)} %concatenate.3.meta_ref, bf16[2048,1024]{1,0:T(8,128)(2,1)S(1)} %get-tuple-element.65.unit_ref, bf16[128,1024]{1,0:T(8,128)(2,1)S(1)} %collective-permute-done.refs_0_, bf16[136,1024]{1,0:T(8,128)(2,1)S(1)} %collective-permute-done.1.refs_1_, ...), custom_call_target="tpu_custom_call" | custom-call | bytes 1024 | tf_op jit(solution)/shard_map/pallas_call | solution.py:270
  28.6 0.7 %collective-permute-start.6 = (f32[3,128]{1,0:T(4,128)S(1)}, f32[3,128]{1,0:T(4,128)S(1)}, u32[]{:S(2)}, u32[]{:S(2)}) collective-permute-start(f32[3,128]{1,0:T(4,128)S(1)} %get-tuple-element.76.swap_cols_ref.here_ref), channel_id=1, source_target_pairs={{8,4},{4,8},{9,5},{5,9},{10,6},{6,10},{11,7},{7,11},{24,20},{20,24... | collective-permute-start | bytes 4616 | tf_op jit(solution)/shard_map/ppermute | solution.py:394
  29.2 0.0 collective-permute-done.6
  29.2 2.9 %collective-permute-done.4.inward_ref = bf16[264,1024]{1,0:T(8,128)(2,1)S(1)} collective-permute-done((bf16[264,1024]{1,0:T(8,128)(2,1)S(1)}, bf16[264,1024]{1,0:T(8,128)(2,1)S(1)}, u32[]{:S(2)}, u32[]{:S(2)}) %collective-permute-start.4) | collective-permute-done | bytes 540704 | tf_op jit(solution)/shard_map/ppermute | solution.py:379
  32.2 1.9 %collective-permute-done.5.high_ref = bf16[136,1024]{1,0:T(8,128)(2,1)S(1)} collective-permute-done((bf16[136,1024]{1,0:T(8,128)(2,1)S(1)}, bf16[136,1024]{1,0:T(8,128)(2,1)S(1)}, u32[]{:S(2)}, u32[]{:S(2)}) %collective-permute-start.5) | collective-permute-done | bytes 278560 | tf_op jit(solution)/shard_map/ppermute | solution.py:392
  34.1 2.3 %shard_map.34 = (f32[8,128]{1,0:T(8,128)S(1)}, f32[8,128]{1,0:T(8,128)S(1)}, f32[5,128]{1,0:T(8,128)S(1)}) custom-call(s32[83]{0:T(128)S(1)} %concatenate.3.meta_ref, bf16[2048,1024]{1,0:T(8,128)(2,1)S(1)} %get-tuple-element.65.unit_ref, bf16[264,1024]{1,0:T(8,128)(2,1)S(1)} %collective-permute-done.4.inward_ref, ...), custom_call_target="tpu_custom_call" | custom-call | bytes 1024 | tf_op jit(solution)/shard_map/pallas_call | solution.py:270
  36.4 3.6 %collective-permute-start.7 = (f32[5,128]{1,0:T(8,128)S(1)}, f32[5,128]{1,0:T(8,128)S(1)}, u32[]{:S(2)}, u32[]{:S(2)}) collective-permute-start(f32[5,128]{1,0:T(8,128)S(1)} %get-tuple-element.82), channel_id=1, source_target_pairs={{4,0},{8,12},{12,4},{0,8},{5,1},{9,13},{13,5},{1,9},{6,2},{10,14},... | collective-permute-start | bytes 7688 | tf_op jit(solution)/shard_map/ppermute | solution.py:405
  40.1 0.0 collective-permute-start.8
  40.1 1.3 %collective-permute-done.7.home_ref = f32[5,128]{1,0:T(8,128)S(1)} collective-permute-done((f32[5,128]{1,0:T(8,128)S(1)}, f32[5,128]{1,0:T(8,128)S(1)}, u32[]{:S(2)}, u32[]{:S(2)}) %collective-permute-start.7) | collective-permute-done | bytes 2592 | tf_op jit(solution)/shard_map/ppermute | solution.py:405
  41.4 0.0 collective-permute-done.8
  41.4 1.6 %collective-permute-start.9 = (f32[4,128]{1,0:T(4,128)S(1)}, f32[4,128]{1,0:T(4,128)S(1)}, u32[]{:S(2)}, u32[]{:S(2)}) collective-permute-start(f32[4,128]{1,0:T(4,128)S(1)} %get-tuple-element.93), channel_id=1, source_target_pairs={{0,2},{1,3},{2,0},{3,1},{4,6},{5,7},{6,4},{7,5},{8,10},{9,11},{10,... | collective-permute-start | bytes 6152 | tf_op jit(solution)/shard_map/ppermute | solution.py:416
  43.0 0.6 %shard_map.35 = s32[1]{0:T(128)} custom-call(f32[3,128]{1,0:T(4,128)S(1)} %get-tuple-element.76.swap_cols_ref.here_ref, f32[5,128]{1,0:T(8,128)S(1)} %collective-permute-done.7.home_ref), custom_call_target="tpu_custom_call" | custom-call | tf_op jit(solution)/shard_map/pallas_call | solution.py:419
  44.3 0.8 %collective-permute-done.9 = f32[4,128]{1,0:T(4,128)S(1)} collective-permute-done((f32[4,128]{1,0:T(4,128)S(1)}, f32[4,128]{1,0:T(4,128)S(1)}, u32[]{:S(2)}, u32[]{:S(2)}) %collective-permute-start.9) | collective-permute-done | bytes 2080 | tf_op jit(solution)/shard_map/ppermute | solution.py:416
  45.1 0.0 copy-start.4
  45.1 0.6 %copy-done.4 = f32[512]{0:T(512)} copy-done((f32[512]{0:T(512)}, f32[512]{0:T(512)S(1)}, u32[]{:S(2)}) %copy-start.4) | copy-done | bytes 2072
  (9 shorter events, 0.1 us)
Async XLA Ops:
  0.0 6.3 %copy-start.3 = (s32[2048]{0:T(1024)S(1)}, s32[2048]{0:T(1024)}, u32[]{:S(2)}) copy-start(s32[2048]{0:T(1024)} %param.5) | copy-start | bytes 24580
  1.4 19.9 %collective-permute-start.3 = (bf16[264,1024]{1,0:T(8,128)(2,1)S(1)}, bf16[264,1024]{1,0:T(8,128)(2,1)S(1)}, u32[]{:S(2)}, u32[]{:S(2)}) collective-permute-start(bf16[264,1024]{1,0:T(8,128)(2,1)S(1)} %get-tuple-element.71), channel_id=1, source_target_pairs={{0,4},{12,8},{1,5},{13,9},{2,6},{14,10},{3,7},{15,11},{16,20},{28,... | collective-permute-start | bytes 1622024 | tf_op jit(solution)/shard_map/ppermute | solution.py:343
  6.6 7.5 %collective-permute-start = (bf16[128,1024]{1,0:T(8,128)(2,1)S(1)}, bf16[128,1024]{1,0:T(8,128)(2,1)S(1)}, u32[]{:S(2)}, u32[]{:S(2)}) collective-permute-start(bf16[128,1024]{1,0:T(8,128)(2,1)S(1)} %get-tuple-element.67), channel_id=1, source_target_pairs={{4,8},{8,4},{5,9},{9,5},{6,10},{10,6},{7,11},{11,7},{20,24},{24,20... | collective-permute-start | bytes 786440 | tf_op jit(solution)/shard_map/ppermute | solution.py:362
  7.3 16.2 %collective-permute-start.1 = (bf16[136,1024]{1,0:T(8,128)(2,1)S(1)}, bf16[136,1024]{1,0:T(8,128)(2,1)S(1)}, u32[]{:S(2)}, u32[]{:S(2)}) collective-permute-start(bf16[136,1024]{1,0:T(8,128)(2,1)S(1)} %get-tuple-element.70), channel_id=1, source_target_pairs={{4,8},{8,4},{5,9},{9,5},{6,10},{10,6},{7,11},{11,7},{20,24},{24,20... | collective-permute-start | bytes 835592 | tf_op jit(solution)/shard_map/ppermute | solution.py:361
  14.2 10.9 %collective-permute-start.2 = (bf16[128,1024]{1,0:T(8,128)(2,1)S(1)}, bf16[128,1024]{1,0:T(8,128)(2,1)S(1)}, u32[]{:S(2)}, u32[]{:S(2)}) collective-permute-start(bf16[128,1024]{1,0:T(8,128)(2,1)S(1)} %collective-permute-done.refs_0_), channel_id=1, source_target_pairs={{4,0},{8,12},{5,1},{9,13},{6,2},{10,14},{7,3},{11,15},{20,16},{24,... | collective-permute-start | bytes 786440 | tf_op jit(solution)/shard_map/ppermute | solution.py:378
  15.5 16.7 %collective-permute-start.4 = (bf16[264,1024]{1,0:T(8,128)(2,1)S(1)}, bf16[264,1024]{1,0:T(8,128)(2,1)S(1)}, u32[]{:S(2)}, u32[]{:S(2)}) collective-permute-start(bf16[264,1024]{1,0:T(8,128)(2,1)S(1)} %get-tuple-element.77), channel_id=1, source_target_pairs={{0,4},{12,8},{1,5},{13,9},{2,6},{14,10},{3,7},{15,11},{16,20},{28,... | collective-permute-start | bytes 1622024 | tf_op jit(solution)/shard_map/ppermute | solution.py:379
  25.0 9.1 %collective-permute-start.5 = (bf16[136,1024]{1,0:T(8,128)(2,1)S(1)}, bf16[136,1024]{1,0:T(8,128)(2,1)S(1)}, u32[]{:S(2)}, u32[]{:S(2)}) collective-permute-start(bf16[136,1024]{1,0:T(8,128)(2,1)S(1)} %collective-permute-done.1.refs_1_), channel_id=1, source_target_pairs={{4,0},{8,12},{5,1},{9,13},{6,2},{10,14},{7,3},{11,15},{20,16},{24,... | collective-permute-start | bytes 835592 | tf_op jit(solution)/shard_map/ppermute | solution.py:392
  28.6 0.7 %collective-permute-start.6 = (f32[3,128]{1,0:T(4,128)S(1)}, f32[3,128]{1,0:T(4,128)S(1)}, u32[]{:S(2)}, u32[]{:S(2)}) collective-permute-start(f32[3,128]{1,0:T(4,128)S(1)} %get-tuple-element.76.swap_cols_ref.here_ref), channel_id=1, source_target_pairs={{8,4},{4,8},{9,5},{5,9},{10,6},{6,10},{11,7},{7,11},{24,20},{20,24... | collective-permute-start | bytes 4616 | tf_op jit(solution)/shard_map/ppermute | solution.py:394
  36.4 5.0 %collective-permute-start.7 = (f32[5,128]{1,0:T(8,128)S(1)}, f32[5,128]{1,0:T(8,128)S(1)}, u32[]{:S(2)}, u32[]{:S(2)}) collective-permute-start(f32[5,128]{1,0:T(8,128)S(1)} %get-tuple-element.82), channel_id=1, source_target_pairs={{4,0},{8,12},{12,4},{0,8},{5,1},{9,13},{13,5},{1,9},{6,2},{10,14},... | collective-permute-start | bytes 7688 | tf_op jit(solution)/shard_map/ppermute | solution.py:405
  40.1 1.3 %collective-permute-start.8 = (f32[8,128]{1,0:T(8,128)S(1)}, f32[8,128]{1,0:T(8,128)S(1)}, u32[]{:S(2)}, u32[]{:S(2)}) collective-permute-start(f32[8,128]{1,0:T(8,128)S(1)} %get-tuple-element.86), channel_id=1, source_target_pairs={{0,1},{1,0},{2,3},{3,2},{4,5},{5,4},{6,7},{7,6},{8,9},{9,8},{10,11... | collective-permute-start | bytes 12296 | tf_op jit(solution)/shard_map/ppermute | solution.py:409
  41.4 3.7 %collective-permute-start.9 = (f32[4,128]{1,0:T(4,128)S(1)}, f32[4,128]{1,0:T(4,128)S(1)}, u32[]{:S(2)}, u32[]{:S(2)}) collective-permute-start(f32[4,128]{1,0:T(4,128)S(1)} %get-tuple-element.93), channel_id=1, source_target_pairs={{0,2},{1,3},{2,0},{3,1},{4,6},{5,7},{6,4},{7,5},{8,10},{9,11},{10,... | collective-permute-start | bytes 6152 | tf_op jit(solution)/shard_map/ppermute | solution.py:416
  45.1 0.6 %copy-start.4 = (f32[512]{0:T(512)}, f32[512]{0:T(512)S(1)}, u32[]{:S(2)}) copy-start(f32[512]{0:T(512)S(1)} %get-tuple-element.133) | copy-start | bytes 6148

commit v14 on v11

--- a/solution.py
+++ b/solution.py
@@ -56,7 +56,7 @@
         near = (dealt // width * 2 + member % 2) * width + dealt % width
         near = jnp.where(part == 1, blocks // 2, 0) + near
         self.first = jnp.where(self.inner, near, member * width)
-        self.second = jnp.where(self.inner, near, member * width + share)
+        self.second = member * width + share
         self.edge = jnp.where(part == 1, blocks // 2 - 1, blocks // 2)
         self.width, self.share = width, share
 
@@ -125,7 +125,7 @@
         return self.ref[5 * self.blocks + index]
 
 
-MEMBER, FIRST_BLOCK, EDGE, INNER = range(4)
+MEMBER, EDGE, INNER = range(3)
 
 
 def self_kernel(blocks, subs, meta_ref, rows_ref, tags_ref, unit_ref, sums_ref, held, sems):
@@ -202,38 +202,65 @@
     cols_ref[share : share + 1, :] = jnp.where(joined, 1.0, 0.0)
 
 
-def last_kernel(
-    blocks, share, width, meta_ref, unit_ref, inward_ref, relayed_ref, before_ref, outer_back_ref, swap_cols_ref,
-    keep_ref, send_ref, cols_ref, piece_unit, sums,
+def inner_last_kernel(
+    blocks, share, meta_ref, unit_ref, piece_ref, before_ref, outer_cols_ref, swap_cols_ref,
+    sums_ref, cols_ref, piece_unit,
 ):
     meta = Meta(meta_ref, blocks)
     size = share * BLOCK
     is_inner = meta.number(INNER) > 0
 
+    @pl.when(jnp.logical_not(is_inner))
+    def _():
+        sums_ref[...] = before_ref[...]
+        cols_ref[...] = jnp.zeros_like(cols_ref)
+
     @pl.when(is_inner)
     def _():
-        piece_unit[...] = normalised(inward_ref[:size, :])
-
-    @pl.when(jnp.logical_not(is_inner))
-    def _():
-        piece_unit[...] = normalised(relayed_ref[:size, :])
-
-    tags = jnp.where(is_inner, chunk_tags(inward_ref, size)[0], chunk_tags(relayed_ref, size)[0])
+        piece_unit[...] = normalised(piece_ref[:size, :])
+        tags, _ = chunk_tags(piece_ref, size)
+
+        def add_rows(block, value):
+            sums_ref[block : block + 1, :] = before_ref[block : block + 1, :] + value
+
+        cols = cross_terms(meta, 2, tags, unit_ref, piece_unit, add_rows)
+        for k in range(share):
+            cols_ref[share + k : share + k + 1, :] = cols[k]
+        cols_ref[:share, :] = outer_cols_ref[:share, :]
+        cols_ref[2 * share :, :] = swap_cols_ref[share:, :]
+
+
+def outer_last_kernel(
+    blocks, share, width, meta_ref, unit_ref, piece_ref, before_ref, keep_ref, send_ref, cols_ref, piece_unit, sums
+):
+    meta = Meta(meta_ref, blocks)
+    size = share * BLOCK
+    is_inner = meta.number(INNER) > 0
 
     def place(block):
         owner = block // width
         return owner % 2 * (blocks // 2) + owner // 2 * width + block % width
 
-    def add_rows(block, value):
-        at = place(block)
-        sums[at : at + 1, :] = before_ref[block : block + 1, :] + value
-
-    cols = cross_terms(meta, 2, tags, unit_ref, piece_unit, add_rows)
-    for k in range(share):
-        cols_ref[k : k + 1, :] = cols[k]
-        at = place(meta.number(FIRST_BLOCK) + k)
-        sums[pl.ds(at, 1), :] += outer_back_ref[k : k + 1, :]
-    cols_ref[share : share + 1, :] = swap_cols_ref[share : share + 1, :]
+    @pl.when(is_inner)
+    def _():
+        for block in range(blocks):
+            at = place(block)
+            sums[at : at + 1, :] = before_ref[block : block + 1, :]
+        cols_ref[...] = jnp.zeros_like(cols_ref)
+
+    @pl.when(jnp.logical_not(is_inner))
+    def _():
+        piece_unit[...] = normalised(piece_ref[:size, :])
+        tags, _ = chunk_tags(piece_ref, size)
+
+        def add_rows(block, value):
+            at = place(block)
+            sums[at : at + 1, :] = before_ref[block : block + 1, :] + value
+
+        cols = cross_terms(meta, 2, tags, unit_ref, piece_unit, add_rows)
+        for k in range(share):
+            cols_ref[k : k + 1, :] = cols[k]
+
     parity = meta.number(MEMBER) % 2
     heap = blocks // 2
     keep_ref[...] = sums[pl.ds(pl.multiple_of(parity * heap, heap), heap), :]
@@ -241,11 +268,11 @@
 
 
 def flag_kernel(share, here_ref, home_ref, flag_ref):
-    flags = jnp.maximum(here_ref[share : share + 1, :], home_ref[share : share + 1, :])
+    flags = jnp.maximum(here_ref[share : share + 1, :], home_ref[2 * share : 2 * share + 1, :])
     flag_ref[0] = jnp.max(flags).astype(jnp.int32)
 
 
-def call(kernel, meta, operands, out_shapes, scratch, flops):
+def call(kernel, meta, operands, out_shapes, scratch):
     vmem, smem = pl.BlockSpec(memory_space=pltpu.VMEM), pl.BlockSpec(memory_space=pltpu.SMEM)
     return pl.pallas_call(
         kernel,
@@ -254,7 +281,7 @@
         out_shape=out_shapes,
         scratch_shapes=scratch,
         compiler_params=pltpu.CompilerParams(vmem_limit_bytes=16 * 1024 * 1024),
-        cost_estimate=pl.CostEstimate(flops=flops, bytes_accessed=1024, transcendentals=0),
+        cost_estimate=pl.CostEstimate(flops=0, bytes_accessed=1024, transcendentals=0),
     )(meta, *operands)
 
 
@@ -313,27 +340,26 @@
     quads = range(0, tiles, QUAD)
     inward = [p for q in quads for p in ((q, q + 1), (q + 3, q + 2))]
     swap = [p for q in quads for p in ((q + 1, q + 2), (q + 2, q + 1))]
-    around = [p for q in quads for p in ((q, q + 1), (q + 3, q + 2), (q + 1, q + 3), (q + 2, q))]
+    across = [p for q in quads for p in ((q + 1, q + 3), (q + 2, q))]
 
     def turned(route):
         return [(b, a) for a, b in route]
 
     by_block = cluster_ids.reshape(blocks, BLOCK)
     first_out, second_out = pack(size, subs, embeddings, by_block)
+    from_inner = lax.ppermute(first_out, "tile", swap)
     from_outer = lax.ppermute(first_out, "tile", inward)
-    from_inner = lax.ppermute(first_out, "tile", swap)
-    relayed = lax.ppermute(from_inner, "tile", turned(inward))
 
     tag = jnp.max(by_block, axis=1)
     used = jnp.sum((by_block >= 0).astype(jnp.int32), axis=1)
     seen = jnp.where(inner, tag, -2)
     swapped = jnp.where(plan.far & (jnp.arange(blocks) >= blocks // 2), -2, seen)
-    numbers = jnp.stack([member, plan.first, plan.edge, inner])
+    numbers = jnp.stack([member, plan.edge, inner])
     meta = jnp.concatenate([tag, used, seen, swapped, tag, numbers]).astype(jnp.int32)
 
     heap = blocks // 2
-    owner = plan.second // width
-    home_row = jnp.arange(heap)[:, None] - (owner // 2 * width + plan.second % width)
+    owner = plan.first // width
+    home_row = jnp.arange(heap)[:, None] - (owner // 2 * width + plan.first % width)
     home_row = jnp.broadcast_to(home_row, (heap, BLOCK)).astype(jnp.int32)
     upper = [
         jnp.broadcast_to((member >> bit) & 1, (heap >> bit, BLOCK)).astype(jnp.int32)
@@ -354,8 +380,9 @@
         compiler_params=pltpu.CompilerParams(vmem_limit_bytes=24 * 1024 * 1024),
         cost_estimate=pl.CostEstimate(flops=0, bytes_accessed=1024, transcendentals=0),
     )(meta, embeddings, lax.dynamic_slice_in_dim(cluster_ids, member * quarter, quarter, 0)[None])
-    second_out, sums = lax.optimization_barrier((second_out, sums))
-    last = lax.ppermute(second_out, "tile", inward)
+    first_out, second_out, sums = lax.optimization_barrier((first_out, second_out, sums))
+    inward_last = lax.ppermute(second_out, "tile", inward)
+    across_last = lax.ppermute(first_out, "tile", across)
 
     def middle(chunk, piece, before):
         return call(
@@ -364,35 +391,42 @@
             (unit, piece, before),
             [row_sums, col_sums],
             [pltpu.VMEM((size, depth), jnp.bfloat16)],
-            2 * rows * size * depth,
         )
 
+    sums, outer_cols = middle(0, from_outer, sums)
     sums, swap_cols = middle(1, from_inner, sums)
-    sums, outer_cols = middle(0, from_outer, sums)
-    outer_back = lax.ppermute(outer_cols, "tile", turned(inward))
     swap_back = lax.ppermute(swap_cols, "tile", turned(swap))
+    swap_back, sums = lax.optimization_barrier((swap_back, sums))
+    sums, cols = call(
+        functools.partial(inner_last_kernel, blocks, share),
+        meta,
+        (unit, inward_last, sums, outer_cols, swap_cols),
+        [row_sums, jax.ShapeDtypeStruct((2 * share + 1, BLOCK), jnp.float32)],
+        [pltpu.VMEM((size, depth), jnp.bfloat16)],
+    )
+    home = lax.ppermute(cols, "tile", turned(inward))
     half = jax.ShapeDtypeStruct((heap, BLOCK), jnp.float32)
     held, leaving, cols = call(
-        functools.partial(last_kernel, blocks, share, width),
+        functools.partial(outer_last_kernel, blocks, share, width),
         meta,
-        (unit, last, relayed, sums, outer_back, swap_cols),
-        [half, half, col_sums],
+        (unit, across_last, sums),
+        [half, half, jax.ShapeDtypeStruct((share, BLOCK), jnp.float32)],
         [pltpu.VMEM((size, depth), jnp.bfloat16), pltpu.VMEM((blocks, BLOCK), jnp.float32)],
-        2 * rows * size * depth,
     )
-
-    home = lax.ppermute(cols, "tile", turned(around))
+    near_home = lax.ppermute(cols, "tile", turned(across))
+    near_home, home = lax.optimization_barrier((near_home, home))
+
     for k in range(share):
-        held = held + jnp.where(home_row == k, home[k : k + 1] + swap_back[k : k + 1], 0.0)
+        held = held + jnp.where(home_row == k, near_home[k : k + 1] + swap_back[k : k + 1], 0.0)
     held = held + lax.ppermute(leaving, "sub", [(i, i ^ 1) for i in range(subs)])
-    home, held = lax.optimization_barrier((home, held))
+    held, home = lax.optimization_barrier((held, home))
     for bit, mine in enumerate(upper, 1):
         pairs = held.reshape(-1, 2, width, BLOCK)
         low, high = pairs[:, 0].reshape(mine.shape), pairs[:, 1].reshape(mine.shape)
         leaving = jnp.where(mine > 0, low, high)
         held = jnp.where(mine > 0, high, low)
         held = held + lax.ppermute(leaving, "sub", [(i, i ^ (1 << bit)) for i in range(subs)])
-    scores = jnp.log(1.0 + held.reshape(-1))
+    scores = jnp.log(1.0 + (held.reshape(width, BLOCK) + home[:width]).reshape(-1))
 
     flag = pl.pallas_call(
         functools.partial(flag_kernel, share),

time: 43.5 us -> 46.7 us (1.074)
  starting transfers between devices: 16.3 us -> 18.7 us
  Pallas kernels: 14.9 us -> 15.4 us
    ppermute x4, starting transfers between devices: 5.81 us -> 10.9 us  [the longest x1 4.25 us: shards(): near_home = lax.ppermute(cols, 'tile', turned(across))]
    ppermute x1, starting transfers between devices: 7.57 us -> 4.78 us  [shards(): from_outer = lax.ppermute(first_out, 'tile', inward)]
    ppermute x1, waiting for transfers between devices: 1.19 us -> 0.01 us  [shards(): from_outer = lax.ppermute(first_out, 'tile', inward)]
    ppermute x4, waiting for transfers between devices: 8.15 us -> 9.12 us  [the longest x1 5.19 us: shards(): inward_last = lax.ppermute(second_out, 'tile', inward)]
    pallas_call x3 -> x4, Pallas kernels: 6.84 us -> 7.3 us  [call(): pl.pallas_call(kernel, in_specs=[smem] + [vmem] * len(operands), out_spec...]
  transfers between devices with their start and end apart: 9 -> 9, of which waited for: 5 -> 4; matrix products, arithmetic and copies ran while one was open for 1% -> 1% of each run, Pallas kernels for 31% -> 30%
where the time goes in v14:
time: 46.7 us; the launch traced here: 46.2 us
  starting transfers between devices  18.7 us (40%)
  Pallas kernels  15.4 us (33%)
  waiting for transfers between devices  9.93 us (21%)
  between operations  0.98 us (2%)
  local copies, waits for them, and re-layouts  0.81 us (2%)
    pallas_call x4, Pallas kernels, call(): pl.pallas_call(kernel, in_specs=[smem] + [vmem] * len(operands), out_spec...  7.3 us
    pallas_call x1, Pallas kernels, shards(): pl.pallas_call(functools.partial(self_kernel, blocks, subs), in_specs=[sm...  6.05 us
    ppermute x1, waiting for transfers between devices, shards(): inward_last = lax.ppermute(second_out, 'tile', inward)  5.19 us
    ppermute x1, starting transfers between devices, shards(): from_outer = lax.ppermute(first_out, 'tile', inward)  4.78 us
    ppermute x1, starting transfers between devices, shards(): near_home = lax.ppermute(cols, 'tile', turned(across))  4.25 us
    ppermute x1, starting transfers between devices, shards(): inward_last = lax.ppermute(second_out, 'tile', inward)  4.08 us
    ppermute x1, waiting for transfers between devices, shards(): across_last = lax.ppermute(first_out, 'tile', across)  2.72 us
    ppermute x1, starting transfers between devices, shards(): lax.ppermute(leaving, 'sub', [(i, i ^ 1 << bit) for i in range(subs)])  1.55 us
  transfers between devices with their start and end apart: 9, of which 4 were waited for; matrix products, arithmetic and copies ran while one was open for 1% of the time, Pallas kernels for 30%

profile of v14, /device:TPU:0, one launch (start us, length us, event | category | flops | bytes accessed | tf_op | source)
XLA Modules:
  0.0 46.2 jit_solution(9378208774073608752)
XLA Ops:
  0.0 0.0 copy-start.3
  0.0 1.4 %shard_map.31 = (bf16[264,1024]{1,0:T(8,128)(2,1)S(1)}, bf16[264,1024]{1,0:T(8,128)(2,1)S(1)}) custom-call(bf16[2048,1024]{1,0:T(8,128)(2,1)} %rows_ref.3, s32[16,128]{1,0:T(8,128)} %bitcast.57), custom_call_target="tpu_custom_call" | custom-call | bytes 1024 | tf_op jit(solution)/shard_map/pallas_call | solution.py:103
  1.4 4.8 %collective-permute-start.1 = (bf16[264,1024]{1,0:T(8,128)(2,1)S(1)}, bf16[264,1024]{1,0:T(8,128)(2,1)S(1)}, u32[]{:S(2)}, u32[]{:S(2)}) collective-permute-start(bf16[264,1024]{1,0:T(8,128)(2,1)S(1)} %get-tuple-element.72), channel_id=1, source_target_pairs={{0,4},{12,8},{1,5},{13,9},{2,6},{14,10},{3,7},{15,11},{16,20},{28,... | collective-permute-start | bytes 1622024 | tf_op jit(solution)/shard_map/ppermute | solution.py:351
  6.2 0.7 %collective-permute-start = (bf16[264,1024]{1,0:T(8,128)(2,1)S(1)}, bf16[264,1024]{1,0:T(8,128)(2,1)S(1)}, u32[]{:S(2)}, u32[]{:S(2)}) collective-permute-start(bf16[264,1024]{1,0:T(8,128)(2,1)S(1)} %get-tuple-element.72), channel_id=1, source_target_pairs={{4,8},{8,4},{5,9},{9,5},{6,10},{10,6},{7,11},{11,7},{20,24},{24,20... | collective-permute-start | bytes 1622024 | tf_op jit(solution)/shard_map/ppermute | solution.py:350
  7.0 0.0 copy-done.3
  7.0 0.1 convert_reduce_fusion
  7.2 0.1 dynamic_slice.47
  7.3 0.1 concatenate.3.meta_ref
  7.3 0.1 broadcast_in_dim.128
  7.4 6.1 %shard_map.30 = (bf16[2048,1024]{1,0:T(8,128)(2,1)S(1)}, f32[16,128]{1,0:T(8,128)S(1)}) custom-call(s32[83]{0:T(128)S(1)} %concatenate.3.meta_ref, bf16[2048,1024]{1,0:T(8,128)(2,1)} %rows_ref.3, s32[1,512]{1,0:T(1,128)S(1)} %bitcast.56), custom_call_target="tpu_custom_call" | custom-call | bytes 1024 | tf_op jit(solution)/shard_map/pallas_call | solution.py:374
  13.5 4.1 %collective-permute-start.3 = (bf16[264,1024]{1,0:T(8,128)(2,1)S(1)}, bf16[264,1024]{1,0:T(8,128)(2,1)S(1)}, u32[]{:S(2)}, u32[]{:S(2)}) collective-permute-start(bf16[264,1024]{1,0:T(8,128)(2,1)S(1)} %get-tuple-element.73), channel_id=1, source_target_pairs={{0,4},{12,8},{1,5},{13,9},{2,6},{14,10},{3,7},{15,11},{16,20},{28,... | collective-permute-start | bytes 1622024 | tf_op jit(solution)/shard_map/ppermute | solution.py:384
  17.6 1.3 %collective-permute-start.2 = (bf16[264,1024]{1,0:T(8,128)(2,1)S(1)}, bf16[264,1024]{1,0:T(8,128)(2,1)S(1)}, u32[]{:S(2)}, u32[]{:S(2)}) collective-permute-start(bf16[264,1024]{1,0:T(8,128)(2,1)S(1)} %get-tuple-element.72), channel_id=1, source_target_pairs={{4,12},{8,0},{5,13},{9,1},{6,14},{10,2},{7,15},{11,3},{20,28},{24,... | collective-permute-start | bytes 1622024 | tf_op jit(solution)/shard_map/ppermute | solution.py:385
  18.9 0.0 collective-permute-done.1.piece_ref
  18.9 2.2 %shard_map.32 = (f32[16,128]{1,0:T(8,128)S(1)}, f32[3,128]{1,0:T(4,128)S(1)}) custom-call(s32[83]{0:T(128)S(1)} %concatenate.3.meta_ref, bf16[2048,1024]{1,0:T(8,128)(2,1)S(1)} %get-tuple-element.65.unit_ref, bf16[264,1024]{1,0:T(8,128)(2,1)S(1)} %collective-permute-done.1.piece_ref, f32[16,128]{1,0:T(8,128)S(1)} %get-tuple-element.69.before_ref), custom_call_target="tpu_custom_call" | custom-call | bytes 1024 | tf_op jit(solution)/shard_map/pallas_call | solution.py:277
  21.1 0.0 collective-permute-done.piece_ref
  21.1 2.2 %shard_map.33 = (f32[16,128]{1,0:T(8,128)S(1)}, f32[3,128]{1,0:T(4,128)S(1)}) custom-call(s32[83]{0:T(128)S(1)} %concatenate.3.meta_ref, bf16[2048,1024]{1,0:T(8,128)(2,1)S(1)} %get-tuple-element.65.unit_ref, bf16[264,1024]{1,0:T(8,128)(2,1)S(1)} %collective-permute-done.piece_ref, f32[16,128]{1,0:T(8,128)S(1)} %get-tuple-element.70.before_ref), custom_call_target="tpu_custom_call" | custom-call | bytes 1024 | tf_op jit(solution)/shard_map/pallas_call | solution.py:277
  23.4 0.7 %collective-permute-start.4 = (f32[3,128]{1,0:T(4,128)S(1)}, f32[3,128]{1,0:T(4,128)S(1)}, u32[]{:S(2)}, u32[]{:S(2)}) collective-permute-start(f32[3,128]{1,0:T(4,128)S(1)} %get-tuple-element.71.swap_cols_ref.here_ref), channel_id=1, source_target_pairs={{8,4},{4,8},{9,5},{5,9},{10,6},{6,10},{11,7},{7,11},{24,20},{20,24... | collective-permute-start | bytes 4616 | tf_op jit(solution)/shard_map/ppermute | solution.py:398
  24.0 0.0 collective-permute-done.4
  24.1 5.2 %collective-permute-done.3.piece_ref = bf16[264,1024]{1,0:T(8,128)(2,1)S(1)} collective-permute-done((bf16[264,1024]{1,0:T(8,128)(2,1)S(1)}, bf16[264,1024]{1,0:T(8,128)(2,1)S(1)}, u32[]{:S(2)}, u32[]{:S(2)}) %collective-permute-start.3) | collective-permute-done | bytes 540704 | tf_op jit(solution)/shard_map/ppermute | solution.py:384
  29.2 0.6 %shard_map.34 = (f32[16,128]{1,0:T(8,128)S(1)}, f32[5,128]{1,0:T(8,128)S(1)}) custom-call(s32[83]{0:T(128)S(1)} %concatenate.3.meta_ref, bf16[2048,1024]{1,0:T(8,128)(2,1)S(1)} %get-tuple-element.65.unit_ref, bf16[264,1024]{1,0:T(8,128)(2,1)S(1)} %collective-permute-done.3.piece_ref, f32[16,128]{1,0:T(8,128)S(1)} %get-tuple-element.75.before_ref, ...), custom_call_target="tpu_custom_call" | custom-call | bytes 1024 | tf_op jit(solution)/shard_map/pallas_call | solution.py:277
  29.8 1.3 %collective-permute-start.6 = (f32[5,128]{1,0:T(8,128)S(1)}, f32[5,128]{1,0:T(8,128)S(1)}, u32[]{:S(2)}, u32[]{:S(2)}) collective-permute-start(f32[5,128]{1,0:T(8,128)S(1)} %get-tuple-element.81), channel_id=1, source_target_pairs={{4,0},{8,12},{5,1},{9,13},{6,2},{10,14},{7,3},{11,15},{20,16},{24,... | collective-permute-start | bytes 7688 | tf_op jit(solution)/shard_map/ppermute | solution.py:407
  31.1 2.7 %collective-permute-done.2.piece_ref = bf16[264,1024]{1,0:T(8,128)(2,1)S(1)} collective-permute-done((bf16[264,1024]{1,0:T(8,128)(2,1)S(1)}, bf16[264,1024]{1,0:T(8,128)(2,1)S(1)}, u32[]{:S(2)}, u32[]{:S(2)}) %collective-permute-start.2) | collective-permute-done | bytes 540704 | tf_op jit(solution)/shard_map/ppermute | solution.py:385
  33.8 2.3 %shard_map.35 = (f32[8,128]{1,0:T(8,128)S(1)}, f32[8,128]{1,0:T(8,128)S(1)}, f32[2,128]{1,0:T(2,128)S(1)}) custom-call(s32[83]{0:T(128)S(1)} %concatenate.3.meta_ref, bf16[2048,1024]{1,0:T(8,128)(2,1)S(1)} %get-tuple-element.65.unit_ref, bf16[264,1024]{1,0:T(8,128)(2,1)S(1)} %collective-permute-done.2.piece_ref, f32[16,128]{1,0:T(8,128)S(1)} %get-tuple-element.77.before_ref), custom_call_target="tpu_custom_call" | custom-call | bytes 1024 | tf_op jit(solution)/shard_map/pallas_call | solution.py:277
  36.1 4.3 %collective-permute-start.5 = (f32[2,128]{1,0:T(2,128)S(1)}, f32[2,128]{1,0:T(2,128)S(1)}, u32[]{:S(2)}, u32[]{:S(2)}) collective-permute-start(f32[2,128]{1,0:T(2,128)S(1)} %get-tuple-element.80), channel_id=1, source_target_pairs={{12,4},{0,8},{13,5},{1,9},{14,6},{2,10},{15,7},{3,11},{28,20},{16,... | collective-permute-start | bytes 3080 | tf_op jit(solution)/shard_map/ppermute | solution.py:416
  40.4 0.1 collective-permute-start.7
  40.4 1.2 %collective-permute-done.5 = f32[2,128]{1,0:T(2,128)S(1)} collective-permute-done((f32[2,128]{1,0:T(2,128)S(1)}, f32[2,128]{1,0:T(2,128)S(1)}, u32[]{:S(2)}, u32[]{:S(2)}) %collective-permute-start.5) | collective-permute-done | bytes 1056 | tf_op jit(solution)/shard_map/ppermute | solution.py:416
  41.6 0.0 collective-permute-done.6.home_ref
  41.6 0.0 collective-permute-done.7
  41.7 1.6 %collective-permute-start.8 = (f32[4,128]{1,0:T(4,128)S(1)}, f32[4,128]{1,0:T(4,128)S(1)}, u32[]{:S(2)}, u32[]{:S(2)}) collective-permute-start(f32[4,128]{1,0:T(4,128)S(1)} %get-tuple-element.92), channel_id=1, source_target_pairs={{0,2},{1,3},{2,0},{3,1},{4,6},{5,7},{6,4},{7,5},{8,10},{9,11},{10,... | collective-permute-start | bytes 6152 | tf_op jit(solution)/shard_map/ppermute | solution.py:428
  43.2 0.6 %shard_map.36 = s32[1]{0:T(128)} custom-call(f32[3,128]{1,0:T(4,128)S(1)} %get-tuple-element.71.swap_cols_ref.here_ref, f32[5,128]{1,0:T(8,128)S(1)} %collective-permute-done.6.home_ref), custom_call_target="tpu_custom_call" | custom-call | tf_op jit(solution)/shard_map/pallas_call | solution.py:431
  44.5 0.8 %collective-permute-done.8 = f32[4,128]{1,0:T(4,128)S(1)} collective-permute-done((f32[4,128]{1,0:T(4,128)S(1)}, f32[4,128]{1,0:T(4,128)S(1)}, u32[]{:S(2)}, u32[]{:S(2)}) %collective-permute-start.8) | collective-permute-done | bytes 2080 | tf_op jit(solution)/shard_map/ppermute | solution.py:428
  45.3 0.2 conditional.1
  45.6 0.0 copy-start.4
  45.6 0.6 %copy-done.4 = f32[512]{0:T(512)} copy-done((f32[512]{0:T(512)}, f32[512]{0:T(512)S(1)}, u32[]{:S(2)}) %copy-start.4) | copy-done | bytes 2072
  (8 shorter events, 0.0 us)
Async XLA Ops:
  0.0 7.0 %copy-start.3 = (s32[2048]{0:T(1024)S(1)}, s32[2048]{0:T(1024)}, u32[]{:S(2)}) copy-start(s32[2048]{0:T(1024)} %param.5) | copy-start | bytes 24580
  1.4 17.5 %collective-permute-start.1 = (bf16[264,1024]{1,0:T(8,128)(2,1)S(1)}, bf16[264,1024]{1,0:T(8,128)(2,1)S(1)}, u32[]{:S(2)}, u32[]{:S(2)}) collective-permute-start(bf16[264,1024]{1,0:T(8,128)(2,1)S(1)} %get-tuple-element.72), channel_id=1, source_target_pairs={{0,4},{12,8},{1,5},{13,9},{2,6},{14,10},{3,7},{15,11},{16,20},{28,... | collective-permute-start | bytes 1622024 | tf_op jit(solution)/shard_map/ppermute | solution.py:351
  6.2 14.9 %collective-permute-start = (bf16[264,1024]{1,0:T(8,128)(2,1)S(1)}, bf16[264,1024]{1,0:T(8,128)(2,1)S(1)}, u32[]{:S(2)}, u32[]{:S(2)}) collective-permute-start(bf16[264,1024]{1,0:T(8,128)(2,1)S(1)} %get-tuple-element.72), channel_id=1, source_target_pairs={{4,8},{8,4},{5,9},{9,5},{6,10},{10,6},{7,11},{11,7},{20,24},{24,20... | collective-permute-start | bytes 1622024 | tf_op jit(solution)/shard_map/ppermute | solution.py:350
  13.5 15.8 %collective-permute-start.3 = (bf16[264,1024]{1,0:T(8,128)(2,1)S(1)}, bf16[264,1024]{1,0:T(8,128)(2,1)S(1)}, u32[]{:S(2)}, u32[]{:S(2)}) collective-permute-start(bf16[264,1024]{1,0:T(8,128)(2,1)S(1)} %get-tuple-element.73), channel_id=1, source_target_pairs={{0,4},{12,8},{1,5},{13,9},{2,6},{14,10},{3,7},{15,11},{16,20},{28,... | collective-permute-start | bytes 1622024 | tf_op jit(solution)/shard_map/ppermute | solution.py:384
  17.6 16.3 %collective-permute-start.2 = (bf16[264,1024]{1,0:T(8,128)(2,1)S(1)}, bf16[264,1024]{1,0:T(8,128)(2,1)S(1)}, u32[]{:S(2)}, u32[]{:S(2)}) collective-permute-start(bf16[264,1024]{1,0:T(8,128)(2,1)S(1)} %get-tuple-element.72), channel_id=1, source_target_pairs={{4,12},{8,0},{5,13},{9,1},{6,14},{10,2},{7,15},{11,3},{20,28},{24,... | collective-permute-start | bytes 1622024 | tf_op jit(solution)/shard_map/ppermute | solution.py:385
  23.4 0.7 %collective-permute-start.4 = (f32[3,128]{1,0:T(4,128)S(1)}, f32[3,128]{1,0:T(4,128)S(1)}, u32[]{:S(2)}, u32[]{:S(2)}) collective-permute-start(f32[3,128]{1,0:T(4,128)S(1)} %get-tuple-element.71.swap_cols_ref.here_ref), channel_id=1, source_target_pairs={{8,4},{4,8},{9,5},{5,9},{10,6},{6,10},{11,7},{7,11},{24,20},{20,24... | collective-permute-start | bytes 4616 | tf_op jit(solution)/shard_map/ppermute | solution.py:398
  29.8 11.8 %collective-permute-start.6 = (f32[5,128]{1,0:T(8,128)S(1)}, f32[5,128]{1,0:T(8,128)S(1)}, u32[]{:S(2)}, u32[]{:S(2)}) collective-permute-start(f32[5,128]{1,0:T(8,128)S(1)} %get-tuple-element.81), channel_id=1, source_target_pairs={{4,0},{8,12},{5,1},{9,13},{6,2},{10,14},{7,3},{11,15},{20,16},{24,... | collective-permute-start | bytes 7688 | tf_op jit(solution)/shard_map/ppermute | solution.py:407
  36.1 5.5 %collective-permute-start.5 = (f32[2,128]{1,0:T(2,128)S(1)}, f32[2,128]{1,0:T(2,128)S(1)}, u32[]{:S(2)}, u32[]{:S(2)}) collective-permute-start(f32[2,128]{1,0:T(2,128)S(1)} %get-tuple-element.80), channel_id=1, source_target_pairs={{12,4},{0,8},{13,5},{1,9},{14,6},{2,10},{15,7},{3,11},{28,20},{16,... | collective-permute-start | bytes 3080 | tf_op jit(solution)/shard_map/ppermute | solution.py:416
  40.4 1.3 %collective-permute-start.7 = (f32[8,128]{1,0:T(8,128)S(1)}, f32[8,128]{1,0:T(8,128)S(1)}, u32[]{:S(2)}, u32[]{:S(2)}) collective-permute-start(f32[8,128]{1,0:T(8,128)S(1)} %get-tuple-element.84), channel_id=1, source_target_pairs={{0,1},{1,0},{2,3},{3,2},{4,5},{5,4},{6,7},{7,6},{8,9},{9,8},{10,11... | collective-permute-start | bytes 12296 | tf_op jit(solution)/shard_map/ppermute | solution.py:421
  41.7 3.7 %collective-permute-start.8 = (f32[4,128]{1,0:T(4,128)S(1)}, f32[4,128]{1,0:T(4,128)S(1)}, u32[]{:S(2)}, u32[]{:S(2)}) collective-permute-start(f32[4,128]{1,0:T(4,128)S(1)} %get-tuple-element.92), channel_id=1, source_target_pairs={{0,2},{1,3},{2,0},{3,1},{4,6},{5,7},{6,4},{7,5},{8,10},{9,11},{10,... | collective-permute-start | bytes 6152 | tf_op jit(solution)/shard_map/ppermute | solution.py:428
  45.6 0.6 %copy-start.4 = (f32[512]{0:T(512)}, f32[512]{0:T(512)S(1)}, u32[]{:S(2)}) copy-start(f32[512]{0:T(512)S(1)} %get-tuple-element.127) | copy-start | bytes 6148

commit v15 on v12

--- a/solution.py
+++ b/solution.py
@@ -18,7 +18,7 @@
 GAIN = inverse_temp * math.log2(math.e)
 OFF = -1000.0
 
-STEPS = (512, 256, 1024)
+STEP = 512
 COPY = 64
 
 
@@ -152,40 +152,49 @@
     return row[:, :size], row[:, size : size + BLOCK]
 
 
-def cross_terms(meta, chunk, column_tags, unit_ref, piece_unit, add_rows, step):
+def cross_terms(meta, chunk, column_tags, unit_ref, piece_unit, before_ref, sums, columns, place):
     size = column_tags.shape[1]
-    columns = None
-    for start in range(0, meta.blocks * BLOCK, step):
-        cosine = products(unit_ref[start : start + step, :], piece_unit[...])
-        for inner in range(0, step, BLOCK):
-            block = (start + inner) // BLOCK
-            bias = column_bias(meta.tag(block, chunk), column_tags)
-            weight = jnp.exp2(cosine[inner : inner + BLOCK] * GAIN + bias)
-            row = lax.broadcasted_iota(jnp.int32, weight.shape, 0)
-            weight = jnp.where(row < meta.used(block), weight, 0.0)
-            add_rows(block, lane_sums(weight))
-            partial = weight[0:8]
-            for down in range(8, BLOCK, 8):
-                partial = partial + weight[down : down + 8]
-            columns = partial if columns is None else columns + partial
-    total = jnp.sum(columns, axis=0, keepdims=True)
-    return [total[:, at : at + BLOCK] for at in range(0, size, BLOCK)]
+    half = meta.blocks // 2
+    columns[...] = jnp.zeros_like(columns)
+    for block in range(meta.blocks):
+        sums[place(block) : place(block) + 1, :] = before_ref[block : block + 1, :]
+    there = [jnp.max(column_tags[:, at : at + BLOCK]) for at in range(0, size, BLOCK)]
+    for first in (0, half):
+        shared = False
+        for block in range(first, first + half):
+            for tag in there:
+                shared = (meta.tag(block, chunk).astype(jnp.float32) == tag) | shared
+
+        @pl.when(shared)
+        def _():
+            total = None
+            for start in range(first * BLOCK, (first + half) * BLOCK, STEP):
+                cosine = products(unit_ref[start : start + STEP, :], piece_unit[...])
+                for inner in range(0, STEP, BLOCK):
+                    block = (start + inner) // BLOCK
+                    bias = column_bias(meta.tag(block, chunk), column_tags)
+                    weight = jnp.exp2(cosine[inner : inner + BLOCK] * GAIN + bias)
+                    row = lax.broadcasted_iota(jnp.int32, weight.shape, 0)
+                    weight = jnp.where(row < meta.used(block), weight, 0.0)
+                    sums[place(block) : place(block) + 1, :] += lane_sums(weight)
+                    partial = weight[0:8]
+                    for down in range(8, BLOCK, 8):
+                        partial = partial + weight[down : down + 8]
+                    total = partial if total is None else total + partial
+            columns[...] += total
 
 
 def middle_kernel(
-    blocks, share, chunk, meta_ref, unit_ref, piece_ref, before_ref, sums_ref, cols_ref, piece_unit
+    blocks, share, chunk, meta_ref, unit_ref, piece_ref, before_ref, sums_ref, cols_ref, piece_unit, columns
 ):
     meta = Meta(meta_ref, blocks)
     size = share * BLOCK
     piece_unit[...] = normalised(piece_ref[:size, :])
     tags, edge = chunk_tags(piece_ref, size)
-
-    def add_rows(block, value):
-        sums_ref[block : block + 1, :] = before_ref[block : block + 1, :] + value
-
-    cols = cross_terms(meta, chunk, tags, unit_ref, piece_unit, add_rows, STEPS[chunk])
+    cross_terms(meta, chunk, tags, unit_ref, piece_unit, before_ref, sums_ref, columns, lambda block: block)
+    total = jnp.sum(columns[...], axis=0, keepdims=True)
     for k in range(share):
-        cols_ref[k : k + 1, :] = cols[k]
+        cols_ref[k : k + 1, :] = total[:, k * BLOCK : (k + 1) * BLOCK]
     mine = meta.tag(meta.number(EDGE)).astype(jnp.float32)
     joined = (edge == mine) & (edge >= 0) & (meta.number(INNER) > 0)
     cols_ref[share : share + 1, :] = jnp.where(joined, 1.0, 0.0)
@@ -193,7 +202,7 @@
 
 def last_kernel(
     blocks, share, width, meta_ref, unit_ref, piece_ref, before_ref, outer_back_ref, swap_cols_ref,
-    keep_ref, send_ref, cols_ref, piece_unit, sums,
+    keep_ref, send_ref, cols_ref, piece_unit, sums, columns,
 ):
     meta = Meta(meta_ref, blocks)
     size = share * BLOCK
@@ -204,13 +213,10 @@
         owner = block // width
         return owner % 2 * (blocks // 2) + owner // 2 * width + block % width
 
-    def add_rows(block, value):
-        at = place(block)
-        sums[at : at + 1, :] = before_ref[block : block + 1, :] + value
-
-    cols = cross_terms(meta, 2, tags, unit_ref, piece_unit, add_rows, STEPS[2])
+    cross_terms(meta, 2, tags, unit_ref, piece_unit, before_ref, sums, columns, place)
+    total = jnp.sum(columns[...], axis=0, keepdims=True)
     for k in range(share):
-        cols_ref[k : k + 1, :] = cols[k]
+        cols_ref[k : k + 1, :] = total[:, k * BLOCK : (k + 1) * BLOCK]
         at = place(meta.number(FIRST_BLOCK) + k)
         sums[pl.ds(at, 1), :] += outer_back_ref[k : k + 1, :]
     cols_ref[share : share + 1, :] = swap_cols_ref[share : share + 1, :]
@@ -342,7 +348,7 @@
             meta,
             (unit, piece, before),
             [row_sums, col_sums],
-            [pltpu.VMEM((size, depth), jnp.bfloat16)],
+            [pltpu.VMEM((size, depth), jnp.bfloat16), pltpu.VMEM((8, size), jnp.float32)],
             2 * rows * size * depth,
         )
 
@@ -356,7 +362,11 @@
         meta,
         (unit, last, sums, outer_back, swap_cols),
         [half, half, col_sums],
-        [pltpu.VMEM((size, depth), jnp.bfloat16), pltpu.VMEM((blocks, BLOCK), jnp.float32)],
+        [
+            pltpu.VMEM((size, depth), jnp.bfloat16),
+            pltpu.VMEM((blocks, BLOCK), jnp.float32),
+            pltpu.VMEM((8, size), jnp.float32),
+        ],
         2 * rows * size * depth,
     )
 

time: 43.1 us -> 41.6 us (0.965)
  Pallas kernels: 14.8 us -> 10.4 us
  starting transfers between devices: 11.6 us -> 13.5 us
  waiting for transfers between devices: 14.6 us -> 15.6 us
    pallas_call x3, Pallas kernels: 6.78 us -> 2.32 us  [call(): pl.pallas_call(kernel, in_specs=[smem] + [vmem] * len(operands), out_spec...]
    ppermute x1, waiting for transfers between devices: 7.26 us -> 10.2 us  [shards(): last = lax.ppermute(second_out, 'tile', around)]
    ppermute x1, starting transfers between devices: 0.28 us -> 2.16 us  [shards(): home = lax.ppermute(cols, 'tile', turned(around))]
    ppermute x1, waiting for transfers between devices: 3.35 us -> 1.48 us  [shards(): home = lax.ppermute(cols, 'tile', turned(around))]
  transfers between devices with their start and end apart: 8 -> 8, of which waited for: 4 -> 4; matrix products, arithmetic and copies ran while one was open for 1% -> 1% of each run, Pallas kernels for 31% -> 22%
where the time goes in v15:
time: 41.6 us; the launch traced here: 41.4 us
  waiting for transfers between devices  15.6 us (38%)
  starting transfers between devices  13.5 us (32%)
  Pallas kernels  10.4 us (25%)
  between operations  0.93 us (2%)
  local copies, waits for them, and re-layouts  0.81 us (2%)
    ppermute x1, waiting for transfers between devices, shards(): last = lax.ppermute(second_out, 'tile', around)  10.2 us
    pallas_call x1, Pallas kernels, shards(): pl.pallas_call(functools.partial(self_kernel, blocks, subs), in_specs=[sm...  6.05 us
    ppermute x1, starting transfers between devices, shards(): from_outer = lax.ppermute(first_out, 'tile', inward)  4.96 us
    ppermute x1, waiting for transfers between devices, shards(): from_outer = lax.ppermute(first_out, 'tile', inward)  3.15 us
    pallas_call x3, Pallas kernels, call(): pl.pallas_call(kernel, in_specs=[smem] + [vmem] * len(operands), out_spec...  2.32 us
    ppermute x1, starting transfers between devices, shards(): last = lax.ppermute(second_out, 'tile', around)  2.2 us
    ppermute x1, starting transfers between devices, shards(): home = lax.ppermute(cols, 'tile', turned(around))  2.16 us
    ppermute x1, starting transfers between devices, shards(): lax.ppermute(leaving, 'sub', [(i, i ^ 1 << bit) for i in range(subs)])  1.56 us
  transfers between devices with their start and end apart: 8, of which 4 were waited for; matrix products, arithmetic and copies ran while one was open for 1% of the time, Pallas kernels for 22%

profile of v15, /device:TPU:0, one launch (start us, length us, event | category | flops | bytes accessed | tf_op | source)
XLA Modules:
  0.0 41.4 jit_solution(4382463347493367939)
XLA Ops:
  0.0 0.0 copy-start.3
  0.0 1.4 %shard_map.31 = (bf16[264,1024]{1,0:T(8,128)(2,1)S(1)}, bf16[264,1024]{1,0:T(8,128)(2,1)S(1)}) custom-call(bf16[2048,1024]{1,0:T(8,128)(2,1)} %rows_ref.3, s32[16,128]{1,0:T(8,128)} %bitcast.58), custom_call_target="tpu_custom_call" | custom-call | bytes 1024 | tf_op jit(solution)/shard_map/pallas_call | solution.py:92
  1.4 5.0 %collective-permute-start.1 = (bf16[264,1024]{1,0:T(8,128)(2,1)S(1)}, bf16[264,1024]{1,0:T(8,128)(2,1)S(1)}, u32[]{:S(2)}, u32[]{:S(2)}) collective-permute-start(bf16[264,1024]{1,0:T(8,128)(2,1)S(1)} %get-tuple-element.54), channel_id=1, source_target_pairs={{0,4},{12,8},{1,5},{13,9},{2,6},{14,10},{3,7},{15,11},{16,20},{28,... | collective-permute-start | bytes 1622024 | tf_op jit(solution)/shard_map/ppermute | solution.py:310
  6.4 0.7 %collective-permute-start = (bf16[264,1024]{1,0:T(8,128)(2,1)S(1)}, bf16[264,1024]{1,0:T(8,128)(2,1)S(1)}, u32[]{:S(2)}, u32[]{:S(2)}) collective-permute-start(bf16[264,1024]{1,0:T(8,128)(2,1)S(1)} %get-tuple-element.54), channel_id=1, source_target_pairs={{4,8},{8,4},{5,9},{9,5},{6,10},{10,6},{7,11},{11,7},{20,24},{24,20... | collective-permute-start | bytes 1622024 | tf_op jit(solution)/shard_map/ppermute | solution.py:309
  7.1 0.0 copy-done.3
  7.1 0.1 convert_reduce_fusion
  7.3 0.1 dynamic_slice.47
  7.4 0.1 concatenate.3.meta_ref
  7.5 0.1 broadcast_in_dim.128
  7.6 6.0 %shard_map.30 = (bf16[2048,1024]{1,0:T(8,128)(2,1)S(1)}, f32[16,128]{1,0:T(8,128)S(1)}) custom-call(s32[84]{0:T(128)S(1)} %concatenate.3.meta_ref, bf16[2048,1024]{1,0:T(8,128)(2,1)} %rows_ref.3, s32[1,512]{1,0:T(1,128)S(1)} %bitcast.57), custom_call_target="tpu_custom_call" | custom-call | bytes 1024 | tf_op jit(solution)/shard_map/pallas_call | solution.py:333
  13.6 2.2 %collective-permute-start.2 = (bf16[264,1024]{1,0:T(8,128)(2,1)S(1)}, bf16[264,1024]{1,0:T(8,128)(2,1)S(1)}, u32[]{:S(2)}, u32[]{:S(2)}) collective-permute-start(bf16[264,1024]{1,0:T(8,128)(2,1)S(1)} %get-tuple-element.60), channel_id=1, source_target_pairs={{0,4},{12,8},{4,12},{8,0},{1,5},{13,9},{5,13},{9,1},{2,6},{14,10},... | collective-permute-start | bytes 1622024 | tf_op jit(solution)/shard_map/ppermute | solution.py:343
  15.8 3.1 %collective-permute-done.1.piece_ref = bf16[264,1024]{1,0:T(8,128)(2,1)S(1)} collective-permute-done((bf16[264,1024]{1,0:T(8,128)(2,1)S(1)}, bf16[264,1024]{1,0:T(8,128)(2,1)S(1)}, u32[]{:S(2)}, u32[]{:S(2)}) %collective-permute-start.1) | collective-permute-done | bytes 540704 | tf_op jit(solution)/shard_map/ppermute | solution.py:310
  19.0 0.8 %shard_map.32 = (f32[16,128]{1,0:T(8,128)S(1)}, f32[3,128]{1,0:T(4,128)S(1)}) custom-call(s32[84]{0:T(128)S(1)} %concatenate.3.meta_ref, bf16[2048,1024]{1,0:T(8,128)(2,1)S(1)} %get-tuple-element.53.unit_ref, bf16[264,1024]{1,0:T(8,128)(2,1)S(1)} %collective-permute-done.1.piece_ref, f32[16,128]{1,0:T(8,128)S(1)} %get-tuple-element.57.before_ref), custom_call_target="tpu_custom_call" | custom-call | flops 1073741824 | bytes 1024 | tf_op jit(solution)/shard_map/pallas_call | solution.py:236
  19.8 1.3 %collective-permute-start.3 = (f32[3,128]{1,0:T(4,128)S(1)}, f32[3,128]{1,0:T(4,128)S(1)}, u32[]{:S(2)}, u32[]{:S(2)}) collective-permute-start(f32[3,128]{1,0:T(4,128)S(1)} %get-tuple-element.62), channel_id=1, source_target_pairs={{4,0},{8,12},{5,1},{9,13},{6,2},{10,14},{7,3},{11,15},{20,16},{24,... | collective-permute-start | bytes 4616 | tf_op jit(solution)/shard_map/ppermute | solution.py:356
  21.1 0.0 collective-permute-done.piece_ref
  21.1 0.8 %shard_map.33 = (f32[16,128]{1,0:T(8,128)S(1)}, f32[3,128]{1,0:T(4,128)S(1)}) custom-call(s32[84]{0:T(128)S(1)} %concatenate.3.meta_ref, bf16[2048,1024]{1,0:T(8,128)(2,1)S(1)} %get-tuple-element.53.unit_ref, bf16[264,1024]{1,0:T(8,128)(2,1)S(1)} %collective-permute-done.piece_ref, f32[16,128]{1,0:T(8,128)S(1)} %get-tuple-element.58.before_ref), custom_call_target="tpu_custom_call" | custom-call | flops 1073741824 | bytes 1024 | tf_op jit(solution)/shard_map/pallas_call | solution.py:236
  21.8 0.7 %collective-permute-start.5 = (f32[3,128]{1,0:T(4,128)S(1)}, f32[3,128]{1,0:T(4,128)S(1)}, u32[]{:S(2)}, u32[]{:S(2)}) collective-permute-start(f32[3,128]{1,0:T(4,128)S(1)} %get-tuple-element.59.swap_cols_ref.here_ref), channel_id=1, source_target_pairs={{8,4},{4,8},{9,5},{5,9},{10,6},{6,10},{11,7},{7,11},{24,20},{20,24... | collective-permute-start | bytes 4616 | tf_op jit(solution)/shard_map/ppermute | solution.py:358
  22.5 10.2 %collective-permute-done.2.piece_ref = bf16[264,1024]{1,0:T(8,128)(2,1)S(1)} collective-permute-done((bf16[264,1024]{1,0:T(8,128)(2,1)S(1)}, bf16[264,1024]{1,0:T(8,128)(2,1)S(1)}, u32[]{:S(2)}, u32[]{:S(2)}) %collective-permute-start.2) | collective-permute-done | bytes 540704 | tf_op jit(solution)/shard_map/ppermute | solution.py:343
  32.7 0.0 collective-permute-done.3.outer_back_ref
  32.7 0.8 %shard_map.34 = (f32[8,128]{1,0:T(8,128)S(1)}, f32[8,128]{1,0:T(8,128)S(1)}, f32[3,128]{1,0:T(4,128)S(1)}) custom-call(s32[84]{0:T(128)S(1)} %concatenate.3.meta_ref, bf16[2048,1024]{1,0:T(8,128)(2,1)S(1)} %get-tuple-element.53.unit_ref, bf16[264,1024]{1,0:T(8,128)(2,1)S(1)} %collective-permute-done.2.piece_ref, f32[16,128]{1,0:T(8,128)S(1)} %get-tuple-element.61.before_ref, ...), custom_call_target="tpu_custom_call" | custom-call | flops 1073741824 | bytes 1024 | tf_op jit(solution)/shard_map/pallas_call | solution.py:236
  33.5 2.2 %collective-permute-start.4 = (f32[3,128]{1,0:T(4,128)S(1)}, f32[3,128]{1,0:T(4,128)S(1)}, u32[]{:S(2)}, u32[]{:S(2)}) collective-permute-start(f32[3,128]{1,0:T(4,128)S(1)} %get-tuple-element.63), channel_id=1, source_target_pairs={{4,0},{8,12},{12,4},{0,8},{5,1},{9,13},{13,5},{1,9},{6,2},{10,14},... | collective-permute-start | bytes 4616 | tf_op jit(solution)/shard_map/ppermute | solution.py:373
  35.6 0.0 collective-permute-start.6
  35.6 0.0 collective-permute-done.5
  35.7 1.5 %collective-permute-done.4.home_ref = f32[3,128]{1,0:T(4,128)S(1)} collective-permute-done((f32[3,128]{1,0:T(4,128)S(1)}, f32[3,128]{1,0:T(4,128)S(1)}, u32[]{:S(2)}, u32[]{:S(2)}) %collective-permute-start.4) | collective-permute-done | bytes 1568 | tf_op jit(solution)/shard_map/ppermute | solution.py:373
  37.1 0.0 collective-permute-done.6
  37.2 1.6 %collective-permute-start.7 = (f32[4,128]{1,0:T(4,128)S(1)}, f32[4,128]{1,0:T(4,128)S(1)}, u32[]{:S(2)}, u32[]{:S(2)}) collective-permute-start(f32[4,128]{1,0:T(4,128)S(1)} %get-tuple-element.73), channel_id=1, source_target_pairs={{0,2},{1,3},{2,0},{3,1},{4,6},{5,7},{6,4},{7,5},{8,10},{9,11},{10,... | collective-permute-start | bytes 6152 | tf_op jit(solution)/shard_map/ppermute | solution.py:383
  38.7 0.6 %shard_map.35 = s32[1]{0:T(128)} custom-call(f32[3,128]{1,0:T(4,128)S(1)} %get-tuple-element.59.swap_cols_ref.here_ref, f32[3,128]{1,0:T(4,128)S(1)} %collective-permute-done.4.home_ref), custom_call_target="tpu_custom_call" | custom-call | tf_op jit(solution)/shard_map/pallas_call | solution.py:386
  40.0 0.8 %collective-permute-done.7 = f32[4,128]{1,0:T(4,128)S(1)} collective-permute-done((f32[4,128]{1,0:T(4,128)S(1)}, f32[4,128]{1,0:T(4,128)S(1)}, u32[]{:S(2)}, u32[]{:S(2)}) %collective-permute-start.7) | collective-permute-done | bytes 2080 | tf_op jit(solution)/shard_map/ppermute | solution.py:383
  40.8 0.0 copy-start.4
  40.8 0.6 %copy-done.4 = f32[512]{0:T(512)} copy-done((f32[512]{0:T(512)}, f32[512]{0:T(512)S(1)}, u32[]{:S(2)}) %copy-start.4) | copy-done | bytes 2072
  (9 shorter events, 0.0 us)
Async XLA Ops:
  0.0 7.1 %copy-start.3 = (s32[2048]{0:T(1024)S(1)}, s32[2048]{0:T(1024)}, u32[]{:S(2)}) copy-start(s32[2048]{0:T(1024)} %param.5) | copy-start | bytes 24580
  1.4 17.6 %collective-permute-start.1 = (bf16[264,1024]{1,0:T(8,128)(2,1)S(1)}, bf16[264,1024]{1,0:T(8,128)(2,1)S(1)}, u32[]{:S(2)}, u32[]{:S(2)}) collective-permute-start(bf16[264,1024]{1,0:T(8,128)(2,1)S(1)} %get-tuple-element.54), channel_id=1, source_target_pairs={{0,4},{12,8},{1,5},{13,9},{2,6},{14,10},{3,7},{15,11},{16,20},{28,... | collective-permute-start | bytes 1622024 | tf_op jit(solution)/shard_map/ppermute | solution.py:310
  6.4 14.7 %collective-permute-start = (bf16[264,1024]{1,0:T(8,128)(2,1)S(1)}, bf16[264,1024]{1,0:T(8,128)(2,1)S(1)}, u32[]{:S(2)}, u32[]{:S(2)}) collective-permute-start(bf16[264,1024]{1,0:T(8,128)(2,1)S(1)} %get-tuple-element.54), channel_id=1, source_target_pairs={{4,8},{8,4},{5,9},{9,5},{6,10},{10,6},{7,11},{11,7},{20,24},{24,20... | collective-permute-start | bytes 1622024 | tf_op jit(solution)/shard_map/ppermute | solution.py:309
  13.6 19.0 %collective-permute-start.2 = (bf16[264,1024]{1,0:T(8,128)(2,1)S(1)}, bf16[264,1024]{1,0:T(8,128)(2,1)S(1)}, u32[]{:S(2)}, u32[]{:S(2)}) collective-permute-start(bf16[264,1024]{1,0:T(8,128)(2,1)S(1)} %get-tuple-element.60), channel_id=1, source_target_pairs={{0,4},{12,8},{4,12},{8,0},{1,5},{13,9},{5,13},{9,1},{2,6},{14,10},... | collective-permute-start | bytes 1622024 | tf_op jit(solution)/shard_map/ppermute | solution.py:343
  19.8 12.9 %collective-permute-start.3 = (f32[3,128]{1,0:T(4,128)S(1)}, f32[3,128]{1,0:T(4,128)S(1)}, u32[]{:S(2)}, u32[]{:S(2)}) collective-permute-start(f32[3,128]{1,0:T(4,128)S(1)} %get-tuple-element.62), channel_id=1, source_target_pairs={{4,0},{8,12},{5,1},{9,13},{6,2},{10,14},{7,3},{11,15},{20,16},{24,... | collective-permute-start | bytes 4616 | tf_op jit(solution)/shard_map/ppermute | solution.py:356
  21.8 13.8 %collective-permute-start.5 = (f32[3,128]{1,0:T(4,128)S(1)}, f32[3,128]{1,0:T(4,128)S(1)}, u32[]{:S(2)}, u32[]{:S(2)}) collective-permute-start(f32[3,128]{1,0:T(4,128)S(1)} %get-tuple-element.59.swap_cols_ref.here_ref), channel_id=1, source_target_pairs={{8,4},{4,8},{9,5},{5,9},{10,6},{6,10},{11,7},{7,11},{24,20},{20,24... | collective-permute-start | bytes 4616 | tf_op jit(solution)/shard_map/ppermute | solution.py:358
  33.5 3.6 %collective-permute-start.4 = (f32[3,128]{1,0:T(4,128)S(1)}, f32[3,128]{1,0:T(4,128)S(1)}, u32[]{:S(2)}, u32[]{:S(2)}) collective-permute-start(f32[3,128]{1,0:T(4,128)S(1)} %get-tuple-element.63), channel_id=1, source_target_pairs={{4,0},{8,12},{12,4},{0,8},{5,1},{9,13},{13,5},{1,9},{6,2},{10,14},... | collective-permute-start | bytes 4616 | tf_op jit(solution)/shard_map/ppermute | solution.py:373
  35.6 1.5 %collective-permute-start.6 = (f32[8,128]{1,0:T(8,128)S(1)}, f32[8,128]{1,0:T(8,128)S(1)}, u32[]{:S(2)}, u32[]{:S(2)}) collective-permute-start(f32[8,128]{1,0:T(8,128)S(1)} %get-tuple-element.66), channel_id=1, source_target_pairs={{0,1},{1,0},{2,3},{3,2},{4,5},{5,4},{6,7},{7,6},{8,9},{9,8},{10,11... | collective-permute-start | bytes 12296 | tf_op jit(solution)/shard_map/ppermute | solution.py:376
  37.2 3.7 %collective-permute-start.7 = (f32[4,128]{1,0:T(4,128)S(1)}, f32[4,128]{1,0:T(4,128)S(1)}, u32[]{:S(2)}, u32[]{:S(2)}) collective-permute-start(f32[4,128]{1,0:T(4,128)S(1)} %get-tuple-element.73), channel_id=1, source_target_pairs={{0,2},{1,3},{2,0},{3,1},{4,6},{5,7},{6,4},{7,5},{8,10},{9,11},{10,... | collective-permute-start | bytes 6152 | tf_op jit(solution)/shard_map/ppermute | solution.py:383
  40.8 0.6 %copy-start.4 = (f32[512]{0:T(512)}, f32[512]{0:T(512)S(1)}, u32[]{:S(2)}) copy-start(f32[512]{0:T(512)S(1)} %get-tuple-element.107) | copy-start | bytes 6148

commit v16 on v15

--- a/solution.py
+++ b/solution.py
@@ -152,46 +152,48 @@
     return row[:, :size], row[:, size : size + BLOCK]
 
 
-def cross_terms(meta, chunk, column_tags, unit_ref, piece_unit, before_ref, sums, columns, place):
+def cross_terms(meta, chunk, column_tags, unit_ref, piece_ref, before_ref, sums, columns, place):
     size = column_tags.shape[1]
-    half = meta.blocks // 2
-    columns[...] = jnp.zeros_like(columns)
+    there = [jnp.max(column_tags[:, at : at + BLOCK]) for at in range(0, size, BLOCK)]
+    shared = False
     for block in range(meta.blocks):
-        sums[place(block) : place(block) + 1, :] = before_ref[block : block + 1, :]
-    there = [jnp.max(column_tags[:, at : at + BLOCK]) for at in range(0, size, BLOCK)]
-    for first in (0, half):
-        shared = False
-        for block in range(first, first + half):
-            for tag in there:
-                shared = (meta.tag(block, chunk).astype(jnp.float32) == tag) | shared
-
-        @pl.when(shared)
-        def _():
-            total = None
-            for start in range(first * BLOCK, (first + half) * BLOCK, STEP):
-                cosine = products(unit_ref[start : start + STEP, :], piece_unit[...])
-                for inner in range(0, STEP, BLOCK):
-                    block = (start + inner) // BLOCK
-                    bias = column_bias(meta.tag(block, chunk), column_tags)
-                    weight = jnp.exp2(cosine[inner : inner + BLOCK] * GAIN + bias)
-                    row = lax.broadcasted_iota(jnp.int32, weight.shape, 0)
-                    weight = jnp.where(row < meta.used(block), weight, 0.0)
-                    sums[place(block) : place(block) + 1, :] += lane_sums(weight)
-                    partial = weight[0:8]
-                    for down in range(8, BLOCK, 8):
-                        partial = partial + weight[down : down + 8]
-                    total = partial if total is None else total + partial
-            columns[...] += total
-
-
-def middle_kernel(
-    blocks, share, chunk, meta_ref, unit_ref, piece_ref, before_ref, sums_ref, cols_ref, piece_unit, columns
-):
+        for tag in there:
+            shared = (meta.tag(block, chunk).astype(jnp.float32) == tag) | shared
+
+    @pl.when(jnp.logical_not(shared))
+    def _():
+        columns[...] = jnp.zeros_like(columns)
+        for block in range(meta.blocks):
+            sums[place(block) : place(block) + 1, :] = before_ref[block : block + 1, :]
+
+    @pl.when(shared)
+    def _():
+        norms = []
+        for at in range(0, size, BLOCK):
+            values = piece_ref[at : at + BLOCK, :].astype(jnp.float32)
+            norms.append(lane_sums(values * values))
+        scale = GAIN * lax.rsqrt(jnp.concatenate(norms, axis=1) + norm_eps)
+        total = None
+        for start in range(0, meta.blocks * BLOCK, STEP):
+            product = products(unit_ref[start : start + STEP, :], piece_ref[:size, :])
+            for inner in range(0, STEP, BLOCK):
+                block = (start + inner) // BLOCK
+                bias = column_bias(meta.tag(block, chunk), column_tags)
+                weight = jnp.exp2(product[inner : inner + BLOCK] * scale + bias)
+                row = lax.broadcasted_iota(jnp.int32, weight.shape, 0)
+                weight = jnp.where(row < meta.used(block), weight, 0.0)
+                sums[place(block) : place(block) + 1, :] = before_ref[block : block + 1, :] + lane_sums(weight)
+                partial = weight[0:8]
+                for down in range(8, BLOCK, 8):
+                    partial = partial + weight[down : down + 8]
+                total = partial if total is None else total + partial
+        columns[...] = total
+
+
+def middle_kernel(blocks, share, chunk, meta_ref, unit_ref, piece_ref, before_ref, sums_ref, cols_ref, columns):
     meta = Meta(meta_ref, blocks)
-    size = share * BLOCK
-    piece_unit[...] = normalised(piece_ref[:size, :])
-    tags, edge = chunk_tags(piece_ref, size)
-    cross_terms(meta, chunk, tags, unit_ref, piece_unit, before_ref, sums_ref, columns, lambda block: block)
+    tags, edge = chunk_tags(piece_ref, share * BLOCK)
+    cross_terms(meta, chunk, tags, unit_ref, piece_ref, before_ref, sums_ref, columns, lambda block: block)
     total = jnp.sum(columns[...], axis=0, keepdims=True)
     for k in range(share):
         cols_ref[k : k + 1, :] = total[:, k * BLOCK : (k + 1) * BLOCK]
@@ -202,18 +204,16 @@
 
 def last_kernel(
     blocks, share, width, meta_ref, unit_ref, piece_ref, before_ref, outer_back_ref, swap_cols_ref,
-    keep_ref, send_ref, cols_ref, piece_unit, sums, columns,
+    keep_ref, send_ref, cols_ref, sums, columns,
 ):
     meta = Meta(meta_ref, blocks)
-    size = share * BLOCK
-    piece_unit[...] = normalised(piece_ref[:size, :])
-    tags, _ = chunk_tags(piece_ref, size)
+    tags, _ = chunk_tags(piece_ref, share * BLOCK)
 
     def place(block):
         owner = block // width
         return owner % 2 * (blocks // 2) + owner // 2 * width + block % width
 
-    cross_terms(meta, 2, tags, unit_ref, piece_unit, before_ref, sums, columns, place)
+    cross_terms(meta, 2, tags, unit_ref, piece_ref, before_ref, sums, columns, place)
     total = jnp.sum(columns[...], axis=0, keepdims=True)
     for k in range(share):
         cols_ref[k : k + 1, :] = total[:, k * BLOCK : (k + 1) * BLOCK]
@@ -348,7 +348,7 @@
             meta,
             (unit, piece, before),
             [row_sums, col_sums],
-            [pltpu.VMEM((size, depth), jnp.bfloat16), pltpu.VMEM((8, size), jnp.float32)],
+            [pltpu.VMEM((8, size), jnp.float32)],
             2 * rows * size * depth,
         )
 
@@ -363,7 +363,6 @@
         (unit, last, sums, outer_back, swap_cols),
         [half, half, col_sums],
         [
-            pltpu.VMEM((size, depth), jnp.bfloat16),
             pltpu.VMEM((blocks, BLOCK), jnp.float32),
             pltpu.VMEM((8, size), jnp.float32),
         ],

time: 41.6 us -> 41.5 us (level)
  transfers between devices with their start and end apart: 8 -> 8, of which waited for: 4 -> 4; matrix products, arithmetic and copies ran while one was open for 1% -> 1% of each run, Pallas kernels for 22% -> 21%
where the time goes in v16:
time: 41.5 us; the launch traced here: 41.3 us
  waiting for transfers between devices  16 us (39%)
  starting transfers between devices  13.2 us (32%)
  Pallas kernels  10.2 us (25%)
  between operations  0.92 us (2%)
  local copies, waits for them, and re-layouts  0.81 us (2%)
    ppermute x1, waiting for transfers between devices, shards(): last = lax.ppermute(second_out, 'tile', around)  10.3 us
    pallas_call x1, Pallas kernels, shards(): pl.pallas_call(functools.partial(self_kernel, blocks, subs), in_specs=[sm...  6.05 us
    ppermute x1, starting transfers between devices, shards(): from_outer = lax.ppermute(first_out, 'tile', inward)  4.96 us
    ppermute x1, waiting for transfers between devices, shards(): from_outer = lax.ppermute(first_out, 'tile', inward)  3.15 us
    ppermute x1, starting transfers between devices, shards(): last = lax.ppermute(second_out, 'tile', around)  2.2 us
    pallas_call x3, Pallas kernels, call(): pl.pallas_call(kernel, in_specs=[smem] + [vmem] * len(operands), out_spec...  2.12 us
    ppermute x1, starting transfers between devices, shards(): home = lax.ppermute(cols, 'tile', turned(around))  1.88 us
    ppermute x1, waiting for transfers between devices, shards(): home = lax.ppermute(cols, 'tile', turned(around))  1.75 us
  transfers between devices with their start and end apart: 8, of which 4 were waited for; matrix products, arithmetic and copies ran while one was open for 1% of the time, Pallas kernels for 21%

profile of v16, /device:TPU:0, one launch (start us, length us, event | category | flops | bytes accessed | tf_op | source)
XLA Modules:
  0.0 41.3 jit_solution(9196620809333538840)
XLA Ops:
  0.0 0.0 copy-start.3
  0.0 1.4 %shard_map.31 = (bf16[264,1024]{1,0:T(8,128)(2,1)S(1)}, bf16[264,1024]{1,0:T(8,128)(2,1)S(1)}) custom-call(bf16[2048,1024]{1,0:T(8,128)(2,1)} %rows_ref.3, s32[16,128]{1,0:T(8,128)} %bitcast.58), custom_call_target="tpu_custom_call" | custom-call | bytes 1024 | tf_op jit(solution)/shard_map/pallas_call | solution.py:92
  1.4 5.0 %collective-permute-start.1 = (bf16[264,1024]{1,0:T(8,128)(2,1)S(1)}, bf16[264,1024]{1,0:T(8,128)(2,1)S(1)}, u32[]{:S(2)}, u32[]{:S(2)}) collective-permute-start(bf16[264,1024]{1,0:T(8,128)(2,1)S(1)} %get-tuple-element.54), channel_id=1, source_target_pairs={{0,4},{12,8},{1,5},{13,9},{2,6},{14,10},{3,7},{15,11},{16,20},{28,... | collective-permute-start | bytes 1622024 | tf_op jit(solution)/shard_map/ppermute | solution.py:310
  6.4 0.7 %collective-permute-start = (bf16[264,1024]{1,0:T(8,128)(2,1)S(1)}, bf16[264,1024]{1,0:T(8,128)(2,1)S(1)}, u32[]{:S(2)}, u32[]{:S(2)}) collective-permute-start(bf16[264,1024]{1,0:T(8,128)(2,1)S(1)} %get-tuple-element.54), channel_id=1, source_target_pairs={{4,8},{8,4},{5,9},{9,5},{6,10},{10,6},{7,11},{11,7},{20,24},{24,20... | collective-permute-start | bytes 1622024 | tf_op jit(solution)/shard_map/ppermute | solution.py:309
  7.1 0.0 copy-done.3
  7.1 0.1 convert_reduce_fusion
  7.3 0.1 dynamic_slice.47
  7.4 0.1 concatenate.3.meta_ref
  7.5 0.1 broadcast_in_dim.128
  7.6 6.0 %shard_map.30 = (bf16[2048,1024]{1,0:T(8,128)(2,1)S(1)}, f32[16,128]{1,0:T(8,128)S(1)}) custom-call(s32[84]{0:T(128)S(1)} %concatenate.3.meta_ref, bf16[2048,1024]{1,0:T(8,128)(2,1)} %rows_ref.3, s32[1,512]{1,0:T(1,128)S(1)} %bitcast.57), custom_call_target="tpu_custom_call" | custom-call | bytes 1024 | tf_op jit(solution)/shard_map/pallas_call | solution.py:333
  13.6 2.2 %collective-permute-start.2 = (bf16[264,1024]{1,0:T(8,128)(2,1)S(1)}, bf16[264,1024]{1,0:T(8,128)(2,1)S(1)}, u32[]{:S(2)}, u32[]{:S(2)}) collective-permute-start(bf16[264,1024]{1,0:T(8,128)(2,1)S(1)} %get-tuple-element.60), channel_id=1, source_target_pairs={{0,4},{12,8},{4,12},{8,0},{1,5},{13,9},{5,13},{9,1},{2,6},{14,10},... | collective-permute-start | bytes 1622024 | tf_op jit(solution)/shard_map/ppermute | solution.py:343
  15.8 3.1 %collective-permute-done.1.piece_ref = bf16[264,1024]{1,0:T(8,128)(2,1)S(1)} collective-permute-done((bf16[264,1024]{1,0:T(8,128)(2,1)S(1)}, bf16[264,1024]{1,0:T(8,128)(2,1)S(1)}, u32[]{:S(2)}, u32[]{:S(2)}) %collective-permute-start.1) | collective-permute-done | bytes 540704 | tf_op jit(solution)/shard_map/ppermute | solution.py:310
  19.0 0.7 %shard_map.32 = (f32[16,128]{1,0:T(8,128)S(1)}, f32[3,128]{1,0:T(4,128)S(1)}) custom-call(s32[84]{0:T(128)S(1)} %concatenate.3.meta_ref, bf16[2048,1024]{1,0:T(8,128)(2,1)S(1)} %get-tuple-element.53.unit_ref, bf16[264,1024]{1,0:T(8,128)(2,1)S(1)} %collective-permute-done.1.piece_ref, f32[16,128]{1,0:T(8,128)S(1)} %get-tuple-element.57.before_ref), custom_call_target="tpu_custom_call" | custom-call | flops 1073741824 | bytes 1024 | tf_op jit(solution)/shard_map/pallas_call | solution.py:236
  19.7 1.3 %collective-permute-start.3 = (f32[3,128]{1,0:T(4,128)S(1)}, f32[3,128]{1,0:T(4,128)S(1)}, u32[]{:S(2)}, u32[]{:S(2)}) collective-permute-start(f32[3,128]{1,0:T(4,128)S(1)} %get-tuple-element.62), channel_id=1, source_target_pairs={{4,0},{8,12},{5,1},{9,13},{6,2},{10,14},{7,3},{11,15},{20,16},{24,... | collective-permute-start | bytes 4616 | tf_op jit(solution)/shard_map/ppermute | solution.py:356
  21.0 0.0 collective-permute-done.piece_ref
  21.0 0.7 %shard_map.33 = (f32[16,128]{1,0:T(8,128)S(1)}, f32[3,128]{1,0:T(4,128)S(1)}) custom-call(s32[84]{0:T(128)S(1)} %concatenate.3.meta_ref, bf16[2048,1024]{1,0:T(8,128)(2,1)S(1)} %get-tuple-element.53.unit_ref, bf16[264,1024]{1,0:T(8,128)(2,1)S(1)} %collective-permute-done.piece_ref, f32[16,128]{1,0:T(8,128)S(1)} %get-tuple-element.58.before_ref), custom_call_target="tpu_custom_call" | custom-call | flops 1073741824 | bytes 1024 | tf_op jit(solution)/shard_map/pallas_call | solution.py:236
  21.7 0.7 %collective-permute-start.5 = (f32[3,128]{1,0:T(4,128)S(1)}, f32[3,128]{1,0:T(4,128)S(1)}, u32[]{:S(2)}, u32[]{:S(2)}) collective-permute-start(f32[3,128]{1,0:T(4,128)S(1)} %get-tuple-element.59.swap_cols_ref.here_ref), channel_id=1, source_target_pairs={{8,4},{4,8},{9,5},{5,9},{10,6},{6,10},{11,7},{7,11},{24,20},{20,24... | collective-permute-start | bytes 4616 | tf_op jit(solution)/shard_map/ppermute | solution.py:358
  22.4 10.3 %collective-permute-done.2.piece_ref = bf16[264,1024]{1,0:T(8,128)(2,1)S(1)} collective-permute-done((bf16[264,1024]{1,0:T(8,128)(2,1)S(1)}, bf16[264,1024]{1,0:T(8,128)(2,1)S(1)}, u32[]{:S(2)}, u32[]{:S(2)}) %collective-permute-start.2) | collective-permute-done | bytes 540704 | tf_op jit(solution)/shard_map/ppermute | solution.py:343
  32.7 0.0 collective-permute-done.3.outer_back_ref
  32.7 0.7 %shard_map.34 = (f32[8,128]{1,0:T(8,128)S(1)}, f32[8,128]{1,0:T(8,128)S(1)}, f32[3,128]{1,0:T(4,128)S(1)}) custom-call(s32[84]{0:T(128)S(1)} %concatenate.3.meta_ref, bf16[2048,1024]{1,0:T(8,128)(2,1)S(1)} %get-tuple-element.53.unit_ref, bf16[264,1024]{1,0:T(8,128)(2,1)S(1)} %collective-permute-done.2.piece_ref, f32[16,128]{1,0:T(8,128)S(1)} %get-tuple-element.61.before_ref, ...), custom_call_target="tpu_custom_call" | custom-call | flops 1073741824 | bytes 1024 | tf_op jit(solution)/shard_map/pallas_call | solution.py:236
  33.4 1.9 %collective-permute-start.4 = (f32[3,128]{1,0:T(4,128)S(1)}, f32[3,128]{1,0:T(4,128)S(1)}, u32[]{:S(2)}, u32[]{:S(2)}) collective-permute-start(f32[3,128]{1,0:T(4,128)S(1)} %get-tuple-element.63), channel_id=1, source_target_pairs={{4,0},{8,12},{12,4},{0,8},{5,1},{9,13},{13,5},{1,9},{6,2},{10,14},... | collective-permute-start | bytes 4616 | tf_op jit(solution)/shard_map/ppermute | solution.py:372
  35.3 0.0 collective-permute-start.6
  35.3 0.0 collective-permute-done.5
  35.3 1.8 %collective-permute-done.4.home_ref = f32[3,128]{1,0:T(4,128)S(1)} collective-permute-done((f32[3,128]{1,0:T(4,128)S(1)}, f32[3,128]{1,0:T(4,128)S(1)}, u32[]{:S(2)}, u32[]{:S(2)}) %collective-permute-start.4) | collective-permute-done | bytes 1568 | tf_op jit(solution)/shard_map/ppermute | solution.py:372
  37.1 0.0 collective-permute-done.6
  37.1 1.6 %collective-permute-start.7 = (f32[4,128]{1,0:T(4,128)S(1)}, f32[4,128]{1,0:T(4,128)S(1)}, u32[]{:S(2)}, u32[]{:S(2)}) collective-permute-start(f32[4,128]{1,0:T(4,128)S(1)} %get-tuple-element.73), channel_id=1, source_target_pairs={{0,2},{1,3},{2,0},{3,1},{4,6},{5,7},{6,4},{7,5},{8,10},{9,11},{10,... | collective-permute-start | bytes 6152 | tf_op jit(solution)/shard_map/ppermute | solution.py:382
  38.7 0.6 %shard_map.35 = s32[1]{0:T(128)} custom-call(f32[3,128]{1,0:T(4,128)S(1)} %get-tuple-element.59.swap_cols_ref.here_ref, f32[3,128]{1,0:T(4,128)S(1)} %collective-permute-done.4.home_ref), custom_call_target="tpu_custom_call" | custom-call | tf_op jit(solution)/shard_map/pallas_call | solution.py:385
  40.0 0.8 %collective-permute-done.7 = f32[4,128]{1,0:T(4,128)S(1)} collective-permute-done((f32[4,128]{1,0:T(4,128)S(1)}, f32[4,128]{1,0:T(4,128)S(1)}, u32[]{:S(2)}, u32[]{:S(2)}) %collective-permute-start.7) | collective-permute-done | bytes 2080 | tf_op jit(solution)/shard_map/ppermute | solution.py:382
  40.8 0.0 copy-start.4
  40.8 0.6 %copy-done.4 = f32[512]{0:T(512)} copy-done((f32[512]{0:T(512)}, f32[512]{0:T(512)S(1)}, u32[]{:S(2)}) %copy-start.4) | copy-done | bytes 2072
  (9 shorter events, 0.0 us)
Async XLA Ops:
  0.0 7.1 %copy-start.3 = (s32[2048]{0:T(1024)S(1)}, s32[2048]{0:T(1024)}, u32[]{:S(2)}) copy-start(s32[2048]{0:T(1024)} %param.5) | copy-start | bytes 24580
  1.4 17.6 %collective-permute-start.1 = (bf16[264,1024]{1,0:T(8,128)(2,1)S(1)}, bf16[264,1024]{1,0:T(8,128)(2,1)S(1)}, u32[]{:S(2)}, u32[]{:S(2)}) collective-permute-start(bf16[264,1024]{1,0:T(8,128)(2,1)S(1)} %get-tuple-element.54), channel_id=1, source_target_pairs={{0,4},{12,8},{1,5},{13,9},{2,6},{14,10},{3,7},{15,11},{16,20},{28,... | collective-permute-start | bytes 1622024 | tf_op jit(solution)/shard_map/ppermute | solution.py:310
  6.4 14.6 %collective-permute-start = (bf16[264,1024]{1,0:T(8,128)(2,1)S(1)}, bf16[264,1024]{1,0:T(8,128)(2,1)S(1)}, u32[]{:S(2)}, u32[]{:S(2)}) collective-permute-start(bf16[264,1024]{1,0:T(8,128)(2,1)S(1)} %get-tuple-element.54), channel_id=1, source_target_pairs={{4,8},{8,4},{5,9},{9,5},{6,10},{10,6},{7,11},{11,7},{20,24},{24,20... | collective-permute-start | bytes 1622024 | tf_op jit(solution)/shard_map/ppermute | solution.py:309
  13.6 19.0 %collective-permute-start.2 = (bf16[264,1024]{1,0:T(8,128)(2,1)S(1)}, bf16[264,1024]{1,0:T(8,128)(2,1)S(1)}, u32[]{:S(2)}, u32[]{:S(2)}) collective-permute-start(bf16[264,1024]{1,0:T(8,128)(2,1)S(1)} %get-tuple-element.60), channel_id=1, source_target_pairs={{0,4},{12,8},{4,12},{8,0},{1,5},{13,9},{5,13},{9,1},{2,6},{14,10},... | collective-permute-start | bytes 1622024 | tf_op jit(solution)/shard_map/ppermute | solution.py:343
  19.7 13.0 %collective-permute-start.3 = (f32[3,128]{1,0:T(4,128)S(1)}, f32[3,128]{1,0:T(4,128)S(1)}, u32[]{:S(2)}, u32[]{:S(2)}) collective-permute-start(f32[3,128]{1,0:T(4,128)S(1)} %get-tuple-element.62), channel_id=1, source_target_pairs={{4,0},{8,12},{5,1},{9,13},{6,2},{10,14},{7,3},{11,15},{20,16},{24,... | collective-permute-start | bytes 4616 | tf_op jit(solution)/shard_map/ppermute | solution.py:356
  21.7 13.6 %collective-permute-start.5 = (f32[3,128]{1,0:T(4,128)S(1)}, f32[3,128]{1,0:T(4,128)S(1)}, u32[]{:S(2)}, u32[]{:S(2)}) collective-permute-start(f32[3,128]{1,0:T(4,128)S(1)} %get-tuple-element.59.swap_cols_ref.here_ref), channel_id=1, source_target_pairs={{8,4},{4,8},{9,5},{5,9},{10,6},{6,10},{11,7},{7,11},{24,20},{20,24... | collective-permute-start | bytes 4616 | tf_op jit(solution)/shard_map/ppermute | solution.py:358
  33.4 3.6 %collective-permute-start.4 = (f32[3,128]{1,0:T(4,128)S(1)}, f32[3,128]{1,0:T(4,128)S(1)}, u32[]{:S(2)}, u32[]{:S(2)}) collective-permute-start(f32[3,128]{1,0:T(4,128)S(1)} %get-tuple-element.63), channel_id=1, source_target_pairs={{4,0},{8,12},{12,4},{0,8},{5,1},{9,13},{13,5},{1,9},{6,2},{10,14},... | collective-permute-start | bytes 4616 | tf_op jit(solution)/shard_map/ppermute | solution.py:372
  35.3 1.8 %collective-permute-start.6 = (f32[8,128]{1,0:T(8,128)S(1)}, f32[8,128]{1,0:T(8,128)S(1)}, u32[]{:S(2)}, u32[]{:S(2)}) collective-permute-start(f32[8,128]{1,0:T(8,128)S(1)} %get-tuple-element.66), channel_id=1, source_target_pairs={{0,1},{1,0},{2,3},{3,2},{4,5},{5,4},{6,7},{7,6},{8,9},{9,8},{10,11... | collective-permute-start | bytes 12296 | tf_op jit(solution)/shard_map/ppermute | solution.py:375
  37.1 3.7 %collective-permute-start.7 = (f32[4,128]{1,0:T(4,128)S(1)}, f32[4,128]{1,0:T(4,128)S(1)}, u32[]{:S(2)}, u32[]{:S(2)}) collective-permute-start(f32[4,128]{1,0:T(4,128)S(1)} %get-tuple-element.73), channel_id=1, source_target_pairs={{0,2},{1,3},{2,0},{3,1},{4,6},{5,7},{6,4},{7,5},{8,10},{9,11},{10,... | collective-permute-start | bytes 6152 | tf_op jit(solution)/shard_map/ppermute | solution.py:382
  40.8 0.6 %copy-start.4 = (f32[512]{0:T(512)}, f32[512]{0:T(512)S(1)}, u32[]{:S(2)}) copy-start(f32[512]{0:T(512)S(1)} %get-tuple-element.107) | copy-start | bytes 6148

commit v17 on v16

--- a/solution.py
+++ b/solution.py
@@ -115,6 +115,7 @@
 
 
 MEMBER, FIRST_BLOCK, EDGE, INNER = range(4)
+INWARD, SWAPPED, FIRST = range(3)
 
 
 def self_kernel(blocks, subs, meta_ref, rows_ref, tags_ref, unit_ref, sums_ref, held, sems):
@@ -168,18 +169,14 @@
 
     @pl.when(shared)
     def _():
-        norms = []
-        for at in range(0, size, BLOCK):
-            values = piece_ref[at : at + BLOCK, :].astype(jnp.float32)
-            norms.append(lane_sums(values * values))
-        scale = GAIN * lax.rsqrt(jnp.concatenate(norms, axis=1) + norm_eps)
+        piece = normalised(piece_ref[:size, :])
         total = None
         for start in range(0, meta.blocks * BLOCK, STEP):
-            product = products(unit_ref[start : start + STEP, :], piece_ref[:size, :])
+            cosine = products(unit_ref[start : start + STEP, :], piece)
             for inner in range(0, STEP, BLOCK):
                 block = (start + inner) // BLOCK
                 bias = column_bias(meta.tag(block, chunk), column_tags)
-                weight = jnp.exp2(product[inner : inner + BLOCK] * scale + bias)
+                weight = jnp.exp2(cosine[inner : inner + BLOCK] * GAIN + bias)
                 row = lax.broadcasted_iota(jnp.int32, weight.shape, 0)
                 weight = jnp.where(row < meta.used(block), weight, 0.0)
                 sums[place(block) : place(block) + 1, :] = before_ref[block : block + 1, :] + lane_sums(weight)
@@ -190,20 +187,26 @@
         columns[...] = total
 
 
-def middle_kernel(blocks, share, chunk, meta_ref, unit_ref, piece_ref, before_ref, sums_ref, cols_ref, columns):
+def middle_kernel(
+    blocks, share, chunk, meta_ref, unit_ref, piece_ref, before_ref, sums_ref, cols_ref, columns
+):
     meta = Meta(meta_ref, blocks)
     tags, edge = chunk_tags(piece_ref, share * BLOCK)
     cross_terms(meta, chunk, tags, unit_ref, piece_ref, before_ref, sums_ref, columns, lambda block: block)
     total = jnp.sum(columns[...], axis=0, keepdims=True)
     for k in range(share):
         cols_ref[k : k + 1, :] = total[:, k * BLOCK : (k + 1) * BLOCK]
-    mine = meta.tag(meta.number(EDGE)).astype(jnp.float32)
-    joined = (edge == mine) & (edge >= 0) & (meta.number(INNER) > 0)
-    cols_ref[share : share + 1, :] = jnp.where(joined, 1.0, 0.0)
+    is_inner = meta.number(INNER) > 0
+    mine = jnp.full(edge.shape, meta.tag(meta.number(EDGE)).astype(jnp.float32))
+    if chunk == SWAPPED:
+        joined = jnp.where((edge == mine) & (edge >= 0), 1.0, 0.0)
+        cols_ref[share : share + 1, :] = jnp.where(is_inner, joined, 2.0)
+    else:
+        cols_ref[share : share + 1, :] = jnp.where(is_inner, mine, edge)
 
 
 def last_kernel(
-    blocks, share, width, meta_ref, unit_ref, piece_ref, before_ref, outer_back_ref, swap_cols_ref,
+    blocks, share, width, meta_ref, unit_ref, piece_ref, before_ref, first_back_ref,
     keep_ref, send_ref, cols_ref, sums, columns,
 ):
     meta = Meta(meta_ref, blocks)
@@ -213,22 +216,23 @@
         owner = block // width
         return owner % 2 * (blocks // 2) + owner // 2 * width + block % width
 
-    cross_terms(meta, 2, tags, unit_ref, piece_ref, before_ref, sums, columns, place)
+    cross_terms(meta, INWARD, tags, unit_ref, piece_ref, before_ref, sums, columns, place)
     total = jnp.sum(columns[...], axis=0, keepdims=True)
     for k in range(share):
         cols_ref[k : k + 1, :] = total[:, k * BLOCK : (k + 1) * BLOCK]
         at = place(meta.number(FIRST_BLOCK) + k)
-        sums[pl.ds(at, 1), :] += outer_back_ref[k : k + 1, :]
-    cols_ref[share : share + 1, :] = swap_cols_ref[share : share + 1, :]
+        sums[pl.ds(at, 1), :] += first_back_ref[k : k + 1, :]
     parity = meta.number(MEMBER) % 2
     heap = blocks // 2
     keep_ref[...] = sums[pl.ds(pl.multiple_of(parity * heap, heap), heap), :]
     send_ref[...] = sums[pl.ds(pl.multiple_of((1 - parity) * heap, heap), heap), :]
 
 
-def flag_kernel(share, here_ref, home_ref, flag_ref):
-    flags = jnp.maximum(here_ref[share : share + 1, :], home_ref[share : share + 1, :])
-    flag_ref[0] = jnp.max(flags).astype(jnp.int32)
+def flag_kernel(share, swap_cols_ref, first_cols_ref, first_back_ref, flag_ref):
+    found = swap_cols_ref[share : share + 1, :]
+    one, other = first_cols_ref[share : share + 1, :], first_back_ref[share : share + 1, :]
+    joined = jnp.where((one == other) & (one >= 0), 1.0, 0.0)
+    flag_ref[0] = jnp.max(jnp.where(found > 1.5, joined, found)).astype(jnp.int32)
 
 
 def call(kernel, meta, operands, out_shapes, scratch, flops):
@@ -306,8 +310,7 @@
 
     by_block = cluster_ids.reshape(blocks, BLOCK)
     first_out, second_out = pack(size, subs, embeddings, by_block)
-    from_inner = lax.ppermute(first_out, "tile", swap)
-    from_outer = lax.ppermute(first_out, "tile", inward)
+    from_first = lax.ppermute(first_out, "tile", around)
 
     tag = jnp.max(by_block, axis=1)
     used = jnp.sum((by_block >= 0).astype(jnp.int32), axis=1)
@@ -317,8 +320,8 @@
     meta = jnp.concatenate([tag, used, seen, swapped, tag, numbers]).astype(jnp.int32)
 
     heap = blocks // 2
-    owner = plan.second // width
-    home_row = jnp.arange(heap)[:, None] - (owner // 2 * width + plan.second % width)
+    owner = plan.first // width
+    home_row = jnp.arange(heap)[:, None] - (owner // 2 * width + plan.first % width)
     home_row = jnp.broadcast_to(home_row, (heap, BLOCK)).astype(jnp.int32)
     upper = [
         jnp.broadcast_to((member >> bit) & 1, (heap >> bit, BLOCK)).astype(jnp.int32)
@@ -339,8 +342,9 @@
         compiler_params=pltpu.CompilerParams(vmem_limit_bytes=24 * 1024 * 1024),
         cost_estimate=pl.CostEstimate(flops=0, bytes_accessed=1024, transcendentals=0),
     )(meta, embeddings, lax.dynamic_slice_in_dim(cluster_ids, member * quarter, quarter, 0)[None])
-    second_out, sums = lax.optimization_barrier((second_out, sums))
-    last = lax.ppermute(second_out, "tile", around)
+    first_out, second_out, sums = lax.optimization_barrier((first_out, second_out, sums))
+    from_swap = lax.ppermute(first_out, "tile", swap)
+    from_last = lax.ppermute(second_out, "tile", inward)
 
     def middle(chunk, piece, before):
         return call(
@@ -352,16 +356,16 @@
             2 * rows * size * depth,
         )
 
-    sums, outer_cols = middle(0, from_outer, sums)
-    outer_back = lax.ppermute(outer_cols, "tile", turned(inward))
-    sums, swap_cols = middle(1, from_inner, sums)
+    sums, first_cols = middle(FIRST, from_first, sums)
+    first_back = lax.ppermute(first_cols, "tile", turned(around))
+    sums, swap_cols = middle(SWAPPED, from_swap, sums)
     swap_back = lax.ppermute(swap_cols, "tile", turned(swap))
     half = jax.ShapeDtypeStruct((heap, BLOCK), jnp.float32)
     held, leaving, cols = call(
         functools.partial(last_kernel, blocks, share, width),
         meta,
-        (unit, last, sums, outer_back, swap_cols),
-        [half, half, col_sums],
+        (unit, from_last, sums, first_back),
+        [half, half, jax.ShapeDtypeStruct((share, BLOCK), jnp.float32)],
         [
             pltpu.VMEM((blocks, BLOCK), jnp.float32),
             pltpu.VMEM((8, size), jnp.float32),
@@ -369,25 +373,26 @@
         2 * rows * size * depth,
     )
 
-    home = lax.ppermute(cols, "tile", turned(around))
+    home = lax.ppermute(cols, "tile", turned(inward))
     for k in range(share):
-        held = held + jnp.where(home_row == k, home[k : k + 1] + swap_back[k : k + 1], 0.0)
+        held = held + jnp.where(home_row == k, swap_back[k : k + 1], 0.0)
     held = held + lax.ppermute(leaving, "sub", [(i, i ^ 1) for i in range(subs)])
-    home, held = lax.optimization_barrier((home, held))
+    held, first_back = lax.optimization_barrier((held, first_back))
     for bit, mine in enumerate(upper, 1):
         pairs = held.reshape(-1, 2, width, BLOCK)
         low, high = pairs[:, 0].reshape(mine.shape), pairs[:, 1].reshape(mine.shape)
         leaving = jnp.where(mine > 0, low, high)
         held = jnp.where(mine > 0, high, low)
         held = held + lax.ppermute(leaving, "sub", [(i, i ^ (1 << bit)) for i in range(subs)])
-    scores = jnp.log(1.0 + held.reshape(-1))
+    home = jnp.concatenate([jnp.zeros_like(home), home])
+    scores = jnp.log(1.0 + (held.reshape(width, BLOCK) + home).reshape(-1))
 
     flag = pl.pallas_call(
         functools.partial(flag_kernel, share),
         out_specs=pl.BlockSpec(memory_space=pltpu.SMEM),
         out_shape=jax.ShapeDtypeStruct((1,), jnp.int32),
         compiler_params=pltpu.CompilerParams(vmem_limit_bytes=4 * 1024 * 1024),
-    )(swap_cols, home)
+    )(swap_cols, first_cols, first_back)
     bad = flag[0] > 0
     if tiles > QUAD:
         bad = lax.pmax(bad.astype(jnp.int32), "tile") > 0

time: 41.5 us -> 43.7 us (1.053)
  starting transfers between devices: 13.2 us -> 15.9 us
  waiting for transfers between devices: 16 us -> 15 us
    ppermute x5, starting transfers between devices: 11 us -> 13.6 us  [the longest x1 5.75 us: shards(): from_last = lax.ppermute(second_out, 'tile', inward)]
    ppermute x5, waiting for transfers between devices: 15.2 us -> 13.9 us  [the longest x1 7.54 us: shards(): home = lax.ppermute(cols, 'tile', turned(inward))]
    ppermute x1, waiting for transfers between devices: 0.01 us -> 1.13 us  [shards(): lax.ppermute(leaving, 'sub', [(i, i ^ 1) for i in range(subs)])]
    ppermute x1, waiting for transfers between devices: 0.8 us -> 0.01 us  [shards(): lax.ppermute(leaving, 'sub', [(i, i ^ 1 << bit) for i in range(subs)])]
  transfers between devices with their start and end apart: 8 -> 8, of which waited for: 4 -> 4; matrix products, arithmetic and copies ran while one was open for 1% -> 1% of each run, Pallas kernels for 21% -> 20%
where the time goes in v17:
time: 43.7 us; the launch traced here: 43.1 us
  starting transfers between devices  15.9 us (36%)
  waiting for transfers between devices  15 us (34%)
  Pallas kernels  10.2 us (23%)
  local copies, waits for them, and re-layouts  0.82 us (2%)
  between operations  0.82 us (2%)
    ppermute x1, waiting for transfers between devices, shards(): home = lax.ppermute(cols, 'tile', turned(inward))  7.54 us
    pallas_call x1, Pallas kernels, shards(): pl.pallas_call(functools.partial(self_kernel, blocks, subs), in_specs=[sm...  6.05 us
    ppermute x1, starting transfers between devices, shards(): from_last = lax.ppermute(second_out, 'tile', inward)  5.75 us
    ppermute x1, waiting for transfers between devices, shards(): from_last = lax.ppermute(second_out, 'tile', inward)  5.3 us
    ppermute x1, starting transfers between devices, shards(): from_first = lax.ppermute(first_out, 'tile', around)  3.08 us
    ppermute x1, starting transfers between devices, shards(): first_back = lax.ppermute(first_cols, 'tile', turned(around))  2.81 us
    pallas_call x3, Pallas kernels, call(): pl.pallas_call(kernel, in_specs=[smem] + [vmem] * len(operands), out_spec...  2.12 us
    ppermute x1, starting transfers between devices, shards(): lax.ppermute(leaving, 'sub', [(i, i ^ 1 << bit) for i in range(subs)])  1.56 us
  transfers between devices with their start and end apart: 8, of which 4 were waited for; matrix products, arithmetic and copies ran while one was open for 1% of the time, Pallas kernels for 20%

profile of v17, /device:TPU:0, one launch (start us, length us, event | category | flops | bytes accessed | tf_op | source)
XLA Modules:
  0.0 43.1 jit_solution(2827891748241078057)
XLA Ops:
  0.0 0.0 copy-start.3
  0.0 1.4 %shard_map.31 = (bf16[264,1024]{1,0:T(8,128)(2,1)S(1)}, bf16[264,1024]{1,0:T(8,128)(2,1)S(1)}) custom-call(bf16[2048,1024]{1,0:T(8,128)(2,1)} %rows_ref.3, s32[16,128]{1,0:T(8,128)} %bitcast.58), custom_call_target="tpu_custom_call" | custom-call | bytes 1024 | tf_op jit(solution)/shard_map/pallas_call | solution.py:92
  1.4 3.1 %collective-permute-start.1 = (bf16[264,1024]{1,0:T(8,128)(2,1)S(1)}, bf16[264,1024]{1,0:T(8,128)(2,1)S(1)}, u32[]{:S(2)}, u32[]{:S(2)}) collective-permute-start(bf16[264,1024]{1,0:T(8,128)(2,1)S(1)} %get-tuple-element.64), channel_id=1, source_target_pairs={{0,4},{12,8},{4,12},{8,0},{1,5},{13,9},{5,13},{9,1},{2,6},{14,10},... | collective-permute-start | bytes 1622024 | tf_op jit(solution)/shard_map/ppermute | solution.py:313
  4.5 0.0 copy-done.3
  4.5 0.1 convert_reduce_fusion
  4.6 0.1 dynamic_slice.47
  4.7 0.1 concatenate.6.meta_ref
  4.8 0.1 broadcast_in_dim.129
  4.9 6.0 %shard_map.30 = (bf16[2048,1024]{1,0:T(8,128)(2,1)S(1)}, f32[16,128]{1,0:T(8,128)S(1)}) custom-call(s32[84]{0:T(128)S(1)} %concatenate.6.meta_ref, bf16[2048,1024]{1,0:T(8,128)(2,1)} %rows_ref.3, s32[1,512]{1,0:T(1,128)S(1)} %bitcast.57), custom_call_target="tpu_custom_call" | custom-call | bytes 1024 | tf_op jit(solution)/shard_map/pallas_call | solution.py:336
  10.9 0.7 %collective-permute-start = (bf16[264,1024]{1,0:T(8,128)(2,1)S(1)}, bf16[264,1024]{1,0:T(8,128)(2,1)S(1)}, u32[]{:S(2)}, u32[]{:S(2)}) collective-permute-start(bf16[264,1024]{1,0:T(8,128)(2,1)S(1)} %get-tuple-element.64), channel_id=1, source_target_pairs={{4,8},{8,4},{5,9},{9,5},{6,10},{10,6},{7,11},{11,7},{20,24},{24,20... | collective-permute-start | bytes 1622024 | tf_op jit(solution)/shard_map/ppermute | solution.py:346
  11.6 5.7 %collective-permute-start.2 = (bf16[264,1024]{1,0:T(8,128)(2,1)S(1)}, bf16[264,1024]{1,0:T(8,128)(2,1)S(1)}, u32[]{:S(2)}, u32[]{:S(2)}) collective-permute-start(bf16[264,1024]{1,0:T(8,128)(2,1)S(1)} %get-tuple-element.69), channel_id=1, source_target_pairs={{0,4},{12,8},{1,5},{13,9},{2,6},{14,10},{3,7},{15,11},{16,20},{28,... | collective-permute-start | bytes 1622024 | tf_op jit(solution)/shard_map/ppermute | solution.py:347
  17.4 1.0 %collective-permute-done.1.piece_ref = bf16[264,1024]{1,0:T(8,128)(2,1)S(1)} collective-permute-done((bf16[264,1024]{1,0:T(8,128)(2,1)S(1)}, bf16[264,1024]{1,0:T(8,128)(2,1)S(1)}, u32[]{:S(2)}, u32[]{:S(2)}) %collective-permute-start.1) | collective-permute-done | bytes 540704 | tf_op jit(solution)/shard_map/ppermute | solution.py:313
  18.4 0.7 %shard_map.32 = (f32[16,128]{1,0:T(8,128)S(1)}, f32[3,128]{1,0:T(4,128)S(1)}) custom-call(s32[84]{0:T(128)S(1)} %concatenate.6.meta_ref, bf16[2048,1024]{1,0:T(8,128)(2,1)S(1)} %get-tuple-element.60.unit_ref, bf16[264,1024]{1,0:T(8,128)(2,1)S(1)} %collective-permute-done.1.piece_ref, f32[16,128]{1,0:T(8,128)S(1)} %get-tuple-element.65.before_ref), custom_call_target="tpu_custom_call" | custom-call | flops 1073741824 | bytes 1024 | tf_op jit(solution)/shard_map/pallas_call | solution.py:240
  19.1 2.8 %collective-permute-start.3 = (f32[3,128]{1,0:T(4,128)S(1)}, f32[3,128]{1,0:T(4,128)S(1)}, u32[]{:S(2)}, u32[]{:S(2)}) collective-permute-start(f32[3,128]{1,0:T(4,128)S(1)} %get-tuple-element.68.first_cols_ref), channel_id=1, source_target_pairs={{4,0},{8,12},{12,4},{0,8},{5,1},{9,13},{13,5},{1,9},{6,2},{10,14},... | collective-permute-start | bytes 4616 | tf_op jit(solution)/shard_map/ppermute | solution.py:360
  22.0 0.0 collective-permute-done.piece_ref
  22.0 0.7 %shard_map.33 = (f32[16,128]{1,0:T(8,128)S(1)}, f32[3,128]{1,0:T(4,128)S(1)}) custom-call(s32[84]{0:T(128)S(1)} %concatenate.6.meta_ref, bf16[2048,1024]{1,0:T(8,128)(2,1)S(1)} %get-tuple-element.60.unit_ref, bf16[264,1024]{1,0:T(8,128)(2,1)S(1)} %collective-permute-done.piece_ref, f32[16,128]{1,0:T(8,128)S(1)} %get-tuple-element.66.before_ref), custom_call_target="tpu_custom_call" | custom-call | flops 1073741824 | bytes 1024 | tf_op jit(solution)/shard_map/pallas_call | solution.py:240
  22.7 0.7 %collective-permute-start.4 = (f32[3,128]{1,0:T(4,128)S(1)}, f32[3,128]{1,0:T(4,128)S(1)}, u32[]{:S(2)}, u32[]{:S(2)}) collective-permute-start(f32[3,128]{1,0:T(4,128)S(1)} %get-tuple-element.67.swap_cols_ref), channel_id=1, source_target_pairs={{8,4},{4,8},{9,5},{5,9},{10,6},{6,10},{11,7},{7,11},{24,20},{20,24... | collective-permute-start | bytes 4616 | tf_op jit(solution)/shard_map/ppermute | solution.py:362
  23.3 5.3 %collective-permute-done.2.piece_ref = bf16[264,1024]{1,0:T(8,128)(2,1)S(1)} collective-permute-done((bf16[264,1024]{1,0:T(8,128)(2,1)S(1)}, bf16[264,1024]{1,0:T(8,128)(2,1)S(1)}, u32[]{:S(2)}, u32[]{:S(2)}) %collective-permute-start.2) | collective-permute-done | bytes 540704 | tf_op jit(solution)/shard_map/ppermute | solution.py:347
  28.6 0.0 collective-permute-done.3.first_back_ref
  28.6 0.7 %shard_map.34 = (f32[8,128]{1,0:T(8,128)S(1)}, f32[8,128]{1,0:T(8,128)S(1)}, f32[2,128]{1,0:T(2,128)S(1)}) custom-call(s32[84]{0:T(128)S(1)} %concatenate.6.meta_ref, bf16[2048,1024]{1,0:T(8,128)(2,1)S(1)} %get-tuple-element.60.unit_ref, bf16[264,1024]{1,0:T(8,128)(2,1)S(1)} %collective-permute-done.2.piece_ref, f32[16,128]{1,0:T(8,128)S(1)} %get-tuple-element.70.before_ref, ...), custom_call_target="tpu_custom_call" | custom-call | flops 1073741824 | bytes 1024 | tf_op jit(solution)/shard_map/pallas_call | solution.py:240
  29.4 1.3 %collective-permute-start.7 = (f32[2,128]{1,0:T(2,128)S(1)}, f32[2,128]{1,0:T(2,128)S(1)}, u32[]{:S(2)}, u32[]{:S(2)}) collective-permute-start(f32[2,128]{1,0:T(2,128)S(1)} %get-tuple-element.77), channel_id=1, source_target_pairs={{4,0},{8,12},{5,1},{9,13},{6,2},{10,14},{7,3},{11,15},{20,16},{24,... | collective-permute-start | bytes 3080 | tf_op jit(solution)/shard_map/ppermute | solution.py:376
  30.7 0.1 collective-permute-start.5
  30.8 0.0 collective-permute-done.4
  30.8 1.1 %collective-permute-done.5 = f32[8,128]{1,0:T(8,128)S(1)} collective-permute-done((f32[8,128]{1,0:T(8,128)S(1)}, f32[8,128]{1,0:T(8,128)S(1)}, u32[]{:S(2)}, u32[]{:S(2)}) %collective-permute-start.5) | collective-permute-done | bytes 4128 | tf_op jit(solution)/shard_map/ppermute | solution.py:379
  31.9 1.6 %collective-permute-start.6 = (f32[4,128]{1,0:T(4,128)S(1)}, f32[4,128]{1,0:T(4,128)S(1)}, u32[]{:S(2)}, u32[]{:S(2)}) collective-permute-start(f32[4,128]{1,0:T(4,128)S(1)} %get-tuple-element.81), channel_id=1, source_target_pairs={{0,2},{1,3},{2,0},{3,1},{4,6},{5,7},{6,4},{7,5},{8,10},{9,11},{10,... | collective-permute-start | bytes 6152 | tf_op jit(solution)/shard_map/ppermute | solution.py:386
  33.5 0.6 %shard_map.35 = s32[1]{0:T(128)} custom-call(f32[3,128]{1,0:T(4,128)S(1)} %get-tuple-element.67.swap_cols_ref, f32[3,128]{1,0:T(4,128)S(1)} %get-tuple-element.68.first_cols_ref, f32[3,128]{1,0:T(4,128)S(1)} %collective-permute-done.3.first_back_ref), custom_call_target="tpu_custom_call" | custom-call | tf_op jit(solution)/shard_map/pallas_call | solution.py:390
  34.8 7.5 %collective-permute-done.7 = f32[2,128]{1,0:T(2,128)S(1)} collective-permute-done((f32[2,128]{1,0:T(2,128)S(1)}, f32[2,128]{1,0:T(2,128)S(1)}, u32[]{:S(2)}, u32[]{:S(2)}) %collective-permute-start.7) | collective-permute-done | bytes 1056 | tf_op jit(solution)/shard_map/ppermute | solution.py:376
  42.3 0.0 collective-permute-done.6
  42.3 0.2 conditional.1
  42.6 0.0 copy-start.4
  42.6 0.6 %copy-done.4 = f32[512]{0:T(512)} copy-done((f32[512]{0:T(512)}, f32[512]{0:T(512)S(1)}, u32[]{:S(2)}) %copy-start.4) | copy-done | bytes 2072
  (8 shorter events, 0.0 us)
Async XLA Ops:
  0.0 4.5 %copy-start.3 = (s32[2048]{0:T(1024)S(1)}, s32[2048]{0:T(1024)}, u32[]{:S(2)}) copy-start(s32[2048]{0:T(1024)} %param.5) | copy-start | bytes 24580
  1.4 17.0 %collective-permute-start.1 = (bf16[264,1024]{1,0:T(8,128)(2,1)S(1)}, bf16[264,1024]{1,0:T(8,128)(2,1)S(1)}, u32[]{:S(2)}, u32[]{:S(2)}) collective-permute-start(bf16[264,1024]{1,0:T(8,128)(2,1)S(1)} %get-tuple-element.64), channel_id=1, source_target_pairs={{0,4},{12,8},{4,12},{8,0},{1,5},{13,9},{5,13},{9,1},{2,6},{14,10},... | collective-permute-start | bytes 1622024 | tf_op jit(solution)/shard_map/ppermute | solution.py:313
  10.9 11.0 %collective-permute-start = (bf16[264,1024]{1,0:T(8,128)(2,1)S(1)}, bf16[264,1024]{1,0:T(8,128)(2,1)S(1)}, u32[]{:S(2)}, u32[]{:S(2)}) collective-permute-start(bf16[264,1024]{1,0:T(8,128)(2,1)S(1)} %get-tuple-element.64), channel_id=1, source_target_pairs={{4,8},{8,4},{5,9},{9,5},{6,10},{10,6},{7,11},{11,7},{20,24},{24,20... | collective-permute-start | bytes 1622024 | tf_op jit(solution)/shard_map/ppermute | solution.py:346
  11.6 17.0 %collective-permute-start.2 = (bf16[264,1024]{1,0:T(8,128)(2,1)S(1)}, bf16[264,1024]{1,0:T(8,128)(2,1)S(1)}, u32[]{:S(2)}, u32[]{:S(2)}) collective-permute-start(bf16[264,1024]{1,0:T(8,128)(2,1)S(1)} %get-tuple-element.69), channel_id=1, source_target_pairs={{0,4},{12,8},{1,5},{13,9},{2,6},{14,10},{3,7},{15,11},{16,20},{28,... | collective-permute-start | bytes 1622024 | tf_op jit(solution)/shard_map/ppermute | solution.py:347
  19.1 9.5 %collective-permute-start.3 = (f32[3,128]{1,0:T(4,128)S(1)}, f32[3,128]{1,0:T(4,128)S(1)}, u32[]{:S(2)}, u32[]{:S(2)}) collective-permute-start(f32[3,128]{1,0:T(4,128)S(1)} %get-tuple-element.68.first_cols_ref), channel_id=1, source_target_pairs={{4,0},{8,12},{12,4},{0,8},{5,1},{9,13},{13,5},{1,9},{6,2},{10,14},... | collective-permute-start | bytes 4616 | tf_op jit(solution)/shard_map/ppermute | solution.py:360
  22.7 8.1 %collective-permute-start.4 = (f32[3,128]{1,0:T(4,128)S(1)}, f32[3,128]{1,0:T(4,128)S(1)}, u32[]{:S(2)}, u32[]{:S(2)}) collective-permute-start(f32[3,128]{1,0:T(4,128)S(1)} %get-tuple-element.67.swap_cols_ref), channel_id=1, source_target_pairs={{8,4},{4,8},{9,5},{5,9},{10,6},{6,10},{11,7},{7,11},{24,20},{20,24... | collective-permute-start | bytes 4616 | tf_op jit(solution)/shard_map/ppermute | solution.py:362
  29.4 12.9 %collective-permute-start.7 = (f32[2,128]{1,0:T(2,128)S(1)}, f32[2,128]{1,0:T(2,128)S(1)}, u32[]{:S(2)}, u32[]{:S(2)}) collective-permute-start(f32[2,128]{1,0:T(2,128)S(1)} %get-tuple-element.77), channel_id=1, source_target_pairs={{4,0},{8,12},{5,1},{9,13},{6,2},{10,14},{7,3},{11,15},{20,16},{24,... | collective-permute-start | bytes 3080 | tf_op jit(solution)/shard_map/ppermute | solution.py:376
  30.7 1.2 %collective-permute-start.5 = (f32[8,128]{1,0:T(8,128)S(1)}, f32[8,128]{1,0:T(8,128)S(1)}, u32[]{:S(2)}, u32[]{:S(2)}) collective-permute-start(f32[8,128]{1,0:T(8,128)S(1)} %get-tuple-element.73), channel_id=1, source_target_pairs={{0,1},{1,0},{2,3},{3,2},{4,5},{5,4},{6,7},{7,6},{8,9},{9,8},{10,11... | collective-permute-start | bytes 12296 | tf_op jit(solution)/shard_map/ppermute | solution.py:379
  31.9 10.4 %collective-permute-start.6 = (f32[4,128]{1,0:T(4,128)S(1)}, f32[4,128]{1,0:T(4,128)S(1)}, u32[]{:S(2)}, u32[]{:S(2)}) collective-permute-start(f32[4,128]{1,0:T(4,128)S(1)} %get-tuple-element.81), channel_id=1, source_target_pairs={{0,2},{1,3},{2,0},{3,1},{4,6},{5,7},{6,4},{7,5},{8,10},{9,11},{10,... | collective-permute-start | bytes 6152 | tf_op jit(solution)/shard_map/ppermute | solution.py:386
  42.6 0.6 %copy-start.4 = (f32[512]{0:T(512)}, f32[512]{0:T(512)S(1)}, u32[]{:S(2)}) copy-start(f32[512]{0:T(512)S(1)} %get-tuple-element.114) | copy-start | bytes 6148

commit v18 on v16

--- a/solution.py
+++ b/solution.py
@@ -168,18 +168,14 @@
 
     @pl.when(shared)
     def _():
-        norms = []
-        for at in range(0, size, BLOCK):
-            values = piece_ref[at : at + BLOCK, :].astype(jnp.float32)
-            norms.append(lane_sums(values * values))
-        scale = GAIN * lax.rsqrt(jnp.concatenate(norms, axis=1) + norm_eps)
+        piece = normalised(piece_ref[:size, :])
         total = None
         for start in range(0, meta.blocks * BLOCK, STEP):
-            product = products(unit_ref[start : start + STEP, :], piece_ref[:size, :])
+            cosine = products(unit_ref[start : start + STEP, :], piece)
             for inner in range(0, STEP, BLOCK):
                 block = (start + inner) // BLOCK
                 bias = column_bias(meta.tag(block, chunk), column_tags)
-                weight = jnp.exp2(product[inner : inner + BLOCK] * scale + bias)
+                weight = jnp.exp2(cosine[inner : inner + BLOCK] * GAIN + bias)
                 row = lax.broadcasted_iota(jnp.int32, weight.shape, 0)
                 weight = jnp.where(row < meta.used(block), weight, 0.0)
                 sums[place(block) : place(block) + 1, :] = before_ref[block : block + 1, :] + lane_sums(weight)

time: 41.5 us -> 41.5 us (level)
  no operation moved by 1% of the time
where the time goes in v18:
time: 41.5 us; the launch traced here: 41.3 us
  waiting for transfers between devices  15.9 us (38%)
  starting transfers between devices  13.4 us (32%)
  Pallas kernels  10.2 us (25%)
  between operations  0.92 us (2%)
  local copies, waits for them, and re-layouts  0.81 us (2%)
    ppermute x1, waiting for transfers between devices, shards(): last = lax.ppermute(second_out, 'tile', around)  10.3 us
    pallas_call x1, Pallas kernels, shards(): pl.pallas_call(functools.partial(self_kernel, blocks, subs), in_specs=[sm...  6.05 us
    ppermute x1, starting transfers between devices, shards(): from_outer = lax.ppermute(first_out, 'tile', inward)  4.96 us
    ppermute x1, waiting for transfers between devices, shards(): from_outer = lax.ppermute(first_out, 'tile', inward)  3.15 us
    ppermute x1, starting transfers between devices, shards(): last = lax.ppermute(second_out, 'tile', around)  2.2 us
    pallas_call x3, Pallas kernels, call(): pl.pallas_call(kernel, in_specs=[smem] + [vmem] * len(operands), out_spec...  2.12 us
    ppermute x1, starting transfers between devices, shards(): home = lax.ppermute(cols, 'tile', turned(around))  1.99 us
    ppermute x1, waiting for transfers between devices, shards(): home = lax.ppermute(cols, 'tile', turned(around))  1.64 us
  transfers between devices with their start and end apart: 8, of which 4 were waited for; matrix products, arithmetic and copies ran while one was open for 1% of the time, Pallas kernels for 21%

profile of v18, /device:TPU:0, one launch (start us, length us, event | category | flops | bytes accessed | tf_op | source)
XLA Modules:
  0.0 41.3 jit_solution(2157167905004415130)
XLA Ops:
  0.0 0.0 copy-start.3
  0.0 1.4 %shard_map.31 = (bf16[264,1024]{1,0:T(8,128)(2,1)S(1)}, bf16[264,1024]{1,0:T(8,128)(2,1)S(1)}) custom-call(bf16[2048,1024]{1,0:T(8,128)(2,1)} %rows_ref.3, s32[16,128]{1,0:T(8,128)} %bitcast.58), custom_call_target="tpu_custom_call" | custom-call | bytes 1024 | tf_op jit(solution)/shard_map/pallas_call | solution.py:92
  1.4 5.0 %collective-permute-start.1 = (bf16[264,1024]{1,0:T(8,128)(2,1)S(1)}, bf16[264,1024]{1,0:T(8,128)(2,1)S(1)}, u32[]{:S(2)}, u32[]{:S(2)}) collective-permute-start(bf16[264,1024]{1,0:T(8,128)(2,1)S(1)} %get-tuple-element.54), channel_id=1, source_target_pairs={{0,4},{12,8},{1,5},{13,9},{2,6},{14,10},{3,7},{15,11},{16,20},{28,... | collective-permute-start | bytes 1622024 | tf_op jit(solution)/shard_map/ppermute | solution.py:306
  6.4 0.7 %collective-permute-start = (bf16[264,1024]{1,0:T(8,128)(2,1)S(1)}, bf16[264,1024]{1,0:T(8,128)(2,1)S(1)}, u32[]{:S(2)}, u32[]{:S(2)}) collective-permute-start(bf16[264,1024]{1,0:T(8,128)(2,1)S(1)} %get-tuple-element.54), channel_id=1, source_target_pairs={{4,8},{8,4},{5,9},{9,5},{6,10},{10,6},{7,11},{11,7},{20,24},{24,20... | collective-permute-start | bytes 1622024 | tf_op jit(solution)/shard_map/ppermute | solution.py:305
  7.1 0.0 copy-done.3
  7.1 0.1 convert_reduce_fusion
  7.3 0.1 dynamic_slice.47
  7.4 0.1 concatenate.3.meta_ref
  7.5 0.1 broadcast_in_dim.128
  7.6 6.0 %shard_map.30 = (bf16[2048,1024]{1,0:T(8,128)(2,1)S(1)}, f32[16,128]{1,0:T(8,128)S(1)}) custom-call(s32[84]{0:T(128)S(1)} %concatenate.3.meta_ref, bf16[2048,1024]{1,0:T(8,128)(2,1)} %rows_ref.3, s32[1,512]{1,0:T(1,128)S(1)} %bitcast.57), custom_call_target="tpu_custom_call" | custom-call | bytes 1024 | tf_op jit(solution)/shard_map/pallas_call | solution.py:329
  13.6 2.2 %collective-permute-start.2 = (bf16[264,1024]{1,0:T(8,128)(2,1)S(1)}, bf16[264,1024]{1,0:T(8,128)(2,1)S(1)}, u32[]{:S(2)}, u32[]{:S(2)}) collective-permute-start(bf16[264,1024]{1,0:T(8,128)(2,1)S(1)} %get-tuple-element.60), channel_id=1, source_target_pairs={{0,4},{12,8},{4,12},{8,0},{1,5},{13,9},{5,13},{9,1},{2,6},{14,10},... | collective-permute-start | bytes 1622024 | tf_op jit(solution)/shard_map/ppermute | solution.py:339
  15.8 3.1 %collective-permute-done.1.piece_ref = bf16[264,1024]{1,0:T(8,128)(2,1)S(1)} collective-permute-done((bf16[264,1024]{1,0:T(8,128)(2,1)S(1)}, bf16[264,1024]{1,0:T(8,128)(2,1)S(1)}, u32[]{:S(2)}, u32[]{:S(2)}) %collective-permute-start.1) | collective-permute-done | bytes 540704 | tf_op jit(solution)/shard_map/ppermute | solution.py:306
  19.0 0.7 %shard_map.32 = (f32[16,128]{1,0:T(8,128)S(1)}, f32[3,128]{1,0:T(4,128)S(1)}) custom-call(s32[84]{0:T(128)S(1)} %concatenate.3.meta_ref, bf16[2048,1024]{1,0:T(8,128)(2,1)S(1)} %get-tuple-element.53.unit_ref, bf16[264,1024]{1,0:T(8,128)(2,1)S(1)} %collective-permute-done.1.piece_ref, f32[16,128]{1,0:T(8,128)S(1)} %get-tuple-element.57.before_ref), custom_call_target="tpu_custom_call" | custom-call | flops 1073741824 | bytes 1024 | tf_op jit(solution)/shard_map/pallas_call | solution.py:232
  19.7 1.3 %collective-permute-start.3 = (f32[3,128]{1,0:T(4,128)S(1)}, f32[3,128]{1,0:T(4,128)S(1)}, u32[]{:S(2)}, u32[]{:S(2)}) collective-permute-start(f32[3,128]{1,0:T(4,128)S(1)} %get-tuple-element.62), channel_id=1, source_target_pairs={{4,0},{8,12},{5,1},{9,13},{6,2},{10,14},{7,3},{11,15},{20,16},{24,... | collective-permute-start | bytes 4616 | tf_op jit(solution)/shard_map/ppermute | solution.py:352
  21.0 0.0 collective-permute-done.piece_ref
  21.0 0.7 %shard_map.33 = (f32[16,128]{1,0:T(8,128)S(1)}, f32[3,128]{1,0:T(4,128)S(1)}) custom-call(s32[84]{0:T(128)S(1)} %concatenate.3.meta_ref, bf16[2048,1024]{1,0:T(8,128)(2,1)S(1)} %get-tuple-element.53.unit_ref, bf16[264,1024]{1,0:T(8,128)(2,1)S(1)} %collective-permute-done.piece_ref, f32[16,128]{1,0:T(8,128)S(1)} %get-tuple-element.58.before_ref), custom_call_target="tpu_custom_call" | custom-call | flops 1073741824 | bytes 1024 | tf_op jit(solution)/shard_map/pallas_call | solution.py:232
  21.7 0.7 %collective-permute-start.5 = (f32[3,128]{1,0:T(4,128)S(1)}, f32[3,128]{1,0:T(4,128)S(1)}, u32[]{:S(2)}, u32[]{:S(2)}) collective-permute-start(f32[3,128]{1,0:T(4,128)S(1)} %get-tuple-element.59.swap_cols_ref.here_ref), channel_id=1, source_target_pairs={{8,4},{4,8},{9,5},{5,9},{10,6},{6,10},{11,7},{7,11},{24,20},{20,24... | collective-permute-start | bytes 4616 | tf_op jit(solution)/shard_map/ppermute | solution.py:354
  22.4 10.3 %collective-permute-done.2.piece_ref = bf16[264,1024]{1,0:T(8,128)(2,1)S(1)} collective-permute-done((bf16[264,1024]{1,0:T(8,128)(2,1)S(1)}, bf16[264,1024]{1,0:T(8,128)(2,1)S(1)}, u32[]{:S(2)}, u32[]{:S(2)}) %collective-permute-start.2) | collective-permute-done | bytes 540704 | tf_op jit(solution)/shard_map/ppermute | solution.py:339
  32.7 0.0 collective-permute-done.3.outer_back_ref
  32.7 0.7 %shard_map.34 = (f32[8,128]{1,0:T(8,128)S(1)}, f32[8,128]{1,0:T(8,128)S(1)}, f32[3,128]{1,0:T(4,128)S(1)}) custom-call(s32[84]{0:T(128)S(1)} %concatenate.3.meta_ref, bf16[2048,1024]{1,0:T(8,128)(2,1)S(1)} %get-tuple-element.53.unit_ref, bf16[264,1024]{1,0:T(8,128)(2,1)S(1)} %collective-permute-done.2.piece_ref, f32[16,128]{1,0:T(8,128)S(1)} %get-tuple-element.61.before_ref, ...), custom_call_target="tpu_custom_call" | custom-call | flops 1073741824 | bytes 1024 | tf_op jit(solution)/shard_map/pallas_call | solution.py:232
  33.4 2.0 %collective-permute-start.4 = (f32[3,128]{1,0:T(4,128)S(1)}, f32[3,128]{1,0:T(4,128)S(1)}, u32[]{:S(2)}, u32[]{:S(2)}) collective-permute-start(f32[3,128]{1,0:T(4,128)S(1)} %get-tuple-element.63), channel_id=1, source_target_pairs={{4,0},{8,12},{12,4},{0,8},{5,1},{9,13},{13,5},{1,9},{6,2},{10,14},... | collective-permute-start | bytes 4616 | tf_op jit(solution)/shard_map/ppermute | solution.py:368
  35.4 0.0 collective-permute-start.6
  35.4 0.0 collective-permute-done.5
  35.4 1.6 %collective-permute-done.4.home_ref = f32[3,128]{1,0:T(4,128)S(1)} collective-permute-done((f32[3,128]{1,0:T(4,128)S(1)}, f32[3,128]{1,0:T(4,128)S(1)}, u32[]{:S(2)}, u32[]{:S(2)}) %collective-permute-start.4) | collective-permute-done | bytes 1568 | tf_op jit(solution)/shard_map/ppermute | solution.py:368
  37.1 0.0 collective-permute-done.6
  37.1 1.6 %collective-permute-start.7 = (f32[4,128]{1,0:T(4,128)S(1)}, f32[4,128]{1,0:T(4,128)S(1)}, u32[]{:S(2)}, u32[]{:S(2)}) collective-permute-start(f32[4,128]{1,0:T(4,128)S(1)} %get-tuple-element.73), channel_id=1, source_target_pairs={{0,2},{1,3},{2,0},{3,1},{4,6},{5,7},{6,4},{7,5},{8,10},{9,11},{10,... | collective-permute-start | bytes 6152 | tf_op jit(solution)/shard_map/ppermute | solution.py:378
  38.7 0.6 %shard_map.35 = s32[1]{0:T(128)} custom-call(f32[3,128]{1,0:T(4,128)S(1)} %get-tuple-element.59.swap_cols_ref.here_ref, f32[3,128]{1,0:T(4,128)S(1)} %collective-permute-done.4.home_ref), custom_call_target="tpu_custom_call" | custom-call | tf_op jit(solution)/shard_map/pallas_call | solution.py:381
  40.0 0.8 %collective-permute-done.7 = f32[4,128]{1,0:T(4,128)S(1)} collective-permute-done((f32[4,128]{1,0:T(4,128)S(1)}, f32[4,128]{1,0:T(4,128)S(1)}, u32[]{:S(2)}, u32[]{:S(2)}) %collective-permute-start.7) | collective-permute-done | bytes 2080 | tf_op jit(solution)/shard_map/ppermute | solution.py:378
  40.8 0.0 copy-start.4
  40.8 0.6 %copy-done.4 = f32[512]{0:T(512)} copy-done((f32[512]{0:T(512)}, f32[512]{0:T(512)S(1)}, u32[]{:S(2)}) %copy-start.4) | copy-done | bytes 2072
  (9 shorter events, 0.0 us)
Async XLA Ops:
  0.0 7.1 %copy-start.3 = (s32[2048]{0:T(1024)S(1)}, s32[2048]{0:T(1024)}, u32[]{:S(2)}) copy-start(s32[2048]{0:T(1024)} %param.5) | copy-start | bytes 24580
  1.4 17.6 %collective-permute-start.1 = (bf16[264,1024]{1,0:T(8,128)(2,1)S(1)}, bf16[264,1024]{1,0:T(8,128)(2,1)S(1)}, u32[]{:S(2)}, u32[]{:S(2)}) collective-permute-start(bf16[264,1024]{1,0:T(8,128)(2,1)S(1)} %get-tuple-element.54), channel_id=1, source_target_pairs={{0,4},{12,8},{1,5},{13,9},{2,6},{14,10},{3,7},{15,11},{16,20},{28,... | collective-permute-start | bytes 1622024 | tf_op jit(solution)/shard_map/ppermute | solution.py:306
  6.4 14.6 %collective-permute-start = (bf16[264,1024]{1,0:T(8,128)(2,1)S(1)}, bf16[264,1024]{1,0:T(8,128)(2,1)S(1)}, u32[]{:S(2)}, u32[]{:S(2)}) collective-permute-start(bf16[264,1024]{1,0:T(8,128)(2,1)S(1)} %get-tuple-element.54), channel_id=1, source_target_pairs={{4,8},{8,4},{5,9},{9,5},{6,10},{10,6},{7,11},{11,7},{20,24},{24,20... | collective-permute-start | bytes 1622024 | tf_op jit(solution)/shard_map/ppermute | solution.py:305
  13.6 19.0 %collective-permute-start.2 = (bf16[264,1024]{1,0:T(8,128)(2,1)S(1)}, bf16[264,1024]{1,0:T(8,128)(2,1)S(1)}, u32[]{:S(2)}, u32[]{:S(2)}) collective-permute-start(bf16[264,1024]{1,0:T(8,128)(2,1)S(1)} %get-tuple-element.60), channel_id=1, source_target_pairs={{0,4},{12,8},{4,12},{8,0},{1,5},{13,9},{5,13},{9,1},{2,6},{14,10},... | collective-permute-start | bytes 1622024 | tf_op jit(solution)/shard_map/ppermute | solution.py:339
  19.7 13.0 %collective-permute-start.3 = (f32[3,128]{1,0:T(4,128)S(1)}, f32[3,128]{1,0:T(4,128)S(1)}, u32[]{:S(2)}, u32[]{:S(2)}) collective-permute-start(f32[3,128]{1,0:T(4,128)S(1)} %get-tuple-element.62), channel_id=1, source_target_pairs={{4,0},{8,12},{5,1},{9,13},{6,2},{10,14},{7,3},{11,15},{20,16},{24,... | collective-permute-start | bytes 4616 | tf_op jit(solution)/shard_map/ppermute | solution.py:352
  21.7 13.7 %collective-permute-start.5 = (f32[3,128]{1,0:T(4,128)S(1)}, f32[3,128]{1,0:T(4,128)S(1)}, u32[]{:S(2)}, u32[]{:S(2)}) collective-permute-start(f32[3,128]{1,0:T(4,128)S(1)} %get-tuple-element.59.swap_cols_ref.here_ref), channel_id=1, source_target_pairs={{8,4},{4,8},{9,5},{5,9},{10,6},{6,10},{11,7},{7,11},{24,20},{20,24... | collective-permute-start | bytes 4616 | tf_op jit(solution)/shard_map/ppermute | solution.py:354
  33.4 3.6 %collective-permute-start.4 = (f32[3,128]{1,0:T(4,128)S(1)}, f32[3,128]{1,0:T(4,128)S(1)}, u32[]{:S(2)}, u32[]{:S(2)}) collective-permute-start(f32[3,128]{1,0:T(4,128)S(1)} %get-tuple-element.63), channel_id=1, source_target_pairs={{4,0},{8,12},{12,4},{0,8},{5,1},{9,13},{13,5},{1,9},{6,2},{10,14},... | collective-permute-start | bytes 4616 | tf_op jit(solution)/shard_map/ppermute | solution.py:368
  35.4 1.7 %collective-permute-start.6 = (f32[8,128]{1,0:T(8,128)S(1)}, f32[8,128]{1,0:T(8,128)S(1)}, u32[]{:S(2)}, u32[]{:S(2)}) collective-permute-start(f32[8,128]{1,0:T(8,128)S(1)} %get-tuple-element.66), channel_id=1, source_target_pairs={{0,1},{1,0},{2,3},{3,2},{4,5},{5,4},{6,7},{7,6},{8,9},{9,8},{10,11... | collective-permute-start | bytes 12296 | tf_op jit(solution)/shard_map/ppermute | solution.py:371
  37.1 3.7 %collective-permute-start.7 = (f32[4,128]{1,0:T(4,128)S(1)}, f32[4,128]{1,0:T(4,128)S(1)}, u32[]{:S(2)}, u32[]{:S(2)}) collective-permute-start(f32[4,128]{1,0:T(4,128)S(1)} %get-tuple-element.73), channel_id=1, source_target_pairs={{0,2},{1,3},{2,0},{3,1},{4,6},{5,7},{6,4},{7,5},{8,10},{9,11},{10,... | collective-permute-start | bytes 6152 | tf_op jit(solution)/shard_map/ppermute | solution.py:378
  40.8 0.6 %copy-start.4 = (f32[512]{0:T(512)}, f32[512]{0:T(512)S(1)}, u32[]{:S(2)}) copy-start(f32[512]{0:T(512)S(1)} %get-tuple-element.107) | copy-start | bytes 6148

commit v19 on v18

--- a/solution.py
+++ b/solution.py
@@ -61,40 +61,39 @@
         self.width, self.share = width, share
 
 
-def pack_kernel(blocks, subs, rows_ref, ids_ref, first_ref, second_ref, ids, sems):
+def pack_kernel(blocks, subs, rows_ref, ids_ref, first_ref, behind_ref, ids, sems):
     plan = Plan(blocks, subs, lax.axis_index("tile"), lax.axis_index("sub"))
     share, size = plan.share, plan.share * BLOCK
-    ids_copy = pltpu.make_async_copy(ids_ref, ids, sems.at[0])
-
-    def copies(block, out, sem):
-        for down in range(0, size, COPY):
-            start = pl.multiple_of(block * BLOCK + down, COPY)
-            yield pltpu.make_async_copy(
-                rows_ref.at[pl.ds(start, COPY), :], out.at[pl.ds(down, COPY), :], sems.at[sem + down // COPY]
+    copies = [pltpu.make_async_copy(ids_ref, ids, sems.at[0])]
+    for index, down in enumerate(range(0, size, COPY)):
+        start = pl.multiple_of(plan.first * BLOCK + down, COPY)
+        copies.append(
+            pltpu.make_async_copy(
+                rows_ref.at[pl.ds(start, COPY), :], first_ref.at[pl.ds(down, COPY), :], sems.at[1 + index]
             )
-
-    first = list(copies(plan.first, first_ref, 1))
-    second = list(copies(plan.second, second_ref, 1 + size // COPY))
-    for copy in [ids_copy] + first + second:
+        )
+    for copy in copies:
         copy.start()
-    ids_copy.wait()
+    copies[0].wait()
     depth = first_ref.shape[1]
     edge = jnp.max(ids[pl.ds(plan.edge, 1), :], axis=1, keepdims=True)
     rest = [jnp.broadcast_to(edge, (1, BLOCK)), jnp.zeros((1, depth - size - BLOCK), jnp.int32)]
-    for block, out in ((plan.first, first_ref), (plan.second, second_ref)):
+    for block, out in ((plan.first, first_ref), (plan.second, behind_ref)):
         row = jnp.concatenate([ids[pl.ds(block + k, 1), :] for k in range(share)] + rest, axis=1)
-        out[size:, :] = jnp.broadcast_to(row.astype(jnp.float32), (8, depth)).astype(jnp.bfloat16)
-    for copy in first + second:
+        row = jnp.broadcast_to(row.astype(jnp.float32), (8, depth)).astype(jnp.bfloat16)
+        out[out.shape[0] - 8 :, :] = row
+    for copy in copies[1:]:
         copy.wait()
 
 
 def pack(size, subs, embeddings, by_block):
+    depth = embeddings.shape[1]
     return pl.pallas_call(
         functools.partial(pack_kernel, by_block.shape[0], subs),
         in_specs=[pl.BlockSpec(memory_space=pl.ANY)] * 2,
         out_specs=[pl.BlockSpec(memory_space=pltpu.VMEM)] * 2,
-        out_shape=[jax.ShapeDtypeStruct((size + 8, embeddings.shape[1]), jnp.bfloat16)] * 2,
-        scratch_shapes=[pltpu.VMEM(by_block.shape, jnp.int32), pltpu.SemaphoreType.DMA((2 * size // COPY + 1,))],
+        out_shape=[jax.ShapeDtypeStruct((count, depth), jnp.bfloat16) for count in (size + 8, 8)],
+        scratch_shapes=[pltpu.VMEM(by_block.shape, jnp.int32), pltpu.SemaphoreType.DMA((size // COPY + 1,))],
         compiler_params=pltpu.CompilerParams(vmem_limit_bytes=8 * 1024 * 1024),
         cost_estimate=pl.CostEstimate(flops=0, bytes_accessed=1024, transcendentals=0),
     )(embeddings, by_block)
@@ -114,10 +113,12 @@
         return self.ref[5 * self.blocks + index]
 
 
-MEMBER, FIRST_BLOCK, EDGE, INNER = range(4)
-
-
-def self_kernel(blocks, subs, meta_ref, rows_ref, tags_ref, unit_ref, sums_ref, held, sems):
+MEMBER, FIRST_BLOCK, EDGE, INNER, SECOND_BLOCK = range(5)
+
+
+def self_kernel(
+    blocks, subs, meta_ref, rows_ref, tags_ref, behind_ref, unit_ref, sums_ref, second_ref, held, sems
+):
     meta = Meta(meta_ref, blocks)
     width = blocks // subs
     quarter = width * BLOCK
@@ -145,6 +146,10 @@
             if turn == 0:
                 keep = keep & (lax.broadcasted_iota(jnp.int32, weight.shape, 1) - row != inner * BLOCK)
             sums_ref[pl.ds(block, 1), :] = lane_sums(jnp.where(keep, weight, 0.0))
+    size = second_ref.shape[0] - 8
+    start = pl.multiple_of(meta.number(SECOND_BLOCK) * BLOCK, BLOCK)
+    second_ref[:size, :] = unit_ref[pl.ds(start, size), :]
+    second_ref[size:, :] = behind_ref[...]
 
 
 def chunk_tags(piece_ref, size):
@@ -168,7 +173,7 @@
 
     @pl.when(shared)
     def _():
-        piece = normalised(piece_ref[:size, :])
+        piece = piece_ref[:size, :] if chunk == 2 else normalised(piece_ref[:size, :])
         total = None
         for start in range(0, meta.blocks * BLOCK, STEP):
             cosine = products(unit_ref[start : start + STEP, :], piece)
@@ -301,7 +306,7 @@
         return [(b, a) for a, b in route]
 
     by_block = cluster_ids.reshape(blocks, BLOCK)
-    first_out, second_out = pack(size, subs, embeddings, by_block)
+    first_out, behind = pack(size, subs, embeddings, by_block)
     from_inner = lax.ppermute(first_out, "tile", swap)
     from_outer = lax.ppermute(first_out, "tile", inward)
 
@@ -309,7 +314,7 @@
     used = jnp.sum((by_block >= 0).astype(jnp.int32), axis=1)
     seen = jnp.where(inner, tag, -2)
     swapped = jnp.where(plan.far & (jnp.arange(blocks) >= blocks // 2), -2, seen)
-    numbers = jnp.stack([member, plan.first, plan.edge, inner])
+    numbers = jnp.stack([member, plan.first, plan.edge, inner, plan.second])
     meta = jnp.concatenate([tag, used, seen, swapped, tag, numbers]).astype(jnp.int32)
 
     heap = blocks // 2
@@ -326,16 +331,19 @@
     col_sums = jax.ShapeDtypeStruct((share + 1, BLOCK), jnp.float32)
     quarter = width * BLOCK
     vmem, smem = pl.BlockSpec(memory_space=pltpu.VMEM), pl.BlockSpec(memory_space=pltpu.SMEM)
-    unit, sums = pl.pallas_call(
+    unit, sums, second_out = pl.pallas_call(
         functools.partial(self_kernel, blocks, subs),
-        in_specs=[smem, pl.BlockSpec(memory_space=pl.ANY), vmem],
-        out_specs=[vmem, vmem],
-        out_shape=[jax.ShapeDtypeStruct((rows, depth), jnp.bfloat16), row_sums],
+        in_specs=[smem, pl.BlockSpec(memory_space=pl.ANY), vmem, vmem],
+        out_specs=[vmem] * 3,
+        out_shape=[
+            jax.ShapeDtypeStruct((rows, depth), jnp.bfloat16),
+            row_sums,
+            jax.ShapeDtypeStruct((size + 8, depth), jnp.bfloat16),
+        ],
         scratch_shapes=[pltpu.VMEM((subs, quarter, depth), jnp.bfloat16), pltpu.SemaphoreType.DMA((subs,))],
         compiler_params=pltpu.CompilerParams(vmem_limit_bytes=24 * 1024 * 1024),
         cost_estimate=pl.CostEstimate(flops=0, bytes_accessed=1024, transcendentals=0),
-    )(meta, embeddings, lax.dynamic_slice_in_dim(cluster_ids, member * quarter, quarter, 0)[None])
-    second_out, sums = lax.optimization_barrier((second_out, sums))
+    )(meta, embeddings, lax.dynamic_slice_in_dim(cluster_ids, member * quarter, quarter, 0)[None], behind)
     last = lax.ppermute(second_out, "tile", around)
 
     def middle(chunk, piece, before):

time: 41.5 us -> 41.3 us (level)
  transfers between devices with their start and end apart: 8 -> 8, of which waited for: 4 -> 4; matrix products, arithmetic and copies ran while one was open for 1% -> 1% of each run, Pallas kernels for 21% -> 22%
where the time goes in v19:
time: 41.3 us; the launch traced here: 41.1 us
  waiting for transfers between devices  15.8 us (38%)
  starting transfers between devices  13.2 us (32%)
  Pallas kernels  10.2 us (25%)
  between operations  0.93 us (2%)
  local copies, waits for them, and re-layouts  0.81 us (2%)
    ppermute x1, waiting for transfers between devices, shards(): last = lax.ppermute(second_out, 'tile', around)  10.3 us
    pallas_call x1, Pallas kernels, shards(): pl.pallas_call(functools.partial(self_kernel, blocks, subs), in_specs=[sm...  6.27 us
    ppermute x1, starting transfers between devices, shards(): from_outer = lax.ppermute(first_out, 'tile', inward)  4.96 us
    ppermute x1, waiting for transfers between devices, shards(): from_outer = lax.ppermute(first_out, 'tile', inward)  2.93 us
    ppermute x1, starting transfers between devices, shards(): last = lax.ppermute(second_out, 'tile', around)  2.19 us
    pallas_call x3, Pallas kernels, call(): pl.pallas_call(kernel, in_specs=[smem] + [vmem] * len(operands), out_spec...  2.12 us
    ppermute x1, starting transfers between devices, shards(): home = lax.ppermute(cols, 'tile', turned(around))  1.86 us
    ppermute x1, waiting for transfers between devices, shards(): home = lax.ppermute(cols, 'tile', turned(around))  1.77 us
  transfers between devices with their start and end apart: 8, of which 4 were waited for; matrix products, arithmetic and copies ran while one was open for 1% of the time, Pallas kernels for 22%

profile of v19, /device:TPU:0, one launch (start us, length us, event | category | flops | bytes accessed | tf_op | source)
XLA Modules:
  0.0 41.1 jit_solution(7037666281743913477)
XLA Ops:
  0.0 0.0 copy-start.3
  0.0 1.2 %shard_map.30 = (bf16[264,1024]{1,0:T(8,128)(2,1)S(1)}, bf16[8,1024]{1,0:T(8,128)(2,1)S(1)}) custom-call(bf16[2048,1024]{1,0:T(8,128)(2,1)} %rows_ref.3, s32[16,128]{1,0:T(8,128)} %bitcast.59), custom_call_target="tpu_custom_call" | custom-call | bytes 1024 | tf_op jit(solution)/shard_map/pallas_call | solution.py:91
  1.2 5.0 %collective-permute-start.1 = (bf16[264,1024]{1,0:T(8,128)(2,1)S(1)}, bf16[264,1024]{1,0:T(8,128)(2,1)S(1)}, u32[]{:S(2)}, u32[]{:S(2)}) collective-permute-start(bf16[264,1024]{1,0:T(8,128)(2,1)S(1)} %get-tuple-element.54), channel_id=1, source_target_pairs={{0,4},{12,8},{1,5},{13,9},{2,6},{14,10},{3,7},{15,11},{16,20},{28,... | collective-permute-start | bytes 1622024 | tf_op jit(solution)/shard_map/ppermute | solution.py:311
  6.1 0.7 %collective-permute-start = (bf16[264,1024]{1,0:T(8,128)(2,1)S(1)}, bf16[264,1024]{1,0:T(8,128)(2,1)S(1)}, u32[]{:S(2)}, u32[]{:S(2)}) collective-permute-start(bf16[264,1024]{1,0:T(8,128)(2,1)S(1)} %get-tuple-element.54), channel_id=1, source_target_pairs={{4,8},{8,4},{5,9},{9,5},{6,10},{10,6},{7,11},{11,7},{20,24},{24,20... | collective-permute-start | bytes 1622024 | tf_op jit(solution)/shard_map/ppermute | solution.py:310
  6.9 0.0 copy-done.3
  6.9 0.1 convert_reduce_fusion
  7.1 0.1 dynamic_slice.47
  7.2 0.1 concatenate.3.meta_ref
  7.3 0.1 broadcast_in_dim.128
  7.4 6.3 %shard_map.31 = (bf16[2048,1024]{1,0:T(8,128)(2,1)S(1)}, f32[16,128]{1,0:T(8,128)S(1)}, bf16[264,1024]{1,0:T(8,128)(2,1)S(1)}) custom-call(s32[85]{0:T(128)S(1)} %concatenate.3.meta_ref, bf16[2048,1024]{1,0:T(8,128)(2,1)} %rows_ref.3, s32[1,512]{1,0:T(1,128)S(1)} %bitcast.58, bf16[8,1024]{1,0:T(8,128)(2,1)S(1)} %get-tuple-element.52.behind_ref), custom_call_target="tpu_custom_call" | custom-call | bytes 1024 | tf_op jit(solution)/shard_map/pallas_call | solution.py:334
  13.7 2.2 %collective-permute-start.2 = (bf16[264,1024]{1,0:T(8,128)(2,1)S(1)}, bf16[264,1024]{1,0:T(8,128)(2,1)S(1)}, u32[]{:S(2)}, u32[]{:S(2)}) collective-permute-start(bf16[264,1024]{1,0:T(8,128)(2,1)S(1)} %get-tuple-element.58), channel_id=1, source_target_pairs={{0,4},{12,8},{4,12},{8,0},{1,5},{13,9},{5,13},{9,1},{2,6},{14,10},... | collective-permute-start | bytes 1622024 | tf_op jit(solution)/shard_map/ppermute | solution.py:347
  15.8 2.9 %collective-permute-done.1.piece_ref = bf16[264,1024]{1,0:T(8,128)(2,1)S(1)} collective-permute-done((bf16[264,1024]{1,0:T(8,128)(2,1)S(1)}, bf16[264,1024]{1,0:T(8,128)(2,1)S(1)}, u32[]{:S(2)}, u32[]{:S(2)}) %collective-permute-start.1) | collective-permute-done | bytes 540704 | tf_op jit(solution)/shard_map/ppermute | solution.py:311
  18.8 0.7 %shard_map.32 = (f32[16,128]{1,0:T(8,128)S(1)}, f32[3,128]{1,0:T(4,128)S(1)}) custom-call(s32[85]{0:T(128)S(1)} %concatenate.3.meta_ref, bf16[2048,1024]{1,0:T(8,128)(2,1)S(1)} %get-tuple-element.53.unit_ref, bf16[264,1024]{1,0:T(8,128)(2,1)S(1)} %collective-permute-done.1.piece_ref, f32[16,128]{1,0:T(8,128)S(1)} %get-tuple-element.55.before_ref), custom_call_target="tpu_custom_call" | custom-call | flops 1073741824 | bytes 1024 | tf_op jit(solution)/shard_map/pallas_call | solution.py:237
  19.5 1.3 %collective-permute-start.3 = (f32[3,128]{1,0:T(4,128)S(1)}, f32[3,128]{1,0:T(4,128)S(1)}, u32[]{:S(2)}, u32[]{:S(2)}) collective-permute-start(f32[3,128]{1,0:T(4,128)S(1)} %get-tuple-element.60), channel_id=1, source_target_pairs={{4,0},{8,12},{5,1},{9,13},{6,2},{10,14},{7,3},{11,15},{20,16},{24,... | collective-permute-start | bytes 4616 | tf_op jit(solution)/shard_map/ppermute | solution.py:360
  20.8 0.0 collective-permute-done.piece_ref
  20.8 0.7 %shard_map.33 = (f32[16,128]{1,0:T(8,128)S(1)}, f32[3,128]{1,0:T(4,128)S(1)}) custom-call(s32[85]{0:T(128)S(1)} %concatenate.3.meta_ref, bf16[2048,1024]{1,0:T(8,128)(2,1)S(1)} %get-tuple-element.53.unit_ref, bf16[264,1024]{1,0:T(8,128)(2,1)S(1)} %collective-permute-done.piece_ref, f32[16,128]{1,0:T(8,128)S(1)} %get-tuple-element.56.before_ref), custom_call_target="tpu_custom_call" | custom-call | flops 1073741824 | bytes 1024 | tf_op jit(solution)/shard_map/pallas_call | solution.py:237
  21.5 0.7 %collective-permute-start.5 = (f32[3,128]{1,0:T(4,128)S(1)}, f32[3,128]{1,0:T(4,128)S(1)}, u32[]{:S(2)}, u32[]{:S(2)}) collective-permute-start(f32[3,128]{1,0:T(4,128)S(1)} %get-tuple-element.57.swap_cols_ref.here_ref), channel_id=1, source_target_pairs={{8,4},{4,8},{9,5},{5,9},{10,6},{6,10},{11,7},{7,11},{24,20},{20,24... | collective-permute-start | bytes 4616 | tf_op jit(solution)/shard_map/ppermute | solution.py:362
  22.2 10.3 %collective-permute-done.2.piece_ref = bf16[264,1024]{1,0:T(8,128)(2,1)S(1)} collective-permute-done((bf16[264,1024]{1,0:T(8,128)(2,1)S(1)}, bf16[264,1024]{1,0:T(8,128)(2,1)S(1)}, u32[]{:S(2)}, u32[]{:S(2)}) %collective-permute-start.2) | collective-permute-done | bytes 540704 | tf_op jit(solution)/shard_map/ppermute | solution.py:347
  32.5 0.0 collective-permute-done.3.outer_back_ref
  32.5 0.7 %shard_map.34 = (f32[8,128]{1,0:T(8,128)S(1)}, f32[8,128]{1,0:T(8,128)S(1)}, f32[3,128]{1,0:T(4,128)S(1)}) custom-call(s32[85]{0:T(128)S(1)} %concatenate.3.meta_ref, bf16[2048,1024]{1,0:T(8,128)(2,1)S(1)} %get-tuple-element.53.unit_ref, bf16[264,1024]{1,0:T(8,128)(2,1)S(1)} %collective-permute-done.2.piece_ref, f32[16,128]{1,0:T(8,128)S(1)} %get-tuple-element.59.before_ref, ...), custom_call_target="tpu_custom_call" | custom-call | flops 1073741824 | bytes 1024 | tf_op jit(solution)/shard_map/pallas_call | solution.py:237
  33.2 1.9 %collective-permute-start.4 = (f32[3,128]{1,0:T(4,128)S(1)}, f32[3,128]{1,0:T(4,128)S(1)}, u32[]{:S(2)}, u32[]{:S(2)}) collective-permute-start(f32[3,128]{1,0:T(4,128)S(1)} %get-tuple-element.61), channel_id=1, source_target_pairs={{4,0},{8,12},{12,4},{0,8},{5,1},{9,13},{13,5},{1,9},{6,2},{10,14},... | collective-permute-start | bytes 4616 | tf_op jit(solution)/shard_map/ppermute | solution.py:376
  35.1 0.0 collective-permute-start.6
  35.1 0.0 collective-permute-done.5
  35.1 1.8 %collective-permute-done.4.home_ref = f32[3,128]{1,0:T(4,128)S(1)} collective-permute-done((f32[3,128]{1,0:T(4,128)S(1)}, f32[3,128]{1,0:T(4,128)S(1)}, u32[]{:S(2)}, u32[]{:S(2)}) %collective-permute-start.4) | collective-permute-done | bytes 1568 | tf_op jit(solution)/shard_map/ppermute | solution.py:376
  36.9 0.0 collective-permute-done.6
  36.9 1.6 %collective-permute-start.7 = (f32[4,128]{1,0:T(4,128)S(1)}, f32[4,128]{1,0:T(4,128)S(1)}, u32[]{:S(2)}, u32[]{:S(2)}) collective-permute-start(f32[4,128]{1,0:T(4,128)S(1)} %get-tuple-element.71), channel_id=1, source_target_pairs={{0,2},{1,3},{2,0},{3,1},{4,6},{5,7},{6,4},{7,5},{8,10},{9,11},{10,... | collective-permute-start | bytes 6152 | tf_op jit(solution)/shard_map/ppermute | solution.py:386
  38.4 0.6 %shard_map.35 = s32[1]{0:T(128)} custom-call(f32[3,128]{1,0:T(4,128)S(1)} %get-tuple-element.57.swap_cols_ref.here_ref, f32[3,128]{1,0:T(4,128)S(1)} %collective-permute-done.4.home_ref), custom_call_target="tpu_custom_call" | custom-call | tf_op jit(solution)/shard_map/pallas_call | solution.py:389
  39.7 0.8 %collective-permute-done.7 = f32[4,128]{1,0:T(4,128)S(1)} collective-permute-done((f32[4,128]{1,0:T(4,128)S(1)}, f32[4,128]{1,0:T(4,128)S(1)}, u32[]{:S(2)}, u32[]{:S(2)}) %collective-permute-start.7) | collective-permute-done | bytes 2080 | tf_op jit(solution)/shard_map/ppermute | solution.py:386
  40.5 0.0 copy-start.4
  40.6 0.6 %copy-done.4 = f32[512]{0:T(512)} copy-done((f32[512]{0:T(512)}, f32[512]{0:T(512)S(1)}, u32[]{:S(2)}) %copy-start.4) | copy-done | bytes 2072
  (9 shorter events, 0.0 us)
Async XLA Ops:
  0.0 6.9 %copy-start.3 = (s32[2048]{0:T(1024)S(1)}, s32[2048]{0:T(1024)}, u32[]{:S(2)}) copy-start(s32[2048]{0:T(1024)} %param.5) | copy-start | bytes 24580
  1.2 17.6 %collective-permute-start.1 = (bf16[264,1024]{1,0:T(8,128)(2,1)S(1)}, bf16[264,1024]{1,0:T(8,128)(2,1)S(1)}, u32[]{:S(2)}, u32[]{:S(2)}) collective-permute-start(bf16[264,1024]{1,0:T(8,128)(2,1)S(1)} %get-tuple-element.54), channel_id=1, source_target_pairs={{0,4},{12,8},{1,5},{13,9},{2,6},{14,10},{3,7},{15,11},{16,20},{28,... | collective-permute-start | bytes 1622024 | tf_op jit(solution)/shard_map/ppermute | solution.py:311
  6.1 14.6 %collective-permute-start = (bf16[264,1024]{1,0:T(8,128)(2,1)S(1)}, bf16[264,1024]{1,0:T(8,128)(2,1)S(1)}, u32[]{:S(2)}, u32[]{:S(2)}) collective-permute-start(bf16[264,1024]{1,0:T(8,128)(2,1)S(1)} %get-tuple-element.54), channel_id=1, source_target_pairs={{4,8},{8,4},{5,9},{9,5},{6,10},{10,6},{7,11},{11,7},{20,24},{24,20... | collective-permute-start | bytes 1622024 | tf_op jit(solution)/shard_map/ppermute | solution.py:310
  13.7 18.8 %collective-permute-start.2 = (bf16[264,1024]{1,0:T(8,128)(2,1)S(1)}, bf16[264,1024]{1,0:T(8,128)(2,1)S(1)}, u32[]{:S(2)}, u32[]{:S(2)}) collective-permute-start(bf16[264,1024]{1,0:T(8,128)(2,1)S(1)} %get-tuple-element.58), channel_id=1, source_target_pairs={{0,4},{12,8},{4,12},{8,0},{1,5},{13,9},{5,13},{9,1},{2,6},{14,10},... | collective-permute-start | bytes 1622024 | tf_op jit(solution)/shard_map/ppermute | solution.py:347
  19.5 13.0 %collective-permute-start.3 = (f32[3,128]{1,0:T(4,128)S(1)}, f32[3,128]{1,0:T(4,128)S(1)}, u32[]{:S(2)}, u32[]{:S(2)}) collective-permute-start(f32[3,128]{1,0:T(4,128)S(1)} %get-tuple-element.60), channel_id=1, source_target_pairs={{4,0},{8,12},{5,1},{9,13},{6,2},{10,14},{7,3},{11,15},{20,16},{24,... | collective-permute-start | bytes 4616 | tf_op jit(solution)/shard_map/ppermute | solution.py:360
  21.5 13.6 %collective-permute-start.5 = (f32[3,128]{1,0:T(4,128)S(1)}, f32[3,128]{1,0:T(4,128)S(1)}, u32[]{:S(2)}, u32[]{:S(2)}) collective-permute-start(f32[3,128]{1,0:T(4,128)S(1)} %get-tuple-element.57.swap_cols_ref.here_ref), channel_id=1, source_target_pairs={{8,4},{4,8},{9,5},{5,9},{10,6},{6,10},{11,7},{7,11},{24,20},{20,24... | collective-permute-start | bytes 4616 | tf_op jit(solution)/shard_map/ppermute | solution.py:362
  33.2 3.6 %collective-permute-start.4 = (f32[3,128]{1,0:T(4,128)S(1)}, f32[3,128]{1,0:T(4,128)S(1)}, u32[]{:S(2)}, u32[]{:S(2)}) collective-permute-start(f32[3,128]{1,0:T(4,128)S(1)} %get-tuple-element.61), channel_id=1, source_target_pairs={{4,0},{8,12},{12,4},{0,8},{5,1},{9,13},{13,5},{1,9},{6,2},{10,14},... | collective-permute-start | bytes 4616 | tf_op jit(solution)/shard_map/ppermute | solution.py:376
  35.1 1.8 %collective-permute-start.6 = (f32[8,128]{1,0:T(8,128)S(1)}, f32[8,128]{1,0:T(8,128)S(1)}, u32[]{:S(2)}, u32[]{:S(2)}) collective-permute-start(f32[8,128]{1,0:T(8,128)S(1)} %get-tuple-element.64), channel_id=1, source_target_pairs={{0,1},{1,0},{2,3},{3,2},{4,5},{5,4},{6,7},{7,6},{8,9},{9,8},{10,11... | collective-permute-start | bytes 12296 | tf_op jit(solution)/shard_map/ppermute | solution.py:379
  36.9 3.7 %collective-permute-start.7 = (f32[4,128]{1,0:T(4,128)S(1)}, f32[4,128]{1,0:T(4,128)S(1)}, u32[]{:S(2)}, u32[]{:S(2)}) collective-permute-start(f32[4,128]{1,0:T(4,128)S(1)} %get-tuple-element.71), channel_id=1, source_target_pairs={{0,2},{1,3},{2,0},{3,1},{4,6},{5,7},{6,4},{7,5},{8,10},{9,11},{10,... | collective-permute-start | bytes 6152 | tf_op jit(solution)/shard_map/ppermute | solution.py:386
  40.5 0.6 %copy-start.4 = (f32[512]{0:T(512)}, f32[512]{0:T(512)S(1)}, u32[]{:S(2)}) copy-start(f32[512]{0:T(512)S(1)} %get-tuple-element.105) | copy-start | bytes 6148

commit v20 on v19

--- a/solution.py
+++ b/solution.py
@@ -157,8 +157,12 @@
     return row[:, :size], row[:, size : size + BLOCK]
 
 
-def cross_terms(meta, chunk, column_tags, unit_ref, piece_ref, before_ref, sums, columns, place):
+def cross_terms(meta, chunk, column_tags, unit_ref, piece_ref, before_ref, sums, columns, place, head=None):
     size = column_tags.shape[1]
+    step = STEP
+    if head is not None:
+        step = head.shape[0]
+        head[...] = products(unit_ref[:step, :], piece_ref[:size, :])
     there = [jnp.max(column_tags[:, at : at + BLOCK]) for at in range(0, size, BLOCK)]
     shared = False
     for block in range(meta.blocks):
@@ -175,9 +179,12 @@
     def _():
         piece = piece_ref[:size, :] if chunk == 2 else normalised(piece_ref[:size, :])
         total = None
-        for start in range(0, meta.blocks * BLOCK, STEP):
-            cosine = products(unit_ref[start : start + STEP, :], piece)
-            for inner in range(0, STEP, BLOCK):
+        for start in range(0, meta.blocks * BLOCK, step):
+            if start == 0 and head is not None:
+                cosine = head[...]
+            else:
+                cosine = products(unit_ref[start : start + step, :], piece)
+            for inner in range(0, step, BLOCK):
                 block = (start + inner) // BLOCK
                 bias = column_bias(meta.tag(block, chunk), column_tags)
                 weight = jnp.exp2(cosine[inner : inner + BLOCK] * GAIN + bias)
@@ -205,7 +212,7 @@
 
 def last_kernel(
     blocks, share, width, meta_ref, unit_ref, piece_ref, before_ref, outer_back_ref, swap_cols_ref,
-    keep_ref, send_ref, cols_ref, sums, columns,
+    keep_ref, send_ref, cols_ref, sums, columns, head,
 ):
     meta = Meta(meta_ref, blocks)
     tags, _ = chunk_tags(piece_ref, share * BLOCK)
@@ -214,7 +221,7 @@
         owner = block // width
         return owner % 2 * (blocks // 2) + owner // 2 * width + block % width
 
-    cross_terms(meta, 2, tags, unit_ref, piece_ref, before_ref, sums, columns, place)
+    cross_terms(meta, 2, tags, unit_ref, piece_ref, before_ref, sums, columns, place, head)
     total = jnp.sum(columns[...], axis=0, keepdims=True)
     for k in range(share):
         cols_ref[k : k + 1, :] = total[:, k * BLOCK : (k + 1) * BLOCK]
@@ -369,6 +376,7 @@
         [
             pltpu.VMEM((blocks, BLOCK), jnp.float32),
             pltpu.VMEM((8, size), jnp.float32),
+            pltpu.VMEM((STEP // 2, size), jnp.float32),
         ],
         2 * rows * size * depth,
     )

time: 41.3 us -> 41.5 us (level)
  no operation moved by 1% of the time
where the time goes in v20:
time: 41.5 us; the launch traced here: 41.3 us
  waiting for transfers between devices  16 us (39%)
  starting transfers between devices  13 us (31%)
  Pallas kernels  10.4 us (25%)
  between operations  0.93 us (2%)
  local copies, waits for them, and re-layouts  0.81 us (2%)
    ppermute x1, waiting for transfers between devices, shards(): last = lax.ppermute(second_out, 'tile', around)  10.3 us
    pallas_call x1, Pallas kernels, shards(): pl.pallas_call(functools.partial(self_kernel, blocks, subs), in_specs=[sm...  6.27 us
    ppermute x1, starting transfers between devices, shards(): from_outer = lax.ppermute(first_out, 'tile', inward)  4.96 us
    ppermute x1, waiting for transfers between devices, shards(): from_outer = lax.ppermute(first_out, 'tile', inward)  2.93 us
    pallas_call x3, Pallas kernels, call(): pl.pallas_call(kernel, in_specs=[smem] + [vmem] * len(operands), out_spec...  2.32 us
    ppermute x1, starting transfers between devices, shards(): last = lax.ppermute(second_out, 'tile', around)  2.19 us
    ppermute x1, waiting for transfers between devices, shards(): home = lax.ppermute(cols, 'tile', turned(around))  1.96 us
    ppermute x1, starting transfers between devices, shards(): home = lax.ppermute(cols, 'tile', turned(around))  1.67 us
  transfers between devices with their start and end apart: 8, of which 4 were waited for; matrix products, arithmetic and copies ran while one was open for 1% of the time, Pallas kernels for 22%

profile of v20, /device:TPU:0, one launch (start us, length us, event | category | flops | bytes accessed | tf_op | source)
XLA Modules:
  0.0 41.3 jit_solution(2686815659606966041)
XLA Ops:
  0.0 0.0 copy-start.3
  0.0 1.2 %shard_map.30 = (bf16[264,1024]{1,0:T(8,128)(2,1)S(1)}, bf16[8,1024]{1,0:T(8,128)(2,1)S(1)}) custom-call(bf16[2048,1024]{1,0:T(8,128)(2,1)} %rows_ref.3, s32[16,128]{1,0:T(8,128)} %bitcast.59), custom_call_target="tpu_custom_call" | custom-call | bytes 1024 | tf_op jit(solution)/shard_map/pallas_call | solution.py:91
  1.2 5.0 %collective-permute-start.1 = (bf16[264,1024]{1,0:T(8,128)(2,1)S(1)}, bf16[264,1024]{1,0:T(8,128)(2,1)S(1)}, u32[]{:S(2)}, u32[]{:S(2)}) collective-permute-start(bf16[264,1024]{1,0:T(8,128)(2,1)S(1)} %get-tuple-element.54), channel_id=1, source_target_pairs={{0,4},{12,8},{1,5},{13,9},{2,6},{14,10},{3,7},{15,11},{16,20},{28,... | collective-permute-start | bytes 1622024 | tf_op jit(solution)/shard_map/ppermute | solution.py:318
  6.1 0.7 %collective-permute-start = (bf16[264,1024]{1,0:T(8,128)(2,1)S(1)}, bf16[264,1024]{1,0:T(8,128)(2,1)S(1)}, u32[]{:S(2)}, u32[]{:S(2)}) collective-permute-start(bf16[264,1024]{1,0:T(8,128)(2,1)S(1)} %get-tuple-element.54), channel_id=1, source_target_pairs={{4,8},{8,4},{5,9},{9,5},{6,10},{10,6},{7,11},{11,7},{20,24},{24,20... | collective-permute-start | bytes 1622024 | tf_op jit(solution)/shard_map/ppermute | solution.py:317
  6.9 0.0 copy-done.3
  6.9 0.1 convert_reduce_fusion
  7.1 0.1 dynamic_slice.47
  7.2 0.1 concatenate.3.meta_ref
  7.3 0.1 broadcast_in_dim.128
  7.4 6.3 %shard_map.31 = (bf16[2048,1024]{1,0:T(8,128)(2,1)S(1)}, f32[16,128]{1,0:T(8,128)S(1)}, bf16[264,1024]{1,0:T(8,128)(2,1)S(1)}) custom-call(s32[85]{0:T(128)S(1)} %concatenate.3.meta_ref, bf16[2048,1024]{1,0:T(8,128)(2,1)} %rows_ref.3, s32[1,512]{1,0:T(1,128)S(1)} %bitcast.58, bf16[8,1024]{1,0:T(8,128)(2,1)S(1)} %get-tuple-element.52.behind_ref), custom_call_target="tpu_custom_call" | custom-call | bytes 1024 | tf_op jit(solution)/shard_map/pallas_call | solution.py:341
  13.7 2.2 %collective-permute-start.2 = (bf16[264,1024]{1,0:T(8,128)(2,1)S(1)}, bf16[264,1024]{1,0:T(8,128)(2,1)S(1)}, u32[]{:S(2)}, u32[]{:S(2)}) collective-permute-start(bf16[264,1024]{1,0:T(8,128)(2,1)S(1)} %get-tuple-element.58), channel_id=1, source_target_pairs={{0,4},{12,8},{4,12},{8,0},{1,5},{13,9},{5,13},{9,1},{2,6},{14,10},... | collective-permute-start | bytes 1622024 | tf_op jit(solution)/shard_map/ppermute | solution.py:354
  15.8 2.9 %collective-permute-done.1.piece_ref = bf16[264,1024]{1,0:T(8,128)(2,1)S(1)} collective-permute-done((bf16[264,1024]{1,0:T(8,128)(2,1)S(1)}, bf16[264,1024]{1,0:T(8,128)(2,1)S(1)}, u32[]{:S(2)}, u32[]{:S(2)}) %collective-permute-start.1) | collective-permute-done | bytes 540704 | tf_op jit(solution)/shard_map/ppermute | solution.py:318
  18.8 0.7 %shard_map.32 = (f32[16,128]{1,0:T(8,128)S(1)}, f32[3,128]{1,0:T(4,128)S(1)}) custom-call(s32[85]{0:T(128)S(1)} %concatenate.3.meta_ref, bf16[2048,1024]{1,0:T(8,128)(2,1)S(1)} %get-tuple-element.53.unit_ref, bf16[264,1024]{1,0:T(8,128)(2,1)S(1)} %collective-permute-done.1.piece_ref, f32[16,128]{1,0:T(8,128)S(1)} %get-tuple-element.55.before_ref), custom_call_target="tpu_custom_call" | custom-call | flops 1073741824 | bytes 1024 | tf_op jit(solution)/shard_map/pallas_call | solution.py:244
  19.5 1.3 %collective-permute-start.3 = (f32[3,128]{1,0:T(4,128)S(1)}, f32[3,128]{1,0:T(4,128)S(1)}, u32[]{:S(2)}, u32[]{:S(2)}) collective-permute-start(f32[3,128]{1,0:T(4,128)S(1)} %get-tuple-element.60), channel_id=1, source_target_pairs={{4,0},{8,12},{5,1},{9,13},{6,2},{10,14},{7,3},{11,15},{20,16},{24,... | collective-permute-start | bytes 4616 | tf_op jit(solution)/shard_map/ppermute | solution.py:367
  20.8 0.0 collective-permute-done.piece_ref
  20.8 0.7 %shard_map.33 = (f32[16,128]{1,0:T(8,128)S(1)}, f32[3,128]{1,0:T(4,128)S(1)}) custom-call(s32[85]{0:T(128)S(1)} %concatenate.3.meta_ref, bf16[2048,1024]{1,0:T(8,128)(2,1)S(1)} %get-tuple-element.53.unit_ref, bf16[264,1024]{1,0:T(8,128)(2,1)S(1)} %collective-permute-done.piece_ref, f32[16,128]{1,0:T(8,128)S(1)} %get-tuple-element.56.before_ref), custom_call_target="tpu_custom_call" | custom-call | flops 1073741824 | bytes 1024 | tf_op jit(solution)/shard_map/pallas_call | solution.py:244
  21.5 0.7 %collective-permute-start.5 = (f32[3,128]{1,0:T(4,128)S(1)}, f32[3,128]{1,0:T(4,128)S(1)}, u32[]{:S(2)}, u32[]{:S(2)}) collective-permute-start(f32[3,128]{1,0:T(4,128)S(1)} %get-tuple-element.57.swap_cols_ref.here_ref), channel_id=1, source_target_pairs={{8,4},{4,8},{9,5},{5,9},{10,6},{6,10},{11,7},{7,11},{24,20},{20,24... | collective-permute-start | bytes 4616 | tf_op jit(solution)/shard_map/ppermute | solution.py:369
  22.2 10.3 %collective-permute-done.2.piece_ref = bf16[264,1024]{1,0:T(8,128)(2,1)S(1)} collective-permute-done((bf16[264,1024]{1,0:T(8,128)(2,1)S(1)}, bf16[264,1024]{1,0:T(8,128)(2,1)S(1)}, u32[]{:S(2)}, u32[]{:S(2)}) %collective-permute-start.2) | collective-permute-done | bytes 540704 | tf_op jit(solution)/shard_map/ppermute | solution.py:354
  32.5 0.0 collective-permute-done.3.outer_back_ref
  32.5 0.9 %shard_map.34 = (f32[8,128]{1,0:T(8,128)S(1)}, f32[8,128]{1,0:T(8,128)S(1)}, f32[3,128]{1,0:T(4,128)S(1)}) custom-call(s32[85]{0:T(128)S(1)} %concatenate.3.meta_ref, bf16[2048,1024]{1,0:T(8,128)(2,1)S(1)} %get-tuple-element.53.unit_ref, bf16[264,1024]{1,0:T(8,128)(2,1)S(1)} %collective-permute-done.2.piece_ref, f32[16,128]{1,0:T(8,128)S(1)} %get-tuple-element.59.before_ref, ...), custom_call_target="tpu_custom_call" | custom-call | flops 1073741824 | bytes 1024 | tf_op jit(solution)/shard_map/pallas_call | solution.py:244
  33.4 1.7 %collective-permute-start.4 = (f32[3,128]{1,0:T(4,128)S(1)}, f32[3,128]{1,0:T(4,128)S(1)}, u32[]{:S(2)}, u32[]{:S(2)}) collective-permute-start(f32[3,128]{1,0:T(4,128)S(1)} %get-tuple-element.61), channel_id=1, source_target_pairs={{4,0},{8,12},{12,4},{0,8},{5,1},{9,13},{13,5},{1,9},{6,2},{10,14},... | collective-permute-start | bytes 4616 | tf_op jit(solution)/shard_map/ppermute | solution.py:384
  35.1 0.0 collective-permute-start.6
  35.1 0.0 collective-permute-done.5
  35.1 2.0 %collective-permute-done.4.home_ref = f32[3,128]{1,0:T(4,128)S(1)} collective-permute-done((f32[3,128]{1,0:T(4,128)S(1)}, f32[3,128]{1,0:T(4,128)S(1)}, u32[]{:S(2)}, u32[]{:S(2)}) %collective-permute-start.4) | collective-permute-done | bytes 1568 | tf_op jit(solution)/shard_map/ppermute | solution.py:384
  37.0 0.0 collective-permute-done.6
  37.1 1.6 %collective-permute-start.7 = (f32[4,128]{1,0:T(4,128)S(1)}, f32[4,128]{1,0:T(4,128)S(1)}, u32[]{:S(2)}, u32[]{:S(2)}) collective-permute-start(f32[4,128]{1,0:T(4,128)S(1)} %get-tuple-element.71), channel_id=1, source_target_pairs={{0,2},{1,3},{2,0},{3,1},{4,6},{5,7},{6,4},{7,5},{8,10},{9,11},{10,... | collective-permute-start | bytes 6152 | tf_op jit(solution)/shard_map/ppermute | solution.py:394
  38.6 0.6 %shard_map.35 = s32[1]{0:T(128)} custom-call(f32[3,128]{1,0:T(4,128)S(1)} %get-tuple-element.57.swap_cols_ref.here_ref, f32[3,128]{1,0:T(4,128)S(1)} %collective-permute-done.4.home_ref), custom_call_target="tpu_custom_call" | custom-call | tf_op jit(solution)/shard_map/pallas_call | solution.py:397
  39.9 0.8 %collective-permute-done.7 = f32[4,128]{1,0:T(4,128)S(1)} collective-permute-done((f32[4,128]{1,0:T(4,128)S(1)}, f32[4,128]{1,0:T(4,128)S(1)}, u32[]{:S(2)}, u32[]{:S(2)}) %collective-permute-start.7) | collective-permute-done | bytes 2080 | tf_op jit(solution)/shard_map/ppermute | solution.py:394
  40.7 0.0 copy-start.4
  40.8 0.6 %copy-done.4 = f32[512]{0:T(512)} copy-done((f32[512]{0:T(512)}, f32[512]{0:T(512)S(1)}, u32[]{:S(2)}) %copy-start.4) | copy-done | bytes 2072
  (9 shorter events, 0.0 us)
Async XLA Ops:
  0.0 6.9 %copy-start.3 = (s32[2048]{0:T(1024)S(1)}, s32[2048]{0:T(1024)}, u32[]{:S(2)}) copy-start(s32[2048]{0:T(1024)} %param.5) | copy-start | bytes 24580
  1.2 17.6 %collective-permute-start.1 = (bf16[264,1024]{1,0:T(8,128)(2,1)S(1)}, bf16[264,1024]{1,0:T(8,128)(2,1)S(1)}, u32[]{:S(2)}, u32[]{:S(2)}) collective-permute-start(bf16[264,1024]{1,0:T(8,128)(2,1)S(1)} %get-tuple-element.54), channel_id=1, source_target_pairs={{0,4},{12,8},{1,5},{13,9},{2,6},{14,10},{3,7},{15,11},{16,20},{28,... | collective-permute-start | bytes 1622024 | tf_op jit(solution)/shard_map/ppermute | solution.py:318
  6.1 14.6 %collective-permute-start = (bf16[264,1024]{1,0:T(8,128)(2,1)S(1)}, bf16[264,1024]{1,0:T(8,128)(2,1)S(1)}, u32[]{:S(2)}, u32[]{:S(2)}) collective-permute-start(bf16[264,1024]{1,0:T(8,128)(2,1)S(1)} %get-tuple-element.54), channel_id=1, source_target_pairs={{4,8},{8,4},{5,9},{9,5},{6,10},{10,6},{7,11},{11,7},{20,24},{24,20... | collective-permute-start | bytes 1622024 | tf_op jit(solution)/shard_map/ppermute | solution.py:317
  13.7 18.8 %collective-permute-start.2 = (bf16[264,1024]{1,0:T(8,128)(2,1)S(1)}, bf16[264,1024]{1,0:T(8,128)(2,1)S(1)}, u32[]{:S(2)}, u32[]{:S(2)}) collective-permute-start(bf16[264,1024]{1,0:T(8,128)(2,1)S(1)} %get-tuple-element.58), channel_id=1, source_target_pairs={{0,4},{12,8},{4,12},{8,0},{1,5},{13,9},{5,13},{9,1},{2,6},{14,10},... | collective-permute-start | bytes 1622024 | tf_op jit(solution)/shard_map/ppermute | solution.py:354
  19.5 13.0 %collective-permute-start.3 = (f32[3,128]{1,0:T(4,128)S(1)}, f32[3,128]{1,0:T(4,128)S(1)}, u32[]{:S(2)}, u32[]{:S(2)}) collective-permute-start(f32[3,128]{1,0:T(4,128)S(1)} %get-tuple-element.60), channel_id=1, source_target_pairs={{4,0},{8,12},{5,1},{9,13},{6,2},{10,14},{7,3},{11,15},{20,16},{24,... | collective-permute-start | bytes 4616 | tf_op jit(solution)/shard_map/ppermute | solution.py:367
  21.5 13.6 %collective-permute-start.5 = (f32[3,128]{1,0:T(4,128)S(1)}, f32[3,128]{1,0:T(4,128)S(1)}, u32[]{:S(2)}, u32[]{:S(2)}) collective-permute-start(f32[3,128]{1,0:T(4,128)S(1)} %get-tuple-element.57.swap_cols_ref.here_ref), channel_id=1, source_target_pairs={{8,4},{4,8},{9,5},{5,9},{10,6},{6,10},{11,7},{7,11},{24,20},{20,24... | collective-permute-start | bytes 4616 | tf_op jit(solution)/shard_map/ppermute | solution.py:369
  33.4 3.6 %collective-permute-start.4 = (f32[3,128]{1,0:T(4,128)S(1)}, f32[3,128]{1,0:T(4,128)S(1)}, u32[]{:S(2)}, u32[]{:S(2)}) collective-permute-start(f32[3,128]{1,0:T(4,128)S(1)} %get-tuple-element.61), channel_id=1, source_target_pairs={{4,0},{8,12},{12,4},{0,8},{5,1},{9,13},{13,5},{1,9},{6,2},{10,14},... | collective-permute-start | bytes 4616 | tf_op jit(solution)/shard_map/ppermute | solution.py:384
  35.1 2.0 %collective-permute-start.6 = (f32[8,128]{1,0:T(8,128)S(1)}, f32[8,128]{1,0:T(8,128)S(1)}, u32[]{:S(2)}, u32[]{:S(2)}) collective-permute-start(f32[8,128]{1,0:T(8,128)S(1)} %get-tuple-element.64), channel_id=1, source_target_pairs={{0,1},{1,0},{2,3},{3,2},{4,5},{5,4},{6,7},{7,6},{8,9},{9,8},{10,11... | collective-permute-start | bytes 12296 | tf_op jit(solution)/shard_map/ppermute | solution.py:387
  37.1 3.7 %collective-permute-start.7 = (f32[4,128]{1,0:T(4,128)S(1)}, f32[4,128]{1,0:T(4,128)S(1)}, u32[]{:S(2)}, u32[]{:S(2)}) collective-permute-start(f32[4,128]{1,0:T(4,128)S(1)} %get-tuple-element.71), channel_id=1, source_target_pairs={{0,2},{1,3},{2,0},{3,1},{4,6},{5,7},{6,4},{7,5},{8,10},{9,11},{10,... | collective-permute-start | bytes 6152 | tf_op jit(solution)/shard_map/ppermute | solution.py:394
  40.7 0.6 %copy-start.4 = (f32[512]{0:T(512)}, f32[512]{0:T(512)S(1)}, u32[]{:S(2)}) copy-start(f32[512]{0:T(512)S(1)} %get-tuple-element.105) | copy-start | bytes 6148

commit v21 on v19

--- a/solution.py
+++ b/solution.py
@@ -204,27 +204,17 @@
 
 
 def last_kernel(
-    blocks, share, width, meta_ref, unit_ref, piece_ref, before_ref, outer_back_ref, swap_cols_ref,
-    keep_ref, send_ref, cols_ref, sums, columns,
+    blocks, share, meta_ref, unit_ref, piece_ref, before_ref, outer_back_ref, swap_cols_ref,
+    sums_ref, cols_ref, columns,
 ):
     meta = Meta(meta_ref, blocks)
     tags, _ = chunk_tags(piece_ref, share * BLOCK)
-
-    def place(block):
-        owner = block // width
-        return owner % 2 * (blocks // 2) + owner // 2 * width + block % width
-
-    cross_terms(meta, 2, tags, unit_ref, piece_ref, before_ref, sums, columns, place)
+    cross_terms(meta, 2, tags, unit_ref, piece_ref, before_ref, sums_ref, columns, lambda block: block)
     total = jnp.sum(columns[...], axis=0, keepdims=True)
     for k in range(share):
         cols_ref[k : k + 1, :] = total[:, k * BLOCK : (k + 1) * BLOCK]
-        at = place(meta.number(FIRST_BLOCK) + k)
-        sums[pl.ds(at, 1), :] += outer_back_ref[k : k + 1, :]
+        sums_ref[pl.ds(meta.number(FIRST_BLOCK) + k, 1), :] += outer_back_ref[k : k + 1, :]
     cols_ref[share : share + 1, :] = swap_cols_ref[share : share + 1, :]
-    parity = meta.number(MEMBER) % 2
-    heap = blocks // 2
-    keep_ref[...] = sums[pl.ds(pl.multiple_of(parity * heap, heap), heap), :]
-    send_ref[...] = sums[pl.ds(pl.multiple_of((1 - parity) * heap, heap), heap), :]
 
 
 def flag_kernel(share, here_ref, home_ref, flag_ref):
@@ -317,15 +307,9 @@
     numbers = jnp.stack([member, plan.first, plan.edge, inner, plan.second])
     meta = jnp.concatenate([tag, used, seen, swapped, tag, numbers]).astype(jnp.int32)
 
-    heap = blocks // 2
-    owner = plan.second // width
-    home_row = jnp.arange(heap)[:, None] - (owner // 2 * width + plan.second % width)
-    home_row = jnp.broadcast_to(home_row, (heap, BLOCK)).astype(jnp.int32)
-    upper = [
-        jnp.broadcast_to((member >> bit) & 1, (heap >> bit, BLOCK)).astype(jnp.int32)
-        for bit in range(1, subs.bit_length() - 1)
-    ]
-    meta, home_row, *upper = lax.optimization_barrier((meta, home_row, *upper))
+    home_row = jnp.arange(blocks)[:, None] - plan.second
+    home_row = jnp.broadcast_to(home_row, (blocks, BLOCK)).astype(jnp.int32)
+    meta, home_row = lax.optimization_barrier((meta, home_row))
 
     row_sums = jax.ShapeDtypeStruct((blocks, BLOCK), jnp.float32)
     col_sums = jax.ShapeDtypeStruct((share + 1, BLOCK), jnp.float32)
@@ -360,31 +344,20 @@
     outer_back = lax.ppermute(outer_cols, "tile", turned(inward))
     sums, swap_cols = middle(1, from_inner, sums)
     swap_back = lax.ppermute(swap_cols, "tile", turned(swap))
-    half = jax.ShapeDtypeStruct((heap, BLOCK), jnp.float32)
-    held, leaving, cols = call(
-        functools.partial(last_kernel, blocks, share, width),
+    held, cols = call(
+        functools.partial(last_kernel, blocks, share),
         meta,
         (unit, last, sums, outer_back, swap_cols),
-        [half, half, col_sums],
-        [
-            pltpu.VMEM((blocks, BLOCK), jnp.float32),
-            pltpu.VMEM((8, size), jnp.float32),
-        ],
-        2 * rows * size * depth,
+        [row_sums, col_sums],
+        [pltpu.VMEM((8, size), jnp.float32)],
+        0,
     )
 
     home = lax.ppermute(cols, "tile", turned(around))
     for k in range(share):
         held = held + jnp.where(home_row == k, home[k : k + 1] + swap_back[k : k + 1], 0.0)
-    held = held + lax.ppermute(leaving, "sub", [(i, i ^ 1) for i in range(subs)])
-    home, held = lax.optimization_barrier((home, held))
-    for bit, mine in enumerate(upper, 1):
-        pairs = held.reshape(-1, 2, width, BLOCK)
-        low, high = pairs[:, 0].reshape(mine.shape), pairs[:, 1].reshape(mine.shape)
-        leaving = jnp.where(mine > 0, low, high)
-        held = jnp.where(mine > 0, high, low)
-        held = held + lax.ppermute(leaving, "sub", [(i, i ^ (1 << bit)) for i in range(subs)])
-    scores = jnp.log(1.0 + held.reshape(-1))
+    parts = lax.all_to_all(held.reshape(subs, quarter), "sub", split_axis=0, concat_axis=0, tiled=True)
+    scores = jnp.log(1.0 + jnp.sum(parts, axis=0))
 
     flag = pl.pallas_call(
         functools.partial(flag_kernel, share),

time: 41.3 us -> 45.6 us (1.10)
  waiting for transfers between devices: 15.8 us -> 17.6 us
  starting transfers between devices: 13.2 us -> 14.9 us
  other arithmetic: 0.15 us -> 0.76 us
    all_to_all x0 -> x1, starting transfers between devices: none -> 3.25 us  [shards(): lax.all_to_all(held.reshape(subs, quarter), 'sub', split_axis=0, concat_a...]
    all_to_all x0 -> x1, waiting for transfers between devices: none -> 2.48 us  [shards(): lax.all_to_all(held.reshape(subs, quarter), 'sub', split_axis=0, concat_a...]
    ppermute x2 -> x0, starting transfers between devices: 1.56 us -> none  [the longest x1 1.56 us: shards(): lax.ppermute(leaving, 'sub', [(i, i ^ 1 << bit) for i in range(subs)])]
    ppermute x2 -> x0, waiting for transfers between devices: 0.8 us -> none  [the longest x1 0.8 us: shards(): lax.ppermute(leaving, 'sub', [(i, i ^ 1 << bit) for i in range(subs)])]
    add x1, other arithmetic: 0.01 us -> 0.6 us  [shards(): held + jnp.where(home_row == k, home[k:k + 1] + swap_back[k:k + 1], 0.0)]
  transfers between devices with their start and end apart: 8 -> 7, of which waited for: 4 -> 4; matrix products, arithmetic and copies ran while one was open for 1% -> 1% of each run, Pallas kernels for 22% -> 20%
where the time goes in v21:
time: 45.6 us; the launch traced here: 45.3 us
  waiting for transfers between devices  17.6 us (39%)
  starting transfers between devices  14.9 us (33%)
  Pallas kernels  10.2 us (22%)
  between operations  0.86 us (2%)
  local copies, waits for them, and re-layouts  0.81 us (2%)
  other arithmetic  0.76 us (2%)
    ppermute x1, waiting for transfers between devices, shards(): last = lax.ppermute(second_out, 'tile', around)  10.3 us
    pallas_call x1, Pallas kernels, shards(): pl.pallas_call(functools.partial(self_kernel, blocks, subs), in_specs=[sm...  6.27 us
    ppermute x1, starting transfers between devices, shards(): from_outer = lax.ppermute(first_out, 'tile', inward)  4.96 us
    all_to_all x1, starting transfers between devices, shards(): lax.all_to_all(held.reshape(subs, quarter), 'sub', split_axis=0, concat_a...  3.25 us
    ppermute x1, waiting for transfers between devices, shards(): from_outer = lax.ppermute(first_out, 'tile', inward)  2.98 us
    all_to_all x1, waiting for transfers between devices, shards(): lax.all_to_all(held.reshape(subs, quarter), 'sub', split_axis=0, concat_a...  2.48 us
    ppermute x1, starting transfers between devices, shards(): last = lax.ppermute(second_out, 'tile', around)  2.2 us
    pallas_call x3, Pallas kernels, call(): pl.pallas_call(kernel, in_specs=[smem] + [vmem] * len(operands), out_spec...  2.09 us
  transfers between devices with their start and end apart: 7, of which 4 were waited for; matrix products, arithmetic and copies ran while one was open for 1% of the time, Pallas kernels for 20%

profile of v21, /device:TPU:0, one launch (start us, length us, event | category | flops | bytes accessed | tf_op | source)
XLA Modules:
  0.0 45.3 jit_solution(10878205801302290248)
XLA Ops:
  0.0 0.0 copy-start.3
  0.0 1.2 %shard_map.30 = (bf16[264,1024]{1,0:T(8,128)(2,1)S(1)}, bf16[8,1024]{1,0:T(8,128)(2,1)S(1)}) custom-call(bf16[2048,1024]{1,0:T(8,128)(2,1)} %rows_ref.3, s32[16,128]{1,0:T(8,128)} %bitcast.49), custom_call_target="tpu_custom_call" | custom-call | bytes 1024 | tf_op jit(solution)/shard_map/pallas_call | solution.py:91
  1.2 5.0 %collective-permute-start.1 = (bf16[264,1024]{1,0:T(8,128)(2,1)S(1)}, bf16[264,1024]{1,0:T(8,128)(2,1)S(1)}, u32[]{:S(2)}, u32[]{:S(2)}) collective-permute-start(bf16[264,1024]{1,0:T(8,128)(2,1)S(1)} %get-tuple-element.38), channel_id=1, source_target_pairs={{0,4},{12,8},{1,5},{13,9},{2,6},{14,10},{3,7},{15,11},{16,20},{28,... | collective-permute-start | bytes 1622024 | tf_op jit(solution)/shard_map/ppermute | solution.py:301
  6.1 0.7 %collective-permute-start = (bf16[264,1024]{1,0:T(8,128)(2,1)S(1)}, bf16[264,1024]{1,0:T(8,128)(2,1)S(1)}, u32[]{:S(2)}, u32[]{:S(2)}) collective-permute-start(bf16[264,1024]{1,0:T(8,128)(2,1)S(1)} %get-tuple-element.38), channel_id=1, source_target_pairs={{4,8},{8,4},{5,9},{9,5},{6,10},{10,6},{7,11},{11,7},{20,24},{24,20... | collective-permute-start | bytes 1622024 | tf_op jit(solution)/shard_map/ppermute | solution.py:300
  6.9 0.0 copy-done.3
  6.9 0.1 convert_reduce_fusion
  7.1 0.1 dynamic_slice.47
  7.2 0.1 concatenate.3.meta_ref
  7.2 0.1 broadcast_in_dim.125
  7.3 6.3 %shard_map.31 = (bf16[2048,1024]{1,0:T(8,128)(2,1)S(1)}, f32[16,128]{1,0:T(8,128)S(1)}, bf16[264,1024]{1,0:T(8,128)(2,1)S(1)}) custom-call(s32[85]{0:T(128)S(1)} %concatenate.3.meta_ref, bf16[2048,1024]{1,0:T(8,128)(2,1)} %rows_ref.3, s32[1,512]{1,0:T(1,128)S(1)} %bitcast.48, bf16[8,1024]{1,0:T(8,128)(2,1)S(1)} %get-tuple-element.36.behind_ref), custom_call_target="tpu_custom_call" | custom-call | bytes 1024 | tf_op jit(solution)/shard_map/pallas_call | solution.py:318
  13.6 2.2 %collective-permute-start.2 = (bf16[264,1024]{1,0:T(8,128)(2,1)S(1)}, bf16[264,1024]{1,0:T(8,128)(2,1)S(1)}, u32[]{:S(2)}, u32[]{:S(2)}) collective-permute-start(bf16[264,1024]{1,0:T(8,128)(2,1)S(1)} %get-tuple-element.42), channel_id=1, source_target_pairs={{0,4},{12,8},{4,12},{8,0},{1,5},{13,9},{5,13},{9,1},{2,6},{14,10},... | collective-permute-start | bytes 1622024 | tf_op jit(solution)/shard_map/ppermute | solution.py:331
  15.8 3.0 %collective-permute-done.1.piece_ref = bf16[264,1024]{1,0:T(8,128)(2,1)S(1)} collective-permute-done((bf16[264,1024]{1,0:T(8,128)(2,1)S(1)}, bf16[264,1024]{1,0:T(8,128)(2,1)S(1)}, u32[]{:S(2)}, u32[]{:S(2)}) %collective-permute-start.1) | collective-permute-done | bytes 540704 | tf_op jit(solution)/shard_map/ppermute | solution.py:301
  18.8 0.7 %shard_map.32 = (f32[16,128]{1,0:T(8,128)S(1)}, f32[3,128]{1,0:T(4,128)S(1)}) custom-call(s32[85]{0:T(128)S(1)} %concatenate.3.meta_ref, bf16[2048,1024]{1,0:T(8,128)(2,1)S(1)} %get-tuple-element.37.unit_ref, bf16[264,1024]{1,0:T(8,128)(2,1)S(1)} %collective-permute-done.1.piece_ref, f32[16,128]{1,0:T(8,128)S(1)} %get-tuple-element.39.before_ref), custom_call_target="tpu_custom_call" | custom-call | flops 1073741824 | bytes 1024 | tf_op jit(solution)/shard_map/pallas_call | solution.py:227
  19.5 1.3 %collective-permute-start.3 = (f32[3,128]{1,0:T(4,128)S(1)}, f32[3,128]{1,0:T(4,128)S(1)}, u32[]{:S(2)}, u32[]{:S(2)}) collective-permute-start(f32[3,128]{1,0:T(4,128)S(1)} %get-tuple-element.44), channel_id=1, source_target_pairs={{4,0},{8,12},{5,1},{9,13},{6,2},{10,14},{7,3},{11,15},{20,16},{24,... | collective-permute-start | bytes 4616 | tf_op jit(solution)/shard_map/ppermute | solution.py:344
  20.8 0.0 collective-permute-done.piece_ref
  20.8 0.7 %shard_map.33 = (f32[16,128]{1,0:T(8,128)S(1)}, f32[3,128]{1,0:T(4,128)S(1)}) custom-call(s32[85]{0:T(128)S(1)} %concatenate.3.meta_ref, bf16[2048,1024]{1,0:T(8,128)(2,1)S(1)} %get-tuple-element.37.unit_ref, bf16[264,1024]{1,0:T(8,128)(2,1)S(1)} %collective-permute-done.piece_ref, f32[16,128]{1,0:T(8,128)S(1)} %get-tuple-element.40.before_ref), custom_call_target="tpu_custom_call" | custom-call | flops 1073741824 | bytes 1024 | tf_op jit(solution)/shard_map/pallas_call | solution.py:227
  21.5 0.7 %collective-permute-start.5 = (f32[3,128]{1,0:T(4,128)S(1)}, f32[3,128]{1,0:T(4,128)S(1)}, u32[]{:S(2)}, u32[]{:S(2)}) collective-permute-start(f32[3,128]{1,0:T(4,128)S(1)} %get-tuple-element.41.swap_cols_ref.here_ref), channel_id=1, source_target_pairs={{8,4},{4,8},{9,5},{5,9},{10,6},{6,10},{11,7},{7,11},{24,20},{20,24... | collective-permute-start | bytes 4616 | tf_op jit(solution)/shard_map/ppermute | solution.py:346
  22.2 10.3 %collective-permute-done.2.piece_ref = bf16[264,1024]{1,0:T(8,128)(2,1)S(1)} collective-permute-done((bf16[264,1024]{1,0:T(8,128)(2,1)S(1)}, bf16[264,1024]{1,0:T(8,128)(2,1)S(1)}, u32[]{:S(2)}, u32[]{:S(2)}) %collective-permute-start.2) | collective-permute-done | bytes 540704 | tf_op jit(solution)/shard_map/ppermute | solution.py:331
  32.5 0.0 collective-permute-done.3.outer_back_ref
  32.5 0.7 %shard_map.34 = (f32[16,128]{1,0:T(8,128)S(1)}, f32[3,128]{1,0:T(4,128)S(1)}) custom-call(s32[85]{0:T(128)S(1)} %concatenate.3.meta_ref, bf16[2048,1024]{1,0:T(8,128)(2,1)S(1)} %get-tuple-element.37.unit_ref, bf16[264,1024]{1,0:T(8,128)(2,1)S(1)} %collective-permute-done.2.piece_ref, f32[16,128]{1,0:T(8,128)S(1)} %get-tuple-element.43.before_ref, ...), custom_call_target="tpu_custom_call" | custom-call | bytes 1024 | tf_op jit(solution)/shard_map/pallas_call | solution.py:227
  33.2 1.9 %collective-permute-start.4 = (f32[3,128]{1,0:T(4,128)S(1)}, f32[3,128]{1,0:T(4,128)S(1)}, u32[]{:S(2)}, u32[]{:S(2)}) collective-permute-start(f32[3,128]{1,0:T(4,128)S(1)} %get-tuple-element.45), channel_id=1, source_target_pairs={{4,0},{8,12},{12,4},{0,8},{5,1},{9,13},{13,5},{1,9},{6,2},{10,14},... | collective-permute-start | bytes 4616 | tf_op jit(solution)/shard_map/ppermute | solution.py:356
  35.0 0.0 collective-permute-done.5
  35.0 1.8 %collective-permute-done.4.home_ref = f32[3,128]{1,0:T(4,128)S(1)} collective-permute-done((f32[3,128]{1,0:T(4,128)S(1)}, f32[3,128]{1,0:T(4,128)S(1)}, u32[]{:S(2)}, u32[]{:S(2)}) %collective-permute-start.4) | collective-permute-done | bytes 1568 | tf_op jit(solution)/shard_map/ppermute | solution.py:356
  36.8 0.6 %select_add_fusion = f32[16,128]{1,0:T(8,128)} fusion(f32[16,128]{1,0:T(8,128)S(1)} %get-tuple-element.46, s32[16,128]{1,0:T(8,128)S(1)} %broadcast_in_dim.125, f32[128]{0:T(128)S(1)} %get-tuple-element.60, f32[128]{0:T(128)S(1)} %get-tuple-element.59), kind=kLoop, calls=%fused_computation.55 | loop fusion | flops 12288 | bytes 25600 | tf_op jit(solution)/shard_map/add | solution.py:358
  37.4 3.2 %all-to-all-start.2 = ((f32[4,1,512]{2,1,0:T(1,128)}), f32[4,1,512]{2,1,0:T(1,128)S(1)}, u32[]{:S(2)}, u32[]{:S(2)}) async-start(f32[4,1,512]{2,1,0:T(1,128)} %bitcast.22), calls=%async_computation.2 | async-start | bytes 16384 | tf_op jit(solution)/shard_map/all_to_all | solution.py:359
  40.7 0.6 %shard_map.35 = s32[1]{0:T(128)} custom-call(f32[3,128]{1,0:T(4,128)S(1)} %get-tuple-element.41.swap_cols_ref.here_ref, f32[3,128]{1,0:T(4,128)S(1)} %collective-permute-done.4.home_ref), custom_call_target="tpu_custom_call" | custom-call | tf_op jit(solution)/shard_map/pallas_call | solution.py:362
  42.0 2.5 %all-to-all-done.2 = f32[4,1,512]{2,1,0:T(1,128)S(1)} async-done(((f32[4,1,512]{2,1,0:T(1,128)}), f32[4,1,512]{2,1,0:T(1,128)S(1)}, u32[]{:S(2)}, u32[]{:S(2)}) %all-to-all-start.2) | async-done | bytes 8224 | tf_op jit(solution)/shard_map/all_to_all | solution.py:359
  44.5 0.3 conditional.1
  44.7 0.0 copy-start.4
  44.7 0.6 %copy-done.4 = f32[512]{0:T(512)} copy-done((f32[512]{0:T(512)}, f32[512]{0:T(512)S(1)}, u32[]{:S(2)}) %copy-start.4) | copy-done | bytes 2072
  (5 shorter events, 0.0 us)
Async XLA Ops:
  0.0 6.9 %copy-start.3 = (s32[2048]{0:T(1024)S(1)}, s32[2048]{0:T(1024)}, u32[]{:S(2)}) copy-start(s32[2048]{0:T(1024)} %param.5) | copy-start | bytes 24580
  1.2 17.6 %collective-permute-start.1 = (bf16[264,1024]{1,0:T(8,128)(2,1)S(1)}, bf16[264,1024]{1,0:T(8,128)(2,1)S(1)}, u32[]{:S(2)}, u32[]{:S(2)}) collective-permute-start(bf16[264,1024]{1,0:T(8,128)(2,1)S(1)} %get-tuple-element.38), channel_id=1, source_target_pairs={{0,4},{12,8},{1,5},{13,9},{2,6},{14,10},{3,7},{15,11},{16,20},{28,... | collective-permute-start | bytes 1622024 | tf_op jit(solution)/shard_map/ppermute | solution.py:301
  6.1 14.6 %collective-permute-start = (bf16[264,1024]{1,0:T(8,128)(2,1)S(1)}, bf16[264,1024]{1,0:T(8,128)(2,1)S(1)}, u32[]{:S(2)}, u32[]{:S(2)}) collective-permute-start(bf16[264,1024]{1,0:T(8,128)(2,1)S(1)} %get-tuple-element.38), channel_id=1, source_target_pairs={{4,8},{8,4},{5,9},{9,5},{6,10},{10,6},{7,11},{11,7},{20,24},{24,20... | collective-permute-start | bytes 1622024 | tf_op jit(solution)/shard_map/ppermute | solution.py:300
  13.6 18.9 %collective-permute-start.2 = (bf16[264,1024]{1,0:T(8,128)(2,1)S(1)}, bf16[264,1024]{1,0:T(8,128)(2,1)S(1)}, u32[]{:S(2)}, u32[]{:S(2)}) collective-permute-start(bf16[264,1024]{1,0:T(8,128)(2,1)S(1)} %get-tuple-element.42), channel_id=1, source_target_pairs={{0,4},{12,8},{4,12},{8,0},{1,5},{13,9},{5,13},{9,1},{2,6},{14,10},... | collective-permute-start | bytes 1622024 | tf_op jit(solution)/shard_map/ppermute | solution.py:331
  19.5 13.0 %collective-permute-start.3 = (f32[3,128]{1,0:T(4,128)S(1)}, f32[3,128]{1,0:T(4,128)S(1)}, u32[]{:S(2)}, u32[]{:S(2)}) collective-permute-start(f32[3,128]{1,0:T(4,128)S(1)} %get-tuple-element.44), channel_id=1, source_target_pairs={{4,0},{8,12},{5,1},{9,13},{6,2},{10,14},{7,3},{11,15},{20,16},{24,... | collective-permute-start | bytes 4616 | tf_op jit(solution)/shard_map/ppermute | solution.py:344
  21.5 13.6 %collective-permute-start.5 = (f32[3,128]{1,0:T(4,128)S(1)}, f32[3,128]{1,0:T(4,128)S(1)}, u32[]{:S(2)}, u32[]{:S(2)}) collective-permute-start(f32[3,128]{1,0:T(4,128)S(1)} %get-tuple-element.41.swap_cols_ref.here_ref), channel_id=1, source_target_pairs={{8,4},{4,8},{9,5},{5,9},{10,6},{6,10},{11,7},{7,11},{24,20},{20,24... | collective-permute-start | bytes 4616 | tf_op jit(solution)/shard_map/ppermute | solution.py:346
  33.2 3.6 %collective-permute-start.4 = (f32[3,128]{1,0:T(4,128)S(1)}, f32[3,128]{1,0:T(4,128)S(1)}, u32[]{:S(2)}, u32[]{:S(2)}) collective-permute-start(f32[3,128]{1,0:T(4,128)S(1)} %get-tuple-element.45), channel_id=1, source_target_pairs={{4,0},{8,12},{12,4},{0,8},{5,1},{9,13},{13,5},{1,9},{6,2},{10,14},... | collective-permute-start | bytes 4616 | tf_op jit(solution)/shard_map/ppermute | solution.py:356
  37.4 7.0 %all-to-all-start.2 = ((f32[4,1,512]{2,1,0:T(1,128)}), f32[4,1,512]{2,1,0:T(1,128)S(1)}, u32[]{:S(2)}, u32[]{:S(2)}) async-start(f32[4,1,512]{2,1,0:T(1,128)} %bitcast.22), calls=%async_computation.2 | async-start | bytes 16384 | tf_op jit(solution)/shard_map/all_to_all | solution.py:359
  44.7 0.6 %copy-start.4 = (f32[512]{0:T(512)}, f32[512]{0:T(512)S(1)}, u32[]{:S(2)}) copy-start(f32[512]{0:T(512)S(1)} %get-tuple-element.78) | copy-start | bytes 6148

commit v22 on v19

--- a/solution.py
+++ b/solution.py
@@ -19,7 +19,7 @@
 OFF = -1000.0
 
 STEP = 512
-COPY = 64
+COPY = 128
 
 
 def normalised(values):
@@ -64,17 +64,18 @@
 def pack_kernel(blocks, subs, rows_ref, ids_ref, first_ref, behind_ref, ids, sems):
     plan = Plan(blocks, subs, lax.axis_index("tile"), lax.axis_index("sub"))
     share, size = plan.share, plan.share * BLOCK
-    copies = [pltpu.make_async_copy(ids_ref, ids, sems.at[0])]
+    copies = []
     for index, down in enumerate(range(0, size, COPY)):
         start = pl.multiple_of(plan.first * BLOCK + down, COPY)
         copies.append(
             pltpu.make_async_copy(
-                rows_ref.at[pl.ds(start, COPY), :], first_ref.at[pl.ds(down, COPY), :], sems.at[1 + index]
+                rows_ref.at[pl.ds(start, COPY), :], first_ref.at[pl.ds(down, COPY), :], sems.at[index]
             )
         )
+    copies.append(pltpu.make_async_copy(ids_ref, ids, sems.at[len(copies)]))
     for copy in copies:
         copy.start()
-    copies[0].wait()
+    copies[-1].wait()
     depth = first_ref.shape[1]
     edge = jnp.max(ids[pl.ds(plan.edge, 1), :], axis=1, keepdims=True)
     rest = [jnp.broadcast_to(edge, (1, BLOCK)), jnp.zeros((1, depth - size - BLOCK), jnp.int32)]
@@ -82,7 +83,7 @@
         row = jnp.concatenate([ids[pl.ds(block + k, 1), :] for k in range(share)] + rest, axis=1)
         row = jnp.broadcast_to(row.astype(jnp.float32), (8, depth)).astype(jnp.bfloat16)
         out[out.shape[0] - 8 :, :] = row
-    for copy in copies[1:]:
+    for copy in copies[:-1]:
         copy.wait()
 
 

time: 41.3 us -> 41.3 us (level)
  no operation moved by 1% of the time
where the time goes in v22:
time: 41.3 us; the launch traced here: 41 us
  waiting for transfers between devices  15.8 us (38%)
  starting transfers between devices  13.2 us (32%)
  Pallas kernels  10.1 us (24%)
  between operations  0.93 us (2%)
  local copies, waits for them, and re-layouts  0.81 us (2%)
    ppermute x1, waiting for transfers between devices, shards(): last = lax.ppermute(second_out, 'tile', around)  10.2 us
    pallas_call x1, Pallas kernels, shards(): pl.pallas_call(functools.partial(self_kernel, blocks, subs), in_specs=[sm...  6.26 us
    ppermute x1, starting transfers between devices, shards(): from_outer = lax.ppermute(first_out, 'tile', inward)  5.05 us
    ppermute x1, waiting for transfers between devices, shards(): from_outer = lax.ppermute(first_out, 'tile', inward)  3.03 us
    pallas_call x3, Pallas kernels, call(): pl.pallas_call(kernel, in_specs=[smem] + [vmem] * len(operands), out_spec...  2.12 us
    ppermute x1, starting transfers between devices, shards(): last = lax.ppermute(second_out, 'tile', around)  2.11 us
    ppermute x1, starting transfers between devices, shards(): home = lax.ppermute(cols, 'tile', turned(around))  1.87 us
    ppermute x1, waiting for transfers between devices, shards(): home = lax.ppermute(cols, 'tile', turned(around))  1.76 us
  transfers between devices with their start and end apart: 8, of which 4 were waited for; matrix products, arithmetic and copies ran while one was open for 1% of the time, Pallas kernels for 22%

profile of v22, /device:TPU:0, one launch (start us, length us, event | category | flops | bytes accessed | tf_op | source)
XLA Modules:
  0.0 41.0 jit_solution(8631581609498166130)
XLA Ops:
  0.0 0.0 copy-start.3
  0.0 1.1 %shard_map.30 = (bf16[264,1024]{1,0:T(8,128)(2,1)S(1)}, bf16[8,1024]{1,0:T(8,128)(2,1)S(1)}) custom-call(bf16[2048,1024]{1,0:T(8,128)(2,1)} %rows_ref.3, s32[16,128]{1,0:T(8,128)} %bitcast.59), custom_call_target="tpu_custom_call" | custom-call | bytes 1024 | tf_op jit(solution)/shard_map/pallas_call | solution.py:92
  1.1 5.0 %collective-permute-start.1 = (bf16[264,1024]{1,0:T(8,128)(2,1)S(1)}, bf16[264,1024]{1,0:T(8,128)(2,1)S(1)}, u32[]{:S(2)}, u32[]{:S(2)}) collective-permute-start(bf16[264,1024]{1,0:T(8,128)(2,1)S(1)} %get-tuple-element.54), channel_id=1, source_target_pairs={{0,4},{12,8},{1,5},{13,9},{2,6},{14,10},{3,7},{15,11},{16,20},{28,... | collective-permute-start | bytes 1622024 | tf_op jit(solution)/shard_map/ppermute | solution.py:312
  6.1 0.7 %collective-permute-start = (bf16[264,1024]{1,0:T(8,128)(2,1)S(1)}, bf16[264,1024]{1,0:T(8,128)(2,1)S(1)}, u32[]{:S(2)}, u32[]{:S(2)}) collective-permute-start(bf16[264,1024]{1,0:T(8,128)(2,1)S(1)} %get-tuple-element.54), channel_id=1, source_target_pairs={{4,8},{8,4},{5,9},{9,5},{6,10},{10,6},{7,11},{11,7},{20,24},{24,20... | collective-permute-start | bytes 1622024 | tf_op jit(solution)/shard_map/ppermute | solution.py:311
  6.8 0.0 copy-done.3
  6.9 0.1 convert_reduce_fusion
  7.1 0.1 dynamic_slice.47
  7.2 0.1 concatenate.3.meta_ref
  7.3 0.1 broadcast_in_dim.128
  7.4 6.3 %shard_map.31 = (bf16[2048,1024]{1,0:T(8,128)(2,1)S(1)}, f32[16,128]{1,0:T(8,128)S(1)}, bf16[264,1024]{1,0:T(8,128)(2,1)S(1)}) custom-call(s32[85]{0:T(128)S(1)} %concatenate.3.meta_ref, bf16[2048,1024]{1,0:T(8,128)(2,1)} %rows_ref.3, s32[1,512]{1,0:T(1,128)S(1)} %bitcast.58, bf16[8,1024]{1,0:T(8,128)(2,1)S(1)} %get-tuple-element.52.behind_ref), custom_call_target="tpu_custom_call" | custom-call | bytes 1024 | tf_op jit(solution)/shard_map/pallas_call | solution.py:335
  13.6 2.1 %collective-permute-start.2 = (bf16[264,1024]{1,0:T(8,128)(2,1)S(1)}, bf16[264,1024]{1,0:T(8,128)(2,1)S(1)}, u32[]{:S(2)}, u32[]{:S(2)}) collective-permute-start(bf16[264,1024]{1,0:T(8,128)(2,1)S(1)} %get-tuple-element.58), channel_id=1, source_target_pairs={{0,4},{12,8},{4,12},{8,0},{1,5},{13,9},{5,13},{9,1},{2,6},{14,10},... | collective-permute-start | bytes 1622024 | tf_op jit(solution)/shard_map/ppermute | solution.py:348
  15.7 3.0 %collective-permute-done.1.piece_ref = bf16[264,1024]{1,0:T(8,128)(2,1)S(1)} collective-permute-done((bf16[264,1024]{1,0:T(8,128)(2,1)S(1)}, bf16[264,1024]{1,0:T(8,128)(2,1)S(1)}, u32[]{:S(2)}, u32[]{:S(2)}) %collective-permute-start.1) | collective-permute-done | bytes 540704 | tf_op jit(solution)/shard_map/ppermute | solution.py:312
  18.8 0.7 %shard_map.32 = (f32[16,128]{1,0:T(8,128)S(1)}, f32[3,128]{1,0:T(4,128)S(1)}) custom-call(s32[85]{0:T(128)S(1)} %concatenate.3.meta_ref, bf16[2048,1024]{1,0:T(8,128)(2,1)S(1)} %get-tuple-element.53.unit_ref, bf16[264,1024]{1,0:T(8,128)(2,1)S(1)} %collective-permute-done.1.piece_ref, f32[16,128]{1,0:T(8,128)S(1)} %get-tuple-element.55.before_ref), custom_call_target="tpu_custom_call" | custom-call | flops 1073741824 | bytes 1024 | tf_op jit(solution)/shard_map/pallas_call | solution.py:238
  19.5 1.3 %collective-permute-start.3 = (f32[3,128]{1,0:T(4,128)S(1)}, f32[3,128]{1,0:T(4,128)S(1)}, u32[]{:S(2)}, u32[]{:S(2)}) collective-permute-start(f32[3,128]{1,0:T(4,128)S(1)} %get-tuple-element.60), channel_id=1, source_target_pairs={{4,0},{8,12},{5,1},{9,13},{6,2},{10,14},{7,3},{11,15},{20,16},{24,... | collective-permute-start | bytes 4616 | tf_op jit(solution)/shard_map/ppermute | solution.py:361
  20.8 0.0 collective-permute-done.piece_ref
  20.8 0.7 %shard_map.33 = (f32[16,128]{1,0:T(8,128)S(1)}, f32[3,128]{1,0:T(4,128)S(1)}) custom-call(s32[85]{0:T(128)S(1)} %concatenate.3.meta_ref, bf16[2048,1024]{1,0:T(8,128)(2,1)S(1)} %get-tuple-element.53.unit_ref, bf16[264,1024]{1,0:T(8,128)(2,1)S(1)} %collective-permute-done.piece_ref, f32[16,128]{1,0:T(8,128)S(1)} %get-tuple-element.56.before_ref), custom_call_target="tpu_custom_call" | custom-call | flops 1073741824 | bytes 1024 | tf_op jit(solution)/shard_map/pallas_call | solution.py:238
  21.5 0.7 %collective-permute-start.5 = (f32[3,128]{1,0:T(4,128)S(1)}, f32[3,128]{1,0:T(4,128)S(1)}, u32[]{:S(2)}, u32[]{:S(2)}) collective-permute-start(f32[3,128]{1,0:T(4,128)S(1)} %get-tuple-element.57.swap_cols_ref.here_ref), channel_id=1, source_target_pairs={{8,4},{4,8},{9,5},{5,9},{10,6},{6,10},{11,7},{7,11},{24,20},{20,24... | collective-permute-start | bytes 4616 | tf_op jit(solution)/shard_map/ppermute | solution.py:363
  22.2 10.2 %collective-permute-done.2.piece_ref = bf16[264,1024]{1,0:T(8,128)(2,1)S(1)} collective-permute-done((bf16[264,1024]{1,0:T(8,128)(2,1)S(1)}, bf16[264,1024]{1,0:T(8,128)(2,1)S(1)}, u32[]{:S(2)}, u32[]{:S(2)}) %collective-permute-start.2) | collective-permute-done | bytes 540704 | tf_op jit(solution)/shard_map/ppermute | solution.py:348
  32.4 0.0 collective-permute-done.3.outer_back_ref
  32.4 0.7 %shard_map.34 = (f32[8,128]{1,0:T(8,128)S(1)}, f32[8,128]{1,0:T(8,128)S(1)}, f32[3,128]{1,0:T(4,128)S(1)}) custom-call(s32[85]{0:T(128)S(1)} %concatenate.3.meta_ref, bf16[2048,1024]{1,0:T(8,128)(2,1)S(1)} %get-tuple-element.53.unit_ref, bf16[264,1024]{1,0:T(8,128)(2,1)S(1)} %collective-permute-done.2.piece_ref, f32[16,128]{1,0:T(8,128)S(1)} %get-tuple-element.59.before_ref, ...), custom_call_target="tpu_custom_call" | custom-call | flops 1073741824 | bytes 1024 | tf_op jit(solution)/shard_map/pallas_call | solution.py:238
  33.1 1.9 %collective-permute-start.4 = (f32[3,128]{1,0:T(4,128)S(1)}, f32[3,128]{1,0:T(4,128)S(1)}, u32[]{:S(2)}, u32[]{:S(2)}) collective-permute-start(f32[3,128]{1,0:T(4,128)S(1)} %get-tuple-element.61), channel_id=1, source_target_pairs={{4,0},{8,12},{12,4},{0,8},{5,1},{9,13},{13,5},{1,9},{6,2},{10,14},... | collective-permute-start | bytes 4616 | tf_op jit(solution)/shard_map/ppermute | solution.py:377
  35.0 0.0 collective-permute-start.6
  35.0 0.0 collective-permute-done.5
  35.0 1.8 %collective-permute-done.4.home_ref = f32[3,128]{1,0:T(4,128)S(1)} collective-permute-done((f32[3,128]{1,0:T(4,128)S(1)}, f32[3,128]{1,0:T(4,128)S(1)}, u32[]{:S(2)}, u32[]{:S(2)}) %collective-permute-start.4) | collective-permute-done | bytes 1568 | tf_op jit(solution)/shard_map/ppermute | solution.py:377
  36.8 0.0 collective-permute-done.6
  36.8 1.6 %collective-permute-start.7 = (f32[4,128]{1,0:T(4,128)S(1)}, f32[4,128]{1,0:T(4,128)S(1)}, u32[]{:S(2)}, u32[]{:S(2)}) collective-permute-start(f32[4,128]{1,0:T(4,128)S(1)} %get-tuple-element.71), channel_id=1, source_target_pairs={{0,2},{1,3},{2,0},{3,1},{4,6},{5,7},{6,4},{7,5},{8,10},{9,11},{10,... | collective-permute-start | bytes 6152 | tf_op jit(solution)/shard_map/ppermute | solution.py:387
  38.3 0.6 %shard_map.35 = s32[1]{0:T(128)} custom-call(f32[3,128]{1,0:T(4,128)S(1)} %get-tuple-element.57.swap_cols_ref.here_ref, f32[3,128]{1,0:T(4,128)S(1)} %collective-permute-done.4.home_ref), custom_call_target="tpu_custom_call" | custom-call | tf_op jit(solution)/shard_map/pallas_call | solution.py:390
  39.6 0.8 %collective-permute-done.7 = f32[4,128]{1,0:T(4,128)S(1)} collective-permute-done((f32[4,128]{1,0:T(4,128)S(1)}, f32[4,128]{1,0:T(4,128)S(1)}, u32[]{:S(2)}, u32[]{:S(2)}) %collective-permute-start.7) | collective-permute-done | bytes 2080 | tf_op jit(solution)/shard_map/ppermute | solution.py:387
  40.4 0.0 copy-start.4
  40.5 0.6 %copy-done.4 = f32[512]{0:T(512)} copy-done((f32[512]{0:T(512)}, f32[512]{0:T(512)S(1)}, u32[]{:S(2)}) %copy-start.4) | copy-done | bytes 2072
  (9 shorter events, 0.0 us)
Async XLA Ops:
  0.0 6.8 %copy-start.3 = (s32[2048]{0:T(1024)S(1)}, s32[2048]{0:T(1024)}, u32[]{:S(2)}) copy-start(s32[2048]{0:T(1024)} %param.5) | copy-start | bytes 24580
  1.1 17.7 %collective-permute-start.1 = (bf16[264,1024]{1,0:T(8,128)(2,1)S(1)}, bf16[264,1024]{1,0:T(8,128)(2,1)S(1)}, u32[]{:S(2)}, u32[]{:S(2)}) collective-permute-start(bf16[264,1024]{1,0:T(8,128)(2,1)S(1)} %get-tuple-element.54), channel_id=1, source_target_pairs={{0,4},{12,8},{1,5},{13,9},{2,6},{14,10},{3,7},{15,11},{16,20},{28,... | collective-permute-start | bytes 1622024 | tf_op jit(solution)/shard_map/ppermute | solution.py:312
  6.1 14.6 %collective-permute-start = (bf16[264,1024]{1,0:T(8,128)(2,1)S(1)}, bf16[264,1024]{1,0:T(8,128)(2,1)S(1)}, u32[]{:S(2)}, u32[]{:S(2)}) collective-permute-start(bf16[264,1024]{1,0:T(8,128)(2,1)S(1)} %get-tuple-element.54), channel_id=1, source_target_pairs={{4,8},{8,4},{5,9},{9,5},{6,10},{10,6},{7,11},{11,7},{20,24},{24,20... | collective-permute-start | bytes 1622024 | tf_op jit(solution)/shard_map/ppermute | solution.py:311
  13.6 18.7 %collective-permute-start.2 = (bf16[264,1024]{1,0:T(8,128)(2,1)S(1)}, bf16[264,1024]{1,0:T(8,128)(2,1)S(1)}, u32[]{:S(2)}, u32[]{:S(2)}) collective-permute-start(bf16[264,1024]{1,0:T(8,128)(2,1)S(1)} %get-tuple-element.58), channel_id=1, source_target_pairs={{0,4},{12,8},{4,12},{8,0},{1,5},{13,9},{5,13},{9,1},{2,6},{14,10},... | collective-permute-start | bytes 1622024 | tf_op jit(solution)/shard_map/ppermute | solution.py:348
  19.5 12.9 %collective-permute-start.3 = (f32[3,128]{1,0:T(4,128)S(1)}, f32[3,128]{1,0:T(4,128)S(1)}, u32[]{:S(2)}, u32[]{:S(2)}) collective-permute-start(f32[3,128]{1,0:T(4,128)S(1)} %get-tuple-element.60), channel_id=1, source_target_pairs={{4,0},{8,12},{5,1},{9,13},{6,2},{10,14},{7,3},{11,15},{20,16},{24,... | collective-permute-start | bytes 4616 | tf_op jit(solution)/shard_map/ppermute | solution.py:361
  21.5 13.5 %collective-permute-start.5 = (f32[3,128]{1,0:T(4,128)S(1)}, f32[3,128]{1,0:T(4,128)S(1)}, u32[]{:S(2)}, u32[]{:S(2)}) collective-permute-start(f32[3,128]{1,0:T(4,128)S(1)} %get-tuple-element.57.swap_cols_ref.here_ref), channel_id=1, source_target_pairs={{8,4},{4,8},{9,5},{5,9},{10,6},{6,10},{11,7},{7,11},{24,20},{20,24... | collective-permute-start | bytes 4616 | tf_op jit(solution)/shard_map/ppermute | solution.py:363
  33.1 3.6 %collective-permute-start.4 = (f32[3,128]{1,0:T(4,128)S(1)}, f32[3,128]{1,0:T(4,128)S(1)}, u32[]{:S(2)}, u32[]{:S(2)}) collective-permute-start(f32[3,128]{1,0:T(4,128)S(1)} %get-tuple-element.61), channel_id=1, source_target_pairs={{4,0},{8,12},{12,4},{0,8},{5,1},{9,13},{13,5},{1,9},{6,2},{10,14},... | collective-permute-start | bytes 4616 | tf_op jit(solution)/shard_map/ppermute | solution.py:377
  35.0 1.8 %collective-permute-start.6 = (f32[8,128]{1,0:T(8,128)S(1)}, f32[8,128]{1,0:T(8,128)S(1)}, u32[]{:S(2)}, u32[]{:S(2)}) collective-permute-start(f32[8,128]{1,0:T(8,128)S(1)} %get-tuple-element.64), channel_id=1, source_target_pairs={{0,1},{1,0},{2,3},{3,2},{4,5},{5,4},{6,7},{7,6},{8,9},{9,8},{10,11... | collective-permute-start | bytes 12296 | tf_op jit(solution)/shard_map/ppermute | solution.py:380
  36.8 3.7 %collective-permute-start.7 = (f32[4,128]{1,0:T(4,128)S(1)}, f32[4,128]{1,0:T(4,128)S(1)}, u32[]{:S(2)}, u32[]{:S(2)}) collective-permute-start(f32[4,128]{1,0:T(4,128)S(1)} %get-tuple-element.71), channel_id=1, source_target_pairs={{0,2},{1,3},{2,0},{3,1},{4,6},{5,7},{6,4},{7,5},{8,10},{9,11},{10,... | collective-permute-start | bytes 6152 | tf_op jit(solution)/shard_map/ppermute | solution.py:387
  40.4 0.6 %copy-start.4 = (f32[512]{0:T(512)}, f32[512]{0:T(512)S(1)}, u32[]{:S(2)}) copy-start(f32[512]{0:T(512)S(1)} %get-tuple-element.105) | copy-start | bytes 6148

commit v23 on v22

--- a/solution.py
+++ b/solution.py
@@ -205,7 +205,7 @@
 
 
 def last_kernel(
-    blocks, share, width, meta_ref, unit_ref, piece_ref, before_ref, outer_back_ref, swap_cols_ref,
+    blocks, share, width, meta_ref, unit_ref, piece_ref, before_ref, outer_cols_ref, swap_cols_ref,
     keep_ref, send_ref, cols_ref, sums, columns,
 ):
     meta = Meta(meta_ref, blocks)
@@ -215,13 +215,14 @@
         owner = block // width
         return owner % 2 * (blocks // 2) + owner // 2 * width + block % width
 
+    is_inner = meta.number(INNER) > 0
     cross_terms(meta, 2, tags, unit_ref, piece_ref, before_ref, sums, columns, place)
     total = jnp.sum(columns[...], axis=0, keepdims=True)
     for k in range(share):
-        cols_ref[k : k + 1, :] = total[:, k * BLOCK : (k + 1) * BLOCK]
-        at = place(meta.number(FIRST_BLOCK) + k)
-        sums[pl.ds(at, 1), :] += outer_back_ref[k : k + 1, :]
-    cols_ref[share : share + 1, :] = swap_cols_ref[share : share + 1, :]
+        value = total[:, k * BLOCK : (k + 1) * BLOCK]
+        cols_ref[k : k + 1, :] = jnp.where(is_inner, outer_cols_ref[k : k + 1, :], value)
+        cols_ref[share + k : share + k + 1, :] = jnp.where(is_inner, value, 0.0)
+    cols_ref[2 * share : 2 * share + 1, :] = swap_cols_ref[share : share + 1, :]
     parity = meta.number(MEMBER) % 2
     heap = blocks // 2
     keep_ref[...] = sums[pl.ds(pl.multiple_of(parity * heap, heap), heap), :]
@@ -229,7 +230,7 @@
 
 
 def flag_kernel(share, here_ref, home_ref, flag_ref):
-    flags = jnp.maximum(here_ref[share : share + 1, :], home_ref[share : share + 1, :])
+    flags = jnp.maximum(here_ref[share : share + 1, :], home_ref[2 * share : 2 * share + 1, :])
     flag_ref[0] = jnp.max(flags).astype(jnp.int32)
 
 
@@ -319,8 +320,8 @@
     meta = jnp.concatenate([tag, used, seen, swapped, tag, numbers]).astype(jnp.int32)
 
     heap = blocks // 2
-    owner = plan.second // width
-    home_row = jnp.arange(heap)[:, None] - (owner // 2 * width + plan.second % width)
+    owner = plan.first // width
+    home_row = jnp.arange(heap)[:, None] - (owner // 2 * width + plan.first % width)
     home_row = jnp.broadcast_to(home_row, (heap, BLOCK)).astype(jnp.int32)
     upper = [
         jnp.broadcast_to((member >> bit) & 1, (heap >> bit, BLOCK)).astype(jnp.int32)
@@ -358,15 +359,14 @@
         )
 
     sums, outer_cols = middle(0, from_outer, sums)
-    outer_back = lax.ppermute(outer_cols, "tile", turned(inward))
     sums, swap_cols = middle(1, from_inner, sums)
     swap_back = lax.ppermute(swap_cols, "tile", turned(swap))
     half = jax.ShapeDtypeStruct((heap, BLOCK), jnp.float32)
     held, leaving, cols = call(
         functools.partial(last_kernel, blocks, share, width),
         meta,
-        (unit, last, sums, outer_back, swap_cols),
-        [half, half, col_sums],
+        (unit, last, sums, outer_cols, swap_cols),
+        [half, half, jax.ShapeDtypeStruct((2 * share + 1, BLOCK), jnp.float32)],
         [
             pltpu.VMEM((blocks, BLOCK), jnp.float32),
             pltpu.VMEM((8, size), jnp.float32),
@@ -375,8 +375,9 @@
     )
 
     home = lax.ppermute(cols, "tile", turned(around))
-    for k in range(share):
-        held = held + jnp.where(home_row == k, home[k : k + 1] + swap_back[k : k + 1], 0.0)
+    for k in range(2 * share):
+        came = home[k : k + 1] + swap_back[k : k + 1] if k < share else home[k : k + 1]
+        held = held + jnp.where(home_row == k, came, 0.0)
     held = held + lax.ppermute(leaving, "sub", [(i, i ^ 1) for i in range(subs)])
     home, held = lax.optimization_barrier((home, held))
     for bit, mine in enumerate(upper, 1):

time: 41.3 us -> 43.7 us (1.058)
  the two profiles are of different devices: /device:TPU:0 before, /device:TPU:16 now
where the time goes in v23:
time: 43.7 us; the launch traced here: 43.4 us
  waiting for transfers between devices  15.4 us (35%)
  Pallas kernels  15.1 us (35%)
  starting transfers between devices  11 us (25%)
  between operations  0.94 us (2%)
  local copies, waits for them, and re-layouts  0.81 us (2%)
    pallas_call x3, Pallas kernels, call(): pl.pallas_call(kernel, in_specs=[smem] + [vmem] * len(operands), out_spec...  7.09 us
    pallas_call x1, Pallas kernels, shards(): pl.pallas_call(functools.partial(self_kernel, blocks, subs), in_specs=[sm...  6.27 us
    ppermute x1, waiting for transfers between devices, shards(): last = lax.ppermute(second_out, 'tile', around)  5.6 us
    ppermute x1, waiting for transfers between devices, shards(): from_outer = lax.ppermute(first_out, 'tile', inward)  5.56 us
    ppermute x1, waiting for transfers between devices, shards(): swap_back = lax.ppermute(swap_cols, 'tile', turned(swap))  3.47 us
    ppermute x1, starting transfers between devices, shards(): home = lax.ppermute(cols, 'tile', turned(around))  2.82 us
    ppermute x1, starting transfers between devices, shards(): from_inner = lax.ppermute(first_out, 'tile', swap)  2.44 us
    ppermute x1, starting transfers between devices, shards(): swap_back = lax.ppermute(swap_cols, 'tile', turned(swap))  1.91 us
  transfers between devices with their start and end apart: 7, of which 4 were waited for; matrix products, arithmetic and copies ran while one was open for 1% of the time, Pallas kernels for 27%

profile of v23, /device:TPU:16, one launch (start us, length us, event | category | flops | bytes accessed | tf_op | source)
XLA Modules:
  0.0 43.4 jit_solution(1447391324988383821)
XLA Ops:
  0.0 0.0 copy-start.3
  0.0 1.1 %shard_map.30 = (bf16[264,1024]{1,0:T(8,128)(2,1)S(1)}, bf16[8,1024]{1,0:T(8,128)(2,1)S(1)}) custom-call(bf16[2048,1024]{1,0:T(8,128)(2,1)} %rows_ref.3, s32[16,128]{1,0:T(8,128)} %bitcast.63), custom_call_target="tpu_custom_call" | custom-call | bytes 1024 | tf_op jit(solution)/shard_map/pallas_call | solution.py:92
  1.1 1.3 %collective-permute-start.1 = (bf16[264,1024]{1,0:T(8,128)(2,1)S(1)}, bf16[264,1024]{1,0:T(8,128)(2,1)S(1)}, u32[]{:S(2)}, u32[]{:S(2)}) collective-permute-start(bf16[264,1024]{1,0:T(8,128)(2,1)S(1)} %get-tuple-element.54), channel_id=1, source_target_pairs={{0,4},{12,8},{1,5},{13,9},{2,6},{14,10},{3,7},{15,11},{16,20},{28,... | collective-permute-start | bytes 1622024 | tf_op jit(solution)/shard_map/ppermute | solution.py:313
  2.4 2.4 %collective-permute-start = (bf16[264,1024]{1,0:T(8,128)(2,1)S(1)}, bf16[264,1024]{1,0:T(8,128)(2,1)S(1)}, u32[]{:S(2)}, u32[]{:S(2)}) collective-permute-start(bf16[264,1024]{1,0:T(8,128)(2,1)S(1)} %get-tuple-element.54), channel_id=1, source_target_pairs={{4,8},{8,4},{5,9},{9,5},{6,10},{10,6},{7,11},{11,7},{20,24},{24,20... | collective-permute-start | bytes 1622024 | tf_op jit(solution)/shard_map/ppermute | solution.py:312
  4.8 0.0 copy-done.3
  4.9 0.1 convert_reduce_fusion
  5.1 0.1 dynamic_slice.47
  5.2 0.1 concatenate.3.meta_ref
  5.3 0.1 broadcast_in_dim.144
  5.4 6.3 %shard_map.31 = (bf16[2048,1024]{1,0:T(8,128)(2,1)S(1)}, f32[16,128]{1,0:T(8,128)S(1)}, bf16[264,1024]{1,0:T(8,128)(2,1)S(1)}) custom-call(s32[85]{0:T(128)S(1)} %concatenate.3.meta_ref, bf16[2048,1024]{1,0:T(8,128)(2,1)} %rows_ref.3, s32[1,512]{1,0:T(1,128)S(1)} %bitcast.62, bf16[8,1024]{1,0:T(8,128)(2,1)S(1)} %get-tuple-element.52.behind_ref), custom_call_target="tpu_custom_call" | custom-call | bytes 1024 | tf_op jit(solution)/shard_map/pallas_call | solution.py:336
  11.6 0.9 %collective-permute-start.2 = (bf16[264,1024]{1,0:T(8,128)(2,1)S(1)}, bf16[264,1024]{1,0:T(8,128)(2,1)S(1)}, u32[]{:S(2)}, u32[]{:S(2)}) collective-permute-start(bf16[264,1024]{1,0:T(8,128)(2,1)S(1)} %get-tuple-element.58), channel_id=1, source_target_pairs={{0,4},{12,8},{4,12},{8,0},{1,5},{13,9},{5,13},{9,1},{2,6},{14,10},... | collective-permute-start | bytes 1622024 | tf_op jit(solution)/shard_map/ppermute | solution.py:349
  12.6 5.6 %collective-permute-done.1.piece_ref = bf16[264,1024]{1,0:T(8,128)(2,1)S(1)} collective-permute-done((bf16[264,1024]{1,0:T(8,128)(2,1)S(1)}, bf16[264,1024]{1,0:T(8,128)(2,1)S(1)}, u32[]{:S(2)}, u32[]{:S(2)}) %collective-permute-start.1) | collective-permute-done | bytes 540704 | tf_op jit(solution)/shard_map/ppermute | solution.py:313
  18.1 2.4 %shard_map.32 = (f32[16,128]{1,0:T(8,128)S(1)}, f32[3,128]{1,0:T(4,128)S(1)}) custom-call(s32[85]{0:T(128)S(1)} %concatenate.3.meta_ref, bf16[2048,1024]{1,0:T(8,128)(2,1)S(1)} %get-tuple-element.53.unit_ref, bf16[264,1024]{1,0:T(8,128)(2,1)S(1)} %collective-permute-done.1.piece_ref, f32[16,128]{1,0:T(8,128)S(1)} %get-tuple-element.55.before_ref), custom_call_target="tpu_custom_call" | custom-call | flops 1073741824 | bytes 1024 | tf_op jit(solution)/shard_map/pallas_call | solution.py:239
  20.5 0.0 collective-permute-done.piece_ref
  20.6 2.4 %shard_map.33 = (f32[16,128]{1,0:T(8,128)S(1)}, f32[3,128]{1,0:T(4,128)S(1)}) custom-call(s32[85]{0:T(128)S(1)} %concatenate.3.meta_ref, bf16[2048,1024]{1,0:T(8,128)(2,1)S(1)} %get-tuple-element.53.unit_ref, bf16[264,1024]{1,0:T(8,128)(2,1)S(1)} %collective-permute-done.piece_ref, f32[16,128]{1,0:T(8,128)S(1)} %get-tuple-element.56.before_ref), custom_call_target="tpu_custom_call" | custom-call | flops 1073741824 | bytes 1024 | tf_op jit(solution)/shard_map/pallas_call | solution.py:239
  23.0 5.6 %collective-permute-done.2.piece_ref = bf16[264,1024]{1,0:T(8,128)(2,1)S(1)} collective-permute-done((bf16[264,1024]{1,0:T(8,128)(2,1)S(1)}, bf16[264,1024]{1,0:T(8,128)(2,1)S(1)}, u32[]{:S(2)}, u32[]{:S(2)}) %collective-permute-start.2) | collective-permute-done | bytes 540704 | tf_op jit(solution)/shard_map/ppermute | solution.py:349
  28.6 2.3 %shard_map.34 = (f32[8,128]{1,0:T(8,128)S(1)}, f32[8,128]{1,0:T(8,128)S(1)}, f32[5,128]{1,0:T(8,128)S(1)}) custom-call(s32[85]{0:T(128)S(1)} %concatenate.3.meta_ref, bf16[2048,1024]{1,0:T(8,128)(2,1)S(1)} %get-tuple-element.53.unit_ref, bf16[264,1024]{1,0:T(8,128)(2,1)S(1)} %collective-permute-done.2.piece_ref, f32[16,128]{1,0:T(8,128)S(1)} %get-tuple-element.59.before_ref, ...), custom_call_target="tpu_custom_call" | custom-call | flops 1073741824 | bytes 1024 | tf_op jit(solution)/shard_map/pallas_call | solution.py:239
  30.9 2.8 %collective-permute-start.3 = (f32[5,128]{1,0:T(8,128)S(1)}, f32[5,128]{1,0:T(8,128)S(1)}, u32[]{:S(2)}, u32[]{:S(2)}) collective-permute-start(f32[5,128]{1,0:T(8,128)S(1)} %get-tuple-element.61), channel_id=1, source_target_pairs={{4,0},{8,12},{12,4},{0,8},{5,1},{9,13},{13,5},{1,9},{6,2},{10,14},... | collective-permute-start | bytes 7688 | tf_op jit(solution)/shard_map/ppermute | solution.py:377
  33.7 1.9 %collective-permute-start.4 = (f32[3,128]{1,0:T(4,128)S(1)}, f32[3,128]{1,0:T(4,128)S(1)}, u32[]{:S(2)}, u32[]{:S(2)}) collective-permute-start(f32[3,128]{1,0:T(4,128)S(1)} %get-tuple-element.57.swap_cols_ref.here_ref), channel_id=1, source_target_pairs={{8,4},{4,8},{9,5},{5,9},{10,6},{6,10},{11,7},{7,11},{24,20},{20,24... | collective-permute-start | bytes 4616 | tf_op jit(solution)/shard_map/ppermute | solution.py:363
  35.6 0.1 collective-permute-start.5
  35.7 3.5 %collective-permute-done.4 = f32[3,128]{1,0:T(4,128)S(1)} collective-permute-done((f32[3,128]{1,0:T(4,128)S(1)}, f32[3,128]{1,0:T(4,128)S(1)}, u32[]{:S(2)}, u32[]{:S(2)}) %collective-permute-start.4) | collective-permute-done | bytes 1568 | tf_op jit(solution)/shard_map/ppermute | solution.py:363
  39.1 0.0 collective-permute-done.3.home_ref
  39.2 0.0 collective-permute-done.5
  39.2 1.5 %collective-permute-start.6 = (f32[4,128]{1,0:T(4,128)S(1)}, f32[4,128]{1,0:T(4,128)S(1)}, u32[]{:S(2)}, u32[]{:S(2)}) collective-permute-start(f32[4,128]{1,0:T(4,128)S(1)} %get-tuple-element.71), channel_id=1, source_target_pairs={{0,2},{1,3},{2,0},{3,1},{4,6},{5,7},{6,4},{7,5},{8,10},{9,11},{10,... | collective-permute-start | bytes 6152 | tf_op jit(solution)/shard_map/ppermute | solution.py:388
  40.7 0.6 %shard_map.35 = s32[1]{0:T(128)} custom-call(f32[3,128]{1,0:T(4,128)S(1)} %get-tuple-element.57.swap_cols_ref.here_ref, f32[5,128]{1,0:T(8,128)S(1)} %collective-permute-done.3.home_ref), custom_call_target="tpu_custom_call" | custom-call | tf_op jit(solution)/shard_map/pallas_call | solution.py:391
  42.0 0.8 %collective-permute-done.6 = f32[4,128]{1,0:T(4,128)S(1)} collective-permute-done((f32[4,128]{1,0:T(4,128)S(1)}, f32[4,128]{1,0:T(4,128)S(1)}, u32[]{:S(2)}, u32[]{:S(2)}) %collective-permute-start.6) | collective-permute-done | bytes 2080 | tf_op jit(solution)/shard_map/ppermute | solution.py:388
  42.9 0.0 copy-start.4
  42.9 0.6 %copy-done.4 = f32[512]{0:T(512)} copy-done((f32[512]{0:T(512)}, f32[512]{0:T(512)S(1)}, u32[]{:S(2)}) %copy-start.4) | copy-done | bytes 2072
  (9 shorter events, 0.1 us)
Async XLA Ops:
  0.0 4.8 %copy-start.3 = (s32[2048]{0:T(1024)S(1)}, s32[2048]{0:T(1024)}, u32[]{:S(2)}) copy-start(s32[2048]{0:T(1024)} %param.5) | copy-start | bytes 24580
  1.1 17.1 %collective-permute-start.1 = (bf16[264,1024]{1,0:T(8,128)(2,1)S(1)}, bf16[264,1024]{1,0:T(8,128)(2,1)S(1)}, u32[]{:S(2)}, u32[]{:S(2)}) collective-permute-start(bf16[264,1024]{1,0:T(8,128)(2,1)S(1)} %get-tuple-element.54), channel_id=1, source_target_pairs={{0,4},{12,8},{1,5},{13,9},{2,6},{14,10},{3,7},{15,11},{16,20},{28,... | collective-permute-start | bytes 1622024 | tf_op jit(solution)/shard_map/ppermute | solution.py:313
  2.4 18.2 %collective-permute-start = (bf16[264,1024]{1,0:T(8,128)(2,1)S(1)}, bf16[264,1024]{1,0:T(8,128)(2,1)S(1)}, u32[]{:S(2)}, u32[]{:S(2)}) collective-permute-start(bf16[264,1024]{1,0:T(8,128)(2,1)S(1)} %get-tuple-element.54), channel_id=1, source_target_pairs={{4,8},{8,4},{5,9},{9,5},{6,10},{10,6},{7,11},{11,7},{20,24},{24,20... | collective-permute-start | bytes 1622024 | tf_op jit(solution)/shard_map/ppermute | solution.py:312
  11.6 16.9 %collective-permute-start.2 = (bf16[264,1024]{1,0:T(8,128)(2,1)S(1)}, bf16[264,1024]{1,0:T(8,128)(2,1)S(1)}, u32[]{:S(2)}, u32[]{:S(2)}) collective-permute-start(bf16[264,1024]{1,0:T(8,128)(2,1)S(1)} %get-tuple-element.58), channel_id=1, source_target_pairs={{0,4},{12,8},{4,12},{8,0},{1,5},{13,9},{5,13},{9,1},{2,6},{14,10},... | collective-permute-start | bytes 1622024 | tf_op jit(solution)/shard_map/ppermute | solution.py:349
  30.9 8.3 %collective-permute-start.3 = (f32[5,128]{1,0:T(8,128)S(1)}, f32[5,128]{1,0:T(8,128)S(1)}, u32[]{:S(2)}, u32[]{:S(2)}) collective-permute-start(f32[5,128]{1,0:T(8,128)S(1)} %get-tuple-element.61), channel_id=1, source_target_pairs={{4,0},{8,12},{12,4},{0,8},{5,1},{9,13},{13,5},{1,9},{6,2},{10,14},... | collective-permute-start | bytes 7688 | tf_op jit(solution)/shard_map/ppermute | solution.py:377
  33.7 5.5 %collective-permute-start.4 = (f32[3,128]{1,0:T(4,128)S(1)}, f32[3,128]{1,0:T(4,128)S(1)}, u32[]{:S(2)}, u32[]{:S(2)}) collective-permute-start(f32[3,128]{1,0:T(4,128)S(1)} %get-tuple-element.57.swap_cols_ref.here_ref), channel_id=1, source_target_pairs={{8,4},{4,8},{9,5},{5,9},{10,6},{6,10},{11,7},{7,11},{24,20},{20,24... | collective-permute-start | bytes 4616 | tf_op jit(solution)/shard_map/ppermute | solution.py:363
  35.6 3.6 %collective-permute-start.5 = (f32[8,128]{1,0:T(8,128)S(1)}, f32[8,128]{1,0:T(8,128)S(1)}, u32[]{:S(2)}, u32[]{:S(2)}) collective-permute-start(f32[8,128]{1,0:T(8,128)S(1)} %get-tuple-element.64), channel_id=1, source_target_pairs={{0,1},{1,0},{2,3},{3,2},{4,5},{5,4},{6,7},{7,6},{8,9},{9,8},{10,11... | collective-permute-start | bytes 12296 | tf_op jit(solution)/shard_map/ppermute | solution.py:381
  39.2 3.7 %collective-permute-start.6 = (f32[4,128]{1,0:T(4,128)S(1)}, f32[4,128]{1,0:T(4,128)S(1)}, u32[]{:S(2)}, u32[]{:S(2)}) collective-permute-start(f32[4,128]{1,0:T(4,128)S(1)} %get-tuple-element.71), channel_id=1, source_target_pairs={{0,2},{1,3},{2,0},{3,1},{4,6},{5,7},{6,4},{7,5},{8,10},{9,11},{10,... | collective-permute-start | bytes 6152 | tf_op jit(solution)/shard_map/ppermute | solution.py:388
  42.9 0.6 %copy-start.4 = (f32[512]{0:T(512)}, f32[512]{0:T(512)S(1)}, u32[]{:S(2)}) copy-start(f32[512]{0:T(512)S(1)} %get-tuple-element.105) | copy-start | bytes 6148

commit v24 on v23

--- a/solution.py
+++ b/solution.py
@@ -361,6 +361,7 @@
     sums, outer_cols = middle(0, from_outer, sums)
     sums, swap_cols = middle(1, from_inner, sums)
     swap_back = lax.ppermute(swap_cols, "tile", turned(swap))
+    swap_back, sums = lax.optimization_barrier((swap_back, sums))
     half = jax.ShapeDtypeStruct((heap, BLOCK), jnp.float32)
     held, leaving, cols = call(
         functools.partial(last_kernel, blocks, share, width),

time: 43.7 us -> 42.1 us (0.963)
  the two profiles are of different devices: /device:TPU:16 before, /device:TPU:0 now
where the time goes in v24:
time: 42.1 us; the launch traced here: 41.9 us
  waiting for transfers between devices  16.6 us (39%)
  starting transfers between devices  13.3 us (32%)
  Pallas kernels  10.1 us (24%)
  between operations  0.92 us (2%)
  local copies, waits for them, and re-layouts  0.81 us (2%)
    ppermute x1, waiting for transfers between devices, shards(): last = lax.ppermute(second_out, 'tile', around)  11.5 us
    pallas_call x1, Pallas kernels, shards(): pl.pallas_call(functools.partial(self_kernel, blocks, subs), in_specs=[sm...  6.26 us
    ppermute x1, starting transfers between devices, shards(): from_outer = lax.ppermute(first_out, 'tile', inward)  5.05 us
    ppermute x1, starting transfers between devices, shards(): home = lax.ppermute(cols, 'tile', turned(around))  3.23 us
    ppermute x1, waiting for transfers between devices, shards(): from_outer = lax.ppermute(first_out, 'tile', inward)  3.02 us
    ppermute x1, starting transfers between devices, shards(): last = lax.ppermute(second_out, 'tile', around)  2.11 us
    pallas_call x3, Pallas kernels, call(): pl.pallas_call(kernel, in_specs=[smem] + [vmem] * len(operands), out_spec...  2.09 us
    ppermute x1, starting transfers between devices, shards(): lax.ppermute(leaving, 'sub', [(i, i ^ 1 << bit) for i in range(subs)])  1.57 us
  transfers between devices with their start and end apart: 7, of which 4 were waited for; matrix products, arithmetic and copies ran while one was open for 1% of the time, Pallas kernels for 20%

profile of v24, /device:TPU:0, one launch (start us, length us, event | category | flops | bytes accessed | tf_op | source)
XLA Modules:
  0.0 41.9 jit_solution(6875079752926426320)
XLA Ops:
  0.0 0.0 copy-start.3
  0.0 1.1 %shard_map.30 = (bf16[264,1024]{1,0:T(8,128)(2,1)S(1)}, bf16[8,1024]{1,0:T(8,128)(2,1)S(1)}) custom-call(bf16[2048,1024]{1,0:T(8,128)(2,1)} %rows_ref.3, s32[16,128]{1,0:T(8,128)} %bitcast.63), custom_call_target="tpu_custom_call" | custom-call | bytes 1024 | tf_op jit(solution)/shard_map/pallas_call | solution.py:92
  1.1 5.0 %collective-permute-start.1 = (bf16[264,1024]{1,0:T(8,128)(2,1)S(1)}, bf16[264,1024]{1,0:T(8,128)(2,1)S(1)}, u32[]{:S(2)}, u32[]{:S(2)}) collective-permute-start(bf16[264,1024]{1,0:T(8,128)(2,1)S(1)} %get-tuple-element.56), channel_id=1, source_target_pairs={{0,4},{12,8},{1,5},{13,9},{2,6},{14,10},{3,7},{15,11},{16,20},{28,... | collective-permute-start | bytes 1622024 | tf_op jit(solution)/shard_map/ppermute | solution.py:313
  6.1 0.7 %collective-permute-start = (bf16[264,1024]{1,0:T(8,128)(2,1)S(1)}, bf16[264,1024]{1,0:T(8,128)(2,1)S(1)}, u32[]{:S(2)}, u32[]{:S(2)}) collective-permute-start(bf16[264,1024]{1,0:T(8,128)(2,1)S(1)} %get-tuple-element.56), channel_id=1, source_target_pairs={{4,8},{8,4},{5,9},{9,5},{6,10},{10,6},{7,11},{11,7},{20,24},{24,20... | collective-permute-start | bytes 1622024 | tf_op jit(solution)/shard_map/ppermute | solution.py:312
  6.8 0.0 copy-done.3
  6.9 0.1 convert_reduce_fusion
  7.1 0.1 dynamic_slice.47
  7.2 0.1 concatenate.3.meta_ref
  7.3 0.1 broadcast_in_dim.144
  7.4 6.3 %shard_map.31 = (bf16[2048,1024]{1,0:T(8,128)(2,1)S(1)}, f32[16,128]{1,0:T(8,128)S(1)}, bf16[264,1024]{1,0:T(8,128)(2,1)S(1)}) custom-call(s32[85]{0:T(128)S(1)} %concatenate.3.meta_ref, bf16[2048,1024]{1,0:T(8,128)(2,1)} %rows_ref.3, s32[1,512]{1,0:T(1,128)S(1)} %bitcast.62, bf16[8,1024]{1,0:T(8,128)(2,1)S(1)} %get-tuple-element.54.behind_ref), custom_call_target="tpu_custom_call" | custom-call | bytes 1024 | tf_op jit(solution)/shard_map/pallas_call | solution.py:336
  13.6 2.1 %collective-permute-start.2 = (bf16[264,1024]{1,0:T(8,128)(2,1)S(1)}, bf16[264,1024]{1,0:T(8,128)(2,1)S(1)}, u32[]{:S(2)}, u32[]{:S(2)}) collective-permute-start(bf16[264,1024]{1,0:T(8,128)(2,1)S(1)} %get-tuple-element.60), channel_id=1, source_target_pairs={{0,4},{12,8},{4,12},{8,0},{1,5},{13,9},{5,13},{9,1},{2,6},{14,10},... | collective-permute-start | bytes 1622024 | tf_op jit(solution)/shard_map/ppermute | solution.py:349
  15.8 3.0 %collective-permute-done.1.piece_ref = bf16[264,1024]{1,0:T(8,128)(2,1)S(1)} collective-permute-done((bf16[264,1024]{1,0:T(8,128)(2,1)S(1)}, bf16[264,1024]{1,0:T(8,128)(2,1)S(1)}, u32[]{:S(2)}, u32[]{:S(2)}) %collective-permute-start.1) | collective-permute-done | bytes 540704 | tf_op jit(solution)/shard_map/ppermute | solution.py:313
  18.8 0.7 %shard_map.32 = (f32[16,128]{1,0:T(8,128)S(1)}, f32[3,128]{1,0:T(4,128)S(1)}) custom-call(s32[85]{0:T(128)S(1)} %concatenate.3.meta_ref, bf16[2048,1024]{1,0:T(8,128)(2,1)S(1)} %get-tuple-element.55.unit_ref, bf16[264,1024]{1,0:T(8,128)(2,1)S(1)} %collective-permute-done.1.piece_ref, f32[16,128]{1,0:T(8,128)S(1)} %get-tuple-element.57.before_ref), custom_call_target="tpu_custom_call" | custom-call | flops 1073741824 | bytes 1024 | tf_op jit(solution)/shard_map/pallas_call | solution.py:239
  19.5 0.0 collective-permute-done.piece_ref
  19.5 0.7 %shard_map.33 = (f32[16,128]{1,0:T(8,128)S(1)}, f32[3,128]{1,0:T(4,128)S(1)}) custom-call(s32[85]{0:T(128)S(1)} %concatenate.3.meta_ref, bf16[2048,1024]{1,0:T(8,128)(2,1)S(1)} %get-tuple-element.55.unit_ref, bf16[264,1024]{1,0:T(8,128)(2,1)S(1)} %collective-permute-done.piece_ref, f32[16,128]{1,0:T(8,128)S(1)} %get-tuple-element.58.before_ref), custom_call_target="tpu_custom_call" | custom-call | flops 1073741824 | bytes 1024 | tf_op jit(solution)/shard_map/pallas_call | solution.py:239
  20.2 0.7 %collective-permute-start.3 = (f32[3,128]{1,0:T(4,128)S(1)}, f32[3,128]{1,0:T(4,128)S(1)}, u32[]{:S(2)}, u32[]{:S(2)}) collective-permute-start(f32[3,128]{1,0:T(4,128)S(1)} %get-tuple-element.59.swap_cols_ref.here_ref), channel_id=1, source_target_pairs={{8,4},{4,8},{9,5},{5,9},{10,6},{6,10},{11,7},{7,11},{24,20},{20,24... | collective-permute-start | bytes 4616 | tf_op jit(solution)/shard_map/ppermute | solution.py:363
  20.9 0.0 collective-permute-done.3
  20.9 11.5 %collective-permute-done.2.piece_ref = bf16[264,1024]{1,0:T(8,128)(2,1)S(1)} collective-permute-done((bf16[264,1024]{1,0:T(8,128)(2,1)S(1)}, bf16[264,1024]{1,0:T(8,128)(2,1)S(1)}, u32[]{:S(2)}, u32[]{:S(2)}) %collective-permute-start.2) | collective-permute-done | bytes 540704 | tf_op jit(solution)/shard_map/ppermute | solution.py:349
  32.4 0.7 %shard_map.34 = (f32[8,128]{1,0:T(8,128)S(1)}, f32[8,128]{1,0:T(8,128)S(1)}, f32[5,128]{1,0:T(8,128)S(1)}) custom-call(s32[85]{0:T(128)S(1)} %concatenate.3.meta_ref, bf16[2048,1024]{1,0:T(8,128)(2,1)S(1)} %get-tuple-element.55.unit_ref, bf16[264,1024]{1,0:T(8,128)(2,1)S(1)} %collective-permute-done.2.piece_ref, f32[16,128]{1,0:T(8,128)S(1)} %get-tuple-element.62.before_ref, ...), custom_call_target="tpu_custom_call" | custom-call | flops 1073741824 | bytes 1024 | tf_op jit(solution)/shard_map/pallas_call | solution.py:239
  33.1 3.2 %collective-permute-start.4 = (f32[5,128]{1,0:T(8,128)S(1)}, f32[5,128]{1,0:T(8,128)S(1)}, u32[]{:S(2)}, u32[]{:S(2)}) collective-permute-start(f32[5,128]{1,0:T(8,128)S(1)} %get-tuple-element.64), channel_id=1, source_target_pairs={{4,0},{8,12},{12,4},{0,8},{5,1},{9,13},{13,5},{1,9},{6,2},{10,14},... | collective-permute-start | bytes 7688 | tf_op jit(solution)/shard_map/ppermute | solution.py:378
  36.3 0.0 collective-permute-start.5
  36.3 1.3 %collective-permute-done.4.home_ref = f32[5,128]{1,0:T(8,128)S(1)} collective-permute-done((f32[5,128]{1,0:T(8,128)S(1)}, f32[5,128]{1,0:T(8,128)S(1)}, u32[]{:S(2)}, u32[]{:S(2)}) %collective-permute-start.4) | collective-permute-done | bytes 2592 | tf_op jit(solution)/shard_map/ppermute | solution.py:378
  37.6 0.0 collective-permute-done.5
  37.7 1.6 %collective-permute-start.6 = (f32[4,128]{1,0:T(4,128)S(1)}, f32[4,128]{1,0:T(4,128)S(1)}, u32[]{:S(2)}, u32[]{:S(2)}) collective-permute-start(f32[4,128]{1,0:T(4,128)S(1)} %get-tuple-element.75), channel_id=1, source_target_pairs={{0,2},{1,3},{2,0},{3,1},{4,6},{5,7},{6,4},{7,5},{8,10},{9,11},{10,... | collective-permute-start | bytes 6152 | tf_op jit(solution)/shard_map/ppermute | solution.py:389
  39.2 0.6 %shard_map.35 = s32[1]{0:T(128)} custom-call(f32[3,128]{1,0:T(4,128)S(1)} %get-tuple-element.59.swap_cols_ref.here_ref, f32[5,128]{1,0:T(8,128)S(1)} %collective-permute-done.4.home_ref), custom_call_target="tpu_custom_call" | custom-call | tf_op jit(solution)/shard_map/pallas_call | solution.py:392
  40.5 0.8 %collective-permute-done.6 = f32[4,128]{1,0:T(4,128)S(1)} collective-permute-done((f32[4,128]{1,0:T(4,128)S(1)}, f32[4,128]{1,0:T(4,128)S(1)}, u32[]{:S(2)}, u32[]{:S(2)}) %collective-permute-start.6) | collective-permute-done | bytes 2080 | tf_op jit(solution)/shard_map/ppermute | solution.py:389
  41.3 0.0 copy-start.4
  41.3 0.6 %copy-done.4 = f32[512]{0:T(512)} copy-done((f32[512]{0:T(512)}, f32[512]{0:T(512)S(1)}, u32[]{:S(2)}) %copy-start.4) | copy-done | bytes 2072
  (9 shorter events, 0.0 us)
Async XLA Ops:
  0.0 6.8 %copy-start.3 = (s32[2048]{0:T(1024)S(1)}, s32[2048]{0:T(1024)}, u32[]{:S(2)}) copy-start(s32[2048]{0:T(1024)} %param.5) | copy-start | bytes 24580
  1.1 17.7 %collective-permute-start.1 = (bf16[264,1024]{1,0:T(8,128)(2,1)S(1)}, bf16[264,1024]{1,0:T(8,128)(2,1)S(1)}, u32[]{:S(2)}, u32[]{:S(2)}) collective-permute-start(bf16[264,1024]{1,0:T(8,128)(2,1)S(1)} %get-tuple-element.56), channel_id=1, source_target_pairs={{0,4},{12,8},{1,5},{13,9},{2,6},{14,10},{3,7},{15,11},{16,20},{28,... | collective-permute-start | bytes 1622024 | tf_op jit(solution)/shard_map/ppermute | solution.py:313
  6.1 13.3 %collective-permute-start = (bf16[264,1024]{1,0:T(8,128)(2,1)S(1)}, bf16[264,1024]{1,0:T(8,128)(2,1)S(1)}, u32[]{:S(2)}, u32[]{:S(2)}) collective-permute-start(bf16[264,1024]{1,0:T(8,128)(2,1)S(1)} %get-tuple-element.56), channel_id=1, source_target_pairs={{4,8},{8,4},{5,9},{9,5},{6,10},{10,6},{7,11},{11,7},{20,24},{24,20... | collective-permute-start | bytes 1622024 | tf_op jit(solution)/shard_map/ppermute | solution.py:312
  13.6 18.7 %collective-permute-start.2 = (bf16[264,1024]{1,0:T(8,128)(2,1)S(1)}, bf16[264,1024]{1,0:T(8,128)(2,1)S(1)}, u32[]{:S(2)}, u32[]{:S(2)}) collective-permute-start(bf16[264,1024]{1,0:T(8,128)(2,1)S(1)} %get-tuple-element.60), channel_id=1, source_target_pairs={{0,4},{12,8},{4,12},{8,0},{1,5},{13,9},{5,13},{9,1},{2,6},{14,10},... | collective-permute-start | bytes 1622024 | tf_op jit(solution)/shard_map/ppermute | solution.py:349
  20.2 0.7 %collective-permute-start.3 = (f32[3,128]{1,0:T(4,128)S(1)}, f32[3,128]{1,0:T(4,128)S(1)}, u32[]{:S(2)}, u32[]{:S(2)}) collective-permute-start(f32[3,128]{1,0:T(4,128)S(1)} %get-tuple-element.59.swap_cols_ref.here_ref), channel_id=1, source_target_pairs={{8,4},{4,8},{9,5},{5,9},{10,6},{6,10},{11,7},{7,11},{24,20},{20,24... | collective-permute-start | bytes 4616 | tf_op jit(solution)/shard_map/ppermute | solution.py:363
  33.1 4.6 %collective-permute-start.4 = (f32[5,128]{1,0:T(8,128)S(1)}, f32[5,128]{1,0:T(8,128)S(1)}, u32[]{:S(2)}, u32[]{:S(2)}) collective-permute-start(f32[5,128]{1,0:T(8,128)S(1)} %get-tuple-element.64), channel_id=1, source_target_pairs={{4,0},{8,12},{12,4},{0,8},{5,1},{9,13},{13,5},{1,9},{6,2},{10,14},... | collective-permute-start | bytes 7688 | tf_op jit(solution)/shard_map/ppermute | solution.py:378
  36.3 1.3 %collective-permute-start.5 = (f32[8,128]{1,0:T(8,128)S(1)}, f32[8,128]{1,0:T(8,128)S(1)}, u32[]{:S(2)}, u32[]{:S(2)}) collective-permute-start(f32[8,128]{1,0:T(8,128)S(1)} %get-tuple-element.68), channel_id=1, source_target_pairs={{0,1},{1,0},{2,3},{3,2},{4,5},{5,4},{6,7},{7,6},{8,9},{9,8},{10,11... | collective-permute-start | bytes 12296 | tf_op jit(solution)/shard_map/ppermute | solution.py:382
  37.7 3.7 %collective-permute-start.6 = (f32[4,128]{1,0:T(4,128)S(1)}, f32[4,128]{1,0:T(4,128)S(1)}, u32[]{:S(2)}, u32[]{:S(2)}) collective-permute-start(f32[4,128]{1,0:T(4,128)S(1)} %get-tuple-element.75), channel_id=1, source_target_pairs={{0,2},{1,3},{2,0},{3,1},{4,6},{5,7},{6,4},{7,5},{8,10},{9,11},{10,... | collective-permute-start | bytes 6152 | tf_op jit(solution)/shard_map/ppermute | solution.py:389
  41.3 0.6 %copy-start.4 = (f32[512]{0:T(512)}, f32[512]{0:T(512)S(1)}, u32[]{:S(2)}) copy-start(f32[512]{0:T(512)S(1)} %get-tuple-element.109) | copy-start | bytes 6148

commit v25 on v22

--- a/solution.py
+++ b/solution.py
@@ -18,7 +18,7 @@
 GAIN = inverse_temp * math.log2(math.e)
 OFF = -1000.0
 
-STEP = 512
+STEP = 256
 COPY = 128
 
 

time: 41.3 us -> 41.3 us (level)
  no operation moved by 1% of the time
where the time goes in v25:
time: 41.3 us; the launch traced here: 41 us
  waiting for transfers between devices  15.9 us (38%)
  starting transfers between devices  13.2 us (32%)
  Pallas kernels  10.1 us (24%)
  between operations  0.93 us (2%)
  local copies, waits for them, and re-layouts  0.81 us (2%)
    ppermute x1, waiting for transfers between devices, shards(): last = lax.ppermute(second_out, 'tile', around)  10.2 us
    pallas_call x1, Pallas kernels, shards(): pl.pallas_call(functools.partial(self_kernel, blocks, subs), in_specs=[sm...  6.26 us
    ppermute x1, starting transfers between devices, shards(): from_outer = lax.ppermute(first_out, 'tile', inward)  5.05 us
    ppermute x1, waiting for transfers between devices, shards(): from_outer = lax.ppermute(first_out, 'tile', inward)  3.03 us
    pallas_call x3, Pallas kernels, call(): pl.pallas_call(kernel, in_specs=[smem] + [vmem] * len(operands), out_spec...  2.12 us
    ppermute x1, starting transfers between devices, shards(): last = lax.ppermute(second_out, 'tile', around)  2.11 us
    ppermute x1, starting transfers between devices, shards(): home = lax.ppermute(cols, 'tile', turned(around))  1.82 us
    ppermute x1, waiting for transfers between devices, shards(): home = lax.ppermute(cols, 'tile', turned(around))  1.81 us
  transfers between devices with their start and end apart: 8, of which 4 were waited for; matrix products, arithmetic and copies ran while one was open for 1% of the time, Pallas kernels for 22%

profile of v25, /device:TPU:0, one launch (start us, length us, event | category | flops | bytes accessed | tf_op | source)
XLA Modules:
  0.0 41.0 jit_solution(17057311025116975414)
XLA Ops:
  0.0 0.0 copy-start.3
  0.0 1.1 %shard_map.30 = (bf16[264,1024]{1,0:T(8,128)(2,1)S(1)}, bf16[8,1024]{1,0:T(8,128)(2,1)S(1)}) custom-call(bf16[2048,1024]{1,0:T(8,128)(2,1)} %rows_ref.3, s32[16,128]{1,0:T(8,128)} %bitcast.59), custom_call_target="tpu_custom_call" | custom-call | bytes 1024 | tf_op jit(solution)/shard_map/pallas_call | solution.py:92
  1.1 5.0 %collective-permute-start.1 = (bf16[264,1024]{1,0:T(8,128)(2,1)S(1)}, bf16[264,1024]{1,0:T(8,128)(2,1)S(1)}, u32[]{:S(2)}, u32[]{:S(2)}) collective-permute-start(bf16[264,1024]{1,0:T(8,128)(2,1)S(1)} %get-tuple-element.54), channel_id=1, source_target_pairs={{0,4},{12,8},{1,5},{13,9},{2,6},{14,10},{3,7},{15,11},{16,20},{28,... | collective-permute-start | bytes 1622024 | tf_op jit(solution)/shard_map/ppermute | solution.py:312
  6.1 0.7 %collective-permute-start = (bf16[264,1024]{1,0:T(8,128)(2,1)S(1)}, bf16[264,1024]{1,0:T(8,128)(2,1)S(1)}, u32[]{:S(2)}, u32[]{:S(2)}) collective-permute-start(bf16[264,1024]{1,0:T(8,128)(2,1)S(1)} %get-tuple-element.54), channel_id=1, source_target_pairs={{4,8},{8,4},{5,9},{9,5},{6,10},{10,6},{7,11},{11,7},{20,24},{24,20... | collective-permute-start | bytes 1622024 | tf_op jit(solution)/shard_map/ppermute | solution.py:311
  6.8 0.0 copy-done.3
  6.9 0.1 convert_reduce_fusion
  7.1 0.1 dynamic_slice.47
  7.2 0.1 concatenate.3.meta_ref
  7.3 0.1 broadcast_in_dim.128
  7.4 6.3 %shard_map.31 = (bf16[2048,1024]{1,0:T(8,128)(2,1)S(1)}, f32[16,128]{1,0:T(8,128)S(1)}, bf16[264,1024]{1,0:T(8,128)(2,1)S(1)}) custom-call(s32[85]{0:T(128)S(1)} %concatenate.3.meta_ref, bf16[2048,1024]{1,0:T(8,128)(2,1)} %rows_ref.3, s32[1,512]{1,0:T(1,128)S(1)} %bitcast.58, bf16[8,1024]{1,0:T(8,128)(2,1)S(1)} %get-tuple-element.52.behind_ref), custom_call_target="tpu_custom_call" | custom-call | bytes 1024 | tf_op jit(solution)/shard_map/pallas_call | solution.py:335
  13.6 2.1 %collective-permute-start.2 = (bf16[264,1024]{1,0:T(8,128)(2,1)S(1)}, bf16[264,1024]{1,0:T(8,128)(2,1)S(1)}, u32[]{:S(2)}, u32[]{:S(2)}) collective-permute-start(bf16[264,1024]{1,0:T(8,128)(2,1)S(1)} %get-tuple-element.58), channel_id=1, source_target_pairs={{0,4},{12,8},{4,12},{8,0},{1,5},{13,9},{5,13},{9,1},{2,6},{14,10},... | collective-permute-start | bytes 1622024 | tf_op jit(solution)/shard_map/ppermute | solution.py:348
  15.7 3.0 %collective-permute-done.1.piece_ref = bf16[264,1024]{1,0:T(8,128)(2,1)S(1)} collective-permute-done((bf16[264,1024]{1,0:T(8,128)(2,1)S(1)}, bf16[264,1024]{1,0:T(8,128)(2,1)S(1)}, u32[]{:S(2)}, u32[]{:S(2)}) %collective-permute-start.1) | collective-permute-done | bytes 540704 | tf_op jit(solution)/shard_map/ppermute | solution.py:312
  18.8 0.7 %shard_map.32 = (f32[16,128]{1,0:T(8,128)S(1)}, f32[3,128]{1,0:T(4,128)S(1)}) custom-call(s32[85]{0:T(128)S(1)} %concatenate.3.meta_ref, bf16[2048,1024]{1,0:T(8,128)(2,1)S(1)} %get-tuple-element.53.unit_ref, bf16[264,1024]{1,0:T(8,128)(2,1)S(1)} %collective-permute-done.1.piece_ref, f32[16,128]{1,0:T(8,128)S(1)} %get-tuple-element.55.before_ref), custom_call_target="tpu_custom_call" | custom-call | flops 1073741824 | bytes 1024 | tf_op jit(solution)/shard_map/pallas_call | solution.py:238
  19.5 1.3 %collective-permute-start.3 = (f32[3,128]{1,0:T(4,128)S(1)}, f32[3,128]{1,0:T(4,128)S(1)}, u32[]{:S(2)}, u32[]{:S(2)}) collective-permute-start(f32[3,128]{1,0:T(4,128)S(1)} %get-tuple-element.60), channel_id=1, source_target_pairs={{4,0},{8,12},{5,1},{9,13},{6,2},{10,14},{7,3},{11,15},{20,16},{24,... | collective-permute-start | bytes 4616 | tf_op jit(solution)/shard_map/ppermute | solution.py:361
  20.8 0.0 collective-permute-done.piece_ref
  20.8 0.7 %shard_map.33 = (f32[16,128]{1,0:T(8,128)S(1)}, f32[3,128]{1,0:T(4,128)S(1)}) custom-call(s32[85]{0:T(128)S(1)} %concatenate.3.meta_ref, bf16[2048,1024]{1,0:T(8,128)(2,1)S(1)} %get-tuple-element.53.unit_ref, bf16[264,1024]{1,0:T(8,128)(2,1)S(1)} %collective-permute-done.piece_ref, f32[16,128]{1,0:T(8,128)S(1)} %get-tuple-element.56.before_ref), custom_call_target="tpu_custom_call" | custom-call | flops 1073741824 | bytes 1024 | tf_op jit(solution)/shard_map/pallas_call | solution.py:238
  21.5 0.7 %collective-permute-start.5 = (f32[3,128]{1,0:T(4,128)S(1)}, f32[3,128]{1,0:T(4,128)S(1)}, u32[]{:S(2)}, u32[]{:S(2)}) collective-permute-start(f32[3,128]{1,0:T(4,128)S(1)} %get-tuple-element.57.swap_cols_ref.here_ref), channel_id=1, source_target_pairs={{8,4},{4,8},{9,5},{5,9},{10,6},{6,10},{11,7},{7,11},{24,20},{20,24... | collective-permute-start | bytes 4616 | tf_op jit(solution)/shard_map/ppermute | solution.py:363
  22.2 10.2 %collective-permute-done.2.piece_ref = bf16[264,1024]{1,0:T(8,128)(2,1)S(1)} collective-permute-done((bf16[264,1024]{1,0:T(8,128)(2,1)S(1)}, bf16[264,1024]{1,0:T(8,128)(2,1)S(1)}, u32[]{:S(2)}, u32[]{:S(2)}) %collective-permute-start.2) | collective-permute-done | bytes 540704 | tf_op jit(solution)/shard_map/ppermute | solution.py:348
  32.4 0.0 collective-permute-done.3.outer_back_ref
  32.4 0.7 %shard_map.34 = (f32[8,128]{1,0:T(8,128)S(1)}, f32[8,128]{1,0:T(8,128)S(1)}, f32[3,128]{1,0:T(4,128)S(1)}) custom-call(s32[85]{0:T(128)S(1)} %concatenate.3.meta_ref, bf16[2048,1024]{1,0:T(8,128)(2,1)S(1)} %get-tuple-element.53.unit_ref, bf16[264,1024]{1,0:T(8,128)(2,1)S(1)} %collective-permute-done.2.piece_ref, f32[16,128]{1,0:T(8,128)S(1)} %get-tuple-element.59.before_ref, ...), custom_call_target="tpu_custom_call" | custom-call | flops 1073741824 | bytes 1024 | tf_op jit(solution)/shard_map/pallas_call | solution.py:238
  33.1 1.8 %collective-permute-start.4 = (f32[3,128]{1,0:T(4,128)S(1)}, f32[3,128]{1,0:T(4,128)S(1)}, u32[]{:S(2)}, u32[]{:S(2)}) collective-permute-start(f32[3,128]{1,0:T(4,128)S(1)} %get-tuple-element.61), channel_id=1, source_target_pairs={{4,0},{8,12},{12,4},{0,8},{5,1},{9,13},{13,5},{1,9},{6,2},{10,14},... | collective-permute-start | bytes 4616 | tf_op jit(solution)/shard_map/ppermute | solution.py:377
  34.9 0.0 collective-permute-start.6
  34.9 0.0 collective-permute-done.5
  34.9 1.8 %collective-permute-done.4.home_ref = f32[3,128]{1,0:T(4,128)S(1)} collective-permute-done((f32[3,128]{1,0:T(4,128)S(1)}, f32[3,128]{1,0:T(4,128)S(1)}, u32[]{:S(2)}, u32[]{:S(2)}) %collective-permute-start.4) | collective-permute-done | bytes 1568 | tf_op jit(solution)/shard_map/ppermute | solution.py:377
  36.8 0.0 collective-permute-done.6
  36.8 1.6 %collective-permute-start.7 = (f32[4,128]{1,0:T(4,128)S(1)}, f32[4,128]{1,0:T(4,128)S(1)}, u32[]{:S(2)}, u32[]{:S(2)}) collective-permute-start(f32[4,128]{1,0:T(4,128)S(1)} %get-tuple-element.71), channel_id=1, source_target_pairs={{0,2},{1,3},{2,0},{3,1},{4,6},{5,7},{6,4},{7,5},{8,10},{9,11},{10,... | collective-permute-start | bytes 6152 | tf_op jit(solution)/shard_map/ppermute | solution.py:387
  38.3 0.6 %shard_map.35 = s32[1]{0:T(128)} custom-call(f32[3,128]{1,0:T(4,128)S(1)} %get-tuple-element.57.swap_cols_ref.here_ref, f32[3,128]{1,0:T(4,128)S(1)} %collective-permute-done.4.home_ref), custom_call_target="tpu_custom_call" | custom-call | tf_op jit(solution)/shard_map/pallas_call | solution.py:390
  39.6 0.8 %collective-permute-done.7 = f32[4,128]{1,0:T(4,128)S(1)} collective-permute-done((f32[4,128]{1,0:T(4,128)S(1)}, f32[4,128]{1,0:T(4,128)S(1)}, u32[]{:S(2)}, u32[]{:S(2)}) %collective-permute-start.7) | collective-permute-done | bytes 2080 | tf_op jit(solution)/shard_map/ppermute | solution.py:387
  40.4 0.0 copy-start.4
  40.5 0.6 %copy-done.4 = f32[512]{0:T(512)} copy-done((f32[512]{0:T(512)}, f32[512]{0:T(512)S(1)}, u32[]{:S(2)}) %copy-start.4) | copy-done | bytes 2072
  (9 shorter events, 0.0 us)
Async XLA Ops:
  0.0 6.8 %copy-start.3 = (s32[2048]{0:T(1024)S(1)}, s32[2048]{0:T(1024)}, u32[]{:S(2)}) copy-start(s32[2048]{0:T(1024)} %param.5) | copy-start | bytes 24580
  1.1 17.7 %collective-permute-start.1 = (bf16[264,1024]{1,0:T(8,128)(2,1)S(1)}, bf16[264,1024]{1,0:T(8,128)(2,1)S(1)}, u32[]{:S(2)}, u32[]{:S(2)}) collective-permute-start(bf16[264,1024]{1,0:T(8,128)(2,1)S(1)} %get-tuple-element.54), channel_id=1, source_target_pairs={{0,4},{12,8},{1,5},{13,9},{2,6},{14,10},{3,7},{15,11},{16,20},{28,... | collective-permute-start | bytes 1622024 | tf_op jit(solution)/shard_map/ppermute | solution.py:312
  6.1 14.6 %collective-permute-start = (bf16[264,1024]{1,0:T(8,128)(2,1)S(1)}, bf16[264,1024]{1,0:T(8,128)(2,1)S(1)}, u32[]{:S(2)}, u32[]{:S(2)}) collective-permute-start(bf16[264,1024]{1,0:T(8,128)(2,1)S(1)} %get-tuple-element.54), channel_id=1, source_target_pairs={{4,8},{8,4},{5,9},{9,5},{6,10},{10,6},{7,11},{11,7},{20,24},{24,20... | collective-permute-start | bytes 1622024 | tf_op jit(solution)/shard_map/ppermute | solution.py:311
  13.6 18.7 %collective-permute-start.2 = (bf16[264,1024]{1,0:T(8,128)(2,1)S(1)}, bf16[264,1024]{1,0:T(8,128)(2,1)S(1)}, u32[]{:S(2)}, u32[]{:S(2)}) collective-permute-start(bf16[264,1024]{1,0:T(8,128)(2,1)S(1)} %get-tuple-element.58), channel_id=1, source_target_pairs={{0,4},{12,8},{4,12},{8,0},{1,5},{13,9},{5,13},{9,1},{2,6},{14,10},... | collective-permute-start | bytes 1622024 | tf_op jit(solution)/shard_map/ppermute | solution.py:348
  19.5 12.9 %collective-permute-start.3 = (f32[3,128]{1,0:T(4,128)S(1)}, f32[3,128]{1,0:T(4,128)S(1)}, u32[]{:S(2)}, u32[]{:S(2)}) collective-permute-start(f32[3,128]{1,0:T(4,128)S(1)} %get-tuple-element.60), channel_id=1, source_target_pairs={{4,0},{8,12},{5,1},{9,13},{6,2},{10,14},{7,3},{11,15},{20,16},{24,... | collective-permute-start | bytes 4616 | tf_op jit(solution)/shard_map/ppermute | solution.py:361
  21.5 13.4 %collective-permute-start.5 = (f32[3,128]{1,0:T(4,128)S(1)}, f32[3,128]{1,0:T(4,128)S(1)}, u32[]{:S(2)}, u32[]{:S(2)}) collective-permute-start(f32[3,128]{1,0:T(4,128)S(1)} %get-tuple-element.57.swap_cols_ref.here_ref), channel_id=1, source_target_pairs={{8,4},{4,8},{9,5},{5,9},{10,6},{6,10},{11,7},{7,11},{24,20},{20,24... | collective-permute-start | bytes 4616 | tf_op jit(solution)/shard_map/ppermute | solution.py:363
  33.1 3.6 %collective-permute-start.4 = (f32[3,128]{1,0:T(4,128)S(1)}, f32[3,128]{1,0:T(4,128)S(1)}, u32[]{:S(2)}, u32[]{:S(2)}) collective-permute-start(f32[3,128]{1,0:T(4,128)S(1)} %get-tuple-element.61), channel_id=1, source_target_pairs={{4,0},{8,12},{12,4},{0,8},{5,1},{9,13},{13,5},{1,9},{6,2},{10,14},... | collective-permute-start | bytes 4616 | tf_op jit(solution)/shard_map/ppermute | solution.py:377
  34.9 1.8 %collective-permute-start.6 = (f32[8,128]{1,0:T(8,128)S(1)}, f32[8,128]{1,0:T(8,128)S(1)}, u32[]{:S(2)}, u32[]{:S(2)}) collective-permute-start(f32[8,128]{1,0:T(8,128)S(1)} %get-tuple-element.64), channel_id=1, source_target_pairs={{0,1},{1,0},{2,3},{3,2},{4,5},{5,4},{6,7},{7,6},{8,9},{9,8},{10,11... | collective-permute-start | bytes 12296 | tf_op jit(solution)/shard_map/ppermute | solution.py:380
  36.8 3.7 %collective-permute-start.7 = (f32[4,128]{1,0:T(4,128)S(1)}, f32[4,128]{1,0:T(4,128)S(1)}, u32[]{:S(2)}, u32[]{:S(2)}) collective-permute-start(f32[4,128]{1,0:T(4,128)S(1)} %get-tuple-element.71), channel_id=1, source_target_pairs={{0,2},{1,3},{2,0},{3,1},{4,6},{5,7},{6,4},{7,5},{8,10},{9,11},{10,... | collective-permute-start | bytes 6152 | tf_op jit(solution)/shard_map/ppermute | solution.py:387
  40.4 0.6 %copy-start.4 = (f32[512]{0:T(512)}, f32[512]{0:T(512)S(1)}, u32[]{:S(2)}) copy-start(f32[512]{0:T(512)S(1)} %get-tuple-element.105) | copy-start | bytes 6148
